TPU v7x, 32 devices: a whole 2x2x4 slice. The times are simulated.
32 devices in a mesh: section: 4 (over y, x), dp: 8 (over z, core).
Axes of the slice: x: 2, y: 2, z: 4, core: 2. Of those that a mesh axis runs over, the one named last changes fastest.
Arguments:
- section_inputs: bfloat16 [2, 4, 4, 1024, 1024], P(None, 'section', None, 'dp'), may hold values from -6 to 6
- top_grad: bfloat16 [2, 4, 1024, 1024], P(None, None, 'dp'), may hold values from -0.15625 to 0.15625
- plan: int32 [2, 4], replicated, may hold values from 0 to 3, each once within a row
- up_weight: bfloat16 [2, 4, 1024, 2048], P(None, 'section'), as said below
- down_weight: bfloat16 [2, 4, 2048, 1024], P(None, 'section'), as said below
- up_moment: float32 [4, 1024, 2048], P('section', 'dp'), may hold values from -6 to 6
- down_moment: float32 [4, 2048, 1024], P('section', 'dp'), may hold values from -6 to 6
Outputs:
- new_up_weight: bfloat16 [2, 4, 1024, 2048], P(None, 'section', 'dp')
- new_down_weight: bfloat16 [2, 4, 2048, 1024], P(None, 'section', 'dp')
- new_up_moment: float32 [4, 1024, 2048], P('section', 'dp')
- new_down_moment: float32 [4, 2048, 1024], P('section', 'dp')
Inputs may be any that keep to these rules, and one draw needn't show every extreme that they name: up_weight[1, s] equals up_weight[0, 3 - s] for every s: both relays hold the same model. down_weight[1, s] equals down_weight[0, 3 - s] for every s. `plan`: each row names every micro-batch once.
All inputs are finite; a program needn't handle non-finite values.
Results may differ from a plain program's by a relative error of at most 0.02.
Values may be sent and summed in bfloat16 or wider, within the bound.
No kernel may reach another device: no remote copies, remote signals or barrier semaphores. Data moves between devices by JAX's collectives and lax.ppermute only.
A program may use at most 128 MiB of HBM per device.

v0:
```python
import jax
import jax.numpy as jnp
from jax import lax
from jax.sharding import PartitionSpec as P

norm_epsilon = 1e-06
momentum_decay = 0.9
step_size = 0.01
root_half = 0.7071067811865476
inv_root_tau = 0.3989422804014327


def for_sending(x):

    def short(part):
        return part.astype(jnp.bfloat16) if part.dtype == jnp.float32 else part

    return jax.tree.map(short, x)


def from_behind(value, axis, steps):
    count = lax.axis_size(axis)
    leading, last = (max(0, -steps), min(count, count - steps))
    return lax.ppermute(value, axis, [(source, source + steps) for source in range(leading, last)])


def partner(x, axis, bit):
    return lax.ppermute(x, axis, [(i, i ^ 1 << bit) for i in range(lax.axis_size(axis))])


def gelu_value(preact):
    return 0.5 * preact * (1.0 + lax.erf(preact * root_half))


def gelu_slope(preact):
    return (
        0.5 * (1.0 + lax.erf(preact * root_half))
        + preact * jnp.exp(-0.5 * preact * preact) * inv_root_tau
    )


def times_transpose(left, right):
    return lax.dot_general(
        left, right, (((1,), (1,)), ((), ())), preferred_element_type=jnp.float32
    )


def contract_rows(left, right):
    return lax.dot_general(
        left, right, (((0,), (0,)), ((), ())), preferred_element_type=jnp.float32
    )


def local_backward(inputs, incoming, w_up, w_down):
    preact = jnp.dot(inputs, w_up, preferred_element_type=jnp.float32)
    hidden = gelu_value(preact).astype(jnp.bfloat16)
    summed = inputs.astype(jnp.float32) + jnp.dot(
        hidden, w_down, preferred_element_type=jnp.float32
    )
    centre = summed - jnp.mean(summed, axis=-1, keepdims=True)
    scale_inv = lax.rsqrt(jnp.mean(centre * centre, axis=-1, keepdims=True) + norm_epsilon)
    normed = centre * scale_inv
    upstream = incoming.astype(jnp.float32)
    grad_sum = scale_inv * (
        upstream
        - jnp.mean(upstream, axis=-1, keepdims=True)
        - normed * jnp.mean(upstream * normed, axis=-1, keepdims=True)
    )
    grad_sum_low = grad_sum.astype(jnp.bfloat16)
    grad_pre = (times_transpose(grad_sum_low, w_down) * gelu_slope(preact)).astype(jnp.bfloat16)
    grad_in = (grad_sum + times_transpose(grad_pre, w_up)).astype(jnp.bfloat16)
    return (grad_in, hidden, grad_pre, grad_sum_low)


def on_device(section_inputs, top_grad, plan, up_weight, down_weight, up_moment, down_moment):
    sections = lax.axis_size("section")
    position = lax.axis_index("section")
    micro = top_grad.shape[1]
    tokens = top_grad.shape[2]
    model = up_weight.shape[2]
    width = up_weight.shape[3]
    ordered = [section_inputs[direction, 0][plan[direction]] for direction in range(2)]
    starts = (sections - 1 - position, position)
    entries = (position == sections - 1, position == 0)

    def keep(state, slot, hidden, grad_pre, grad_sum_low):
        return (
            lax.dynamic_update_index_in_dim(state[0], hidden, slot, 0),
            lax.dynamic_update_index_in_dim(state[1], grad_pre, slot, 0),
            lax.dynamic_update_index_in_dim(state[2], grad_sum_low, slot, 0),
        )

    blank = (
        jnp.zeros((micro, tokens, width), jnp.bfloat16),
        jnp.zeros((micro, tokens, width), jnp.bfloat16),
        jnp.zeros((micro, tokens, model), jnp.bfloat16),
    )
    states = (blank, blank)

    def work(operand):
        state, incoming, inputs, slot, w_up, w_down = operand
        grad_in, hidden, grad_pre, grad_sum_low = local_backward(inputs, incoming, w_up, w_down)
        return (grad_in, keep(state, slot, hidden, grad_pre, grad_sum_low))

    def skip(operand):
        return (jnp.zeros_like(operand[1]), operand[0])

    def advance(tick, received, states):
        sent = []
        kept = []
        for direction in range(2):
            slot = tick - starts[direction]
            active = jnp.logical_and(slot >= 0, slot < micro)
            slot_safe = jnp.clip(slot, 0, micro - 1)
            inputs = lax.dynamic_index_in_dim(ordered[direction], slot_safe, 0, keepdims=False)
            arrived = lax.dynamic_index_in_dim(top_grad[direction], slot_safe, 0, keepdims=False)
            incoming = jnp.where(entries[direction], arrived, received[direction])
            operand = (
                states[direction],
                incoming,
                inputs,
                slot_safe,
                up_weight[direction, 0],
                down_weight[direction, 0],
            )
            grad_in, state = lax.cond(active, work, skip, operand)
            sent.append(grad_in)
            kept.append(state)
        return ((sent[0], sent[1]), (kept[0], kept[1]))

    def loop_step(tick, carry):
        received, states = carry
        sent, states = advance(tick, received, states)
        down_next = from_behind(for_sending(sent[0]), "section", -1)
        up_next = from_behind(for_sending(sent[1]), "section", 1)
        return ((down_next, up_next), states)

    empty = jnp.zeros((tokens, model), jnp.bfloat16)
    received, states = lax.fori_loop(0, sections + micro - 2, loop_step, ((empty, empty), states))
    sent, states = advance(sections + micro - 2, received, states)
    rows_up = up_moment.shape[1]
    rows_down = down_moment.shape[1]
    flat_inputs = [ordered[direction].reshape(micro * tokens, model) for direction in range(2)]
    flat_hidden = [states[direction][0].reshape(micro * tokens, width) for direction in range(2)]
    flat_pre = [states[direction][1].reshape(micro * tokens, width) for direction in range(2)]
    flat_sum = [states[direction][2].reshape(micro * tokens, model) for direction in range(2)]
    parts = [contract_rows(flat_inputs[direction], flat_pre[direction]) for direction in range(2)]
    summed_up = lax.psum_scatter(
        jnp.concatenate(parts, axis=1).astype(jnp.bfloat16), "dp", scatter_dimension=0, tiled=True
    ).astype(jnp.float32)
    parts = [contract_rows(flat_hidden[direction], flat_sum[direction]) for direction in range(2)]
    summed_down = lax.psum_scatter(
        jnp.concatenate(parts, axis=1).astype(jnp.bfloat16), "dp", scatter_dimension=0, tiled=True
    ).astype(jnp.float32)
    own_up, far_up = (summed_up[:, :width], summed_up[:, width:])
    own_down, far_down = (summed_down[:, :model], summed_down[:, model:])
    replica = lax.axis_index("dp")
    up_rows_held = lax.dynamic_slice_in_dim(up_weight[:, 0], replica * rows_up, rows_up, 1)
    down_rows_held = lax.dynamic_slice_in_dim(down_weight[:, 0], replica * rows_down, rows_down, 1)
    bits = sections.bit_length() - 1
    parcel = (far_up, far_down)
    for bit in range(bits):
        parcel = (
            partner(parcel[0].astype(jnp.bfloat16), "section", bit).astype(jnp.float32),
            partner(parcel[1].astype(jnp.bfloat16), "section", bit).astype(jnp.float32),
        )
    moment_up_new = momentum_decay * up_moment[0] + (own_up + parcel[0])
    moment_down_new = momentum_decay * down_moment[0] + (own_down + parcel[1])
    fresh_up = (up_rows_held[0].astype(jnp.float32) - step_size * moment_up_new).astype(
        jnp.bfloat16
    )
    fresh_down = (down_rows_held[0].astype(jnp.float32) - step_size * moment_down_new).astype(
        jnp.bfloat16
    )
    returned = (fresh_up, fresh_down)
    for bit in range(bits):
        returned = partner((returned[0], returned[1]), "section", bit)
    mirror_fresh_up, mirror_fresh_down = returned
    new_up_weight = jnp.stack([fresh_up, mirror_fresh_up])[:, None]
    new_down_weight = jnp.stack([fresh_down, mirror_fresh_down])[:, None]
    return (new_up_weight, new_down_weight, moment_up_new[None], moment_down_new[None])


def solution(mesh):
    in_specs = (
        P(None, "section", None, "dp", None),
        P(None, None, "dp", None),
        P(),
        P(None, "section", None, None),
        P(None, "section", None, None),
        P("section", "dp", None),
        P("section", "dp", None),
    )
    out_specs = (
        P(None, "section", "dp", None),
        P(None, "section", "dp", None),
        P("section", "dp", None),
        P("section", "dp", None),
    )
    return jax.shard_map(
        on_device, mesh=mesh, in_specs=in_specs, out_specs=out_specs, check_vma=False
    )
```

profile of v0, /device:TPU:0, one launch (start us, length us, event | category | flops | bytes accessed | tf_op | source)
XLA Modules:
  0.0 488.7 jit_solution(4034651854015491656)
XLA Ops:
  21.5 196.1 %while.27 = (s32[]{:T(128)}, bf16[128,1024]{1,0:T(8,128)(2,1)S(1)}, bf16[128,1024]{1,0:T(8,128)(2,1)S(1)}, bf16[4,128,2048]{2,1,0:T(8,128)(2,1)}, bf16[4,128,204...) while((s32[]{:T(128)}, bf16[128,1024]{1,0:T(8,128)(2,1)S(1)}, ...), condition=%wide.region_13.14_spmd, body=%wide.region_0.13_spmd.sunk | while | flops 4315414528 | bytes 162559888 | solution.py:139
  21.5 12.9 %conditional.9 = (bf16[128,1024]{1,0:T(8,128)(2,1)S(1)}, bf16[4,128,2048]{2,1,0:T(8,128)(2,1)}, bf16[4,128,2048]{2,1,0:T(8,128)(2,1)}, bf16[4,128,1024]{2,1,0:T(8,128)(2,1)}) conditional(s32[]{:T(128)} %convert_element_type.315, (bf16[4,128,2048]{2,1,0:T(8,128)(2,1)}, bf16[4,128,2048]{2,1,0:T(8,128)(2,1)}, ...), branch_computations={%region_7.7_spmd, %region_8.12_spmd} | conditional | flops 2157707264 | bytes 80231088 | solution.py:126
  21.6 4.1 bitcast_dynamic-update-slice_fusion.4
  25.6 3.2 fusion.157
  37.1 5.1 %collective-permute-done.1 = bf16[128,1024]{1,0:T(8,128)(2,1)S(1)} collective-permute-done((bf16[128,1024]{1,0:T(8,128)(2,1)S(1)}, bf16[128,1024]{1,0:T(8,128)(2,1)S(1)}, u32[]{:S(2)}, u32[]{:S(2)}) %collective-permute-start.1) | collective-permute-done | bytes 262176 | tf_op jit(solution)/shard_map/while/body/eval_jaxpr/ppermute | solution.py:24
  42.2 4.2 collective-permute-done
  46.4 12.9 %conditional.9 = (bf16[128,1024]{1,0:T(8,128)(2,1)S(1)}, bf16[4,128,2048]{2,1,0:T(8,128)(2,1)}, bf16[4,128,2048]{2,1,0:T(8,128)(2,1)}, bf16[4,128,1024]{2,1,0:T(8,128)(2,1)}) conditional(s32[]{:T(128)} %convert_element_type.315, (bf16[4,128,2048]{2,1,0:T(8,128)(2,1)}, bf16[4,128,2048]{2,1,0:T(8,128)(2,1)}, ...), branch_computations={%region_7.7_spmd, %region_8.12_spmd} | conditional | flops 2157707264 | bytes 80231088 | solution.py:126
  46.4 4.0 bitcast_dynamic-update-slice_fusion.4
  50.4 3.2 fusion.157
  62.1 4.1 collective-permute-done.1
  66.2 6.3 %collective-permute-done = bf16[128,1024]{1,0:T(8,128)(2,1)S(1)} collective-permute-done((bf16[128,1024]{1,0:T(8,128)(2,1)S(1)}, bf16[128,1024]{1,0:T(8,128)(2,1)S(1)}, u32[]{:S(2)}, u32[]{:S(2)}) %collective-permute-start) | collective-permute-done | bytes 262176 | tf_op jit(solution)/shard_map/while/body/eval_jaxpr/ppermute | solution.py:24
  72.4 12.8 %conditional.9 = (bf16[128,1024]{1,0:T(8,128)(2,1)S(1)}, bf16[4,128,2048]{2,1,0:T(8,128)(2,1)}, bf16[4,128,2048]{2,1,0:T(8,128)(2,1)}, bf16[4,128,1024]{2,1,0:T(8,128)(2,1)}) conditional(s32[]{:T(128)} %convert_element_type.315, (bf16[4,128,2048]{2,1,0:T(8,128)(2,1)}, bf16[4,128,2048]{2,1,0:T(8,128)(2,1)}, ...), branch_computations={%region_7.7_spmd, %region_8.12_spmd} | conditional | flops 2157707264 | bytes 80231088 | solution.py:126
  72.4 4.1 bitcast_dynamic-update-slice_fusion.4
  76.5 3.2 fusion.157
  88.1 3.5 collective-permute-done.1
  91.7 16.0 %collective-permute-done = bf16[128,1024]{1,0:T(8,128)(2,1)S(1)} collective-permute-done((bf16[128,1024]{1,0:T(8,128)(2,1)S(1)}, bf16[128,1024]{1,0:T(8,128)(2,1)S(1)}, u32[]{:S(2)}, u32[]{:S(2)}) %collective-permute-start) | collective-permute-done | bytes 262176 | tf_op jit(solution)/shard_map/while/body/eval_jaxpr/ppermute | solution.py:24
  107.7 12.8 %conditional.9 = (bf16[128,1024]{1,0:T(8,128)(2,1)S(1)}, bf16[4,128,2048]{2,1,0:T(8,128)(2,1)}, bf16[4,128,2048]{2,1,0:T(8,128)(2,1)}, bf16[4,128,1024]{2,1,0:T(8,128)(2,1)}) conditional(s32[]{:T(128)} %convert_element_type.315, (bf16[4,128,2048]{2,1,0:T(8,128)(2,1)}, bf16[4,128,2048]{2,1,0:T(8,128)(2,1)}, ...), branch_computations={%region_7.7_spmd, %region_8.12_spmd} | conditional | flops 2157707264 | bytes 80231088 | solution.py:126
  107.7 4.0 bitcast_dynamic-update-slice_fusion.4
  111.7 3.2 fusion.157
  120.5 4.6 collective-permute-start.1
  125.2 12.9 %conditional.8 = (bf16[128,1024]{1,0:T(8,128)(2,1)S(1)}, bf16[4,128,2048]{2,1,0:T(8,128)(2,1)}, bf16[4,128,2048]{2,1,0:T(8,128)(2,1)}, bf16[4,128,1024]{2,1,0:T(8,128)(2,1)}) conditional(s32[]{:T(128)} %convert_element_type.314, (bf16[4,128,2048]{2,1,0:T(8,128)(2,1)}, bf16[4,128,2048]{2,1,0:T(8,128)(2,1)}, ...), branch_computations={%region_1.1_spmd, %region_2.6_spmd} | conditional | flops 2157707264 | bytes 80231088 | solution.py:126
  125.2 4.1 bitcast_dynamic-update-slice_fusion.1
  129.3 3.2 fusion.156
  139.4 7.0 %collective-permute-done = bf16[128,1024]{1,0:T(8,128)(2,1)S(1)} collective-permute-done((bf16[128,1024]{1,0:T(8,128)(2,1)S(1)}, bf16[128,1024]{1,0:T(8,128)(2,1)S(1)}, u32[]{:S(2)}, u32[]{:S(2)}) %collective-permute-start) | collective-permute-done | bytes 262176 | tf_op jit(solution)/shard_map/while/body/eval_jaxpr/ppermute | solution.py:24
  146.4 15.6 %collective-permute-start.1 = (bf16[128,1024]{1,0:T(8,128)(2,1)S(1)}, bf16[128,1024]{1,0:T(8,128)(2,1)S(1)}, u32[]{:S(2)}, u32[]{:S(2)}) collective-permute-start(bf16[128,1024]{1,0:T(8,128)(2,1)S(1)} %get-tuple-element.954), channel_id=1, source_target_pairs={{0,8},{8,16},{16,24},{1,9},{9,17},{17,25},{2,10},{10,18},{18,26},{... | collective-permute-start | bytes 786440 | tf_op jit(solution)/shard_map/while/body/eval_jaxpr/ppermute | solution.py:24
  162.1 12.9 %conditional.8 = (bf16[128,1024]{1,0:T(8,128)(2,1)S(1)}, bf16[4,128,2048]{2,1,0:T(8,128)(2,1)}, bf16[4,128,2048]{2,1,0:T(8,128)(2,1)}, bf16[4,128,1024]{2,1,0:T(8,128)(2,1)}) conditional(s32[]{:T(128)} %convert_element_type.314, (bf16[4,128,2048]{2,1,0:T(8,128)(2,1)}, bf16[4,128,2048]{2,1,0:T(8,128)(2,1)}, ...), branch_computations={%region_1.1_spmd, %region_2.6_spmd} | conditional | flops 2157707264 | bytes 80231088 | solution.py:126
  162.1 4.1 bitcast_dynamic-update-slice_fusion.1
  166.2 3.2 fusion.156
  176.3 7.0 %collective-permute-done = bf16[128,1024]{1,0:T(8,128)(2,1)S(1)} collective-permute-done((bf16[128,1024]{1,0:T(8,128)(2,1)S(1)}, bf16[128,1024]{1,0:T(8,128)(2,1)S(1)}, u32[]{:S(2)}, u32[]{:S(2)}) %collective-permute-start) | collective-permute-done | bytes 262176 | tf_op jit(solution)/shard_map/while/body/eval_jaxpr/ppermute | solution.py:24
  186.2 12.9 %conditional.8 = (bf16[128,1024]{1,0:T(8,128)(2,1)S(1)}, bf16[4,128,2048]{2,1,0:T(8,128)(2,1)}, bf16[4,128,2048]{2,1,0:T(8,128)(2,1)}, bf16[4,128,1024]{2,1,0:T(8,128)(2,1)}) conditional(s32[]{:T(128)} %convert_element_type.314, (bf16[4,128,2048]{2,1,0:T(8,128)(2,1)}, bf16[4,128,2048]{2,1,0:T(8,128)(2,1)}, ...), branch_computations={%region_1.1_spmd, %region_2.6_spmd} | conditional | flops 2157707264 | bytes 80231088 | solution.py:126
  186.2 4.1 bitcast_dynamic-update-slice_fusion.1
  190.3 3.2 fusion.156
  200.4 17.2 %collective-permute-done = bf16[128,1024]{1,0:T(8,128)(2,1)S(1)} collective-permute-done((bf16[128,1024]{1,0:T(8,128)(2,1)S(1)}, bf16[128,1024]{1,0:T(8,128)(2,1)S(1)}, u32[]{:S(2)}, u32[]{:S(2)}) %collective-permute-start) | collective-permute-done | bytes 262176 | tf_op jit(solution)/shard_map/while/body/eval_jaxpr/ppermute | solution.py:24
  217.6 11.2 %conditional.4 = ((bf16[4,128,2048]{2,1,0:T(8,128)(2,1)}, bf16[4,128,2048]{2,1,0:T(8,128)(2,1)}, bf16[4,128,1024]{2,1,0:T(8,128)(2,1)})) conditional(s32[]{:T(128)} %convert_element_type.166, (bf16[4,128,2048]{2,1,0:T(8,128)(2,1)}, bf16[4,128,2048]{2,1,0:T(8,128)(2,1)}, bf16[4,128,1024]{2,1,0:T(8,128)(2,1)}) %tuple.69, (s32[]{:T(128)}, ...), branch_computations={%region_14.15_spmd, %region_15.20_spmd} | conditional | flops 1619656832 | bytes 48771704 | solution.py:126
  217.6 4.0 bitcast_dynamic-update-slice_fusion.6
  221.7 3.2 fusion.158
  228.9 6.2 %bitcast_convert_fusion.1 = bf16[2048,1024]{0,1:T(8,128)(2,1)} fusion(bf16[4,128,2048]{2,1,0:T(8,128)(2,1)} %get-tuple-element.742, bf16[4,128,1024]{2,1,0:T(8,128)(2,1)} %get-tuple-element.743), kind=kOutput, calls=%fused_computation.169 | convolution fusion | flops 2149580800 | bytes 7340032 | tf_op jit(solution)/shard_map/dot_general | solution.py:49
  235.1 6.2 %bitcast_convert_fusion = bf16[2048,1024]{0,1:T(8,128)(2,1)} fusion(bf16[4,128,2048]{2,1,0:T(8,128)(2,1)} %get-tuple-element.744, bf16[4,128,1024]{2,1,0:T(8,128)(2,1)} %get-tuple-element.745), kind=kOutput, calls=%fused_computation.168 | convolution fusion | flops 2149580800 | bytes 7340032 | tf_op jit(solution)/shard_map/dot_general | solution.py:49
  241.2 8.4 %pad_maximum_fusion.1 = bf16[2048,2048]{0,1:T(8,128)(2,1)} fusion(bf16[2048,1024]{0,1:T(8,128)(2,1)} %bitcast_convert_fusion, bf16[2048,1024]{0,1:T(8,128)(2,1)} %bitcast_convert_fusion.1), kind=kLoop, calls=%fused_computation.167 | loop fusion | flops 16777216 | bytes 16777216 | tf_op jit(solution)/shard_map/concatenate | solution.py:153
  251.2 5.7 %bitcast_convert_fusion.3 = bf16[1024,2048]{1,0:T(8,128)(2,1)} fusion(bf16[4,128,1024]{2,1,0:T(8,128)(2,1)} %get-tuple-element.1071, bf16[4,128,2048]{2,1,0:T(8,128)(2,1)S(1)} %copy-done.1), kind=kOutput, calls=%fused_computation.171 | convolution fusion | flops 2149580800 | bytes 7340032 | tf_op jit(solution)/shard_map/dot_general | solution.py:49
  256.9 4.4 bitcast_convert_fusion.2
  261.4 7.9 %pad_maximum_fusion = bf16[1024,4096]{1,0:T(8,128)(2,1)} fusion(bf16[1024,2048]{1,0:T(8,128)(2,1)} %bitcast_convert_fusion.2, bf16[1024,2048]{1,0:T(8,128)(2,1)} %bitcast_convert_fusion.3), kind=kLoop, calls=%fused_computation.166 | loop fusion | flops 16777216 | bytes 16777216 | tf_op jit(solution)/shard_map/concatenate | solution.py:149
  269.3 69.6 %reduce-scatter.5.cloned.1.call-done = bf16[256,2048]{0,1:T(8,128)(2,1)} async-done(((bf16[2048,2048]{0,1:T(8,128)(2,1)}), bf16[256,2048]{0,1:T(8,128)(2,1)}) %reduce-scatter.5.cloned.1.call-update) | async-done | bytes 1048592 | tf_op jit(solution)/shard_map/reduce_scatter | solution.py:152
  341.4 87.7 %reduce-scatter.3.cloned.1.call-done = bf16[128,4096]{1,0:T(8,128)(2,1)} async-done(((bf16[1024,4096]{1,0:T(8,128)(2,1)}), bf16[128,4096]{1,0:T(8,128)(2,1)}) %reduce-scatter.3.cloned.1.call-update) | async-done | bytes 1048592 | tf_op jit(solution)/shard_map/reduce_scatter | solution.py:148
  433.2 8.7 %collective-permute-done.2 = bf16[128,2048]{1,0:T(8,128)(2,1)} collective-permute-done((bf16[128,2048]{1,0:T(8,128)(2,1)S(1)}, bf16[128,2048]{1,0:T(8,128)(2,1)}, u32[]{:S(2)}, u32[]{:S(2)}) %collective-permute-start.2) | collective-permute-done | bytes 524320 | tf_op jit(solution)/shard_map/ppermute | solution.py:28
  449.3 5.1 %collective-permute-done.3 = bf16[128,2048]{1,0:T(8,128)(2,1)} collective-permute-done((bf16[128,2048]{1,0:T(8,128)(2,1)}, bf16[128,2048]{1,0:T(8,128)(2,1)}, u32[]{:S(2)}, u32[]{:S(2)}) %collective-permute-start.3) | collective-permute-done | bytes 524320 | tf_op jit(solution)/shard_map/ppermute | solution.py:28
  459.3 10.1 %collective-permute-done.4 = bf16[128,2048]{1,0:T(8,128)(2,1)} collective-permute-done((bf16[128,2048]{1,0:T(8,128)(2,1)S(1)}, bf16[128,2048]{1,0:T(8,128)(2,1)}, u32[]{:S(2)}, u32[]{:S(2)}) %collective-permute-start.4) | collective-permute-done | bytes 524320 | tf_op jit(solution)/shard_map/ppermute | solution.py:28
  472.8 8.0 %collective-permute-done.5 = bf16[128,2048]{1,0:T(8,128)(2,1)S(1)} collective-permute-done((bf16[128,2048]{1,0:T(8,128)(2,1)}, bf16[128,2048]{1,0:T(8,128)(2,1)S(1)}, u32[]{:S(2)}, u32[]{:S(2)}) %collective-permute-start.5) | collective-permute-done | bytes 524320 | tf_op jit(solution)/shard_map/ppermute | solution.py:28
  (218 shorter events, 97.1 us)
Async XLA Ops:
  7.2 331.7 %reduce-scatter.5.cloned.1.call-start = ((), (), s32[]{:S(2)}) async-start(), calls=%async_computation.3 | async-start | bytes 9437184 | tf_op jit(solution)/shard_map/reduce_scatter | solution.py:152
  14.5 7.0 %copy-start = (bf16[2,4,128,1024]{3,2,1,0:T(8,128)(2,1)S(1)}, bf16[2,4,128,1024]{3,2,1,0:T(8,128)(2,1)}, u32[]{:S(2)}) copy-start(bf16[2,4,128,1024]{3,2,1,0:T(8,128)(2,1)} %param.18) | copy-start | bytes 6291460
  21.5 8.8 %slice-start.4 = ((s8[8388608]{0:T(1024)(128)(4,1)}), s8[4194304]{0:T(1024)(128)(4,1)S(1)}, s32[]{:S(2)}) async-start(s8[8388608]{0:T(1024)(128)(4,1)} %bitcast.232), calls=%async_computation.8 | async-start | bytes 8388608 | tf_op jit(solution)/shard_map/while/body/eval_jaxpr/cond
  25.6 4.7 slice-start.5
  25.6 7.2 %slice-start = ((s8[8388608]{0:T(1024)(128)(4,1)}), s8[4194304]{0:T(1024)(128)(4,1)S(1)}, s32[]{:S(2)}) async-start(s8[8388608]{0:T(1024)(128)(4,1)} %bitcast.228), calls=%async_computation.4 | async-start | bytes 8388608 | tf_op jit(solution)/shard_map/while/body/eval_jaxpr/cond
  34.4 7.7 %collective-permute-start.1 = (bf16[128,1024]{1,0:T(8,128)(2,1)S(1)}, bf16[128,1024]{1,0:T(8,128)(2,1)S(1)}, u32[]{:S(2)}, u32[]{:S(2)}) collective-permute-start(bf16[128,1024]{1,0:T(8,128)(2,1)S(1)} %get-tuple-element.954), channel_id=1, source_target_pairs={{0,8},{8,16},{16,24},{1,9},{9,17},{17,25},{2,10},{10,18},{18,26},{... | collective-permute-start | bytes 786440 | tf_op jit(solution)/shard_map/while/body/eval_jaxpr/ppermute | solution.py:24
  35.8 10.6 %collective-permute-start = (bf16[128,1024]{1,0:T(8,128)(2,1)S(1)}, bf16[128,1024]{1,0:T(8,128)(2,1)S(1)}, u32[]{:S(2)}, u32[]{:S(2)}) collective-permute-start(bf16[128,1024]{1,0:T(8,128)(2,1)S(1)} %get-tuple-element.953), channel_id=1, source_target_pairs={{8,0},{16,8},{24,16},{9,1},{17,9},{25,17},{10,2},{18,10},{26,18},{... | collective-permute-start | bytes 786440 | tf_op jit(solution)/shard_map/while/body/eval_jaxpr/ppermute | solution.py:24
  46.4 8.8 %slice-start.4 = ((s8[8388608]{0:T(1024)(128)(4,1)}), s8[4194304]{0:T(1024)(128)(4,1)S(1)}, s32[]{:S(2)}) async-start(s8[8388608]{0:T(1024)(128)(4,1)} %bitcast.232), calls=%async_computation.8 | async-start | bytes 8388608 | tf_op jit(solution)/shard_map/while/body/eval_jaxpr/cond
  50.4 4.7 slice-start.5
  50.4 7.2 %slice-start = ((s8[8388608]{0:T(1024)(128)(4,1)}), s8[4194304]{0:T(1024)(128)(4,1)S(1)}, s32[]{:S(2)}) async-start(s8[8388608]{0:T(1024)(128)(4,1)} %bitcast.228), calls=%async_computation.4 | async-start | bytes 8388608 | tf_op jit(solution)/shard_map/while/body/eval_jaxpr/cond
  59.2 7.0 %collective-permute-start.1 = (bf16[128,1024]{1,0:T(8,128)(2,1)S(1)}, bf16[128,1024]{1,0:T(8,128)(2,1)S(1)}, u32[]{:S(2)}, u32[]{:S(2)}) collective-permute-start(bf16[128,1024]{1,0:T(8,128)(2,1)S(1)} %get-tuple-element.954), channel_id=1, source_target_pairs={{0,8},{8,16},{16,24},{1,9},{9,17},{17,25},{2,10},{10,18},{18,26},{... | collective-permute-start | bytes 786440 | tf_op jit(solution)/shard_map/while/body/eval_jaxpr/ppermute | solution.py:24
  60.8 11.7 %collective-permute-start = (bf16[128,1024]{1,0:T(8,128)(2,1)S(1)}, bf16[128,1024]{1,0:T(8,128)(2,1)S(1)}, u32[]{:S(2)}, u32[]{:S(2)}) collective-permute-start(bf16[128,1024]{1,0:T(8,128)(2,1)S(1)} %get-tuple-element.953), channel_id=1, source_target_pairs={{8,0},{16,8},{24,16},{9,1},{17,9},{25,17},{10,2},{18,10},{26,18},{... | collective-permute-start | bytes 786440 | tf_op jit(solution)/shard_map/while/body/eval_jaxpr/ppermute | solution.py:24
  72.4 8.8 %slice-start.4 = ((s8[8388608]{0:T(1024)(128)(4,1)}), s8[4194304]{0:T(1024)(128)(4,1)S(1)}, s32[]{:S(2)}) async-start(s8[8388608]{0:T(1024)(128)(4,1)} %bitcast.232), calls=%async_computation.8 | async-start | bytes 8388608 | tf_op jit(solution)/shard_map/while/body/eval_jaxpr/cond
  76.5 4.7 slice-start.5
  76.5 7.2 %slice-start = ((s8[8388608]{0:T(1024)(128)(4,1)}), s8[4194304]{0:T(1024)(128)(4,1)S(1)}, s32[]{:S(2)}) async-start(s8[8388608]{0:T(1024)(128)(4,1)} %bitcast.228), calls=%async_computation.4 | async-start | bytes 8388608 | tf_op jit(solution)/shard_map/while/body/eval_jaxpr/cond
  85.3 6.4 %collective-permute-start.1 = (bf16[128,1024]{1,0:T(8,128)(2,1)S(1)}, bf16[128,1024]{1,0:T(8,128)(2,1)S(1)}, u32[]{:S(2)}, u32[]{:S(2)}) collective-permute-start(bf16[128,1024]{1,0:T(8,128)(2,1)S(1)} %get-tuple-element.954), channel_id=1, source_target_pairs={{0,8},{8,16},{16,24},{1,9},{9,17},{17,25},{2,10},{10,18},{18,26},{... | collective-permute-start | bytes 786440 | tf_op jit(solution)/shard_map/while/body/eval_jaxpr/ppermute | solution.py:24
  86.8 20.8 %collective-permute-start = (bf16[128,1024]{1,0:T(8,128)(2,1)S(1)}, bf16[128,1024]{1,0:T(8,128)(2,1)S(1)}, u32[]{:S(2)}, u32[]{:S(2)}) collective-permute-start(bf16[128,1024]{1,0:T(8,128)(2,1)S(1)} %get-tuple-element.953), channel_id=1, source_target_pairs={{8,0},{16,8},{24,16},{9,1},{17,9},{25,17},{10,2},{18,10},{26,18},{... | collective-permute-start | bytes 786440 | tf_op jit(solution)/shard_map/while/body/eval_jaxpr/ppermute | solution.py:24
  107.7 8.8 %slice-start.4 = ((s8[8388608]{0:T(1024)(128)(4,1)}), s8[4194304]{0:T(1024)(128)(4,1)S(1)}, s32[]{:S(2)}) async-start(s8[8388608]{0:T(1024)(128)(4,1)} %bitcast.232), calls=%async_computation.8 | async-start | bytes 8388608 | tf_op jit(solution)/shard_map/while/body/eval_jaxpr/cond
  111.7 4.7 slice-start.5
  111.7 7.3 %slice-start = ((s8[8388608]{0:T(1024)(128)(4,1)}), s8[4194304]{0:T(1024)(128)(4,1)S(1)}, s32[]{:S(2)}) async-start(s8[8388608]{0:T(1024)(128)(4,1)} %bitcast.228), calls=%async_computation.4 | async-start | bytes 8388608 | tf_op jit(solution)/shard_map/while/body/eval_jaxpr/cond
  120.5 18.9 %collective-permute-start.1 = (bf16[128,1024]{1,0:T(8,128)(2,1)S(1)}, bf16[128,1024]{1,0:T(8,128)(2,1)S(1)}, u32[]{:S(2)}, u32[]{:S(2)}) collective-permute-start(bf16[128,1024]{1,0:T(8,128)(2,1)S(1)} %get-tuple-element.954), channel_id=1, source_target_pairs={{0,8},{8,16},{16,24},{1,9},{9,17},{17,25},{2,10},{10,18},{18,26},{... | collective-permute-start | bytes 786440 | tf_op jit(solution)/shard_map/while/body/eval_jaxpr/ppermute | solution.py:24
  125.2 8.8 %slice-start.6 = ((s8[8388608]{0:T(1024)(128)(4,1)}), s8[4194304]{0:T(1024)(128)(4,1)S(1)}, s32[]{:S(2)}) async-start(s8[8388608]{0:T(1024)(128)(4,1)} %bitcast.234), calls=%async_computation.10 | async-start | bytes 8388608 | tf_op jit(solution)/shard_map/while/body/eval_jaxpr/cond
  129.3 4.7 slice-start.7
  129.3 7.2 %slice-start.2 = ((s8[8388608]{0:T(1024)(128)(4,1)}), s8[4194304]{0:T(1024)(128)(4,1)S(1)}, s32[]{:S(2)}) async-start(s8[8388608]{0:T(1024)(128)(4,1)} %bitcast.230), calls=%async_computation.6 | async-start | bytes 8388608 | tf_op jit(solution)/shard_map/while/body/eval_jaxpr/cond
  138.1 8.3 %collective-permute-start = (bf16[128,1024]{1,0:T(8,128)(2,1)S(1)}, bf16[128,1024]{1,0:T(8,128)(2,1)S(1)}, u32[]{:S(2)}, u32[]{:S(2)}) collective-permute-start(bf16[128,1024]{1,0:T(8,128)(2,1)S(1)} %get-tuple-element.953), channel_id=1, source_target_pairs={{8,0},{16,8},{24,16},{9,1},{17,9},{25,17},{10,2},{18,10},{26,18},{... | collective-permute-start | bytes 786440 | tf_op jit(solution)/shard_map/while/body/eval_jaxpr/ppermute | solution.py:24
  146.4 29.9 %collective-permute-start.1 = (bf16[128,1024]{1,0:T(8,128)(2,1)S(1)}, bf16[128,1024]{1,0:T(8,128)(2,1)S(1)}, u32[]{:S(2)}, u32[]{:S(2)}) collective-permute-start(bf16[128,1024]{1,0:T(8,128)(2,1)S(1)} %get-tuple-element.954), channel_id=1, source_target_pairs={{0,8},{8,16},{16,24},{1,9},{9,17},{17,25},{2,10},{10,18},{18,26},{... | collective-permute-start | bytes 786440 | tf_op jit(solution)/shard_map/while/body/eval_jaxpr/ppermute | solution.py:24
  162.1 8.8 %slice-start.6 = ((s8[8388608]{0:T(1024)(128)(4,1)}), s8[4194304]{0:T(1024)(128)(4,1)S(1)}, s32[]{:S(2)}) async-start(s8[8388608]{0:T(1024)(128)(4,1)} %bitcast.234), calls=%async_computation.10 | async-start | bytes 8388608 | tf_op jit(solution)/shard_map/while/body/eval_jaxpr/cond
  166.2 4.7 slice-start.7
  166.2 7.2 %slice-start.2 = ((s8[8388608]{0:T(1024)(128)(4,1)}), s8[4194304]{0:T(1024)(128)(4,1)S(1)}, s32[]{:S(2)}) async-start(s8[8388608]{0:T(1024)(128)(4,1)} %bitcast.230), calls=%async_computation.6 | async-start | bytes 8388608 | tf_op jit(solution)/shard_map/while/body/eval_jaxpr/cond
  175.0 8.3 %collective-permute-start = (bf16[128,1024]{1,0:T(8,128)(2,1)S(1)}, bf16[128,1024]{1,0:T(8,128)(2,1)S(1)}, u32[]{:S(2)}, u32[]{:S(2)}) collective-permute-start(bf16[128,1024]{1,0:T(8,128)(2,1)S(1)} %get-tuple-element.953), channel_id=1, source_target_pairs={{8,0},{16,8},{24,16},{9,1},{17,9},{25,17},{10,2},{18,10},{26,18},{... | collective-permute-start | bytes 786440 | tf_op jit(solution)/shard_map/while/body/eval_jaxpr/ppermute | solution.py:24
  183.3 17.1 %collective-permute-start.1 = (bf16[128,1024]{1,0:T(8,128)(2,1)S(1)}, bf16[128,1024]{1,0:T(8,128)(2,1)S(1)}, u32[]{:S(2)}, u32[]{:S(2)}) collective-permute-start(bf16[128,1024]{1,0:T(8,128)(2,1)S(1)} %get-tuple-element.954), channel_id=1, source_target_pairs={{0,8},{8,16},{16,24},{1,9},{9,17},{17,25},{2,10},{10,18},{18,26},{... | collective-permute-start | bytes 786440 | tf_op jit(solution)/shard_map/while/body/eval_jaxpr/ppermute | solution.py:24
  186.2 8.8 %slice-start.6 = ((s8[8388608]{0:T(1024)(128)(4,1)}), s8[4194304]{0:T(1024)(128)(4,1)S(1)}, s32[]{:S(2)}) async-start(s8[8388608]{0:T(1024)(128)(4,1)} %bitcast.234), calls=%async_computation.10 | async-start | bytes 8388608 | tf_op jit(solution)/shard_map/while/body/eval_jaxpr/cond
  190.3 4.7 slice-start.7
  190.3 7.3 %slice-start.2 = ((s8[8388608]{0:T(1024)(128)(4,1)}), s8[4194304]{0:T(1024)(128)(4,1)S(1)}, s32[]{:S(2)}) async-start(s8[8388608]{0:T(1024)(128)(4,1)} %bitcast.230), calls=%async_computation.6 | async-start | bytes 8388608 | tf_op jit(solution)/shard_map/while/body/eval_jaxpr/cond
  199.1 18.5 %collective-permute-start = (bf16[128,1024]{1,0:T(8,128)(2,1)S(1)}, bf16[128,1024]{1,0:T(8,128)(2,1)S(1)}, u32[]{:S(2)}, u32[]{:S(2)}) collective-permute-start(bf16[128,1024]{1,0:T(8,128)(2,1)S(1)} %get-tuple-element.953), channel_id=1, source_target_pairs={{8,0},{16,8},{24,16},{9,1},{17,9},{25,17},{10,2},{18,10},{26,18},{... | collective-permute-start | bytes 786440 | tf_op jit(solution)/shard_map/while/body/eval_jaxpr/ppermute | solution.py:24
  217.6 8.8 %slice-start.8 = ((s8[8388608]{0:T(1024)(128)(4,1)}), s8[4194304]{0:T(1024)(128)(4,1)S(1)}, s32[]{:S(2)}) async-start(s8[8388608]{0:T(1024)(128)(4,1)} %bitcast.236), calls=%async_computation.12 | async-start | bytes 8388608 | tf_op jit(solution)/shard_map/cond
  221.7 4.7 slice-start.9
  249.7 179.4 %reduce-scatter.3.cloned.1.call-start = ((), (), s32[]{:S(2)}) async-start(), calls=%async_computation.2 | async-start | bytes 9437184 | tf_op jit(solution)/shard_map/reduce_scatter | solution.py:148
  251.2 5.7 %copy-start.2 = (bf16[4,128,2048]{2,1,0:T(8,128)(2,1)S(1)}, bf16[4,128,2048]{2,1,0:T(8,128)(2,1)}, u32[]{:S(2)}) copy-start(bf16[4,128,2048]{2,1,0:T(8,128)(2,1)} %get-tuple-element.741) | copy-start | bytes 6291460
  251.2 5.7 %copy-start.3 = (bf16[4,128,1024]{2,1,0:T(8,128)(2,1)S(1)}, bf16[4,128,1024]{2,1,0:T(8,128)(2,1)}, u32[]{:S(2)}) copy-start(bf16[4,128,1024]{2,1,0:T(8,128)(2,1)} %get-tuple-element.1072) | copy-start | bytes 3145732
  339.9 91.8 %collective-permute-start.6 = (bf16[256,1024]{0,1:T(8,128)(2,1)S(1)}, bf16[256,1024]{0,1:T(8,128)(2,1)S(1)}, u32[]{:S(2)}, u32[]{:S(2)}) collective-permute-start(bf16[256,1024]{0,1:T(8,128)(2,1)S(1)} %slice.155), channel_id=1, source_target_pairs={{0,8},{8,0},{16,24},{24,16},{1,9},{9,1},{17,25},{25,17},{2,10},{10... | collective-permute-start | bytes 1572872 | tf_op jit(solution)/shard_map/ppermute | solution.py:28
  430.2 11.7 %collective-permute-start.2 = (bf16[128,2048]{1,0:T(8,128)(2,1)S(1)}, bf16[128,2048]{1,0:T(8,128)(2,1)}, u32[]{:S(2)}, u32[]{:S(2)}) collective-permute-start(bf16[128,2048]{1,0:T(8,128)(2,1)S(1)} %slice.153), channel_id=1, source_target_pairs={{0,8},{8,0},{16,24},{24,16},{1,9},{9,1},{17,25},{25,17},{2,10},{10... | collective-permute-start | bytes 1572872 | tf_op jit(solution)/shard_map/ppermute | solution.py:28
  431.7 14.5 %collective-permute-start.7 = (bf16[256,1024]{0,1:T(8,128)(2,1)S(1)}, bf16[256,1024]{0,1:T(8,128)(2,1)}, u32[]{:S(2)}, u32[]{:S(2)}) collective-permute-start(bf16[256,1024]{0,1:T(8,128)(2,1)S(1)} %collective-permute-done.6), channel_id=1, source_target_pairs={{0,16},{8,24},{16,0},{24,8},{1,17},{9,25},{17,1},{25,9},{2,18},{10... | collective-permute-start | bytes 1572872 | tf_op jit(solution)/shard_map/ppermute | solution.py:28
  441.9 12.4 %collective-permute-start.3 = (bf16[128,2048]{1,0:T(8,128)(2,1)}, bf16[128,2048]{1,0:T(8,128)(2,1)}, u32[]{:S(2)}, u32[]{:S(2)}) collective-permute-start(bf16[128,2048]{1,0:T(8,128)(2,1)} %collective-permute-done.2), channel_id=1, source_target_pairs={{0,16},{8,24},{16,0},{24,8},{1,17},{9,25},{17,1},{25,9},{2,18},{10... | collective-permute-start | bytes 1572872 | tf_op jit(solution)/shard_map/ppermute | solution.py:28
  447.7 11.3 %collective-permute-start.8 = (bf16[256,1024]{0,1:T(8,128)(2,1)S(1)}, bf16[256,1024]{0,1:T(8,128)(2,1)}, u32[]{:S(2)}, u32[]{:S(2)}) collective-permute-start(bf16[256,1024]{0,1:T(8,128)(2,1)S(1)} %get-tuple-element.827), channel_id=1, source_target_pairs={{0,8},{8,0},{16,24},{24,16},{1,9},{9,1},{17,25},{25,17},{2,10},{10... | collective-permute-start | bytes 1572872 | tf_op jit(solution)/shard_map/ppermute | solution.py:28
  457.3 12.2 %collective-permute-start.4 = (bf16[128,2048]{1,0:T(8,128)(2,1)S(1)}, bf16[128,2048]{1,0:T(8,128)(2,1)}, u32[]{:S(2)}, u32[]{:S(2)}) collective-permute-start(bf16[128,2048]{1,0:T(8,128)(2,1)S(1)} %get-tuple-element.829), channel_id=1, source_target_pairs={{0,8},{8,0},{16,24},{24,16},{1,9},{9,1},{17,25},{25,17},{2,10},{10... | collective-permute-start | bytes 1572872 | tf_op jit(solution)/shard_map/ppermute | solution.py:28
  459.1 12.3 %collective-permute-start.9 = (bf16[256,1024]{0,1:T(8,128)(2,1)}, bf16[256,1024]{0,1:T(8,128)(2,1)S(1)}, u32[]{:S(2)}, u32[]{:S(2)}) collective-permute-start(bf16[256,1024]{0,1:T(8,128)(2,1)} %collective-permute-done.8), channel_id=1, source_target_pairs={{0,16},{8,24},{16,0},{24,8},{1,17},{9,25},{17,1},{25,9},{2,18},{10... | collective-permute-start | bytes 1572872 | tf_op jit(solution)/shard_map/ppermute | solution.py:28
  469.5 11.4 %collective-permute-start.5 = (bf16[128,2048]{1,0:T(8,128)(2,1)}, bf16[128,2048]{1,0:T(8,128)(2,1)S(1)}, u32[]{:S(2)}, u32[]{:S(2)}) collective-permute-start(bf16[128,2048]{1,0:T(8,128)(2,1)} %collective-permute-done.4), channel_id=1, source_target_pairs={{0,16},{8,24},{16,0},{24,8},{1,17},{9,25},{17,1},{25,9},{2,18},{10... | collective-permute-start | bytes 1572872 | tf_op jit(solution)/shard_map/ppermute | solution.py:28
  (8 other events, 27.4 us)
Sparse Core Ops, SparseCore 0:
  249.8 88.9 reduce-scatter.4
  341.1 87.9 reduce-scatter.2
where the time goes:
time: 494 us; the launch traced here: 489 us
  waiting for transfers between devices  261 us (53%)
  matrix products  112 us (23%)
  starting transfers between devices  44.2 us (9%)
  other arithmetic  33.7 us (7%)
  local copies, waits for them, and re-layouts  23.4 us (5%)
  between operations  14.2 us (3%)
    reduce_scatter x2, waiting for transfers between devices, on_device(): lax.psum_scatter(jnp.concatenate(parts, axis=1).astype(jnp.bfloat16), 'dp...  157 us
    ppermute x12, waiting for transfers between devices, from_behind(): lax.ppermute(value, axis, [(source, source + steps) for source in range(l...  70.3 us
    ppermute x12, starting transfers between devices, from_behind(): lax.ppermute(value, axis, [(source, source + steps) for source in range(l...  35.1 us
    ppermute x8, waiting for transfers between devices, partner(): lax.ppermute(x, axis, [(i, i ^ 1 << bit) for i in range(lax.axis_size(axi...  33.1 us
    dot_general x8, matrix products, local_backward(): preact = jnp.dot(inputs, w_up, preferred_element_type=jnp.float32)  32.4 us
    dot_general x15, matrix products, times_transpose(): lax.dot_general(left, right, (((1,), (1,)), ((), ())), preferred_element_...  30.8 us
    dot_general x8, matrix products, local_backward(): jnp.dot(hidden, w_down, preferred_element_type=jnp.float32)  25.9 us
    dot_general x4, matrix products, contract_rows(): lax.dot_general(left, right, (((0,), (0,)), ((), ())), preferred_element_...  22.5 us
  transfers between devices with their start and end apart: 22, of which 16 were waited for; matrix products, arithmetic and copies ran while one was open for 14% of the time, Pallas kernels for 0%

commit v1 on v0

v1 whole, which is shorter than its diff:
```python
import functools

import jax
import jax.numpy as jnp
from jax import lax
from jax.experimental import pallas as pl
from jax.experimental.pallas import tpu as pltpu
from jax.sharding import PartitionSpec as P

norm_epsilon = 1e-06
momentum_decay = 0.9
step_size = 0.01
root_half = 0.7071067811865476
inv_root_tau = 0.3989422804014327

f32 = jnp.float32
bf16 = jnp.bfloat16
lag = 2
any_space = pl.BlockSpec(memory_space=pl.ANY)


def params(mib):
    return pltpu.CompilerParams(
        dimension_semantics=("arbitrary",), vmem_limit_bytes=mib * 1024 * 1024
    )


def dot(left, right, over):
    return lax.dot_general(left, right, (over, ((), ())), preferred_element_type=f32)


def tile_of(width):
    return min(512, width)


def forward_body(info, u_ref, p_ref, q_ref, *rest):
    h_ref, slope_ref, y_ref, r_ref, total = rest[-5:]
    j = pl.program_id(0)
    rows, model = total.shape
    u = u_ref[...].reshape(rows, model)
    pre = dot(u, p_ref[0, 0], ((1,), (0,)))
    cdf = 0.5 * (1.0 + lax.erf(pre * root_half))
    hidden = (pre * cdf).astype(bf16)
    slope = cdf + pre * (jnp.exp(-0.5 * pre * pre) * inv_root_tau)
    h_ref[...] = hidden.reshape(h_ref.shape)
    slope_ref[...] = slope.astype(bf16).reshape(slope_ref.shape)
    part = dot(hidden, q_ref[0, 0], ((1,), (0,)))

    @pl.when(j == 0)
    def _():
        total[...] = u.astype(f32) + part

    @pl.when(j > 0)
    def _():
        total[...] += part

    @pl.when(j == pl.num_programs(0) - 1)
    def _():
        z = total[...]
        centre = z - jnp.mean(z, axis=-1, keepdims=True)
        r = lax.rsqrt(jnp.mean(centre * centre, axis=-1, keepdims=True) + norm_epsilon)
        y_ref[...] = (centre * r).astype(bf16).reshape(y_ref.shape)
        r_ref[...] = r.reshape(r_ref.shape)


def forward(inputs, w_up, w_down, source, weights, place, places, previous=None):
    _, _, micro, tokens, model = inputs.shape
    width = w_up.shape[3]
    tile = tile_of(width)
    info = jnp.stack([source, weights, place]).astype(jnp.int32)
    shapes = (
        jax.ShapeDtypeStruct((places, micro, tokens, width), bf16),
        jax.ShapeDtypeStruct((places, micro, tokens, width), bf16),
        jax.ShapeDtypeStruct((places, micro, tokens, model), bf16),
        jax.ShapeDtypeStruct((places, micro, tokens, 1), f32),
    )
    in_specs = [
        pl.BlockSpec((1, 1, micro, tokens, model), lambda j, i: (i[0], 0, 0, 0, 0)),
        pl.BlockSpec((1, 1, model, tile), lambda j, i: (i[1], 0, 0, j)),
        pl.BlockSpec((1, 1, tile, model), lambda j, i: (i[1], 0, j, 0)),
    ]
    operands = [inputs, w_up, w_down]
    aliases = {}
    if previous is not None:
        in_specs += [any_space] * 4
        operands += list(previous)
        aliases = {4 + k: k for k in range(4)}
    flops = 4 * micro * tokens * model * width
    return pl.pallas_call(
        forward_body,
        grid_spec=pltpu.PrefetchScalarGridSpec(
            num_scalar_prefetch=1,
            grid=(width // tile,),
            in_specs=in_specs,
            out_specs=[
                pl.BlockSpec((1, micro, tokens, tile), lambda j, i: (i[2], 0, 0, j)),
                pl.BlockSpec((1, micro, tokens, tile), lambda j, i: (i[2], 0, 0, j)),
                pl.BlockSpec((1, micro, tokens, model), lambda j, i: (i[2], 0, 0, 0)),
                pl.BlockSpec((1, micro, tokens, 1), lambda j, i: (i[2], 0, 0, 0)),
            ],
            scratch_shapes=[pltpu.VMEM((micro * tokens, model), f32)],
        ),
        out_shape=shapes,
        input_output_aliases=aliases,
        compiler_params=params(40),
        cost_estimate=pl.CostEstimate(
            flops=2 * flops, bytes_accessed=4 * model * width, transcendentals=0
        ),
        name="forward",
    )(info, *operands)


def sum_gradient(e, y, r):
    mean_e = jnp.mean(e, axis=-1, keepdims=True)
    mean_ey = jnp.mean(e * y, axis=-1, keepdims=True)
    return r * (e - mean_e - y * mean_ey)


def chain_body(kept, info, recv_ref, top_ref, y_ref, r_ref, slope_ref, p_ref, q_ref, *rest):
    if kept:
        out_ref, pre_ref, sum_ref, whole, low, total = rest[-6:]
    else:
        out_ref, whole, low, total = rest[-4:]
        pre_ref = sum_ref = None
    j = pl.program_id(0)
    active = info[0] > 0

    @pl.when(jnp.logical_and(active, j == 0))
    def _():
        e = jnp.where(info[4] > 0, top_ref[0, 0], recv_ref[...]).astype(f32)
        grad = sum_gradient(e, y_ref[0, 0].astype(f32), r_ref[0, 0])
        whole[...] = grad
        low[...] = grad.astype(bf16)
        if kept:
            sum_ref[0] = grad.astype(bf16)

    @pl.when(active)
    def _():
        grad_pre = (
            dot(low[...], q_ref[0, 0], ((1,), (1,))) * slope_ref[0, 0].astype(f32)
        ).astype(bf16)
        if kept:
            pre_ref[0] = grad_pre

        @pl.when(info[5] > 0)
        def _():
            part = dot(grad_pre, p_ref[0, 0], ((1,), (1,)))

            @pl.when(j == 0)
            def _():
                total[...] = whole[...] + part

            @pl.when(j > 0)
            def _():
                total[...] += part

            @pl.when(j == pl.num_programs(0) - 1)
            def _():
                out_ref[...] = total[...].astype(bf16)


def chain_step(relay, kept, scalars, recv, top_grad, saved, w_up, w_down, previous):
    _, slopes, ys, rs = saved
    tokens, model = recv.shape
    width = w_up.shape[3]
    micro = top_grad.shape[1]
    tile = tile_of(width)
    in_specs = [
        pl.BlockSpec((tokens, model), lambda j, i: (0, 0)),
        pl.BlockSpec((1, 1, tokens, model), lambda j, i: (relay, i[1], 0, 0)),
        pl.BlockSpec((1, 1, tokens, model), lambda j, i: (relay, i[2], 0, 0)),
        pl.BlockSpec((1, 1, tokens, 1), lambda j, i: (relay, i[2], 0, 0)),
        pl.BlockSpec((1, 1, tokens, tile), lambda j, i: (relay, i[2], 0, j * i[0])),
        pl.BlockSpec((1, 1, model, tile), lambda j, i: (relay, 0, 0, j * i[5])),
        pl.BlockSpec((1, 1, tile, model), lambda j, i: (relay, 0, j * i[0], 0)),
    ]
    operands = [recv, top_grad, ys, rs, slopes, w_up, w_down]
    out_shape = [jax.ShapeDtypeStruct((tokens, model), bf16)]
    out_specs = [pl.BlockSpec((tokens, model), lambda j, i: (0, 0))]
    aliases = {}
    if kept:
        out_shape += [
            jax.ShapeDtypeStruct((micro + 1, tokens, width), bf16),
            jax.ShapeDtypeStruct((micro + 1, tokens, model), bf16),
        ]
        out_specs += [
            pl.BlockSpec((1, tokens, tile), lambda j, i: (i[3], 0, j * i[0])),
            pl.BlockSpec((1, tokens, model), lambda j, i: (i[3], 0, 0)),
        ]
        if previous is not None:
            in_specs += [any_space] * 2
            operands += list(previous)
            aliases = {8: 1, 9: 2}
    flops = 4 * tokens * model * width
    return pl.pallas_call(
        functools.partial(chain_body, kept),
        grid_spec=pltpu.PrefetchScalarGridSpec(
            num_scalar_prefetch=1,
            grid=(width // tile,),
            in_specs=in_specs,
            out_specs=out_specs,
            scratch_shapes=[
                pltpu.VMEM((tokens, model), f32),
                pltpu.VMEM((tokens, model), bf16),
                pltpu.VMEM((tokens, model), f32),
            ],
        ),
        out_shape=out_shape,
        input_output_aliases=aliases,
        compiler_params=params(24),
        cost_estimate=pl.CostEstimate(
            flops=2 * flops, bytes_accessed=4 * model * width, transcendentals=0
        ),
        name="chain",
    )(scalars, *operands)


def home_body(micro, info, *refs):
    e_refs = refs[:micro]
    top_ref, y_ref, r_ref, slope_ref, q_ref, pre_ref, sum_ref = refs[micro:]
    j = pl.program_id(0)
    tokens, model = top_ref.shape[2:]

    @pl.when(j == 0)
    def _():
        for slot in range(micro):
            place = info[1 + slot]
            e = jnp.where(info[0] > 0, top_ref[0, slot], e_refs[slot][0]).astype(f32)
            grad = sum_gradient(e, y_ref[0, place].astype(f32), r_ref[0, place])
            sum_ref[place] = grad.astype(bf16)

    low = sum_ref[...].reshape(micro * tokens, model)
    slope = slope_ref[...].reshape(micro * tokens, slope_ref.shape[3])
    grad_pre = dot(low, q_ref[0, 0], ((1,), (1,))) * slope.astype(f32)
    pre_ref[...] = grad_pre.astype(bf16).reshape(pre_ref.shape)


def home_step(info, arrived, top_grad, saved, w_down):
    _, slopes, ys, rs = saved
    _, micro, tokens, model = top_grad.shape
    width = w_down.shape[2]
    tile = tile_of(width)

    def slot_spec(slot):
        return pl.BlockSpec((1, tokens, model), lambda j, i: (i[1 + micro + slot], 0, 0))

    return pl.pallas_call(
        functools.partial(home_body, micro),
        grid_spec=pltpu.PrefetchScalarGridSpec(
            num_scalar_prefetch=1,
            grid=(width // tile,),
            in_specs=[slot_spec(slot) for slot in range(micro)]
            + [
                pl.BlockSpec((1, micro, tokens, model), lambda j, i: (1, 0, 0, 0)),
                pl.BlockSpec((1, micro, tokens, model), lambda j, i: (0, 0, 0, 0)),
                pl.BlockSpec((1, micro, tokens, 1), lambda j, i: (0, 0, 0, 0)),
                pl.BlockSpec((1, micro, tokens, tile), lambda j, i: (0, 0, 0, j)),
                pl.BlockSpec((1, 1, tile, model), lambda j, i: (0, 0, j, 0)),
            ],
            out_specs=[
                pl.BlockSpec((micro, tokens, tile), lambda j, i: (0, 0, j)),
                pl.BlockSpec((micro, tokens, model), lambda j, i: (0, 0, 0)),
            ],
        ),
        out_shape=[
            jax.ShapeDtypeStruct((micro, tokens, width), bf16),
            jax.ShapeDtypeStruct((micro, tokens, model), bf16),
        ],
        compiler_params=params(32),
        cost_estimate=pl.CostEstimate(
            flops=4 * micro * tokens * model * width,
            bytes_accessed=2 * model * width,
            transcendentals=0,
        ),
        name="home",
    )(info, *([arrived] * micro), top_grad, ys, rs, slopes, w_down)


def weight_body(la_ref, ra_ref, lb_ref, rb_ref, out_ref):
    def flat(ref):
        value = ref[...]
        return value.reshape(-1, value.shape[-1])

    total = dot(flat(la_ref), flat(ra_ref), ((0,), (0,)))
    total += dot(flat(lb_ref), flat(rb_ref), ((0,), (0,)))
    out_ref[...] = total.astype(bf16)


def weight_gradient(left_a, right_a, left_b, right_b, micro, split_left):
    tokens = right_a.shape[-2]
    rows, columns = left_a.shape[-1], right_a.shape[-1]
    tile = tile_of(rows if split_left else columns)

    def spec(array, split):
        lead = array.ndim - 3
        block = (1,) * lead + (micro, tokens, tile if split else array.shape[-1])
        if split:
            return pl.BlockSpec(block, lambda j: (0,) * (lead + 2) + (j,))
        return pl.BlockSpec(block, lambda j: (0,) * (lead + 3))

    out_block = (tile, columns) if split_left else (rows, tile)
    return pl.pallas_call(
        weight_body,
        grid=((rows if split_left else columns) // tile,),
        in_specs=[
            spec(left_a, split_left),
            spec(right_a, not split_left),
            spec(left_b, split_left),
            spec(right_b, not split_left),
        ],
        out_specs=pl.BlockSpec(out_block, (lambda j: (j, 0)) if split_left else (lambda j: (0, j))),
        out_shape=jax.ShapeDtypeStruct((rows, columns), bf16),
        compiler_params=params(40),
        cost_estimate=pl.CostEstimate(
            flops=4 * micro * tokens * rows * columns,
            bytes_accessed=2 * rows * columns,
            transcendentals=0,
        ),
        name="weights",
    )(left_a, right_a, left_b, right_b)


def on_device(section_inputs, top_grad, plan, up_weight, down_weight, up_moment, down_moment):
    sections = lax.axis_size("section")
    position = lax.axis_index("section")
    replica = lax.axis_index("dp")
    micro, tokens, model = top_grad.shape[1:]
    plan = plan.astype(jnp.int32)
    zero = jnp.int32(0)
    last = sections - 1

    def hop(value, pairs):
        return lax.ppermute(value, "section", pairs) if pairs else None

    mirrored = lax.ppermute(
        section_inputs[1, 0], "section", [(i, last - i) for i in range(sections)]
    )

    first = jnp.where(position >= sections // 2, 0, 1).astype(jnp.int32)
    saved = forward(section_inputs, up_weight, down_weight, first, first, first, 2)
    saved = forward(
        section_inputs, up_weight, down_weight, 1 - first, 1 - first, 1 - first, 2, saved
    )
    saved_home = forward(mirrored[None, None], up_weight, down_weight, zero, zero, zero, 1)

    blank = jnp.zeros((tokens, model), bf16)
    ticks = micro + lag * last
    received = [{}, {}]
    home = []
    kept = None
    for tick in range(ticks):
        for relay in range(2):
            start = (last - position) if relay == 0 else position
            slot = tick - lag * start
            active = jnp.logical_and(slot >= 0, slot < micro)
            if relay == 1:
                active = jnp.logical_and(active, position < last)

            def busy(i, tick=tick, relay=relay):
                return 0 <= tick - lag * ((last - i) if relay == 0 else i) < micro

            if relay == 1 and not any(busy(i) for i in range(last)):
                continue
            slot = jnp.clip(slot, 0, micro - 1)
            place = plan[relay, slot]
            asked = active if relay == 1 else jnp.logical_and(active, position > 0)
            scalars = jnp.stack(
                [
                    active.astype(jnp.int32),
                    slot,
                    place,
                    jnp.where(active, place, micro),
                    (start == 0).astype(jnp.int32),
                    asked.astype(jnp.int32),
                ]
            ).astype(jnp.int32)
            recv = received[relay].pop(tick, None)
            if recv is None:
                recv = blank
            done = chain_step(
                relay, relay == 0, scalars, recv, top_grad, saved, up_weight, down_weight, kept
            )
            out = done[0]
            if relay == 0:
                kept = done[1:]
                pairs = [(i, i - 1) for i in range(1, sections) if busy(i)]
            else:
                pairs = [(i, i + 1) for i in range(sections - 2) if busy(i)]
                home.append(hop(out, [(i, last - 1 - i) for i in range(last) if busy(i)]))
            got = hop(out, pairs)
            if got is not None:
                received[relay][tick + lag] = got

    origin = jnp.clip(last - 1 - position, 0, last - 1)
    info = jnp.concatenate(
        [
            (position == last).astype(jnp.int32)[None],
            plan[1],
            jnp.arange(micro, dtype=jnp.int32) + lag * origin,
        ]
    )
    home_pre, home_sum = home_step(info, jnp.stack(home), top_grad, saved_home, down_weight)

    up_part = weight_gradient(section_inputs[0], kept[0], mirrored, home_pre, micro, False)
    up_sum = lax.psum_scatter(up_part, "dp", scatter_dimension=0, tiled=True)
    down_part = weight_gradient(saved[0], kept[1], saved_home[0], home_sum, micro, True)
    down_sum = lax.psum_scatter(down_part, "dp", scatter_dimension=0, tiled=True)

    def update(weight, moment, total):
        rows = moment.shape[1]
        held = lax.dynamic_slice_in_dim(weight[0, 0], replica * rows, rows, 0)
        fresh_moment = momentum_decay * moment[0] + total.astype(f32)
        fresh = (held.astype(f32) - step_size * fresh_moment).astype(bf16)
        far = lax.ppermute(fresh, "section", [(i, last - i) for i in range(sections)])
        return jnp.stack([fresh, far])[:, None], fresh_moment[None]

    new_up_weight, new_up_moment = update(up_weight, up_moment, up_sum)
    new_down_weight, new_down_moment = update(down_weight, down_moment, down_sum)
    return (new_up_weight, new_down_weight, new_up_moment, new_down_moment)


def solution(mesh):
    in_specs = (
        P(None, "section", None, "dp", None),
        P(None, None, "dp", None),
        P(),
        P(None, "section", None, None),
        P(None, "section", None, None),
        P("section", "dp", None),
        P("section", "dp", None),
    )
    out_specs = (
        P(None, "section", "dp", None),
        P(None, "section", "dp", None),
        P("section", "dp", None),
        P("section", "dp", None),
    )
    return jax.shard_map(
        on_device, mesh=mesh, in_specs=in_specs, out_specs=out_specs, check_vma=False
    )
```

time: 494 us -> 400 us (0.81)
  waiting for transfers between devices: 261 us -> 117 us
  matrix products: 112 us -> 0 us
  local copies, waits for them, and re-layouts: 23.4 us -> 120 us
  Pallas kernels: 0 us -> 92.7 us
  other arithmetic: 33.7 us -> 7.05 us
  between operations: 14.2 us -> 26.4 us
  starting transfers between devices: 44.2 us -> 35 us
    dot_general x35 -> x0, matrix products: 112 us -> none  [the longest x8 32.4 us: local_backward(): preact = jnp.dot(inputs, w_up, preferred_element_type=jnp.float32)]
    pallas_call x0 -> x24, Pallas kernels: none -> 92.7 us  [the longest x18 46.5 us: chain_step(): pl.pallas_call(functools.partial(chain_body, kept), grid_spec=pltpu.Prefe...]
    unnamed x12 -> x141, local copies, waits for them, and re-layouts: 5.91 us -> 93.5 us
    reduce_scatter x2, waiting for transfers between devices: 157 us -> 72.6 us  [the longest x1 45.7 us: on_device(): lax.psum_scatter(down_part, 'dp', scatter_dimension=0, tiled=True)]
    ppermute x20 -> x25, waiting for transfers between devices: 103 us -> 44 us  [the longest x22 35 us: hop(): return lax.ppermute(value, 'section', pairs) if pairs else None]
    concatenate x2 -> x1, other arithmetic: 16.3 us -> 0.08 us  [on_device(): jnp.concatenate([(position == last).astype(jnp.int32)[None], plan[1], jnp...]
    ppermute x20 -> x25, starting transfers between devices: 44.1 us -> 34.9 us  [the longest x22 27.6 us: hop(): return lax.ppermute(value, 'section', pairs) if pairs else None]
    dynamic_update_slice x8 -> x0, other arithmetic: 7.36 us -> none  [keep(): lax.dynamic_update_index_in_dim(state[2], grad_sum_low, slot, 0)]
  transfers between devices with their start and end apart: 22 -> 27, of which waited for: 16 -> 8; matrix products, arithmetic and copies ran while one was open for 14% -> 8% of each run, Pallas kernels for 0% -> 15%
where the time goes in v1:
time: 400 us; the launch traced here: 398 us
  local copies, waits for them, and re-layouts  120 us (30%)
  waiting for transfers between devices  117 us (29%)
  Pallas kernels  92.7 us (23%)
  starting transfers between devices  35 us (9%)
  between operations  26.4 us (7%)
  other arithmetic  7.05 us (2%)
    unnamed x141, local copies, waits for them, and re-layouts  93.5 us
    pallas_call x18, Pallas kernels, chain_step(): pl.pallas_call(functools.partial(chain_body, kept), grid_spec=pltpu.Prefe...  46.5 us
    reduce_scatter x1, waiting for transfers between devices, on_device(): lax.psum_scatter(down_part, 'dp', scatter_dimension=0, tiled=True)  45.7 us
    ppermute x22, waiting for transfers between devices, hop(): return lax.ppermute(value, 'section', pairs) if pairs else None  35 us
    pallas_call x3, Pallas kernels, forward(): pl.pallas_call(forward_body, grid_spec=pltpu.PrefetchScalarGridSpec(num_s...  30.1 us
    ppermute x22, starting transfers between devices, hop(): return lax.ppermute(value, 'section', pairs) if pairs else None  27.6 us
    reduce_scatter x1, waiting for transfers between devices, on_device(): up_sum = lax.psum_scatter(up_part, 'dp', scatter_dimension=0, tiled=True)  27 us
    another operation x18, local copies, waits for them, and re-layouts, on_device(): jnp.stack([active.astype(jnp.int32), slot, place, jnp.where(active, place...  12.8 us
  transfers between devices with their start and end apart: 27, of which 8 were waited for; matrix products, arithmetic and copies ran while one was open for 8% of the time, Pallas kernels for 15%

profile of v1, /device:TPU:0, one launch (start us, length us, event | category | flops | bytes accessed | tf_op | source)
XLA Modules:
  0.0 397.6 jit_solution(9113134644059289499)
XLA Ops:
  7.3 2.1 constant_dynamic-slice_fusion.10
  11.6 9.8 %forward.3 = (bf16[2,4,128,2048]{3,2,1,0:T(8,128)(2,1)S(1)}, bf16[2,4,128,2048]{3,2,1,0:T(8,128)(2,1)S(1)}, bf16[2,4,128,1024]{3,2,1,0:T(8,128)(2,1)S(1)}, f32[2,4,128,1]{3,2,1,0:T(8,128)S(1)}) custom-call(s32[3]{0:T(128)S(1)} %stack.461.info, bf16[2,1,4,128,1024]{4,3,2,1,0:T(8,128)(2,1)S(1)} %copy-done.48, bf16[2,1,1024,2048]{3,2,1,0:T(8,128)(2,1)} %p_ref.41, ...), custom_call_target="tpu_custom_call" | custom-call | flops 8589934592 | bytes 8388608 | tf_op jit(solution)/shard_map/forward/pallas_call | solution.py:89
  21.4 9.9 %forward.4 = (bf16[2,4,128,2048]{3,2,1,0:T(8,128)(2,1)S(1)}, bf16[2,4,128,2048]{3,2,1,0:T(8,128)(2,1)S(1)}, bf16[2,4,128,1024]{3,2,1,0:T(8,128)(2,1)S(1)}, f32[2,4,128,1]{3,2,1,0:T(8,128)S(1)}) custom-call(s32[3]{0:T(128)S(1)} %stack.460.info, ...), custom_call_target="tpu_custom_call", output_to_operand_aliasing={{0}: (4, {}), {1}: (5, {}), {2}: (6, {}), {3}: (7, {})} | custom-call | flops 8589934592 | bytes 8388608 | tf_op jit(solution)/shard_map/forward/pallas_call | solution.py:89
  34.7 2.0 copy-done.56
  37.4 3.4 copy-done
  40.7 3.4 copy-done.5
  44.1 2.2 copy-done.11
  47.9 5.4 %chain.28 = bf16[128,1024]{1,0:T(8,128)(2,1)S(1)} custom-call(s32[6]{0:T(128)S(1)} %stack.503.info, bf16[128,1024]{1,0:T(8,128)(2,1)S(1)} %broadcast_in_dim.24.recv_ref, bf16[2,4,128,1024]{3,2,1,0:T(8,128)(2,1)S(1)} %copy-done.17, bf16[2,4,128,1024]{3,2,1,0:T(8,128)(2,1)S(1)} %copy-done.19, f32[2,4,128,1]{3,2,1,0:T(8,128)S(1)} %get-tuple-element.51.r_ref, ...), custom_call_target="tpu_custom_call" | custom-call | flops 2147483648 | bytes 8388608 | tf_op jit(solution)/shard_map/chain/pallas_call | solution.py:195
  58.0 3.4 copy-done.1
  61.4 3.4 copy-done.6
  64.8 2.2 copy-done.12
  68.5 6.1 %chain.29 = bf16[128,1024]{1,0:T(8,128)(2,1)} custom-call(s32[6]{0:T(128)S(1)} %stack.509.info, bf16[128,1024]{1,0:T(8,128)(2,1)S(1)} %broadcast_in_dim.24.recv_ref, bf16[2,4,128,1024]{3,2,1,0:T(8,128)(2,1)S(1)} %copy-done.17, bf16[2,4,128,1024]{3,2,1,0:T(8,128)(2,1)S(1)} %copy-done.20, f32[2,4,128,1]{3,2,1,0:T(8,128)S(1)} %get-tuple-element.51.r_ref, ...), custom_call_target="tpu_custom_call" | custom-call | flops 2147483648 | bytes 8388608 | tf_op jit(solution)/shard_map/chain/pallas_call | solution.py:195
  80.7 3.4 copy-done.2
  84.1 3.4 copy-done.7
  87.5 2.2 copy-done.13
  96.0 3.4 copy-done.3
  99.4 3.4 copy-done.8
  102.8 2.2 copy-done.14
  134.5 2.6 collective-permute-start.8
  137.0 3.4 copy-done.4
  140.4 3.4 copy-done.9
  143.8 2.2 copy-done.15
  147.5 5.4 %chain.30 = bf16[128,1024]{1,0:T(8,128)(2,1)S(1)} custom-call(s32[6]{0:T(128)S(1)} %stack.515.info, bf16[128,1024]{1,0:T(8,128)(2,1)S(1)} %collective-permute-done.11.recv_ref, bf16[2,4,128,1024]{3,2,1,0:T(8,128)(2,1)S(1)} %copy-done.17, bf16[2,4,128,1024]{3,2,1,0:T(8,128)(2,1)S(1)} %copy-done.23, f32[2,4,128,1]{3,2,1,0:T(8,128)S(1)} %get-tuple-element.51.r_ref, ...), custom_call_target="tpu_custom_call" | custom-call | flops 2147483648 | bytes 8388608 | tf_op jit(solution)/shard_map/chain/pallas_call | solution.py:195
  157.1 6.2 %chain.31 = bf16[128,1024]{1,0:T(8,128)(2,1)S(1)} custom-call(s32[6]{0:T(128)S(1)} %stack.521.info, bf16[128,1024]{1,0:T(8,128)(2,1)} %collective-permute-done.13.recv_ref, bf16[2,4,128,1024]{3,2,1,0:T(8,128)(2,1)S(1)} %copy-done.17, bf16[2,4,128,1024]{3,2,1,0:T(8,128)(2,1)S(1)} %copy-done.23, f32[2,4,128,1]{3,2,1,0:T(8,128)S(1)} %get-tuple-element.51.r_ref, ...), custom_call_target="tpu_custom_call" | custom-call | flops 2147483648 | bytes 8388608 | tf_op jit(solution)/shard_map/chain/pallas_call | solution.py:195
  170.0 2.6 collective-permute-done.14
  179.9 21.4 %collective-permute-done.5.recv_ref = bf16[128,1024]{1,0:T(8,128)(2,1)S(1)} collective-permute-done((bf16[128,1024]{1,0:T(8,128)(2,1)S(1)}, bf16[128,1024]{1,0:T(8,128)(2,1)S(1)}, u32[]{:S(2)}, u32[]{:S(2)}) %collective-permute-start.5) | collective-permute-done | bytes 262176 | tf_op jit(solution)/shard_map/ppermute | solution.py:333
  202.6 3.1 chain.24
  205.8 3.0 collective-permute-done.4.recv_ref
  209.5 3.1 chain.25
  219.9 10.5 %forward.5 = (bf16[1,4,128,2048]{3,2,1,0:T(8,128)(2,1)S(1)}, bf16[1,4,128,2048]{3,2,1,0:T(8,128)(2,1)S(1)}, bf16[1,4,128,1024]{3,2,1,0:T(8,128)(2,1)S(1)}, f32[1,4,128,1]{3,2,1,0:T(8,128)S(1)}) custom-call(s32[3]{0:T(128)S(1)} %broadcast_1_info.2.info, bf16[1,1,4,128,1024]{4,3,2,1,0:T(8,128)(2,1)S(1)} %bitcast.164, bf16[2,1,1024,2048]{3,2,1,0:T(8,128)(2,1)} %p_ref.41, ...), custom_call_target="tpu_custom_call" | custom-call | flops 8589934592 | bytes 8388608 | tf_op jit(solution)/shard_map/forward/pallas_call | solution.py:89
  233.1 5.0 %collective-permute-done.20 = bf16[128,1024]{1,0:T(8,128)(2,1)S(1)} collective-permute-done((bf16[128,1024]{1,0:T(8,128)(2,1)S(1)}, bf16[128,1024]{1,0:T(8,128)(2,1)S(1)}, u32[]{:S(2)}, u32[]{:S(2)}) %collective-permute-start.20) | collective-permute-done | bytes 262176 | tf_op jit(solution)/shard_map/ppermute | solution.py:333
  238.0 3.0 collective-permute-done.22
  245.9 4.9 %home.1 = (bf16[4,128,2048]{2,1,0:T(8,128)(2,1)S(1)}, bf16[4,128,1024]{2,1,0:T(8,128)(2,1)S(1)}) custom-call(s32[9]{0:T(128)S(1)} %pad_add_fusion.info, bf16[8,128,1024]{2,1,0:T(8,128)(2,1)S(1)} %copy-done.43, bf16[8,128,1024]{2,1,0:T(8,128)(2,1)S(1)} %copy-done.43, bf16[8,128,1024]{2,1,0:T(8,128)(2,1)S(1)} %copy-done.43, ...), custom_call_target="tpu_custom_call" | custom-call | flops 4294967296 | bytes 4194304 | tf_op jit(solution)/shard_map/home/pallas_call | solution.py:247
  250.8 2.5 copy-done.16
  255.1 3.8 chain.26
  258.9 3.8 chain.27
  267.1 5.8 %weights.2 = bf16[1024,2048]{1,0:T(8,128)(2,1)S(1)} custom-call(bf16[1,4,128,1024]{3,2,1,0:T(8,128)(2,1)S(1)} %copy-done.50, bf16[5,128,2048]{2,1,0:T(8,128)(2,1)S(1)} %copy-done.33, bf16[4,128,1024]{2,1,0:T(8,128)(2,1)S(1)} %copy-done.52, bf16[4,128,2048]{2,1,0:T(8,128)(2,1)S(1)} %get-tuple-element.83.rb_ref), custom_call_target="tpu_custom_call" | custom-call | flops 4294967296 | bytes 4194304 | tf_op jit(solution)/shard_map/weights/pallas_call | solution.py:302
  276.5 2.2 copy-done.57
  280.3 5.5 %weights.3 = bf16[2048,1024]{1,0:T(8,128)(2,1)S(1)} custom-call(bf16[2,4,128,2048]{3,2,1,0:T(8,128)(2,1)S(1)} %copy-done.57, bf16[5,128,1024]{2,1,0:T(8,128)(2,1)S(1)} %copy-done.41, bf16[1,4,128,2048]{3,2,1,0:T(8,128)(2,1)S(1)} %copy-done.59, bf16[4,128,1024]{2,1,0:T(8,128)(2,1)S(1)} %copy-done.54), custom_call_target="tpu_custom_call" | custom-call | flops 4294967296 | bytes 4194304 | tf_op jit(solution)/shard_map/weights/pallas_call | solution.py:302
  287.8 4.8 %slice.15 = bf16[1,1,1024,2048]{3,2,1,0:T(8,128)(2,1)} slice(bf16[2,1,1024,2048]{3,2,1,0:T(8,128)(2,1)} %p_ref.41), slice={[0:1], [0:1], [0:1024], [0:2048]} | slice | bytes 8388608 | tf_op jit(solution)/shard_map/slice | solution.py:411
  292.6 4.9 %slice.19 = bf16[1,1,2048,1024]{3,2,1,0:T(8,128)(2,1)} slice(bf16[2,1,2048,1024]{3,2,1,0:T(8,128)(2,1)} %refs_8_.1), slice={[0:1], [0:1], [0:2048], [0:1024]} | slice | bytes 8388608 | tf_op jit(solution)/shard_map/slice | solution.py:411
  297.5 27.0 %reduce-scatter.3.cloned.1.call-done = bf16[128,2048]{1,0:T(8,128)(2,1)} async-done(((bf16[1024,2048]{1,0:T(8,128)(2,1)}), bf16[128,2048]{1,0:T(8,128)(2,1)}) %reduce-scatter.3.cloned.1.call-update) | async-done | bytes 524304 | tf_op jit(solution)/shard_map/reduce_scatter | solution.py:405
  324.4 2.4 fusion.2
  326.9 2.3 collective-permute-start.23
  329.2 45.7 %reduce-scatter.5.cloned.1.call-done = bf16[256,1024]{1,0:T(8,128)(2,1)} async-done(((bf16[2048,1024]{1,0:T(8,128)(2,1)}), bf16[256,1024]{1,0:T(8,128)(2,1)}) %reduce-scatter.5.cloned.1.call-update) | async-done | bytes 524304 | tf_op jit(solution)/shard_map/reduce_scatter | solution.py:407
  374.9 2.4 fusion.3
  377.3 2.4 collective-permute-start.24
  380.8 9.0 %collective-permute-done.24 = bf16[256,1024]{1,0:T(8,128)(2,1)S(1)} collective-permute-done((bf16[256,1024]{1,0:T(8,128)(2,1)S(1)}, bf16[256,1024]{1,0:T(8,128)(2,1)S(1)}, u32[]{:S(2)}, u32[]{:S(2)}) %collective-permute-start.24) | collective-permute-done | bytes 524320 | tf_op jit(solution)/shard_map/ppermute | solution.py:414
  (209 shorter events, 96.0 us)
Async XLA Ops:
  7.2 317.3 %reduce-scatter.3.cloned.1.call-start = ((), (), s32[]{:S(2)}) async-start(), calls=%async_computation.2 | async-start | bytes 4718592 | tf_op jit(solution)/shard_map/reduce_scatter | solution.py:405
  21.4 15.9 %copy-start.17 = (bf16[2,4,128,1024]{3,2,1,0:T(8,128)(2,1)S(1)}, bf16[2,4,128,1024]{3,2,1,0:T(8,128)(2,1)}, u32[]{:S(2)}) copy-start(bf16[2,4,128,1024]{3,2,1,0:T(8,128)(2,1)} %refs_4_.1) | copy-start | bytes 6291460
  37.4 3.4 copy-start
  40.7 3.4 copy-start.5
  53.3 79.5 %collective-permute-start.9 = (bf16[128,1024]{1,0:T(8,128)(2,1)S(1)}, bf16[128,1024]{1,0:T(8,128)(2,1)}, u32[]{:S(2)}, u32[]{:S(2)}) collective-permute-start(bf16[128,1024]{1,0:T(8,128)(2,1)S(1)} %chain.28), channel_id=1, source_target_pairs={{0,16},{1,17},{2,18},{3,19},{4,20},{5,21},{6,22},{7,23}} | collective-permute-start | bytes 786440 | tf_op jit(solution)/shard_map/ppermute | solution.py:333
  55.3 79.1 %collective-permute-start.11 = (bf16[128,1024]{1,0:T(8,128)(2,1)S(1)}, bf16[128,1024]{1,0:T(8,128)(2,1)S(1)}, u32[]{:S(2)}, u32[]{:S(2)}) collective-permute-start(bf16[128,1024]{1,0:T(8,128)(2,1)S(1)} %chain.28), channel_id=1, source_target_pairs={{0,8},{1,9},{2,10},{3,11},{4,12},{5,13},{6,14},{7,15}} | collective-permute-start | bytes 786440 | tf_op jit(solution)/shard_map/ppermute | solution.py:333
  58.0 3.4 copy-start.1
  74.7 78.3 %collective-permute-start.10 = (bf16[128,1024]{1,0:T(8,128)(2,1)}, bf16[128,1024]{1,0:T(8,128)(2,1)}, u32[]{:S(2)}, u32[]{:S(2)}) collective-permute-start(bf16[128,1024]{1,0:T(8,128)(2,1)} %chain.29), channel_id=1, source_target_pairs={{0,16},{1,17},{2,18},{3,19},{4,20},{5,21},{6,22},{7,23}} | collective-permute-start | bytes 786440 | tf_op jit(solution)/shard_map/ppermute | solution.py:333
  76.7 78.6 %collective-permute-start.13 = (bf16[128,1024]{1,0:T(8,128)(2,1)}, bf16[128,1024]{1,0:T(8,128)(2,1)}, u32[]{:S(2)}, u32[]{:S(2)}) collective-permute-start(bf16[128,1024]{1,0:T(8,128)(2,1)} %chain.29), channel_id=1, source_target_pairs={{0,8},{1,9},{2,10},{3,11},{4,12},{5,13},{6,14},{7,15}} | collective-permute-start | bytes 786440 | tf_op jit(solution)/shard_map/ppermute | solution.py:333
  80.7 3.4 copy-start.2
  96.0 3.4 copy-start.3
  111.2 54.4 %collective-permute-start = (bf16[128,1024]{1,0:T(8,128)(2,1)}, bf16[128,1024]{1,0:T(8,128)(2,1)S(1)}, u32[]{:S(2)}, u32[]{:S(2)}) collective-permute-start(bf16[128,1024]{1,0:T(8,128)(2,1)} %get-tuple-element.55), channel_id=1, source_target_pairs={{24,16},{25,17},{26,18},{27,19},{28,20},{29,21},{30,22},{31,23}} | collective-permute-start | bytes 786440 | tf_op jit(solution)/shard_map/ppermute | solution.py:333
  132.8 30.5 %collective-permute-start.1 = (bf16[128,1024]{1,0:T(8,128)(2,1)}, bf16[128,1024]{1,0:T(8,128)(2,1)S(1)}, u32[]{:S(2)}, u32[]{:S(2)}) collective-permute-start(bf16[128,1024]{1,0:T(8,128)(2,1)} %copy-done.55), channel_id=1, source_target_pairs={{24,16},{25,17},{26,18},{27,19},{28,20},{29,21},{30,22},{31,23}} | collective-permute-start | bytes 786440 | tf_op jit(solution)/shard_map/ppermute | solution.py:333
  134.5 85.4 %collective-permute-start.8 = (bf16[4,128,1024]{2,1,0:T(8,128)(2,1)}, bf16[4,128,1024]{2,1,0:T(8,128)(2,1)S(1)}, u32[]{:S(2)}, u32[]{:S(2)}) collective-permute-start(bf16[4,128,1024]{2,1,0:T(8,128)(2,1)} %get-tuple-element.92), channel_id=1, source_target_pairs={{0,24},{8,16},{16,8},{24,0},{1,25},{9,17},{17,9},{25,1},{2,26},{10... | collective-permute-start | bytes 3145736 | tf_op jit(solution)/shard_map/ppermute | solution.py:335
  153.0 14.8 %collective-permute-start.12 = (bf16[128,1024]{1,0:T(8,128)(2,1)S(1)}, bf16[128,1024]{1,0:T(8,128)(2,1)S(1)}, u32[]{:S(2)}, u32[]{:S(2)}) collective-permute-start(bf16[128,1024]{1,0:T(8,128)(2,1)S(1)} %chain.30), channel_id=1, source_target_pairs={{0,16},{8,8},{1,17},{9,9},{2,18},{10,10},{3,19},{11,11},{4,20},{12... | collective-permute-start | bytes 786440 | tf_op jit(solution)/shard_map/ppermute | solution.py:333
  155.3 9.4 %copy-start.24 = (bf16[2,4,128,1024]{3,2,1,0:T(8,128)(2,1)S(1)}, bf16[2,4,128,1024]{3,2,1,0:T(8,128)(2,1)}, u32[]{:S(2)}) copy-start(bf16[2,4,128,1024]{3,2,1,0:T(8,128)(2,1)} %copy-done.18) | copy-start | bytes 6291460
  155.3 9.4 %copy-start.29 = (bf16[5,128,2048]{2,1,0:T(8,128)(2,1)S(1)}, bf16[5,128,2048]{2,1,0:T(8,128)(2,1)}, u32[]{:S(2)}) copy-start(bf16[5,128,2048]{2,1,0:T(8,128)(2,1)} %copy-done.28) | copy-start | bytes 7864324
  155.3 9.4 %copy-start.37 = (bf16[5,128,1024]{2,1,0:T(8,128)(2,1)S(1)}, bf16[5,128,1024]{2,1,0:T(8,128)(2,1)}, u32[]{:S(2)}) copy-start(bf16[5,128,1024]{2,1,0:T(8,128)(2,1)} %copy-done.36) | copy-start | bytes 3932164
  155.3 13.2 %collective-permute-start.15 = (bf16[128,1024]{1,0:T(8,128)(2,1)S(1)}, bf16[128,1024]{1,0:T(8,128)(2,1)S(1)}, u32[]{:S(2)}, u32[]{:S(2)}) collective-permute-start(bf16[128,1024]{1,0:T(8,128)(2,1)S(1)} %chain.30), channel_id=1, source_target_pairs={{0,8},{8,16},{1,9},{9,17},{2,10},{10,18},{3,11},{11,19},{4,12},{12... | collective-permute-start | bytes 786440 | tf_op jit(solution)/shard_map/ppermute | solution.py:333
  163.3 9.4 %collective-permute-start.14 = (bf16[128,1024]{1,0:T(8,128)(2,1)S(1)}, bf16[128,1024]{1,0:T(8,128)(2,1)S(1)}, u32[]{:S(2)}, u32[]{:S(2)}) collective-permute-start(bf16[128,1024]{1,0:T(8,128)(2,1)S(1)} %chain.31), channel_id=1, source_target_pairs={{0,16},{8,8},{1,17},{9,9},{2,18},{10,10},{3,19},{11,11},{4,20},{12... | collective-permute-start | bytes 786440 | tf_op jit(solution)/shard_map/ppermute | solution.py:333
  165.6 12.2 %collective-permute-start.17 = (bf16[128,1024]{1,0:T(8,128)(2,1)S(1)}, bf16[128,1024]{1,0:T(8,128)(2,1)S(1)}, u32[]{:S(2)}, u32[]{:S(2)}) collective-permute-start(bf16[128,1024]{1,0:T(8,128)(2,1)S(1)} %chain.31), channel_id=1, source_target_pairs={{0,8},{8,16},{1,9},{9,17},{2,10},{10,18},{3,11},{11,19},{4,12},{12... | collective-permute-start | bytes 786440 | tf_op jit(solution)/shard_map/ppermute | solution.py:333
  167.8 7.8 %collective-permute-start.2 = (bf16[128,1024]{1,0:T(8,128)(2,1)S(1)}, bf16[128,1024]{1,0:T(8,128)(2,1)S(1)}, u32[]{:S(2)}, u32[]{:S(2)}) collective-permute-start(bf16[128,1024]{1,0:T(8,128)(2,1)S(1)} %get-tuple-element.61), channel_id=1, source_target_pairs={{16,8},{24,16},{17,9},{25,17},{18,10},{26,18},{19,11},{27,19},{20,... | collective-permute-start | bytes 786440 | tf_op jit(solution)/shard_map/ppermute | solution.py:333
  168.5 5.5 %collective-permute-start.3 = (bf16[128,1024]{1,0:T(8,128)(2,1)S(1)}, bf16[128,1024]{1,0:T(8,128)(2,1)S(1)}, u32[]{:S(2)}, u32[]{:S(2)}) collective-permute-start(bf16[128,1024]{1,0:T(8,128)(2,1)S(1)} %get-tuple-element.62), channel_id=1, source_target_pairs={{16,8},{24,16},{17,9},{25,17},{18,10},{26,18},{19,11},{27,19},{20,... | collective-permute-start | bytes 786440 | tf_op jit(solution)/shard_map/ppermute | solution.py:333
  172.7 44.5 %collective-permute-start.16 = (bf16[128,1024]{1,0:T(8,128)(2,1)S(1)}, bf16[128,1024]{1,0:T(8,128)(2,1)S(1)}, u32[]{:S(2)}, u32[]{:S(2)}) collective-permute-start(bf16[128,1024]{1,0:T(8,128)(2,1)S(1)} %chain.32), channel_id=1, source_target_pairs={{8,8},{16,0},{9,9},{17,1},{10,10},{18,2},{11,11},{19,3},{12,12},{2... | collective-permute-start | bytes 786440 | tf_op jit(solution)/shard_map/ppermute | solution.py:333
  174.0 38.6 %collective-permute-start.19 = (bf16[128,1024]{1,0:T(8,128)(2,1)S(1)}, bf16[128,1024]{1,0:T(8,128)(2,1)S(1)}, u32[]{:S(2)}, u32[]{:S(2)}) collective-permute-start(bf16[128,1024]{1,0:T(8,128)(2,1)S(1)} %chain.32), channel_id=1, source_target_pairs={{8,16},{9,17},{10,18},{11,19},{12,20},{13,21},{14,22},{15,23}} | collective-permute-start | bytes 786440 | tf_op jit(solution)/shard_map/ppermute | solution.py:333
  175.6 25.7 %collective-permute-start.5 = (bf16[128,1024]{1,0:T(8,128)(2,1)S(1)}, bf16[128,1024]{1,0:T(8,128)(2,1)S(1)}, u32[]{:S(2)}, u32[]{:S(2)}) collective-permute-start(bf16[128,1024]{1,0:T(8,128)(2,1)S(1)} %get-tuple-element.68), channel_id=1, source_target_pairs={{8,0},{16,8},{9,1},{17,9},{10,2},{18,10},{11,3},{19,11},{12,4},{20... | collective-permute-start | bytes 786440 | tf_op jit(solution)/shard_map/ppermute | solution.py:333
  177.8 31.0 %collective-permute-start.4 = (bf16[128,1024]{1,0:T(8,128)(2,1)S(1)}, bf16[128,1024]{1,0:T(8,128)(2,1)S(1)}, u32[]{:S(2)}, u32[]{:S(2)}) collective-permute-start(bf16[128,1024]{1,0:T(8,128)(2,1)S(1)} %get-tuple-element.67), channel_id=1, source_target_pairs={{8,0},{16,8},{9,1},{17,9},{10,2},{18,10},{11,3},{19,11},{12,4},{20... | collective-permute-start | bytes 786440 | tf_op jit(solution)/shard_map/ppermute | solution.py:333
  201.3 17.2 %collective-permute-start.18 = (bf16[128,1024]{1,0:T(8,128)(2,1)S(1)}, bf16[128,1024]{1,0:T(8,128)(2,1)S(1)}, u32[]{:S(2)}, u32[]{:S(2)}) collective-permute-start(bf16[128,1024]{1,0:T(8,128)(2,1)S(1)} %chain.33), channel_id=1, source_target_pairs={{8,8},{16,0},{9,9},{17,1},{10,10},{18,2},{11,11},{19,3},{12,12},{2... | collective-permute-start | bytes 786440 | tf_op jit(solution)/shard_map/ppermute | solution.py:333
  208.8 6.0 %collective-permute-start.21 = (bf16[128,1024]{1,0:T(8,128)(2,1)S(1)}, bf16[128,1024]{1,0:T(8,128)(2,1)S(1)}, u32[]{:S(2)}, u32[]{:S(2)}) collective-permute-start(bf16[128,1024]{1,0:T(8,128)(2,1)S(1)} %chain.33), channel_id=1, source_target_pairs={{8,16},{9,17},{10,18},{11,19},{12,20},{13,21},{14,22},{15,23}} | collective-permute-start | bytes 786440 | tf_op jit(solution)/shard_map/ppermute | solution.py:333
  212.6 46.3 %collective-permute-start.6 = (bf16[128,1024]{1,0:T(8,128)(2,1)S(1)}, bf16[128,1024]{1,0:T(8,128)(2,1)S(1)}, u32[]{:S(2)}, u32[]{:S(2)}) collective-permute-start(bf16[128,1024]{1,0:T(8,128)(2,1)S(1)} %get-tuple-element.73), channel_id=1, source_target_pairs={{8,0},{9,1},{10,2},{11,3},{12,4},{13,5},{14,6},{15,7}} | collective-permute-start | bytes 786440 | tf_op jit(solution)/shard_map/ppermute | solution.py:333
  214.8 35.9 %collective-permute-start.7 = (bf16[128,1024]{1,0:T(8,128)(2,1)S(1)}, bf16[128,1024]{1,0:T(8,128)(2,1)S(1)}, u32[]{:S(2)}, u32[]{:S(2)}) collective-permute-start(bf16[128,1024]{1,0:T(8,128)(2,1)S(1)} %get-tuple-element.74), channel_id=1, source_target_pairs={{8,0},{9,1},{10,2},{11,3},{12,4},{13,5},{14,6},{15,7}} | collective-permute-start | bytes 786440 | tf_op jit(solution)/shard_map/ppermute | solution.py:333
  217.2 20.8 %collective-permute-start.20 = (bf16[128,1024]{1,0:T(8,128)(2,1)S(1)}, bf16[128,1024]{1,0:T(8,128)(2,1)S(1)}, u32[]{:S(2)}, u32[]{:S(2)}) collective-permute-start(bf16[128,1024]{1,0:T(8,128)(2,1)S(1)} %chain.34), channel_id=1, source_target_pairs={{16,0},{17,1},{18,2},{19,3},{20,4},{21,5},{22,6},{23,7}} | collective-permute-start | bytes 786440 | tf_op jit(solution)/shard_map/ppermute | solution.py:333
  218.6 22.5 %collective-permute-start.22 = (bf16[128,1024]{1,0:T(8,128)(2,1)S(1)}, bf16[128,1024]{1,0:T(8,128)(2,1)S(1)}, u32[]{:S(2)}, u32[]{:S(2)}) collective-permute-start(bf16[128,1024]{1,0:T(8,128)(2,1)S(1)} %chain.35), channel_id=1, source_target_pairs={{16,0},{17,1},{18,2},{19,3},{20,4},{21,5},{22,6},{23,7}} | collective-permute-start | bytes 786440 | tf_op jit(solution)/shard_map/ppermute | solution.py:333
  219.9 10.5 %copy-start.51 = (bf16[4,128,1024]{2,1,0:T(8,128)(2,1)}, bf16[4,128,1024]{2,1,0:T(8,128)(2,1)S(1)}, u32[]{:S(2)}) copy-start(bf16[4,128,1024]{2,1,0:T(8,128)(2,1)S(1)} %collective-permute-done.8.lb_ref) | copy-start | bytes 3145732
  219.9 22.5 %slice-start = ((s8[8388608]{0:T(1024)(128)(4,1)}), s8[4194304]{0:T(1024)(128)(4,1)S(1)}, s32[]{:S(2)}) async-start(s8[8388608]{0:T(1024)(128)(4,1)} %bitcast.160), calls=%async_computation.4 | async-start | bytes 8388608
  219.9 22.5 %slice-start.1 = ((s8[8388608]{0:T(1024)(128)(4,1)}), s8[4194304]{0:T(1024)(128)(4,1)S(1)}, s32[]{:S(2)}) async-start(s8[8388608]{0:T(1024)(128)(4,1)} %bitcast.160), calls=%async_computation.5 | async-start | bytes 8388608
  242.4 8.4 %slice-start.2 = ((s8[8388608]{0:T(1024)(128)(4,1)}), s8[4194304]{0:T(1024)(128)(4,1)S(1)}, s32[]{:S(2)}) async-start(s8[8388608]{0:T(1024)(128)(4,1)} %bitcast.162), calls=%async_computation.6 | async-start | bytes 8388608
  245.9 4.9 %slice-start.3 = ((s8[8388608]{0:T(1024)(128)(4,1)}), s8[4194304]{0:T(1024)(128)(4,1)S(1)}, s32[]{:S(2)}) async-start(s8[8388608]{0:T(1024)(128)(4,1)} %bitcast.162), calls=%async_computation.7 | async-start | bytes 8388608
  245.9 4.9 %copy-start.25 = (bf16[2,4,128,1024]{3,2,1,0:T(8,128)(2,1)S(1)}, bf16[2,4,128,1024]{3,2,1,0:T(8,128)(2,1)}, u32[]{:S(2)}) copy-start(bf16[2,4,128,1024]{3,2,1,0:T(8,128)(2,1)} %copy-done.18) | copy-start | bytes 6291460
  245.9 4.9 %copy-start.39 = (bf16[5,128,1024]{2,1,0:T(8,128)(2,1)S(1)}, bf16[5,128,1024]{2,1,0:T(8,128)(2,1)}, u32[]{:S(2)}) copy-start(bf16[5,128,1024]{2,1,0:T(8,128)(2,1)} %copy-done.38) | copy-start | bytes 3932164
  250.8 8.1 %copy-start.53 = (bf16[4,128,1024]{2,1,0:T(8,128)(2,1)}, bf16[4,128,1024]{2,1,0:T(8,128)(2,1)S(1)}, u32[]{:S(2)}) copy-start(bf16[4,128,1024]{2,1,0:T(8,128)(2,1)S(1)} %get-tuple-element.87.rb_ref) | copy-start | bytes 3145732
  258.9 6.4 %copy-start.50 = (bf16[1,4,128,1024]{3,2,1,0:T(8,128)(2,1)S(1)}, bf16[1,4,128,1024]{3,2,1,0:T(8,128)(2,1)}, u32[]{:S(2)}) copy-start(bf16[1,4,128,1024]{3,2,1,0:T(8,128)(2,1)} %get-tuple-element.93.la_ref) | copy-start | bytes 3145732
  258.9 6.4 %copy-start.52 = (bf16[4,128,1024]{2,1,0:T(8,128)(2,1)S(1)}, bf16[4,128,1024]{2,1,0:T(8,128)(2,1)}, u32[]{:S(2)}) copy-start(bf16[4,128,1024]{2,1,0:T(8,128)(2,1)} %copy-done.51) | copy-start | bytes 3145732
  274.9 100.0 %reduce-scatter.5.cloned.1.call-start = ((), (), s32[]{:S(2)}) async-start(), calls=%async_computation.3 | async-start | bytes 4718592 | tf_op jit(solution)/shard_map/reduce_scatter | solution.py:407
  292.6 31.8 %copy-start.60 = (f32[1,128,2048]{2,1,0:T(8,128)S(1)}, f32[1,128,2048]{2,1,0:T(8,128)}, u32[]{:S(2)}) copy-start(f32[1,128,2048]{2,1,0:T(8,128)} %param.12) | copy-start | bytes 3145732
  297.5 77.4 %copy-start.61 = (f32[1,256,1024]{2,1,0:T(8,128)S(1)}, f32[1,256,1024]{2,1,0:T(8,128)}, u32[]{:S(2)}) copy-start(f32[1,256,1024]{2,1,0:T(8,128)} %param.13) | copy-start | bytes 3145732
  326.9 52.8 %collective-permute-start.23 = (bf16[128,2048]{1,0:T(8,128)(2,1)S(1)}, bf16[128,2048]{1,0:T(8,128)(2,1)S(1)}, u32[]{:S(2)}, u32[]{:S(2)}) collective-permute-start(bf16[128,2048]{1,0:T(8,128)(2,1)S(1)} %get-tuple-element.97), channel_id=1, source_target_pairs={{0,24},{8,16},{16,8},{24,0},{1,25},{9,17},{17,9},{25,1},{2,26},{10... | collective-permute-start | bytes 1572872 | tf_op jit(solution)/shard_map/ppermute | solution.py:414
  377.3 12.4 %collective-permute-start.24 = (bf16[256,1024]{1,0:T(8,128)(2,1)S(1)}, bf16[256,1024]{1,0:T(8,128)(2,1)S(1)}, u32[]{:S(2)}, u32[]{:S(2)}) collective-permute-start(bf16[256,1024]{1,0:T(8,128)(2,1)S(1)} %get-tuple-element.95), channel_id=1, source_target_pairs={{0,24},{8,16},{16,8},{24,0},{1,25},{9,17},{17,9},{25,1},{2,26},{10... | collective-permute-start | bytes 1572872 | tf_op jit(solution)/shard_map/ppermute | solution.py:414
  (46 other events, 90.5 us)
Sparse Core Ops, SparseCore 0:
  275.0 49.3 reduce-scatter.2
  326.7 48.0 reduce-scatter.4

commit v2 on v1

v2 whole, which is shorter than its diff:
```python
import jax
import jax.numpy as jnp
import numpy as np
from jax import lax
from jax.experimental import pallas as pl
from jax.experimental.pallas import tpu as pltpu
from jax.sharding import PartitionSpec as P

norm_epsilon = 1e-06
momentum_decay = 0.9
step_size = 0.01
root_half = 0.7071067811865476
inv_root_tau = 0.3989422804014327

f32 = jnp.float32
bf16 = jnp.bfloat16
any_space = pl.BlockSpec(memory_space=pl.ANY)


def params(mib):
    return pltpu.CompilerParams(
        dimension_semantics=("arbitrary",), vmem_limit_bytes=mib * 1024 * 1024
    )


def in_hbm(x):
    return pltpu.with_memory_space_constraint(x, pltpu.HBM)


def dot(left, right, over):
    return lax.dot_general(left, right, (over, ((), ())), preferred_element_type=f32)


def tile_of(width):
    return min(512, width)


def forward_body(per, info, plan, *refs):
    u_refs = refs[:per]
    p_ref, q_ref = refs[per : per + 2]
    us_ref, h_ref, slope_ref, y_ref, r_ref, rows_ref, total = refs[-7:]
    j = pl.program_id(0)

    @pl.when(j == 0)
    def _():
        tokens = u_refs[0].shape[3]
        for k in range(per):
            u = u_refs[k][0, 0, 0]
            rows_ref[k * tokens : (k + 1) * tokens] = u
            us_ref[0, 0, k * tokens : (k + 1) * tokens] = u

    u = rows_ref[...]
    pre = dot(u, p_ref[0, 0], ((1,), (0,)))
    cdf = 0.5 * (1.0 + lax.erf(pre * root_half))
    hidden = (pre * cdf).astype(bf16)
    slope = cdf + pre * (jnp.exp(-0.5 * pre * pre) * inv_root_tau)
    h_ref[0, 0] = hidden
    slope_ref[0, 0] = slope.astype(bf16)
    part = dot(hidden, q_ref[0, 0], ((1,), (0,)))

    @pl.when(j == 0)
    def _():
        total[...] = u.astype(f32) + part

    @pl.when(j > 0)
    def _():
        total[...] += part

    @pl.when(j == pl.num_programs(0) - 1)
    def _():
        z = total[...]
        centre = z - jnp.mean(z, axis=-1, keepdims=True)
        r = lax.rsqrt(jnp.mean(centre * centre, axis=-1, keepdims=True) + norm_epsilon)
        y_ref[0, 0] = (centre * r).astype(bf16)
        r_ref[0, 0] = r


def forward(group, per, inputs, w_up, w_down, info, plan, previous, after, places):
    _, _, micro, tokens, model = inputs.shape
    width = w_up.shape[3]
    tile = tile_of(width)
    groups, rows = micro // per, per * tokens

    def u_spec(k):
        return pl.BlockSpec(
            (1, 1, 1, tokens, model), lambda j, i, p: (i[0], 0, p[i[2], group * per + k], 0, 0)
        )

    def out(columns, split=False, dtype=bf16):
        shape = pltpu.HBM((places, groups, rows, columns), dtype)
        block = (1, 1, rows, tile if split else columns)
        if split:
            return shape, pl.BlockSpec(block, lambda j, i, p: (i[3], group, 0, j))
        return shape, pl.BlockSpec(block, lambda j, i, p: (i[3], group, 0, 0))

    outs = [out(model), out(width, True), out(width, True), out(model), out(1, False, f32)]
    in_specs = [u_spec(k) for k in range(per)] + [
        pl.BlockSpec((1, 1, model, tile), lambda j, i, p: (i[1], 0, 0, j)),
        pl.BlockSpec((1, 1, tile, model), lambda j, i, p: (i[1], 0, j, 0)),
    ]
    operands = [in_hbm(inputs)] * per + [in_hbm(w_up), in_hbm(w_down)]
    aliases = {}
    if previous is not None:
        aliases = {2 + len(operands) + k: k for k in range(5)}
        in_specs += [any_space] * 5
        operands += [in_hbm(x) for x in previous]
    for x in after:
        if previous is None or not any(x is y for y in previous):
            in_specs.append(any_space)
            operands.append(in_hbm(x) if x.ndim > 2 else x)

    def body(*refs):
        forward_body(per, *refs)

    return pl.pallas_call(
        body,
        grid_spec=pltpu.PrefetchScalarGridSpec(
            num_scalar_prefetch=2,
            grid=(width // tile,),
            in_specs=in_specs,
            out_specs=[spec for _, spec in outs],
            scratch_shapes=[pltpu.VMEM((rows, model), bf16), pltpu.VMEM((rows, model), f32)],
        ),
        out_shape=[shape for shape, _ in outs],
        input_output_aliases=aliases,
        compiler_params=params(40),
        cost_estimate=pl.CostEstimate(
            flops=8 * rows * model * width, bytes_accessed=4 * model * width, transcendentals=0
        ),
        name="forward",
    )(info, plan, *operands)


def sum_gradient(e, y, r):
    mean_e = jnp.mean(e, axis=-1, keepdims=True)
    mean_ey = jnp.mean(e * y, axis=-1, keepdims=True)
    return r * (e - mean_e - y * mean_ey)


columns_of_table = 6


def chain_step(call, table, recv, top_grad, saved, w_up, w_down, previous, after):
    base = call * columns_of_table
    _, _, slopes, ys, rs = saved
    rows, model = recv[0].shape
    width = w_up.shape[3]
    tile = tile_of(width)
    groups = slopes.shape[1]
    tokens = top_grad.shape[2]
    per = rows // tokens

    def body(info, *rest):
        recv_refs, rest = rest[: len(recv)], rest[len(recv) :]
        top_ref, y_ref, r_ref, slope_ref, p_ref, q_ref = rest[:6]
        out_ref, pre_ref, sum_ref, whole, low, total = rest[-6:]
        j = pl.program_id(0)
        active = info[base] > 0

        @pl.when(jnp.logical_and(active, j == 0))
        def _():
            top = top_ref[0].reshape(rows, model)
            e = jnp.where(info[base + 4] == 1, top, recv_refs[-1][...])
            if len(recv) > 1:
                e = jnp.where(info[base + 4] == 2, recv_refs[0][...], e)
            e = e.astype(f32)
            grad = sum_gradient(e, y_ref[0, 0].astype(f32), r_ref[0, 0])
            whole[...] = grad
            low[...] = grad.astype(bf16)
            sum_ref[0] = grad.astype(bf16)

        @pl.when(active)
        def _():
            grad_pre = (
                dot(low[...], q_ref[0, 0], ((1,), (1,))) * slope_ref[0, 0].astype(f32)
            ).astype(bf16)
            pre_ref[0] = grad_pre

            @pl.when(info[base + 5] > 0)
            def _():
                part = dot(grad_pre, p_ref[0, 0], ((1,), (1,)))

                @pl.when(j == 0)
                def _():
                    total[...] = whole[...] + part

                @pl.when(j > 0)
                def _():
                    total[...] += part

                @pl.when(j == pl.num_programs(0) - 1)
                def _():
                    out_ref[...] = total[...].astype(bf16)

    in_specs = [pl.BlockSpec((rows, model), lambda j, i: (0, 0))] * len(recv) + [
        pl.BlockSpec((1, per, tokens, model), lambda j, i: (i[base + 1], i[base + 2], 0, 0)),
        pl.BlockSpec((1, 1, rows, model), lambda j, i: (i[base + 1], i[base + 2], 0, 0)),
        pl.BlockSpec((1, 1, rows, 1), lambda j, i: (i[base + 1], i[base + 2], 0, 0)),
        pl.BlockSpec(
            (1, 1, rows, tile), lambda j, i: (i[base + 1], i[base + 2], 0, j * i[base])
        ),
        pl.BlockSpec((1, 1, model, tile), lambda j, i: (i[base + 1], 0, 0, j * i[base + 5])),
        pl.BlockSpec((1, 1, tile, model), lambda j, i: (i[base + 1], 0, j * i[base], 0)),
    ]
    operands = list(recv) + [in_hbm(x) for x in (top_grad, ys, rs, slopes, w_up, w_down)]
    aliases = {}
    if previous is not None:
        aliases = {1 + len(operands): 1, 2 + len(operands): 2}
        in_specs += [any_space] * 2
        operands += [in_hbm(x) for x in previous]
    for x in after:
        if previous is None or not any(x is y for y in previous):
            in_specs.append(any_space)
            operands.append(in_hbm(x) if x.ndim > 2 else x)
    return pl.pallas_call(
        body,
        grid_spec=pltpu.PrefetchScalarGridSpec(
            num_scalar_prefetch=1,
            grid=(width // tile,),
            in_specs=in_specs,
            out_specs=[
                pl.BlockSpec((rows, model), lambda j, i: (0, 0)),
                pl.BlockSpec((1, rows, tile), lambda j, i: (i[base + 3], 0, j * i[base])),
                pl.BlockSpec((1, rows, model), lambda j, i: (i[base + 3], 0, 0)),
            ],
            scratch_shapes=[
                pltpu.VMEM((rows, model), f32),
                pltpu.VMEM((rows, model), bf16),
                pltpu.VMEM((rows, model), f32),
            ],
        ),
        out_shape=[
            jax.ShapeDtypeStruct((rows, model), bf16),
            pltpu.HBM((groups + 1, rows, width), bf16),
            pltpu.HBM((groups + 1, rows, model), bf16),
        ],
        input_output_aliases=aliases,
        compiler_params=params(32),
        cost_estimate=pl.CostEstimate(
            flops=8 * rows * model * width, bytes_accessed=4 * model * width, transcendentals=0
        ),
        name="chain",
    )(table, *operands)


def home_step(info, arrived, top_grad, saved, w_down, after):
    _, _, slopes, ys, rs = saved
    groups, rows, model = slopes.shape[1], slopes.shape[2], ys.shape[3]
    micro, tokens = top_grad.shape[1:3]
    width = w_down.shape[2]
    tile = tile_of(width)

    def body(info, *refs):
        e_refs = refs[:groups]
        top_ref, y_ref, r_ref, slope_ref, q_ref = refs[groups : groups + 5]
        pre_ref, sum_ref = refs[-2:]

        @pl.when(pl.program_id(0) == 0)
        def _():
            for g in range(groups):
                top = top_ref[0].reshape(groups, rows, model)[g]
                e = jnp.where(info[0] > 0, top, e_refs[g][...]).astype(f32)
                grad = sum_gradient(e, y_ref[0, g].astype(f32), r_ref[0, g])
                sum_ref[g] = grad.astype(bf16)

        low = sum_ref[...].reshape(groups * rows, model)
        slope = slope_ref[0].reshape(groups * rows, tile)
        grad_pre = dot(low, q_ref[0, 0], ((1,), (1,))) * slope.astype(f32)
        pre_ref[...] = grad_pre.astype(bf16).reshape(pre_ref.shape)

    return pl.pallas_call(
        body,
        grid_spec=pltpu.PrefetchScalarGridSpec(
            num_scalar_prefetch=1,
            grid=(width // tile,),
            in_specs=[pl.BlockSpec((rows, model), lambda j, i: (0, 0))] * groups
            + [
                pl.BlockSpec((1, micro, tokens, model), lambda j, i: (1, 0, 0, 0)),
                pl.BlockSpec((1, groups, rows, model), lambda j, i: (0, 0, 0, 0)),
                pl.BlockSpec((1, groups, rows, 1), lambda j, i: (0, 0, 0, 0)),
                pl.BlockSpec((1, groups, rows, tile), lambda j, i: (0, 0, 0, j)),
                pl.BlockSpec((1, 1, tile, model), lambda j, i: (0, 0, j, 0)),
            ]
            + [any_space] * len(after),
            out_specs=[
                pl.BlockSpec((groups, rows, tile), lambda j, i: (0, 0, j)),
                pl.BlockSpec((groups, rows, model), lambda j, i: (0, 0, 0)),
            ],
        ),
        out_shape=[
            pltpu.HBM((groups, rows, width), bf16),
            pltpu.HBM((groups, rows, model), bf16),
        ],
        compiler_params=params(40),
        cost_estimate=pl.CostEstimate(
            flops=4 * groups * rows * model * width,
            bytes_accessed=2 * model * width,
            transcendentals=0,
        ),
        name="home",
    )(
        info,
        *arrived,
        *[in_hbm(x) for x in (top_grad, ys, rs, slopes, w_down)],
        *[in_hbm(x) if x.ndim > 2 else x for x in after],
    )


def weight_gradient(left_a, right_a, left_b, right_b, groups, split_left, after):
    tokens = right_a.shape[-2]
    rows, columns = left_a.shape[-1], right_a.shape[-1]
    tile = tile_of(rows if split_left else columns)

    def body(la_ref, ra_ref, lb_ref, rb_ref, *rest):
        def flat(ref):
            return ref[...].reshape(-1, ref.shape[-1])

        total = dot(flat(la_ref), flat(ra_ref), ((0,), (0,)))
        total += dot(flat(lb_ref), flat(rb_ref), ((0,), (0,)))
        rest[-1][...] = total.astype(bf16)

    def spec(array, split):
        lead = array.ndim - 3
        block = (1,) * lead + (groups, tokens, tile if split else array.shape[-1])
        if split:
            return pl.BlockSpec(block, lambda j: (0,) * (lead + 2) + (j,))
        return pl.BlockSpec(block, lambda j: (0,) * (lead + 3))

    out_block = (tile, columns) if split_left else (rows, tile)
    return pl.pallas_call(
        body,
        grid=((rows if split_left else columns) // tile,),
        in_specs=[
            spec(left_a, split_left),
            spec(right_a, not split_left),
            spec(left_b, split_left),
            spec(right_b, not split_left),
        ]
        + [any_space] * len(after),
        out_specs=pl.BlockSpec(out_block, (lambda j: (j, 0)) if split_left else (lambda j: (0, j))),
        out_shape=pltpu.HBM((rows, columns), bf16),
        compiler_params=params(40),
        cost_estimate=pl.CostEstimate(
            flops=4 * groups * tokens * rows * columns,
            bytes_accessed=2 * rows * columns,
            transcendentals=0,
        ),
        name="weights",
    )(*[in_hbm(x) for x in (left_a, right_a, left_b, right_b)], *[in_hbm(x) for x in after])


def update(replica, weight, moment, total):
    _, rows, columns = moment.shape
    tile = min(64, rows)
    steps = rows // tile

    def body(info, weight_ref, moment_ref, total_ref, fresh_ref, out_ref):
        fresh_moment = momentum_decay * moment_ref[0] + total_ref[...].astype(f32)
        out_ref[0] = fresh_moment
        fresh_ref[...] = (weight_ref[0, 0].astype(f32) - step_size * fresh_moment).astype(bf16)

    return pl.pallas_call(
        body,
        grid_spec=pltpu.PrefetchScalarGridSpec(
            num_scalar_prefetch=1,
            grid=(steps,),
            in_specs=[
                pl.BlockSpec((1, 1, tile, columns), lambda j, i: (0, 0, i[0] * steps + j, 0)),
                pl.BlockSpec((1, tile, columns), lambda j, i: (0, j, 0)),
                pl.BlockSpec((tile, columns), lambda j, i: (j, 0)),
            ],
            out_specs=[
                pl.BlockSpec((tile, columns), lambda j, i: (j, 0)),
                pl.BlockSpec((1, tile, columns), lambda j, i: (0, j, 0)),
            ],
        ),
        out_shape=[
            jax.ShapeDtypeStruct((rows, columns), bf16),
            pltpu.HBM((1, rows, columns), f32),
        ],
        compiler_params=params(24),
        cost_estimate=pl.CostEstimate(
            flops=4 * rows * columns, bytes_accessed=12 * rows * columns, transcendentals=0
        ),
        name="update",
    )(replica, in_hbm(weight), in_hbm(moment), total)


def on_device(section_inputs, top_grad, plan, up_weight, down_weight, up_moment, down_moment):
    sections = lax.axis_size("section")
    position = lax.axis_index("section").astype(jnp.int32)
    micro, tokens, model = top_grad.shape[1:]
    plan = plan.astype(jnp.int32)
    per = 2 if micro % 2 == 0 else 1
    groups, rows = micro // per, per * tokens
    last, half = sections - 1, sections // 2

    def hop(value, pairs):
        return lax.ppermute(value, "section", pairs) if pairs else None

    mirrored = lax.ppermute(
        section_inputs[1, 0], "section", [(i, last - i) for i in range(sections)]
    )[None, None]

    upper = (position >= half).astype(jnp.int32)
    near = jnp.minimum(position, last - position)
    start = (near, last - near)
    relay = (1 - upper, upper)

    def begins(kind, i):
        return min(i, last - i) if kind == 0 else last - min(i, last - i)

    calls = [
        (tick, kind)
        for tick in range(groups + last)
        for kind in range(2)
        if any(0 <= tick - begins(kind, i) < groups for i in range(sections))
    ]
    ticks = np.array([tick for tick, _ in calls], np.int32)
    second = np.array([kind for _, kind in calls], np.int32)
    group = jnp.where(second == 1, ticks - start[1], ticks - start[0])
    of = jnp.where(second == 1, relay[1], relay[0])
    needless = jnp.logical_and(of == 1, position == last)
    active = (group >= 0) & (group < groups) & ~needless
    group = jnp.clip(group, 0, groups - 1)
    asked = active & ~((of == 0) & (position == 0))
    table = jnp.stack(
        [
            active.astype(jnp.int32),
            of,
            group,
            jnp.where(active & (of == 0), group, groups),
            jnp.where(
                jnp.where(of == 0, position == last, position == 0),
                1,
                jnp.where((second == 1) & (near == half - 1), 2, 0),
            ),
            asked.astype(jnp.int32),
        ],
        axis=1,
    ).reshape(-1)
    kinds = [jnp.stack([relay[k]] * 4) for k in range(2)]
    home_kind = jnp.array([0, 0, 1, 0], jnp.int32)

    saved = None
    saved_home = None
    order = []

    def run_forward(kind, g):
        nonlocal saved, order
        saved = forward(
            g, per, section_inputs, up_weight, down_weight, kinds[kind], plan, saved, order, 2
        )
        order = [saved[0]]

    def run_home_forward(g):
        nonlocal saved_home, order
        saved_home = forward(
            g, per, mirrored, up_weight, down_weight, home_kind, plan, saved_home, order, 1
        )
        order = [saved_home[0]]

    pending = [(0, g) for g in range(groups)] + [(1, g) for g in range(groups)]
    late = []
    blank = jnp.zeros((rows, model), bf16)
    received = {}
    arrived = {}
    kept = None
    for call, (tick, kind) in enumerate(calls):
        newest = min(tick - (sections - half if kind else 0), groups - 1)
        while pending and any(k < kind or (k == kind and g <= newest) for k, g in pending):
            run_forward(*pending.pop(0))
        if call == len(calls) - 1:
            for g in range(groups):
                run_home_forward(g)

        def busy(i):
            return 0 <= tick - begins(kind, i) < groups

        recv = [
            received.pop((tick, kind, way))
            for way in range(2)
            if (tick, kind, way) in received
        ] or [blank]
        out, *kept = chain_step(
            call, table, recv, top_grad, saved, up_weight, down_weight, kept, order
        )
        order = [kept[0]] + [x for n, x in late if n < call]
        late = [(n, x) for n, x in late if n >= call]
        relay_of = [(0 if i >= half else 1) if kind == 0 else (1 if i >= half else 0) for i in range(sections)]
        to = [i - 1 if relay_of[i] == 0 else i + 1 for i in range(sections)]
        live = [
            i
            for i in range(sections)
            if busy(i) and 0 <= to[i] <= last and not (relay_of[i] == 1 and to[i] == last)
        ]
        crossing = [i for i in live if kind == 0 and (i >= half) != (to[i] >= half)]
        for pairs, kind_after, way in (
            ([(i, to[i]) for i in live if i in crossing], 1, 0),
            ([(i, to[i]) for i in live if i not in crossing], kind, 1),
        ):
            got = hop(out, pairs)
            if got is not None:
                received[(tick + 1, kind_after, way)] = got
        pairs = [(i, last - 1 - i) for i in range(last) if busy(i) and relay_of[i] == 1]
        got = hop(out, pairs)
        if got is not None:
            for i, k in pairs:
                arrived[(k, tick - begins(kind, i))] = got
            late.append((call, got))
        if pending and (kind == 1 or pending[0][0] == 0 or tick + 1 >= groups):
            run_forward(*pending.pop(0))

    came = []
    for g in range(groups):
        options = []
        for k in range(last):
            value = arrived[(k, g)]
            if not any(value is x for x, _ in options):
                options.append((value, []))
            next(places for x, places in options if x is value).append(k)
        value = options[0][0]
        for other, places in options[1:]:
            here = either([position == k for k in places])
            value = jnp.where(here, other, value)
        came.append(value)
    home_pre, home_sum = home_step(
        (position == last).astype(jnp.int32)[None], came, top_grad, saved_home, down_weight, order
    )

    up_part = weight_gradient(saved[0], kept[0], saved_home[0], home_pre, groups, False, [])
    up_sum = lax.psum_scatter(up_part, "dp", scatter_dimension=0, tiled=True)
    down_part = weight_gradient(
        saved[1], kept[1], saved_home[1], home_sum, groups, True, [up_part]
    )
    down_sum = lax.psum_scatter(down_part, "dp", scatter_dimension=0, tiled=True)
    replica = lax.axis_index("dp").astype(jnp.int32)[None]

    def finish(weight, moment, total):
        fresh, fresh_moment = update(replica, weight, moment, total)
        far = lax.ppermute(fresh, "section", [(i, last - i) for i in range(sections)])
        return jnp.stack([fresh, far])[:, None], fresh_moment

    new_up_weight, new_up_moment = finish(up_weight, up_moment, up_sum)
    new_down_weight, new_down_moment = finish(down_weight, down_moment, down_sum)
    return (new_up_weight, new_down_weight, new_up_moment, new_down_moment)


def either(conditions):
    result = conditions[0]
    for condition in conditions[1:]:
        result = jnp.logical_or(result, condition)
    return result


def solution(mesh):
    in_specs = (
        P(None, "section", None, "dp", None),
        P(None, None, "dp", None),
        P(),
        P(None, "section", None, None),
        P(None, "section", None, None),
        P("section", "dp", None),
        P("section", "dp", None),
    )
    out_specs = (
        P(None, "section", "dp", None),
        P(None, "section", "dp", None),
        P("section", "dp", None),
        P("section", "dp", None),
    )
    return jax.shard_map(
        on_device, mesh=mesh, in_specs=in_specs, out_specs=out_specs, check_vma=False
    )
```

time: 400 us -> 327 us (0.82)
  local copies, waits for them, and re-layouts: 120 us -> 4.07 us
  waiting for transfers between devices: 117 us -> 154 us
  Pallas kernels: 92.7 us -> 125 us
  between operations: 26.4 us -> 14.3 us
  starting transfers between devices: 35 us -> 24.1 us
    unnamed x141 -> x12, local copies, waits for them, and re-layouts: 93.5 us -> 2.77 us
    pallas_call x24 -> x17, Pallas kernels: 92.7 us -> 125 us  [the longest x6 53.9 us: forward(): pl.pallas_call(body, grid_spec=pltpu.PrefetchScalarGridSpec(num_scalar_pr...]
    reduce_scatter x1, waiting for transfers between devices: 27 us -> 43.5 us  [on_device(): up_sum = lax.psum_scatter(up_part, 'dp', scatter_dimension=0, tiled=True)]
    ppermute x22 -> x11, waiting for transfers between devices: 35 us -> 49 us  [hop(): return lax.ppermute(value, 'section', pairs) if pairs else None]
    another operation x22 -> x4, local copies, waits for them, and re-layouts: 12.8 us -> 0.12 us  [the longest x2 0.12 us: on_device(): jnp.stack([active.astype(jnp.int32), of, group, jnp.where(active & (of ==...]
    ppermute x22 -> x11, starting transfers between devices: 27.6 us -> 16 us  [hop(): return lax.ppermute(value, 'section', pairs) if pairs else None]
    slice x2 -> x0, local copies, waits for them, and re-layouts: 9.66 us -> none  [update(): held = lax.dynamic_slice_in_dim(weight[0, 0], replica * rows, rows, 0)]
    reduce_scatter x1, waiting for transfers between devices: 45.7 us -> 52.3 us  [on_device(): lax.psum_scatter(down_part, 'dp', scatter_dimension=0, tiled=True)]
  transfers between devices with their start and end apart: 27 -> 16, of which waited for: 8 -> 7; matrix products, arithmetic and copies ran while one was open for 8% -> 1% of each run, Pallas kernels for 15% -> 23%
where the time goes in v2:
time: 327 us; the launch traced here: 325 us
  waiting for transfers between devices  154 us (47%)
  Pallas kernels  125 us (38%)
  starting transfers between devices  24.1 us (7%)
  between operations  14.3 us (4%)
  local copies, waits for them, and re-layouts  4.07 us (1%)
  other arithmetic  3.7 us (1%)
    pallas_call x6, Pallas kernels, forward(): pl.pallas_call(body, grid_spec=pltpu.PrefetchScalarGridSpec(num_scalar_pr...  53.9 us
    reduce_scatter x1, waiting for transfers between devices, on_device(): lax.psum_scatter(down_part, 'dp', scatter_dimension=0, tiled=True)  52.3 us
    ppermute x11, waiting for transfers between devices, hop(): return lax.ppermute(value, 'section', pairs) if pairs else None  49 us
    reduce_scatter x1, waiting for transfers between devices, on_device(): up_sum = lax.psum_scatter(up_part, 'dp', scatter_dimension=0, tiled=True)  43.5 us
    pallas_call x6, Pallas kernels, chain_step(): pl.pallas_call(body, grid_spec=pltpu.PrefetchScalarGridSpec(num_scalar_pr...  40.5 us
    pallas_call x2, Pallas kernels, weight_gradient(): pl.pallas_call(body, grid=((rows if split_left else columns) // tile,), i...  16.9 us
    ppermute x11, starting transfers between devices, hop(): return lax.ppermute(value, 'section', pairs) if pairs else None  16 us
    ppermute x2, waiting for transfers between devices, finish(): lax.ppermute(fresh, 'section', [(i, last - i) for i in range(sections)])  8.97 us
  transfers between devices with their start and end apart: 16, of which 7 were waited for; matrix products, arithmetic and copies ran while one was open for 1% of the time, Pallas kernels for 23%

profile of v2, /device:TPU:0, one launch (start us, length us, event | category | flops | bytes accessed | tf_op | source)
XLA Modules:
  0.0 325.5 jit_solution(15080590536673606675)
XLA Ops:
  7.2 0.7 fusion.2
  7.9 0.7 fusion.1
  8.8 0.7 copy-done.2
  9.5 9.0 %forward.6 = (bf16[2,2,256,1024]{3,2,1,0:T(8,128)(2,1)}, bf16[2,2,256,2048]{3,2,1,0:T(8,128)(2,1)}, bf16[2,2,256,2048]{3,2,1,0:T(8,128)(2,1)}, bf16[2,2,256,1024]{3,2,1,0:T(8,128)(2,1)}, f32[2,2,256,1]{3,2,1,0:T(8,128)}) custom-call(s32[4]{0:T(128)S(1)} %stack.60.refs_0_, s32[2,4]{1,0:T(2,128)S(1)} %copy-done.2, bf16[2,1,4,128,1024]{4,3,2,1,0:T(8,128)(2,1)} %refs_3_.7, ...), custom_call_target="tpu_custom_call" | custom-call | flops 4294967296 | bytes 8388608 | tf_op jit(solution)/shard_map/forward/pallas_call | solution.py:115
  18.6 9.5 %chain.6 = (bf16[256,1024]{1,0:T(8,128)(2,1)S(1)}, bf16[3,256,2048]{2,1,0:T(8,128)(2,1)}, bf16[3,256,1024]{2,1,0:T(8,128)(2,1)}) custom-call(s32[36]{0:T(128)S(1)} %reshape.15.info, bf16[256,1024]{1,0:T(8,128)(2,1)S(1)} %broadcast_in_dim.46.rest_0_, bf16[2,4,128,1024]{3,2,1,0:T(8,128)(2,1)} %refs_2_.9, ...), custom_call_target="tpu_custom_call" | custom-call | flops 4294967296 | bytes 8388608 | tf_op jit(solution)/shard_map/chain/pallas_call | solution.py:215
  28.0 1.3 collective-permute-start
  29.3 1.3 collective-permute-start.1
  30.7 9.0 %forward.7 = (bf16[2,2,256,1024]{3,2,1,0:T(8,128)(2,1)}, bf16[2,2,256,2048]{3,2,1,0:T(8,128)(2,1)}, bf16[2,2,256,2048]{3,2,1,0:T(8,128)(2,1)}, bf16[2,2,256,1024]{3,2,1,0:T(8,128)(2,1)}, f32[2,2,256,1]{3,2,1,0:T(8,128)}) custom-call(s32[4]{0:T(128)S(1)} %stack.60.refs_0_, ...), custom_call_target="tpu_custom_call", output_to_operand_aliasing={{0}: (6, {}), {1}: (7, {}), {2}: (8, {}), {3}: (9, {}), {4}... | custom-call | flops 4294967296 | bytes 8388608 | tf_op jit(solution)/shard_map/forward/pallas_call | solution.py:115
  39.7 1.7 collective-permute-done.rest_0_
  41.4 9.5 %chain.7 = (bf16[256,1024]{1,0:T(8,128)(2,1)S(1)}, bf16[3,256,2048]{2,1,0:T(8,128)(2,1)}, bf16[3,256,1024]{2,1,0:T(8,128)(2,1)}) custom-call(s32[36]{0:T(128)S(1)} %reshape.15.info, bf16[256,1024]{1,0:T(8,128)(2,1)S(1)} %collective-permute-done.rest_0_, bf16[2,4,128,1024]{3,2,1,0:T(8,128)(2,1)} %refs_2_.9, ...), custom_call_target="tpu_custom_call", output_to_operand_aliasing={{1}: (8, {}), {2}: (9, {})} | custom-call | flops 4294967296 | bytes 8388608 | tf_op jit(solution)/shard_map/chain/pallas_call | solution.py:215
  50.9 4.4 %collective-permute-start.2 = (bf16[256,1024]{1,0:T(8,128)(2,1)S(1)}, bf16[256,1024]{1,0:T(8,128)(2,1)S(1)}, u32[]{:S(2)}, u32[]{:S(2)}) collective-permute-start(bf16[256,1024]{1,0:T(8,128)(2,1)S(1)} %get-tuple-element.76), channel_id=1, source_target_pairs={{0,8},{24,16},{1,9},{25,17},{2,10},{26,18},{3,11},{27,19},{4,12},{... | collective-permute-start | bytes 1572872 | tf_op jit(solution)/shard_map/ppermute | solution.py:399
  55.3 1.0 slice_bitcast_fusion
  56.3 3.2 collective-permute-start.9
  59.6 1.3 collective-permute-start.3
  60.9 0.9 collective-permute-start.5
  61.8 9.0 %forward.8 = (bf16[2,2,256,1024]{3,2,1,0:T(8,128)(2,1)}, bf16[2,2,256,2048]{3,2,1,0:T(8,128)(2,1)}, bf16[2,2,256,2048]{3,2,1,0:T(8,128)(2,1)}, bf16[2,2,256,1024]{3,2,1,0:T(8,128)(2,1)}, f32[2,2,256,1]{3,2,1,0:T(8,128)}) custom-call(s32[4]{0:T(128)S(1)} %stack.59.refs_0_, ...), custom_call_target="tpu_custom_call", output_to_operand_aliasing={{0}: (6, {}), {1}: (7, {}), {2}: (8, {}), {3}: (9, {}), {4}... | custom-call | flops 4294967296 | bytes 8388608 | tf_op jit(solution)/shard_map/forward/pallas_call | solution.py:115
  70.8 3.6 %chain.8 = (bf16[256,1024]{1,0:T(8,128)(2,1)}, bf16[3,256,2048]{2,1,0:T(8,128)(2,1)}, bf16[3,256,1024]{2,1,0:T(8,128)(2,1)}) custom-call(s32[36]{0:T(128)S(1)} %reshape.15.info, bf16[256,1024]{1,0:T(8,128)(2,1)S(1)} %collective-permute-done.2.rest_0_, bf16[2,4,128,1024]{3,2,1,0:T(8,128)(2,1)} %refs_2_.9, ...), custom_call_target="tpu_custom_call", output_to_operand_aliasing={{1}: (8, {}), {2}: (9, {})} | custom-call | flops 4294967296 | bytes 8388608 | tf_op jit(solution)/shard_map/chain/pallas_call | solution.py:215
  74.4 28.5 %collective-permute-done.3.refs_12_ = bf16[256,1024]{1,0:T(8,128)(2,1)S(1)} collective-permute-done((bf16[256,1024]{1,0:T(8,128)(2,1)S(1)}, bf16[256,1024]{1,0:T(8,128)(2,1)S(1)}, u32[]{:S(2)}, u32[]{:S(2)}) %collective-permute-start.3) | collective-permute-done | bytes 524320 | tf_op jit(solution)/shard_map/ppermute | solution.py:399
  102.9 9.0 %forward.9 = (bf16[2,2,256,1024]{3,2,1,0:T(8,128)(2,1)}, bf16[2,2,256,2048]{3,2,1,0:T(8,128)(2,1)}, bf16[2,2,256,2048]{3,2,1,0:T(8,128)(2,1)}, bf16[2,2,256,1024]{3,2,1,0:T(8,128)(2,1)}, f32[2,2,256,1]{3,2,1,0:T(8,128)}) custom-call(s32[4]{0:T(128)S(1)} %stack.59.refs_0_, ...), custom_call_target="tpu_custom_call", output_to_operand_aliasing={{0}: (6, {}), {1}: (7, {}), {2}: (8, {}), {3}: (9, {}), {4}... | custom-call | flops 4294967296 | bytes 8388608 | tf_op jit(solution)/shard_map/forward/pallas_call | solution.py:115
  111.9 3.6 %chain.9 = (bf16[256,1024]{1,0:T(8,128)(2,1)}, bf16[3,256,2048]{2,1,0:T(8,128)(2,1)}, bf16[3,256,1024]{2,1,0:T(8,128)(2,1)}) custom-call(s32[36]{0:T(128)S(1)} %reshape.15.info, bf16[256,1024]{1,0:T(8,128)(2,1)S(1)} %collective-permute-done.5.rest_0_, bf16[2,4,128,1024]{3,2,1,0:T(8,128)(2,1)} %refs_2_.9, ...), custom_call_target="tpu_custom_call", output_to_operand_aliasing={{1}: (8, {}), {2}: (9, {})} | custom-call | flops 4294967296 | bytes 8388608 | tf_op jit(solution)/shard_map/chain/pallas_call | solution.py:215
  115.5 1.3 collective-permute-start.6
  116.8 0.7 collective-permute-start.4
  117.5 0.7 collective-permute-start.7
  118.2 1.3 collective-permute-start.10
  119.5 12.9 %collective-permute-done.6.rest_1_ = bf16[256,1024]{1,0:T(8,128)(2,1)S(1)} collective-permute-done((bf16[256,1024]{1,0:T(8,128)(2,1)}, bf16[256,1024]{1,0:T(8,128)(2,1)S(1)}, u32[]{:S(2)}, u32[]{:S(2)}) %collective-permute-start.6) | collective-permute-done | bytes 524320 | tf_op jit(solution)/shard_map/ppermute | solution.py:399
  132.4 7.1 %chain.10 = (bf16[256,1024]{1,0:T(8,128)(2,1)S(1)}, bf16[3,256,2048]{2,1,0:T(8,128)(2,1)}, bf16[3,256,1024]{2,1,0:T(8,128)(2,1)}) custom-call(s32[36]{0:T(128)S(1)} %reshape.15.info, bf16[256,1024]{1,0:T(8,128)(2,1)S(1)} %collective-permute-done.4.rest_0_, ...), custom_call_target="tpu_custom_call", output_to_operand_aliasing={{1}: (9, {}), {2}: (10, {})} | custom-call | flops 4294967296 | bytes 8388608 | tf_op jit(solution)/shard_map/chain/pallas_call | solution.py:215
  139.5 1.3 collective-permute-start.11
  140.8 1.5 collective-permute-start.8
  142.3 9.0 %forward.10 = (bf16[1,2,256,1024]{3,2,1,0:T(8,128)(2,1)}, bf16[1,2,256,2048]{3,2,1,0:T(8,128)(2,1)}, bf16[1,2,256,2048]{3,2,1,0:T(8,128)(2,1)}, bf16[1,2,256,1024]{3,2,1,0:T(8,128)(2,1)}, f32[1,2,256,1]{3,2,1,0:T(8,128)}) custom-call(s32[4]{0:T(128)S(1)} %copy-done.4, s32[2,4]{1,0:T(2,128)S(1)} %copy-done.3, ...), custom_call_target="tpu_custom_call" | custom-call | flops 4294967296 | bytes 8388608 | tf_op jit(solution)/shard_map/forward/pallas_call | solution.py:115
  151.3 9.0 %forward.11 = (bf16[1,2,256,1024]{3,2,1,0:T(8,128)(2,1)}, bf16[1,2,256,2048]{3,2,1,0:T(8,128)(2,1)}, bf16[1,2,256,2048]{3,2,1,0:T(8,128)(2,1)}, bf16[1,2,256,1024]{3,2,1,0:T(8,128)(2,1)}, f32[1,2,256,1]{3,2,1,0:T(8,128)}) custom-call(s32[4]{0:T(128)S(1)} %copy-done.4, ...), custom_call_target="tpu_custom_call", output_to_operand_aliasing={{0}: (6, {}), {1}: (7, {}), {2}: (8, {}), {3}: (9, {}), {4}... | custom-call | flops 4294967296 | bytes 8388608 | tf_op jit(solution)/shard_map/forward/pallas_call | solution.py:115
  160.3 5.9 %collective-permute-done.11.refs_8_ = bf16[256,1024]{1,0:T(8,128)(2,1)S(1)} collective-permute-done((bf16[256,1024]{1,0:T(8,128)(2,1)S(1)}, bf16[256,1024]{1,0:T(8,128)(2,1)S(1)}, u32[]{:S(2)}, u32[]{:S(2)}) %collective-permute-start.11) | collective-permute-done | bytes 524320 | tf_op jit(solution)/shard_map/ppermute | solution.py:399
  166.1 0.2 select_select_fusion
  166.4 7.2 %chain.11 = (bf16[256,1024]{1,0:T(8,128)(2,1)}, bf16[3,256,2048]{2,1,0:T(8,128)(2,1)}, bf16[3,256,1024]{2,1,0:T(8,128)(2,1)}) custom-call(s32[36]{0:T(128)S(1)} %reshape.15.info, bf16[256,1024]{1,0:T(8,128)(2,1)S(1)} %collective-permute-done.8.rest_0_, bf16[2,4,128,1024]{3,2,1,0:T(8,128)(2,1)} %refs_2_.9, ...), custom_call_target="tpu_custom_call", output_to_operand_aliasing={{1}: (8, {}), {2}: (9, {})} | custom-call | flops 4294967296 | bytes 8388608 | tf_op jit(solution)/shard_map/chain/pallas_call | solution.py:215
  173.6 7.9 %home.1 = (bf16[2,256,2048]{2,1,0:T(8,128)(2,1)}, bf16[2,256,1024]{2,1,0:T(8,128)(2,1)}) custom-call(s32[1]{0:T(128)} %bitcast.9.info, bf16[256,1024]{1,0:T(8,128)(2,1)S(1)} %get-tuple-element.117.refs_0_, bf16[256,1024]{1,0:T(8,128)(2,1)S(1)} %get-tuple-element.116.refs_1_, bf16[2,4,128,1024]{3,2,1,0:T(8,128)(2,1)} %refs_2_.9, ...), custom_call_target="tpu_custom_call" | custom-call | flops 4294967296 | bytes 4194304 | tf_op jit(solution)/shard_map/home/pallas_call | solution.py:271
  181.5 8.5 %weights.2.rest_0_ = bf16[1024,2048]{1,0:T(8,128)(2,1)} custom-call(bf16[2,2,256,1024]{3,2,1,0:T(8,128)(2,1)} %get-tuple-element.79.rest_9_.la_ref, bf16[3,256,2048]{2,1,0:T(8,128)(2,1)} %get-tuple-element.97.refs_7_.ra_ref, bf16[1,2,256,1024]{3,2,1,0:T(8,128)(2,1)} %get-tuple-element.96.rest_9_.lb_ref, bf16[2,256,2048]{2,1,0:T(8,128)(2,1)} %get-tuple-element.101.rb_ref), custom_call_target="tpu_custom_call" | custom-call | flops 4294967296 | bytes 4194304 | tf_op jit(solution)/shard_map/weights/pallas_call | solution.py:330
  189.9 8.4 %weights.3 = bf16[2048,1024]{1,0:T(8,128)(2,1)} custom-call(bf16[2,2,256,2048]{3,2,1,0:T(8,128)(2,1)} %get-tuple-element.103.la_ref, bf16[3,256,1024]{2,1,0:T(8,128)(2,1)} %get-tuple-element.104.ra_ref, bf16[1,2,256,2048]{3,2,1,0:T(8,128)(2,1)} %get-tuple-element.105.lb_ref, bf16[2,256,1024]{2,1,0:T(8,128)(2,1)} %get-tuple-element.106.rb_ref, ...), custom_call_target="tpu_custom_call" | custom-call | flops 4294967296 | bytes 4194304 | tf_op jit(solution)/shard_map/weights/pallas_call | solution.py:330
  198.4 0.7 reduce-scatter.3.cloned.1.call-update
  199.1 52.3 %reduce-scatter.5.cloned.1.call-done.total_ref = bf16[256,1024]{1,0:T(8,128)(2,1)} async-done(((bf16[2048,1024]{1,0:T(8,128)(2,1)}), bf16[256,1024]{1,0:T(8,128)(2,1)}) %reduce-scatter.5.cloned.1.call-update) | async-done | bytes 524304 | tf_op jit(solution)/shard_map/reduce_scatter | solution.py:536
  251.4 1.0 copy-done.1
  252.5 3.5 %update.3 = (bf16[256,1024]{1,0:T(8,128)(2,1)S(1)}, f32[1,256,1024]{2,1,0:T(8,128)}) custom-call(s32[1]{0:T(128)} %bitcast.info, bf16[2,1,2048,1024]{3,2,1,0:T(8,128)(2,1)} %weight_ref.3, f32[1,256,1024]{2,1,0:T(8,128)} %moment_ref.3, bf16[256,1024]{1,0:T(8,128)(2,1)S(1)} %copy-done.1), custom_call_target="tpu_custom_call" | custom-call | flops 1048576 | bytes 3145728 | tf_op jit(solution)/shard_map/update/pallas_call | solution.py:362
  256.0 2.4 collective-permute-start.13
  258.4 43.5 %reduce-scatter.3.cloned.1.call-done.total_ref = bf16[128,2048]{1,0:T(8,128)(2,1)} async-done(((bf16[1024,2048]{1,0:T(8,128)(2,1)}), bf16[128,2048]{1,0:T(8,128)(2,1)}) %reduce-scatter.3.cloned.1.call-update) | async-done | bytes 524304 | tf_op jit(solution)/shard_map/reduce_scatter | solution.py:532
  301.9 1.0 copy-done
  303.0 2.2 update.2
  305.2 2.4 collective-permute-start.12
  307.6 1.1 maximum_bitcast_fusion.1
  308.6 9.0 %collective-permute-done.12 = bf16[128,2048]{1,0:T(8,128)(2,1)S(1)} collective-permute-done((bf16[128,2048]{1,0:T(8,128)(2,1)S(1)}, bf16[128,2048]{1,0:T(8,128)(2,1)S(1)}, u32[]{:S(2)}, u32[]{:S(2)}) %collective-permute-start.12) | collective-permute-done | bytes 524320 | tf_op jit(solution)/shard_map/ppermute | solution.py:541
  317.6 1.1 maximum_bitcast_fusion
  (28 shorter events, 0.4 us)
Async XLA Ops:
  7.2 244.3 %reduce-scatter.5.cloned.1.call-start = ((), (), s32[]{:S(2)}) async-start(), calls=%async_computation.3 | async-start | bytes 4718592 | tf_op jit(solution)/shard_map/reduce_scatter | solution.py:536
  8.8 0.7 copy-start.2
  28.0 13.3 %collective-permute-start = (bf16[256,1024]{1,0:T(8,128)(2,1)S(1)}, bf16[256,1024]{1,0:T(8,128)(2,1)S(1)}, u32[]{:S(2)}, u32[]{:S(2)}) collective-permute-start(bf16[256,1024]{1,0:T(8,128)(2,1)S(1)} %get-tuple-element.68), channel_id=1, source_target_pairs={{0,8},{24,16},{1,9},{25,17},{2,10},{26,18},{3,11},{27,19},{4,12},{... | collective-permute-start | bytes 1572872 | tf_op jit(solution)/shard_map/ppermute | solution.py:399
  29.3 32.5 %collective-permute-start.1 = (bf16[256,1024]{1,0:T(8,128)(2,1)S(1)}, bf16[256,1024]{1,0:T(8,128)(2,1)S(1)}, u32[]{:S(2)}, u32[]{:S(2)}) collective-permute-start(bf16[256,1024]{1,0:T(8,128)(2,1)S(1)} %get-tuple-element.68), channel_id=1, source_target_pairs={{0,16},{1,17},{2,18},{3,19},{4,20},{5,21},{6,22},{7,23}} | collective-permute-start | bytes 1572872 | tf_op jit(solution)/shard_map/ppermute | solution.py:399
  41.4 13.9 %copy-start.5 = (bf16[2,1,4,128,1024]{4,3,2,1,0:T(8,128)(2,1)S(1)}, bf16[2,1,4,128,1024]{4,3,2,1,0:T(8,128)(2,1)}, u32[]{:S(2)}) copy-start(bf16[2,1,4,128,1024]{4,3,2,1,0:T(8,128)(2,1)} %refs_3_.7) | copy-start | bytes 6291460
  50.8 11.0 %copy-start.3 = (s32[2,4]{1,0:T(2,128)S(1)}, s32[2,4]{1,0:T(2,128)}, u32[]{:S(2)}) copy-start(s32[2,4]{1,0:T(2,128)} %refs_1_.11) | copy-start | bytes 100
  50.9 19.9 %collective-permute-start.2 = (bf16[256,1024]{1,0:T(8,128)(2,1)S(1)}, bf16[256,1024]{1,0:T(8,128)(2,1)S(1)}, u32[]{:S(2)}, u32[]{:S(2)}) collective-permute-start(bf16[256,1024]{1,0:T(8,128)(2,1)S(1)} %get-tuple-element.76), channel_id=1, source_target_pairs={{0,8},{24,16},{1,9},{25,17},{2,10},{26,18},{3,11},{27,19},{4,12},{... | collective-permute-start | bytes 1572872 | tf_op jit(solution)/shard_map/ppermute | solution.py:399
  56.3 86.0 %collective-permute-start.9 = (bf16[4,128,1024]{2,1,0:T(8,128)(2,1)}, bf16[4,128,1024]{2,1,0:T(8,128)(2,1)}, u32[]{:S(2)}, u32[]{:S(2)}) collective-permute-start(bf16[4,128,1024]{2,1,0:T(8,128)(2,1)} %slice_bitcast_fusion), channel_id=1, source_target_pairs={{0,24},{8,16},{16,8},{24,0},{1,25},{9,17},{17,9},{25,1},{2,26},{10... | collective-permute-start | bytes 3145736 | tf_op jit(solution)/shard_map/ppermute | solution.py:401
  59.6 43.3 %collective-permute-start.3 = (bf16[256,1024]{1,0:T(8,128)(2,1)S(1)}, bf16[256,1024]{1,0:T(8,128)(2,1)S(1)}, u32[]{:S(2)}, u32[]{:S(2)}) collective-permute-start(bf16[256,1024]{1,0:T(8,128)(2,1)S(1)} %get-tuple-element.76), channel_id=1, source_target_pairs={{0,16},{8,8},{1,17},{9,9},{2,18},{10,10},{3,19},{11,11},{4,20},{12... | collective-permute-start | bytes 1572872 | tf_op jit(solution)/shard_map/ppermute | solution.py:399
  60.9 51.0 %collective-permute-start.5 = (bf16[256,1024]{1,0:T(8,128)(2,1)S(1)}, bf16[256,1024]{1,0:T(8,128)(2,1)S(1)}, u32[]{:S(2)}, u32[]{:S(2)}) collective-permute-start(bf16[256,1024]{1,0:T(8,128)(2,1)S(1)} %get-tuple-element.76), channel_id=1, source_target_pairs={{8,16},{16,8},{9,17},{17,9},{10,18},{18,10},{11,19},{19,11},{12,20... | collective-permute-start | bytes 1572872 | tf_op jit(solution)/shard_map/ppermute | solution.py:399
  115.5 16.9 %collective-permute-start.6 = (bf16[256,1024]{1,0:T(8,128)(2,1)}, bf16[256,1024]{1,0:T(8,128)(2,1)S(1)}, u32[]{:S(2)}, u32[]{:S(2)}) collective-permute-start(bf16[256,1024]{1,0:T(8,128)(2,1)} %get-tuple-element.85), channel_id=1, source_target_pairs={{8,0},{9,1},{10,2},{11,3},{12,4},{13,5},{14,6},{15,7}} | collective-permute-start | bytes 1572872 | tf_op jit(solution)/shard_map/ppermute | solution.py:399
  116.8 15.6 %collective-permute-start.4 = (bf16[256,1024]{1,0:T(8,128)(2,1)}, bf16[256,1024]{1,0:T(8,128)(2,1)S(1)}, u32[]{:S(2)}, u32[]{:S(2)}) collective-permute-start(bf16[256,1024]{1,0:T(8,128)(2,1)} %get-tuple-element.80), channel_id=1, source_target_pairs={{8,16},{16,8},{9,17},{17,9},{10,18},{18,10},{11,19},{19,11},{12,20... | collective-permute-start | bytes 1572872 | tf_op jit(solution)/shard_map/ppermute | solution.py:399
  117.5 14.9 %collective-permute-start.7 = (bf16[256,1024]{1,0:T(8,128)(2,1)}, bf16[256,1024]{1,0:T(8,128)(2,1)S(1)}, u32[]{:S(2)}, u32[]{:S(2)}) collective-permute-start(bf16[256,1024]{1,0:T(8,128)(2,1)} %get-tuple-element.80), channel_id=1, source_target_pairs={{8,8},{9,9},{10,10},{11,11},{12,12},{13,13},{14,14},{15,15}} | collective-permute-start | bytes 1572872 | tf_op jit(solution)/shard_map/ppermute | solution.py:399
  118.2 24.1 %collective-permute-start.10 = (bf16[256,1024]{1,0:T(8,128)(2,1)}, bf16[256,1024]{1,0:T(8,128)(2,1)S(1)}, u32[]{:S(2)}, u32[]{:S(2)}) collective-permute-start(bf16[256,1024]{1,0:T(8,128)(2,1)} %get-tuple-element.85), channel_id=1, source_target_pairs={{16,0},{17,1},{18,2},{19,3},{20,4},{21,5},{22,6},{23,7}} | collective-permute-start | bytes 1572872 | tf_op jit(solution)/shard_map/ppermute | solution.py:399
  132.4 9.9 %copy-start.4 = (s32[4]{0:T(128)S(1)}, s32[4]{0:T(128)}, u32[]{:S(2)}) copy-start(s32[4]{0:T(128)} %constant.29.clone.refs_0_) | copy-start | bytes 52
  139.5 26.7 %collective-permute-start.11 = (bf16[256,1024]{1,0:T(8,128)(2,1)S(1)}, bf16[256,1024]{1,0:T(8,128)(2,1)S(1)}, u32[]{:S(2)}, u32[]{:S(2)}) collective-permute-start(bf16[256,1024]{1,0:T(8,128)(2,1)S(1)} %get-tuple-element.88), channel_id=1, source_target_pairs={{16,0},{17,1},{18,2},{19,3},{20,4},{21,5},{22,6},{23,7}} | collective-permute-start | bytes 1572872 | tf_op jit(solution)/shard_map/ppermute | solution.py:399
  140.8 25.6 %collective-permute-start.8 = (bf16[256,1024]{1,0:T(8,128)(2,1)S(1)}, bf16[256,1024]{1,0:T(8,128)(2,1)S(1)}, u32[]{:S(2)}, u32[]{:S(2)}) collective-permute-start(bf16[256,1024]{1,0:T(8,128)(2,1)S(1)} %get-tuple-element.88), channel_id=1, source_target_pairs={{8,0},{9,1},{10,2},{11,3},{12,4},{13,5},{14,6},{15,7}} | collective-permute-start | bytes 1572872 | tf_op jit(solution)/shard_map/ppermute | solution.py:399
  198.4 103.5 %reduce-scatter.3.cloned.1.call-start = ((), (), s32[]{:S(2)}) async-start(), calls=%async_computation.2 | async-start | bytes 4718592 | tf_op jit(solution)/shard_map/reduce_scatter | solution.py:532
  251.4 1.0 copy-start.1
  256.0 51.5 %collective-permute-start.13 = (bf16[256,1024]{1,0:T(8,128)(2,1)S(1)}, bf16[256,1024]{1,0:T(8,128)(2,1)S(1)}, u32[]{:S(2)}, u32[]{:S(2)}) collective-permute-start(bf16[256,1024]{1,0:T(8,128)(2,1)S(1)} %get-tuple-element.107), channel_id=1, source_target_pairs={{0,24},{8,16},{16,8},{24,0},{1,25},{9,17},{17,9},{25,1},{2,26},{10... | collective-permute-start | bytes 1572872 | tf_op jit(solution)/shard_map/ppermute | solution.py:541
  301.9 1.0 copy-start
  305.2 12.4 %collective-permute-start.12 = (bf16[128,2048]{1,0:T(8,128)(2,1)S(1)}, bf16[128,2048]{1,0:T(8,128)(2,1)S(1)}, u32[]{:S(2)}, u32[]{:S(2)}) collective-permute-start(bf16[128,2048]{1,0:T(8,128)(2,1)S(1)} %get-tuple-element.102), channel_id=1, source_target_pairs={{0,24},{8,16},{16,8},{24,0},{1,25},{9,17},{17,9},{25,1},{2,26},{10... | collective-permute-start | bytes 1572872 | tf_op jit(solution)/shard_map/ppermute | solution.py:541
Sparse Core Ops, SparseCore 0:
  198.5 52.8 reduce-scatter.4
  253.7 48.1 reduce-scatter.2

commit v3 on v2

--- a/solution.py
+++ b/solution.py
@@ -23,6 +23,10 @@
     )
 
 
+def in_vmem(x):
+    return pltpu.with_memory_space_constraint(x, pltpu.VMEM)
+
+
 def in_hbm(x):
     return pltpu.with_memory_space_constraint(x, pltpu.HBM)
 
@@ -35,97 +39,104 @@
     return min(512, width)
 
 
-def forward_body(per, info, plan, *refs):
-    u_refs = refs[:per]
-    p_ref, q_ref = refs[per : per + 2]
-    us_ref, h_ref, slope_ref, y_ref, r_ref, rows_ref, total = refs[-7:]
-    j = pl.program_id(0)
-
-    @pl.when(j == 0)
-    def _():
-        tokens = u_refs[0].shape[3]
-        for k in range(per):
-            u = u_refs[k][0, 0, 0]
-            rows_ref[k * tokens : (k + 1) * tokens] = u
-            us_ref[0, 0, k * tokens : (k + 1) * tokens] = u
-
-    u = rows_ref[...]
-    pre = dot(u, p_ref[0, 0], ((1,), (0,)))
-    cdf = 0.5 * (1.0 + lax.erf(pre * root_half))
-    hidden = (pre * cdf).astype(bf16)
-    slope = cdf + pre * (jnp.exp(-0.5 * pre * pre) * inv_root_tau)
-    h_ref[0, 0] = hidden
-    slope_ref[0, 0] = slope.astype(bf16)
-    part = dot(hidden, q_ref[0, 0], ((1,), (0,)))
-
-    @pl.when(j == 0)
-    def _():
-        total[...] = u.astype(f32) + part
-
-    @pl.when(j > 0)
-    def _():
-        total[...] += part
-
-    @pl.when(j == pl.num_programs(0) - 1)
-    def _():
-        z = total[...]
-        centre = z - jnp.mean(z, axis=-1, keepdims=True)
-        r = lax.rsqrt(jnp.mean(centre * centre, axis=-1, keepdims=True) + norm_epsilon)
-        y_ref[0, 0] = (centre * r).astype(bf16)
-        r_ref[0, 0] = r
-
-
-def forward(group, per, inputs, w_up, w_down, info, plan, previous, after, places):
+def forward(per, inputs, w_up, w_down, info, plan, previous, after, places, resident):
     _, _, micro, tokens, model = inputs.shape
     width = w_up.shape[3]
     tile = tile_of(width)
-    groups, rows = micro // per, per * tokens
+    groups, rows, every = micro // per, per * tokens, micro * tokens
+
+    def body(info_ref, plan_ref, *refs):
+        u_refs = refs[:micro]
+        p_ref, q_ref = refs[micro : micro + 2]
+        outs = refs[len(operands) :]
+        us_ref, h_ref, slope_ref, y_ref, r_ref = outs[:5]
+        rows_ref, total = outs[-2:]
+        j = pl.program_id(0)
+
+        @pl.when(j == 0)
+        def _():
+            for k in range(micro):
+                u = u_refs[k][0, 0, 0]
+                rows_ref[k * tokens : (k + 1) * tokens] = u
+                us_ref[0, k // per, k % per * tokens : (k % per + 1) * tokens] = u
+
+        if resident:
+            outs[5][...] = p_ref[0, 0]
+            outs[6][...] = q_ref[0, 0]
+        for g in range(groups):
+            here = slice(g * rows, (g + 1) * rows)
+            u = rows_ref[here]
+            pre = dot(u, p_ref[0, 0], ((1,), (0,)))
+            cdf = 0.5 * (1.0 + lax.erf(pre * root_half))
+            hidden = (pre * cdf).astype(bf16)
+            slope = cdf + pre * (jnp.exp(-0.5 * pre * pre) * inv_root_tau)
+            h_ref[0, g] = hidden
+            slope_ref[g] = slope.astype(bf16)
+            part = dot(hidden, q_ref[0, 0], ((1,), (0,)))
+            base = jnp.where(j == 0, u.astype(f32), total[here])
+            total[here] = base + part
+
+        @pl.when(j == pl.num_programs(0) - 1)
+        def _():
+            for g in range(groups):
+                z = total[g * rows : (g + 1) * rows]
+                centre = z - jnp.mean(z, axis=-1, keepdims=True)
+                r = lax.rsqrt(jnp.mean(centre * centre, axis=-1, keepdims=True) + norm_epsilon)
+                y_ref[g] = (centre * r).astype(bf16)
+                r_ref[g] = r
 
     def u_spec(k):
         return pl.BlockSpec(
-            (1, 1, 1, tokens, model), lambda j, i, p: (i[0], 0, p[i[2], group * per + k], 0, 0)
+            (1, 1, 1, tokens, model), lambda j, i, p: (i[0], 0, p[i[2], k], 0, 0)
         )
 
-    def out(columns, split=False, dtype=bf16):
-        shape = pltpu.HBM((places, groups, rows, columns), dtype)
-        block = (1, 1, rows, tile if split else columns)
-        if split:
-            return shape, pl.BlockSpec(block, lambda j, i, p: (i[3], group, 0, j))
-        return shape, pl.BlockSpec(block, lambda j, i, p: (i[3], group, 0, 0))
-
-    outs = [out(model), out(width, True), out(width, True), out(model), out(1, False, f32)]
-    in_specs = [u_spec(k) for k in range(per)] + [
+    in_specs = [u_spec(k) for k in range(micro)] + [
         pl.BlockSpec((1, 1, model, tile), lambda j, i, p: (i[1], 0, 0, j)),
         pl.BlockSpec((1, 1, tile, model), lambda j, i, p: (i[1], 0, j, 0)),
     ]
-    operands = [in_hbm(inputs)] * per + [in_hbm(w_up), in_hbm(w_down)]
+    operands = [in_hbm(inputs)] * micro + [in_hbm(w_up), in_hbm(w_down)]
     aliases = {}
     if previous is not None:
-        aliases = {2 + len(operands) + k: k for k in range(5)}
-        in_specs += [any_space] * 5
+        aliases = {2 + len(operands) + k: k for k in range(2)}
+        in_specs += [any_space] * 2
         operands += [in_hbm(x) for x in previous]
     for x in after:
-        if previous is None or not any(x is y for y in previous):
-            in_specs.append(any_space)
-            operands.append(in_hbm(x) if x.ndim > 2 else x)
-
-    def body(*refs):
-        forward_body(per, *refs)
-
+        in_specs.append(any_space)
+        operands.append(in_hbm(x) if x.ndim > 2 else x)
+    out_shape = [
+        pltpu.HBM((places, groups, rows, model), bf16),
+        pltpu.HBM((places, groups, rows, width), bf16),
+        pltpu.VMEM((groups, rows, width), bf16),
+        pltpu.VMEM((groups, rows, model), bf16),
+        pltpu.VMEM((groups, rows, 1), f32),
+    ]
+    out_specs = [
+        pl.BlockSpec((1, groups, rows, model), lambda j, i, p: (i[3], 0, 0, 0)),
+        pl.BlockSpec((1, groups, rows, tile), lambda j, i, p: (i[3], 0, 0, j)),
+        pl.BlockSpec((groups, rows, tile), lambda j, i, p: (0, 0, j)),
+        pl.BlockSpec((groups, rows, model), lambda j, i, p: (0, 0, 0)),
+        pl.BlockSpec((groups, rows, 1), lambda j, i, p: (0, 0, 0)),
+    ]
+    if resident:
+        out_shape += [pltpu.VMEM((model, width), bf16), pltpu.VMEM((width, model), bf16)]
+        out_specs += [
+            pl.BlockSpec((model, tile), lambda j, i, p: (0, j)),
+            pl.BlockSpec((tile, model), lambda j, i, p: (j, 0)),
+        ]
     return pl.pallas_call(
         body,
         grid_spec=pltpu.PrefetchScalarGridSpec(
             num_scalar_prefetch=2,
             grid=(width // tile,),
             in_specs=in_specs,
-            out_specs=[spec for _, spec in outs],
-            scratch_shapes=[pltpu.VMEM((rows, model), bf16), pltpu.VMEM((rows, model), f32)],
-        ),
-        out_shape=[shape for shape, _ in outs],
+            out_specs=out_specs,
+            scratch_shapes=[pltpu.VMEM((every, model), bf16), pltpu.VMEM((every, model), f32)],
+        ),
+        out_shape=out_shape,
         input_output_aliases=aliases,
-        compiler_params=params(40),
+        compiler_params=params(30),
         cost_estimate=pl.CostEstimate(
-            flops=8 * rows * model * width, bytes_accessed=4 * model * width, transcendentals=0
+            flops=8 * every * model * width, bytes_accessed=4 * model * width, transcendentals=0
         ),
         name="forward",
     )(info, plan, *operands)
@@ -140,13 +151,13 @@
 columns_of_table = 6
 
 
-def chain_step(call, table, recv, top_grad, saved, w_up, w_down, previous, after):
+def chain_step(call, table, recv, top_grad, saved, previous, after):
     base = call * columns_of_table
-    _, _, slopes, ys, rs = saved
+    slopes, ys, rs, w_up, w_down = saved
     rows, model = recv[0].shape
-    width = w_up.shape[3]
+    width = w_up.shape[1]
     tile = tile_of(width)
-    groups = slopes.shape[1]
+    groups = slopes.shape[0]
     tokens = top_grad.shape[2]
     per = rows // tokens
 
@@ -164,7 +175,7 @@
             if len(recv) > 1:
                 e = jnp.where(info[base + 4] == 2, recv_refs[0][...], e)
             e = e.astype(f32)
-            grad = sum_gradient(e, y_ref[0, 0].astype(f32), r_ref[0, 0])
+            grad = sum_gradient(e, y_ref[0].astype(f32), r_ref[0])
             whole[...] = grad
             low[...] = grad.astype(bf16)
             sum_ref[0] = grad.astype(bf16)
@@ -172,13 +183,13 @@
         @pl.when(active)
         def _():
             grad_pre = (
-                dot(low[...], q_ref[0, 0], ((1,), (1,))) * slope_ref[0, 0].astype(f32)
+                dot(low[...], q_ref[...], ((1,), (1,))) * slope_ref[0].astype(f32)
             ).astype(bf16)
             pre_ref[0] = grad_pre
 
             @pl.when(info[base + 5] > 0)
             def _():
-                part = dot(grad_pre, p_ref[0, 0], ((1,), (1,)))
+                part = dot(grad_pre, p_ref[...], ((1,), (1,)))
 
                 @pl.when(j == 0)
                 def _():
@@ -194,15 +205,14 @@
 
     in_specs = [pl.BlockSpec((rows, model), lambda j, i: (0, 0))] * len(recv) + [
         pl.BlockSpec((1, per, tokens, model), lambda j, i: (i[base + 1], i[base + 2], 0, 0)),
-        pl.BlockSpec((1, 1, rows, model), lambda j, i: (i[base + 1], i[base + 2], 0, 0)),
-        pl.BlockSpec((1, 1, rows, 1), lambda j, i: (i[base + 1], i[base + 2], 0, 0)),
-        pl.BlockSpec(
-            (1, 1, rows, tile), lambda j, i: (i[base + 1], i[base + 2], 0, j * i[base])
-        ),
-        pl.BlockSpec((1, 1, model, tile), lambda j, i: (i[base + 1], 0, 0, j * i[base + 5])),
-        pl.BlockSpec((1, 1, tile, model), lambda j, i: (i[base + 1], 0, j * i[base], 0)),
+        pl.BlockSpec((1, rows, model), lambda j, i: (i[base + 2], 0, 0)),
+        pl.BlockSpec((1, rows, 1), lambda j, i: (i[base + 2], 0, 0)),
+        pl.BlockSpec((1, rows, tile), lambda j, i: (i[base + 2], 0, j * i[base])),
+        pl.BlockSpec((model, tile), lambda j, i: (0, j * i[base + 5])),
+        pl.BlockSpec((tile, model), lambda j, i: (j * i[base], 0)),
     ]
-    operands = list(recv) + [in_hbm(x) for x in (top_grad, ys, rs, slopes, w_up, w_down)]
+    operands = list(recv) + [in_hbm(top_grad)]
+    operands += [in_vmem(x) for x in (ys, rs, slopes, w_up, w_down)]
     aliases = {}
     if previous is not None:
         aliases = {1 + len(operands): 1, 2 + len(operands): 2}
@@ -235,7 +245,7 @@
             pltpu.HBM((groups + 1, rows, model), bf16),
         ],
         input_output_aliases=aliases,
-        compiler_params=params(32),
+        compiler_params=params(20),
         cost_estimate=pl.CostEstimate(
             flops=8 * rows * model * width, bytes_accessed=4 * model * width, transcendentals=0
         ),
@@ -244,8 +254,8 @@
 
 
 def home_step(info, arrived, top_grad, saved, w_down, after):
-    _, _, slopes, ys, rs = saved
-    groups, rows, model = slopes.shape[1], slopes.shape[2], ys.shape[3]
+    slopes, ys, rs = saved
+    groups, rows, model = ys.shape
     micro, tokens = top_grad.shape[1:3]
     width = w_down.shape[2]
     tile = tile_of(width)
@@ -260,11 +270,11 @@
             for g in range(groups):
                 top = top_ref[0].reshape(groups, rows, model)[g]
                 e = jnp.where(info[0] > 0, top, e_refs[g][...]).astype(f32)
-                grad = sum_gradient(e, y_ref[0, g].astype(f32), r_ref[0, g])
+                grad = sum_gradient(e, y_ref[g].astype(f32), r_ref[g])
                 sum_ref[g] = grad.astype(bf16)
 
         low = sum_ref[...].reshape(groups * rows, model)
-        slope = slope_ref[0].reshape(groups * rows, tile)
+        slope = slope_ref[...].reshape(groups * rows, tile)
         grad_pre = dot(low, q_ref[0, 0], ((1,), (1,))) * slope.astype(f32)
         pre_ref[...] = grad_pre.astype(bf16).reshape(pre_ref.shape)
 
@@ -276,9 +286,9 @@
             in_specs=[pl.BlockSpec((rows, model), lambda j, i: (0, 0))] * groups
             + [
                 pl.BlockSpec((1, micro, tokens, model), lambda j, i: (1, 0, 0, 0)),
-                pl.BlockSpec((1, groups, rows, model), lambda j, i: (0, 0, 0, 0)),
-                pl.BlockSpec((1, groups, rows, 1), lambda j, i: (0, 0, 0, 0)),
-                pl.BlockSpec((1, groups, rows, tile), lambda j, i: (0, 0, 0, j)),
+                pl.BlockSpec((groups, rows, model), lambda j, i: (0, 0, 0)),
+                pl.BlockSpec((groups, rows, 1), lambda j, i: (0, 0, 0)),
+                pl.BlockSpec((groups, rows, tile), lambda j, i: (0, 0, j)),
                 pl.BlockSpec((1, 1, tile, model), lambda j, i: (0, 0, j, 0)),
             ]
             + [any_space] * len(after),
@@ -291,7 +301,7 @@
             pltpu.HBM((groups, rows, width), bf16),
             pltpu.HBM((groups, rows, model), bf16),
         ],
-        compiler_params=params(40),
+        compiler_params=params(28),
         cost_estimate=pl.CostEstimate(
             flops=4 * groups * rows * model * width,
             bytes_accessed=2 * model * width,
@@ -301,7 +311,9 @@
     )(
         info,
         *arrived,
-        *[in_hbm(x) for x in (top_grad, ys, rs, slopes, w_down)],
+        in_hbm(top_grad),
+        *[in_vmem(x) for x in (ys, rs, slopes)],
+        in_hbm(w_down),
         *[in_hbm(x) if x.ndim > 2 else x for x in after],
     )
 
@@ -339,7 +351,7 @@
         + [any_space] * len(after),
         out_specs=pl.BlockSpec(out_block, (lambda j: (j, 0)) if split_left else (lambda j: (0, j))),
         out_shape=pltpu.HBM((rows, columns), bf16),
-        compiler_params=params(40),
+        compiler_params=params(32),
         cost_estimate=pl.CostEstimate(
             flops=4 * groups * tokens * rows * columns,
             bytes_accessed=2 * rows * columns,
@@ -442,37 +454,33 @@
     kinds = [jnp.stack([relay[k]] * 4) for k in range(2)]
     home_kind = jnp.array([0, 0, 1, 0], jnp.int32)
 
-    saved = None
-    saved_home = None
+    blocks = None
+    saved = [None, None]
     order = []
 
-    def run_forward(kind, g):
-        nonlocal saved, order
-        saved = forward(
-            g, per, section_inputs, up_weight, down_weight, kinds[kind], plan, saved, order, 2
+    def run_forward(kind, after):
+        nonlocal blocks, order
+        *blocks, slopes, ys, rs, w_up, w_down = forward(
+            per, section_inputs, up_weight, down_weight, kinds[kind], plan, blocks, order + after, 2, True
         )
-        order = [saved[0]]
-
-    def run_home_forward(g):
-        nonlocal saved_home, order
-        saved_home = forward(
-            g, per, mirrored, up_weight, down_weight, home_kind, plan, saved_home, order, 1
-        )
-        order = [saved_home[0]]
-
-    pending = [(0, g) for g in range(groups)] + [(1, g) for g in range(groups)]
+        saved[kind] = (slopes, ys, rs, w_up, w_down)
+        order = [blocks[0]]
+
     late = []
+    run_forward(0, [])
     blank = jnp.zeros((rows, model), bf16)
     received = {}
     arrived = {}
     kept = None
     for call, (tick, kind) in enumerate(calls):
-        newest = min(tick - (sections - half if kind else 0), groups - 1)
-        while pending and any(k < kind or (k == kind and g <= newest) for k, g in pending):
-            run_forward(*pending.pop(0))
+        if kind == 1 and saved[1] is None:
+            run_forward(1, [])
         if call == len(calls) - 1:
-            for g in range(groups):
-                run_home_forward(g)
+            *home_blocks, slopes, ys, rs = forward(
+                per, mirrored, up_weight, down_weight, home_kind, plan, None, order + late, 1, False
+            )
+            saved_home = (slopes, ys, rs)
+            order = [home_blocks[0]]
 
         def busy(i):
             return 0 <= tick - begins(kind, i) < groups
@@ -482,11 +490,8 @@
             for way in range(2)
             if (tick, kind, way) in received
         ] or [blank]
-        out, *kept = chain_step(
-            call, table, recv, top_grad, saved, up_weight, down_weight, kept, order
-        )
-        order = [kept[0]] + [x for n, x in late if n < call]
-        late = [(n, x) for n, x in late if n >= call]
+        out, *kept = chain_step(call, table, recv, top_grad, saved[kind], kept, order)
+        order = [kept[0]]
         relay_of = [(0 if i >= half else 1) if kind == 0 else (1 if i >= half else 0) for i in range(sections)]
         to = [i - 1 if relay_of[i] == 0 else i + 1 for i in range(sections)]
         live = [
@@ -507,9 +512,10 @@
         if got is not None:
             for i, k in pairs:
                 arrived[(k, tick - begins(kind, i))] = got
-            late.append((call, got))
-        if pending and (kind == 1 or pending[0][0] == 0 or tick + 1 >= groups):
-            run_forward(*pending.pop(0))
+            if tick < half:
+                late.append(got)
+        if saved[1] is None and tick + 1 >= groups:
+            run_forward(1, [mirrored[0, 0]])
 
     came = []
     for g in range(groups):
@@ -528,11 +534,9 @@
         (position == last).astype(jnp.int32)[None], came, top_grad, saved_home, down_weight, order
     )
 
-    up_part = weight_gradient(saved[0], kept[0], saved_home[0], home_pre, groups, False, [])
+    up_part = weight_gradient(blocks[0], kept[0], home_blocks[0], home_pre, groups, False, [])
     up_sum = lax.psum_scatter(up_part, "dp", scatter_dimension=0, tiled=True)
-    down_part = weight_gradient(
-        saved[1], kept[1], saved_home[1], home_sum, groups, True, [up_part]
-    )
+    down_part = weight_gradient(blocks[1], kept[1], home_blocks[1], home_sum, groups, True, [])
     down_sum = lax.psum_scatter(down_part, "dp", scatter_dimension=0, tiled=True)
     replica = lax.axis_index("dp").astype(jnp.int32)[None]
 

time: 327 us -> 291 us (0.89)
  waiting for transfers between devices: 154 us -> 120 us
  Pallas kernels: 125 us -> 100 us
  starting transfers between devices: 24.1 us -> 41 us
  local copies, waits for them, and re-layouts: 4.07 us -> 9.67 us
    ppermute x11, waiting for transfers between devices: 49 us -> 26.5 us  [hop(): return lax.ppermute(value, 'section', pairs) if pairs else None]
    pallas_call x6 -> x3, Pallas kernels: 53.9 us -> 36.3 us  [forward(): pl.pallas_call(body, grid_spec=pltpu.PrefetchScalarGridSpec(num_scalar_pr...]
    ppermute x11, starting transfers between devices: 16 us -> 32.3 us  [hop(): return lax.ppermute(value, 'section', pairs) if pairs else None]
    reduce_scatter x1, waiting for transfers between devices: 52.3 us -> 40.7 us  [on_device(): lax.psum_scatter(down_part, 'dp', scatter_dimension=0, tiled=True)]
    pallas_call x6, Pallas kernels: 40.5 us -> 33.7 us  [chain_step(): pl.pallas_call(body, grid_spec=pltpu.PrefetchScalarGridSpec(num_scalar_pr...]
    unnamed x12 -> x24, local copies, waits for them, and re-layouts: 2.77 us -> 8.12 us
  transfers between devices with their start and end apart: 16 -> 16, of which waited for: 7 -> 7; matrix products, arithmetic and copies ran while one was open for 1% -> 1% of each run, Pallas kernels for 23% -> 28%
where the time goes in v3:
time: 291 us; the launch traced here: 289 us
  waiting for transfers between devices  120 us (41%)
  Pallas kernels  100 us (34%)
  starting transfers between devices  41 us (14%)
  between operations  14.2 us (5%)
  local copies, waits for them, and re-layouts  9.67 us (3%)
  other arithmetic  4.69 us (2%)
    reduce_scatter x1, waiting for transfers between devices, on_device(): up_sum = lax.psum_scatter(up_part, 'dp', scatter_dimension=0, tiled=True)  43.5 us
    reduce_scatter x1, waiting for transfers between devices, on_device(): lax.psum_scatter(down_part, 'dp', scatter_dimension=0, tiled=True)  40.7 us
    pallas_call x3, Pallas kernels, forward(): pl.pallas_call(body, grid_spec=pltpu.PrefetchScalarGridSpec(num_scalar_pr...  36.3 us
    pallas_call x6, Pallas kernels, chain_step(): pl.pallas_call(body, grid_spec=pltpu.PrefetchScalarGridSpec(num_scalar_pr...  33.7 us
    ppermute x11, starting transfers between devices, hop(): return lax.ppermute(value, 'section', pairs) if pairs else None  32.3 us
    ppermute x11, waiting for transfers between devices, hop(): return lax.ppermute(value, 'section', pairs) if pairs else None  26.5 us
    pallas_call x2, Pallas kernels, weight_gradient(): pl.pallas_call(body, grid=((rows if split_left else columns) // tile,), i...  17 us
    ppermute x2, waiting for transfers between devices, finish(): lax.ppermute(fresh, 'section', [(i, last - i) for i in range(sections)])  8.99 us
  transfers between devices with their start and end apart: 16, of which 7 were waited for; matrix products, arithmetic and copies ran while one was open for 1% of the time, Pallas kernels for 28%

profile of v3, /device:TPU:0, one launch (start us, length us, event | category | flops | bytes accessed | tf_op | source)
XLA Modules:
  0.0 289.4 jit_solution(7566839990015031154)
XLA Ops:
  7.2 1.3 slice_bitcast_fusion
  8.5 4.0 %collective-permute-start.1 = (bf16[4,128,1024]{2,1,0:T(8,128)(2,1)S(1)}, bf16[4,128,1024]{2,1,0:T(8,128)(2,1)S(1)}, u32[]{:S(2)}, u32[]{:S(2)}) collective-permute-start(bf16[4,128,1024]{2,1,0:T(8,128)(2,1)S(1)} %slice_bitcast_fusion), channel_id=1, source_target_pairs={{0,24},{8,16},{16,8},{24,0},{1,25},{9,17},{17,9},{25,1},{2,26},{10... | collective-permute-start | bytes 3145736 | tf_op jit(solution)/shard_map/ppermute | solution.py:413
  12.5 0.7 fusion.2
  13.2 0.7 fusion.1
  13.9 0.1 copy.28
  14.0 0.7 copy-done.8
  14.7 12.3 %forward.3 = (bf16[2,2,256,1024]{3,2,1,0:T(8,128)(2,1)}, bf16[2,2,256,2048]{3,2,1,0:T(8,128)(2,1)}, bf16[2,256,2048]{2,1,0:T(8,128)(2,1)S(1)}, bf16[2,256,1024]{...) custom-call(s32[4]{0:T(128)S(1)} %stack.60.info_ref, ...), custom_call_target="tpu_custom_call" | custom-call | flops 8589934592 | bytes 8388608 | tf_op jit(solution)/shard_map/forward/pallas_call | solution.py:126
  27.1 7.9 %chain.6 = (bf16[256,1024]{1,0:T(8,128)(2,1)}, bf16[3,256,2048]{2,1,0:T(8,128)(2,1)}, bf16[3,256,1024]{2,1,0:T(8,128)(2,1)}) custom-call(s32[36]{0:T(128)S(1)} %reshape.15.info, bf16[256,1024]{1,0:T(8,128)(2,1)S(1)} %broadcast_in_dim.46.rest_0_, bf16[2,4,128,1024]{3,2,1,0:T(8,128)(2,1)} %refs_2_.5, bf16[2,256,1024]{2,1,0:T(8,128)(2,1)S(1)} %get-tuple-element.48.rest_2_, ...), custom_call_target="tpu_custom_call" | custom-call | flops 4294967296 | bytes 8388608 | tf_op jit(solution)/shard_map/chain/pallas_call | solution.py:225
  35.0 1.3 collective-permute-start
  36.3 11.5 %collective-permute-done.rest_0_ = bf16[256,1024]{1,0:T(8,128)(2,1)S(1)} collective-permute-done((bf16[256,1024]{1,0:T(8,128)(2,1)}, bf16[256,1024]{1,0:T(8,128)(2,1)S(1)}, u32[]{:S(2)}, u32[]{:S(2)}) %collective-permute-start) | collective-permute-done | bytes 524320 | tf_op jit(solution)/shard_map/ppermute | solution.py:411
  47.8 7.9 %chain.7 = (bf16[256,1024]{1,0:T(8,128)(2,1)}, bf16[3,256,2048]{2,1,0:T(8,128)(2,1)}, bf16[3,256,1024]{2,1,0:T(8,128)(2,1)}) custom-call(s32[36]{0:T(128)S(1)} %reshape.15.info, bf16[256,1024]{1,0:T(8,128)(2,1)S(1)} %collective-permute-done.rest_0_, bf16[2,4,128,1024]{3,2,1,0:T(8,128)(2,1)} %refs_2_.5, ...), custom_call_target="tpu_custom_call", output_to_operand_aliasing={{1}: (8, {}), {2}: (9, {})} | custom-call | flops 4294967296 | bytes 8388608 | tf_op jit(solution)/shard_map/chain/pallas_call | solution.py:225
  55.7 4.3 %collective-permute-start.2 = (bf16[256,1024]{1,0:T(8,128)(2,1)}, bf16[256,1024]{1,0:T(8,128)(2,1)S(1)}, u32[]{:S(2)}, u32[]{:S(2)}) collective-permute-start(bf16[256,1024]{1,0:T(8,128)(2,1)} %get-tuple-element.58), channel_id=1, source_target_pairs={{0,8},{24,16},{1,9},{25,17},{2,10},{26,18},{3,11},{27,19},{4,12},{... | collective-permute-start | bytes 1572872 | tf_op jit(solution)/shard_map/ppermute | solution.py:411
  60.0 0.9 collective-permute-start.4
  60.9 1.0 copy-done.11
  61.9 12.3 %forward.4 = (bf16[2,2,256,1024]{3,2,1,0:T(8,128)(2,1)}, bf16[2,2,256,2048]{3,2,1,0:T(8,128)(2,1)}, bf16[2,256,2048]{2,1,0:T(8,128)(2,1)S(1)}, bf16[2,256,1024]{...) custom-call(s32[4]{0:T(128)S(1)} %stack.59.info_ref, ...), custom_call_target="tpu_custom_call", output_to_operand_aliasing={{0}: (8, {}), {1}: (9, {})} | custom-call | flops 8589934592 | bytes 8388608 | tf_op jit(solution)/shard_map/forward/pallas_call | solution.py:126
  74.2 3.6 %chain.8 = (bf16[256,1024]{1,0:T(8,128)(2,1)}, bf16[3,256,2048]{2,1,0:T(8,128)(2,1)}, bf16[3,256,1024]{2,1,0:T(8,128)(2,1)}) custom-call(s32[36]{0:T(128)S(1)} %reshape.15.info, bf16[256,1024]{1,0:T(8,128)(2,1)S(1)} %collective-permute-done.2.rest_0_, bf16[2,4,128,1024]{3,2,1,0:T(8,128)(2,1)} %refs_2_.5, ...), custom_call_target="tpu_custom_call", output_to_operand_aliasing={{1}: (8, {}), {2}: (9, {})} | custom-call | flops 4294967296 | bytes 8388608 | tf_op jit(solution)/shard_map/chain/pallas_call | solution.py:225
  77.8 2.8 chain.9
  80.7 1.3 collective-permute-start.5
  81.9 1.5 collective-permute-start.3
  83.4 16.2 %collective-permute-start.7 = (bf16[256,1024]{1,0:T(8,128)(2,1)}, bf16[256,1024]{1,0:T(8,128)(2,1)}, u32[]{:S(2)}, u32[]{:S(2)}) collective-permute-start(bf16[256,1024]{1,0:T(8,128)(2,1)} %get-tuple-element.53), channel_id=1, source_target_pairs={{0,16},{1,17},{2,18},{3,19},{4,20},{5,21},{6,22},{7,23}} | collective-permute-start | bytes 1572872 | tf_op jit(solution)/shard_map/ppermute | solution.py:411
  99.6 2.1 collective-permute-start.8
  101.7 1.3 collective-permute-start.9
  103.0 2.9 collective-permute-done.5.rest_1_
  105.8 0.7 collective-permute-start.10
  106.5 2.2 copy-done.1
  108.7 2.2 copy-done.4
  110.9 5.8 %chain.10 = (bf16[256,1024]{1,0:T(8,128)(2,1)S(1)}, bf16[3,256,2048]{2,1,0:T(8,128)(2,1)}, bf16[3,256,1024]{2,1,0:T(8,128)(2,1)}) custom-call(s32[36]{0:T(128)S(1)} %reshape.15.info, bf16[256,1024]{1,0:T(8,128)(2,1)} %collective-permute-done.3.rest_0_, ...), custom_call_target="tpu_custom_call", output_to_operand_aliasing={{1}: (9, {}), {2}: (10, {})} | custom-call | flops 4294967296 | bytes 8388608 | tf_op jit(solution)/shard_map/chain/pallas_call | solution.py:225
  116.7 1.3 collective-permute-start.11
  118.0 4.7 %collective-permute-done.7.refs_7_ = bf16[256,1024]{1,0:T(8,128)(2,1)} collective-permute-done((bf16[256,1024]{1,0:T(8,128)(2,1)}, bf16[256,1024]{1,0:T(8,128)(2,1)}, u32[]{:S(2)}, u32[]{:S(2)}) %collective-permute-start.7) | collective-permute-done | bytes 524320 | tf_op jit(solution)/shard_map/ppermute | solution.py:411
  122.7 1.5 collective-permute-start.6
  124.2 7.4 %collective-permute-done.8.refs_8_ = bf16[256,1024]{1,0:T(8,128)(2,1)} collective-permute-done((bf16[256,1024]{1,0:T(8,128)(2,1)}, bf16[256,1024]{1,0:T(8,128)(2,1)}, u32[]{:S(2)}, u32[]{:S(2)}) %collective-permute-start.8) | collective-permute-done | bytes 524320 | tf_op jit(solution)/shard_map/ppermute | solution.py:411
  131.7 11.8 %forward.5 = (bf16[1,2,256,1024]{3,2,1,0:T(8,128)(2,1)}, bf16[1,2,256,2048]{3,2,1,0:T(8,128)(2,1)}, bf16[2,256,2048]{2,1,0:T(8,128)(2,1)S(1)}, bf16[2,256,1024]{2,1,0:T(8,128)(2,1)S(1)}, f32[2,256,1]{2,1,0:T(8,128)S(1)}) custom-call(s32[4]{0:T(128)S(1)} %copy-done.10, s32[2,4]{1,0:T(2,128)S(1)} %copy-done.9, bf16[1,1,4,128,1024]{4,3,2,1,0:T(8,128)(2,1)} %bitcast.31, ...), custom_call_target="tpu_custom_call" | custom-call | flops 8589934592 | bytes 8388608 | tf_op jit(solution)/shard_map/forward/pallas_call | solution.py:126
  143.4 5.6 %chain.11 = (bf16[256,1024]{1,0:T(8,128)(2,1)}, bf16[3,256,2048]{2,1,0:T(8,128)(2,1)}, bf16[3,256,1024]{2,1,0:T(8,128)(2,1)}) custom-call(s32[36]{0:T(128)S(1)} %reshape.15.info, bf16[256,1024]{1,0:T(8,128)(2,1)S(1)} %collective-permute-done.6.rest_0_, bf16[2,4,128,1024]{3,2,1,0:T(8,128)(2,1)} %refs_2_.5, ...), custom_call_target="tpu_custom_call", output_to_operand_aliasing={{1}: (8, {}), {2}: (9, {})} | custom-call | flops 4294967296 | bytes 8388608 | tf_op jit(solution)/shard_map/chain/pallas_call | solution.py:225
  149.1 1.2 select_select_fusion
  150.3 7.3 %home.1 = (bf16[2,256,2048]{2,1,0:T(8,128)(2,1)}, bf16[2,256,1024]{2,1,0:T(8,128)(2,1)}) custom-call(s32[1]{0:T(128)} %bitcast.9.info, bf16[256,1024]{1,0:T(8,128)(2,1)S(1)} %get-tuple-element.95.refs_0_, bf16[256,1024]{1,0:T(8,128)(2,1)S(1)} %get-tuple-element.94.refs_1_, bf16[2,4,128,1024]{3,2,1,0:T(8,128)(2,1)} %refs_2_.5, ...), custom_call_target="tpu_custom_call" | custom-call | flops 4294967296 | bytes 4194304 | tf_op jit(solution)/shard_map/home/pallas_call | solution.py:281
  157.6 8.4 %weights.3 = bf16[2048,1024]{1,0:T(8,128)(2,1)} custom-call(bf16[2,2,256,2048]{3,2,1,0:T(8,128)(2,1)} %get-tuple-element.81.la_ref, bf16[3,256,1024]{2,1,0:T(8,128)(2,1)} %get-tuple-element.82.ra_ref, bf16[1,2,256,2048]{3,2,1,0:T(8,128)(2,1)} %get-tuple-element.83.lb_ref, bf16[2,256,1024]{2,1,0:T(8,128)(2,1)} %get-tuple-element.84.rb_ref), custom_call_target="tpu_custom_call" | custom-call | flops 4294967296 | bytes 4194304 | tf_op jit(solution)/shard_map/weights/pallas_call | solution.py:342
  166.0 8.6 %weights.2 = bf16[1024,2048]{1,0:T(8,128)(2,1)} custom-call(bf16[2,2,256,1024]{3,2,1,0:T(8,128)(2,1)} %get-tuple-element.57.rest_9_.la_ref, bf16[3,256,2048]{2,1,0:T(8,128)(2,1)} %get-tuple-element.75.refs_7_.ra_ref, bf16[1,2,256,1024]{3,2,1,0:T(8,128)(2,1)} %get-tuple-element.74.rest_9_.lb_ref, bf16[2,256,2048]{2,1,0:T(8,128)(2,1)} %get-tuple-element.79.rb_ref), custom_call_target="tpu_custom_call" | custom-call | flops 4294967296 | bytes 4194304 | tf_op jit(solution)/shard_map/weights/pallas_call | solution.py:342
  174.6 40.7 %reduce-scatter.5.cloned.1.call-done.total_ref = bf16[256,1024]{1,0:T(8,128)(2,1)} async-done(((bf16[2048,1024]{1,0:T(8,128)(2,1)}), bf16[256,1024]{1,0:T(8,128)(2,1)}) %reduce-scatter.5.cloned.1.call-update) | async-done | bytes 524304 | tf_op jit(solution)/shard_map/reduce_scatter | solution.py:540
  215.4 1.0 copy-done.6
  216.4 3.5 %update.3 = (bf16[256,1024]{1,0:T(8,128)(2,1)S(1)}, f32[1,256,1024]{2,1,0:T(8,128)}) custom-call(s32[1]{0:T(128)} %bitcast.info, bf16[2,1,2048,1024]{3,2,1,0:T(8,128)(2,1)} %weight_ref.3, f32[1,256,1024]{2,1,0:T(8,128)} %moment_ref.3, bf16[256,1024]{1,0:T(8,128)(2,1)S(1)} %copy-done.6), custom_call_target="tpu_custom_call" | custom-call | flops 1048576 | bytes 3145728 | tf_op jit(solution)/shard_map/update/pallas_call | solution.py:374
  219.9 2.4 collective-permute-start.13
  222.3 43.5 %reduce-scatter.3.cloned.1.call-done.total_ref = bf16[128,2048]{1,0:T(8,128)(2,1)} async-done(((bf16[1024,2048]{1,0:T(8,128)(2,1)}), bf16[128,2048]{1,0:T(8,128)(2,1)}) %reduce-scatter.3.cloned.1.call-update) | async-done | bytes 524304 | tf_op jit(solution)/shard_map/reduce_scatter | solution.py:538
  265.8 1.0 copy-done.7
  266.9 2.2 update.2
  269.1 2.4 collective-permute-start.12
  271.5 1.1 maximum_bitcast_fusion.1
  272.5 9.0 %collective-permute-done.12 = bf16[128,2048]{1,0:T(8,128)(2,1)S(1)} collective-permute-done((bf16[128,2048]{1,0:T(8,128)(2,1)S(1)}, bf16[128,2048]{1,0:T(8,128)(2,1)S(1)}, u32[]{:S(2)}, u32[]{:S(2)}) %collective-permute-start.12) | collective-permute-done | bytes 524320 | tf_op jit(solution)/shard_map/ppermute | solution.py:545
  281.5 1.1 maximum_bitcast_fusion
  (37 shorter events, 0.3 us)
Async XLA Ops:
  7.2 208.2 %reduce-scatter.5.cloned.1.call-start = ((), (), s32[]{:S(2)}) async-start(), calls=%async_computation.3 | async-start | bytes 4718592 | tf_op jit(solution)/shard_map/reduce_scatter | solution.py:540
  8.5 52.4 %collective-permute-start.1 = (bf16[4,128,1024]{2,1,0:T(8,128)(2,1)S(1)}, bf16[4,128,1024]{2,1,0:T(8,128)(2,1)S(1)}, u32[]{:S(2)}, u32[]{:S(2)}) collective-permute-start(bf16[4,128,1024]{2,1,0:T(8,128)(2,1)S(1)} %slice_bitcast_fusion), channel_id=1, source_target_pairs={{0,24},{8,16},{16,8},{24,0},{1,25},{9,17},{17,9},{25,1},{2,26},{10... | collective-permute-start | bytes 3145736 | tf_op jit(solution)/shard_map/ppermute | solution.py:413
  14.0 0.7 copy-start.8
  35.0 12.8 %collective-permute-start = (bf16[256,1024]{1,0:T(8,128)(2,1)}, bf16[256,1024]{1,0:T(8,128)(2,1)S(1)}, u32[]{:S(2)}, u32[]{:S(2)}) collective-permute-start(bf16[256,1024]{1,0:T(8,128)(2,1)} %get-tuple-element.53), channel_id=1, source_target_pairs={{0,8},{24,16},{1,9},{25,17},{2,10},{26,18},{3,11},{27,19},{4,12},{... | collective-permute-start | bytes 1572872 | tf_op jit(solution)/shard_map/ppermute | solution.py:411
  47.8 14.1 %copy-start.9 = (s32[2,4]{1,0:T(2,128)S(1)}, s32[2,4]{1,0:T(2,128)}, u32[]{:S(2)}) copy-start(s32[2,4]{1,0:T(2,128)} %plan_ref.5) | copy-start | bytes 100
  55.7 18.5 %collective-permute-start.2 = (bf16[256,1024]{1,0:T(8,128)(2,1)}, bf16[256,1024]{1,0:T(8,128)(2,1)S(1)}, u32[]{:S(2)}, u32[]{:S(2)}) collective-permute-start(bf16[256,1024]{1,0:T(8,128)(2,1)} %get-tuple-element.58), channel_id=1, source_target_pairs={{0,8},{24,16},{1,9},{25,17},{2,10},{26,18},{3,11},{27,19},{4,12},{... | collective-permute-start | bytes 1572872 | tf_op jit(solution)/shard_map/ppermute | solution.py:411
  60.0 17.8 %collective-permute-start.4 = (bf16[256,1024]{1,0:T(8,128)(2,1)}, bf16[256,1024]{1,0:T(8,128)(2,1)S(1)}, u32[]{:S(2)}, u32[]{:S(2)}) collective-permute-start(bf16[256,1024]{1,0:T(8,128)(2,1)} %get-tuple-element.58), channel_id=1, source_target_pairs={{8,16},{16,8},{9,17},{17,9},{10,18},{18,10},{11,19},{19,11},{12,20... | collective-permute-start | bytes 1572872 | tf_op jit(solution)/shard_map/ppermute | solution.py:411
  60.9 1.0 copy-start.11
  74.2 3.7 %copy-start = (bf16[1024,2048]{1,0:T(8,128)(2,1)}, bf16[1024,2048]{1,0:T(8,128)(2,1)S(1)}, u32[]{:S(2)}) copy-start(bf16[1024,2048]{1,0:T(8,128)(2,1)S(1)} %get-tuple-element.64.rest_5_.rest_6_) | copy-start | bytes 12582916
  74.2 3.7 %copy-start.3 = (bf16[2048,1024]{1,0:T(8,128)(2,1)}, bf16[2048,1024]{1,0:T(8,128)(2,1)S(1)}, u32[]{:S(2)}) copy-start(bf16[2048,1024]{1,0:T(8,128)(2,1)S(1)} %get-tuple-element.65.rest_6_.rest_7_) | copy-start | bytes 12582916
  80.7 25.2 %collective-permute-start.5 = (bf16[256,1024]{1,0:T(8,128)(2,1)}, bf16[256,1024]{1,0:T(8,128)(2,1)}, u32[]{:S(2)}, u32[]{:S(2)}) collective-permute-start(bf16[256,1024]{1,0:T(8,128)(2,1)} %get-tuple-element.68), channel_id=1, source_target_pairs={{8,0},{9,1},{10,2},{11,3},{12,4},{13,5},{14,6},{15,7}} | collective-permute-start | bytes 1572872 | tf_op jit(solution)/shard_map/ppermute | solution.py:411
  81.9 24.6 %collective-permute-start.3 = (bf16[256,1024]{1,0:T(8,128)(2,1)}, bf16[256,1024]{1,0:T(8,128)(2,1)}, u32[]{:S(2)}, u32[]{:S(2)}) collective-permute-start(bf16[256,1024]{1,0:T(8,128)(2,1)} %get-tuple-element.60), channel_id=1, source_target_pairs={{8,16},{16,8},{9,17},{17,9},{10,18},{18,10},{11,19},{19,11},{12,20... | collective-permute-start | bytes 1572872 | tf_op jit(solution)/shard_map/ppermute | solution.py:411
  83.4 39.3 %collective-permute-start.7 = (bf16[256,1024]{1,0:T(8,128)(2,1)}, bf16[256,1024]{1,0:T(8,128)(2,1)}, u32[]{:S(2)}, u32[]{:S(2)}) collective-permute-start(bf16[256,1024]{1,0:T(8,128)(2,1)} %get-tuple-element.53), channel_id=1, source_target_pairs={{0,16},{1,17},{2,18},{3,19},{4,20},{5,21},{6,22},{7,23}} | collective-permute-start | bytes 1572872 | tf_op jit(solution)/shard_map/ppermute | solution.py:411
  99.6 32.0 %collective-permute-start.8 = (bf16[256,1024]{1,0:T(8,128)(2,1)}, bf16[256,1024]{1,0:T(8,128)(2,1)}, u32[]{:S(2)}, u32[]{:S(2)}) collective-permute-start(bf16[256,1024]{1,0:T(8,128)(2,1)} %get-tuple-element.58), channel_id=1, source_target_pairs={{0,16},{8,8},{1,17},{9,9},{2,18},{10,10},{3,19},{11,11},{4,20},{12... | collective-permute-start | bytes 1572872 | tf_op jit(solution)/shard_map/ppermute | solution.py:411
  101.7 47.4 %collective-permute-start.9 = (bf16[256,1024]{1,0:T(8,128)(2,1)}, bf16[256,1024]{1,0:T(8,128)(2,1)S(1)}, u32[]{:S(2)}, u32[]{:S(2)}) collective-permute-start(bf16[256,1024]{1,0:T(8,128)(2,1)} %get-tuple-element.68), channel_id=1, source_target_pairs={{16,0},{17,1},{18,2},{19,3},{20,4},{21,5},{22,6},{23,7}} | collective-permute-start | bytes 1572872 | tf_op jit(solution)/shard_map/ppermute | solution.py:411
  105.8 43.2 %collective-permute-start.10 = (bf16[256,1024]{1,0:T(8,128)(2,1)}, bf16[256,1024]{1,0:T(8,128)(2,1)S(1)}, u32[]{:S(2)}, u32[]{:S(2)}) collective-permute-start(bf16[256,1024]{1,0:T(8,128)(2,1)} %get-tuple-element.60), channel_id=1, source_target_pairs={{8,8},{9,9},{10,10},{11,11},{12,12},{13,13},{14,14},{15,15}} | collective-permute-start | bytes 1572872 | tf_op jit(solution)/shard_map/ppermute | solution.py:411
  106.5 2.2 copy-start.1
  108.7 2.2 copy-start.4
  110.9 20.7 %copy-start.10 = (s32[4]{0:T(128)S(1)}, s32[4]{0:T(128)}, u32[]{:S(2)}) copy-start(s32[4]{0:T(128)} %constant.29.clone.info_ref) | copy-start | bytes 52
  116.7 32.4 %collective-permute-start.11 = (bf16[256,1024]{1,0:T(8,128)(2,1)S(1)}, bf16[256,1024]{1,0:T(8,128)(2,1)S(1)}, u32[]{:S(2)}, u32[]{:S(2)}) collective-permute-start(bf16[256,1024]{1,0:T(8,128)(2,1)S(1)} %get-tuple-element.71), channel_id=1, source_target_pairs={{16,0},{17,1},{18,2},{19,3},{20,4},{21,5},{22,6},{23,7}} | collective-permute-start | bytes 1572872 | tf_op jit(solution)/shard_map/ppermute | solution.py:411
  122.7 20.7 %collective-permute-start.6 = (bf16[256,1024]{1,0:T(8,128)(2,1)S(1)}, bf16[256,1024]{1,0:T(8,128)(2,1)S(1)}, u32[]{:S(2)}, u32[]{:S(2)}) collective-permute-start(bf16[256,1024]{1,0:T(8,128)(2,1)S(1)} %get-tuple-element.71), channel_id=1, source_target_pairs={{8,0},{9,1},{10,2},{11,3},{12,4},{13,5},{14,6},{15,7}} | collective-permute-start | bytes 1572872 | tf_op jit(solution)/shard_map/ppermute | solution.py:411
  131.6 11.8 %copy-start.2 = (bf16[1024,2048]{1,0:T(8,128)(2,1)S(1)}, bf16[1024,2048]{1,0:T(8,128)(2,1)}, u32[]{:S(2)}) copy-start(bf16[1024,2048]{1,0:T(8,128)(2,1)} %copy-done) | copy-start | bytes 12582916
  131.7 11.8 %copy-start.5 = (bf16[2048,1024]{1,0:T(8,128)(2,1)S(1)}, bf16[2048,1024]{1,0:T(8,128)(2,1)}, u32[]{:S(2)}) copy-start(bf16[2048,1024]{1,0:T(8,128)(2,1)} %copy-done.3) | copy-start | bytes 12582916
  166.0 99.8 %reduce-scatter.3.cloned.1.call-start = ((), (), s32[]{:S(2)}) async-start(), calls=%async_computation.2 | async-start | bytes 4718592 | tf_op jit(solution)/shard_map/reduce_scatter | solution.py:538
  215.3 1.0 copy-start.6
  219.9 51.5 %collective-permute-start.13 = (bf16[256,1024]{1,0:T(8,128)(2,1)S(1)}, bf16[256,1024]{1,0:T(8,128)(2,1)S(1)}, u32[]{:S(2)}, u32[]{:S(2)}) collective-permute-start(bf16[256,1024]{1,0:T(8,128)(2,1)S(1)} %get-tuple-element.85), channel_id=1, source_target_pairs={{0,24},{8,16},{16,8},{24,0},{1,25},{9,17},{17,9},{25,1},{2,26},{10... | collective-permute-start | bytes 1572872 | tf_op jit(solution)/shard_map/ppermute | solution.py:545
  265.8 1.0 copy-start.7
  269.1 12.4 %collective-permute-start.12 = (bf16[128,2048]{1,0:T(8,128)(2,1)S(1)}, bf16[128,2048]{1,0:T(8,128)(2,1)S(1)}, u32[]{:S(2)}, u32[]{:S(2)}) collective-permute-start(bf16[128,2048]{1,0:T(8,128)(2,1)S(1)} %get-tuple-element.80), channel_id=1, source_target_pairs={{0,24},{8,16},{16,8},{24,0},{1,25},{9,17},{17,9},{25,1},{2,26},{10... | collective-permute-start | bytes 1572872 | tf_op jit(solution)/shard_map/ppermute | solution.py:545
Sparse Core Ops, SparseCore 0:
  166.1 49.1 reduce-scatter.4
  217.6 48.1 reduce-scatter.2

commit v4 on v3

--- a/solution.py
+++ b/solution.py
@@ -148,33 +148,26 @@
     return r * (e - mean_e - y * mean_ey)
 
 
-columns_of_table = 6
-
-
-def chain_step(call, table, recv, top_grad, saved, previous, after):
+columns_of_table = 4
+
+
+def chain_step(call, group, table, recv, top_grad, saved, previous, after):
     base = call * columns_of_table
     slopes, ys, rs, w_up, w_down = saved
-    rows, model = recv[0].shape
+    groups, rows, model = ys.shape
     width = w_up.shape[1]
     tile = tile_of(width)
-    groups = slopes.shape[0]
     tokens = top_grad.shape[2]
     per = rows // tokens
 
-    def body(info, *rest):
-        recv_refs, rest = rest[: len(recv)], rest[len(recv) :]
-        top_ref, y_ref, r_ref, slope_ref, p_ref, q_ref = rest[:6]
+    def body(info, e_ref, y_ref, r_ref, slope_ref, p_ref, q_ref, *rest):
         out_ref, pre_ref, sum_ref, whole, low, total = rest[-6:]
         j = pl.program_id(0)
         active = info[base] > 0
 
         @pl.when(jnp.logical_and(active, j == 0))
         def _():
-            top = top_ref[0].reshape(rows, model)
-            e = jnp.where(info[base + 4] == 1, top, recv_refs[-1][...])
-            if len(recv) > 1:
-                e = jnp.where(info[base + 4] == 2, recv_refs[0][...], e)
-            e = e.astype(f32)
+            e = e_ref[...].reshape(rows, model).astype(f32)
             grad = sum_gradient(e, y_ref[0].astype(f32), r_ref[0])
             whole[...] = grad
             low[...] = grad.astype(bf16)
@@ -187,7 +180,7 @@
             ).astype(bf16)
             pre_ref[0] = grad_pre
 
-            @pl.when(info[base + 5] > 0)
+            @pl.when(info[base + 3] > 0)
             def _():
                 part = dot(grad_pre, p_ref[...], ((1,), (1,)))
 
@@ -203,15 +196,20 @@
                 def _():
                     out_ref[...] = total[...].astype(bf16)
 
-    in_specs = [pl.BlockSpec((rows, model), lambda j, i: (0, 0))] * len(recv) + [
-        pl.BlockSpec((1, per, tokens, model), lambda j, i: (i[base + 1], i[base + 2], 0, 0)),
-        pl.BlockSpec((1, rows, model), lambda j, i: (i[base + 2], 0, 0)),
-        pl.BlockSpec((1, rows, 1), lambda j, i: (i[base + 2], 0, 0)),
-        pl.BlockSpec((1, rows, tile), lambda j, i: (i[base + 2], 0, j * i[base])),
-        pl.BlockSpec((model, tile), lambda j, i: (0, j * i[base + 5])),
+    if recv is None:
+        e_spec = pl.BlockSpec((1, per, tokens, model), lambda j, i: (i[base + 1], group, 0, 0))
+        operands = [in_hbm(top_grad)]
+    else:
+        e_spec = pl.BlockSpec((rows, model), lambda j, i: (0, 0))
+        operands = [recv]
+    in_specs = [
+        e_spec,
+        pl.BlockSpec((1, rows, model), lambda j, i: (group, 0, 0)),
+        pl.BlockSpec((1, rows, 1), lambda j, i: (group, 0, 0)),
+        pl.BlockSpec((1, rows, tile), lambda j, i: (group, 0, j * i[base])),
+        pl.BlockSpec((model, tile), lambda j, i: (0, j * i[base + 3])),
         pl.BlockSpec((tile, model), lambda j, i: (j * i[base], 0)),
     ]
-    operands = list(recv) + [in_hbm(top_grad)]
     operands += [in_vmem(x) for x in (ys, rs, slopes, w_up, w_down)]
     aliases = {}
     if previous is not None:
@@ -230,8 +228,8 @@
             in_specs=in_specs,
             out_specs=[
                 pl.BlockSpec((rows, model), lambda j, i: (0, 0)),
-                pl.BlockSpec((1, rows, tile), lambda j, i: (i[base + 3], 0, j * i[base])),
-                pl.BlockSpec((1, rows, model), lambda j, i: (i[base + 3], 0, 0)),
+                pl.BlockSpec((1, rows, tile), lambda j, i: (i[base + 2], 0, j * i[base])),
+                pl.BlockSpec((1, rows, model), lambda j, i: (i[base + 2], 0, 0)),
             ],
             scratch_shapes=[
                 pltpu.VMEM((rows, model), f32),
@@ -415,39 +413,20 @@
     )[None, None]
 
     upper = (position >= half).astype(jnp.int32)
-    near = jnp.minimum(position, last - position)
-    start = (near, last - near)
     relay = (1 - upper, upper)
-
-    def begins(kind, i):
-        return min(i, last - i) if kind == 0 else last - min(i, last - i)
-
-    calls = [
-        (tick, kind)
-        for tick in range(groups + last)
-        for kind in range(2)
-        if any(0 <= tick - begins(kind, i) < groups for i in range(sections))
-    ]
-    ticks = np.array([tick for tick, _ in calls], np.int32)
-    second = np.array([kind for _, kind in calls], np.int32)
-    group = jnp.where(second == 1, ticks - start[1], ticks - start[0])
-    of = jnp.where(second == 1, relay[1], relay[0])
-    needless = jnp.logical_and(of == 1, position == last)
-    active = (group >= 0) & (group < groups) & ~needless
-    group = jnp.clip(group, 0, groups - 1)
-    asked = active & ~((of == 0) & (position == 0))
+    calls = [(stage, group) for stage in range(sections) for group in range(groups)]
+    stages = np.array([stage for stage, _ in calls], np.int32)
+    own = np.array([group for _, group in calls], np.int32)
+    of = jnp.where(stages < half, relay[0], relay[1])
+    active = (jnp.where(of == 0, last - position, position) == stages) & ~(
+        (of == 1) & (position == last)
+    )
     table = jnp.stack(
         [
             active.astype(jnp.int32),
             of,
-            group,
-            jnp.where(active & (of == 0), group, groups),
-            jnp.where(
-                jnp.where(of == 0, position == last, position == 0),
-                1,
-                jnp.where((second == 1) & (near == half - 1), 2, 0),
-            ),
-            asked.astype(jnp.int32),
+            jnp.where(active & (of == 0), own, groups),
+            (active & (stages < last)).astype(jnp.int32),
         ],
         axis=1,
     ).reshape(-1)
@@ -461,74 +440,47 @@
     def run_forward(kind, after):
         nonlocal blocks, order
         *blocks, slopes, ys, rs, w_up, w_down = forward(
-            per, section_inputs, up_weight, down_weight, kinds[kind], plan, blocks, order + after, 2, True
+            per, section_inputs, up_weight, down_weight, kinds[kind], plan, blocks, after, 2, True
         )
         saved[kind] = (slopes, ys, rs, w_up, w_down)
         order = [blocks[0]]
 
+    run_forward(0, [])
     late = []
-    run_forward(0, [])
-    blank = jnp.zeros((rows, model), bf16)
     received = {}
     arrived = {}
     kept = None
-    for call, (tick, kind) in enumerate(calls):
-        if kind == 1 and saved[1] is None:
-            run_forward(1, [])
-        if call == len(calls) - 1:
+    for call, (stage, group) in enumerate(calls):
+        if stage == last and group == 0:
             *home_blocks, slopes, ys, rs = forward(
                 per, mirrored, up_weight, down_weight, home_kind, plan, None, order + late, 1, False
             )
             saved_home = (slopes, ys, rs)
             order = [home_blocks[0]]
-
-        def busy(i):
-            return 0 <= tick - begins(kind, i) < groups
-
-        recv = [
-            received.pop((tick, kind, way))
-            for way in range(2)
-            if (tick, kind, way) in received
-        ] or [blank]
-        out, *kept = chain_step(call, table, recv, top_grad, saved[kind], kept, order)
+        recv = received.pop((stage, group), None)
+        out, *kept = chain_step(
+            call, group, table, recv, top_grad, saved[int(stage >= half)], kept, order
+        )
         order = [kept[0]]
-        relay_of = [(0 if i >= half else 1) if kind == 0 else (1 if i >= half else 0) for i in range(sections)]
-        to = [i - 1 if relay_of[i] == 0 else i + 1 for i in range(sections)]
-        live = [
-            i
-            for i in range(sections)
-            if busy(i) and 0 <= to[i] <= last and not (relay_of[i] == 1 and to[i] == last)
-        ]
-        crossing = [i for i in live if kind == 0 and (i >= half) != (to[i] >= half)]
-        for pairs, kind_after, way in (
-            ([(i, to[i]) for i in live if i in crossing], 1, 0),
-            ([(i, to[i]) for i in live if i not in crossing], kind, 1),
-        ):
-            got = hop(out, pairs)
-            if got is not None:
-                received[(tick + 1, kind_after, way)] = got
-        pairs = [(i, last - 1 - i) for i in range(last) if busy(i) and relay_of[i] == 1]
+        pairs = [(last - stage, last - stage - 1)] if stage < last else []
+        if stage < last - 1:
+            pairs.append((stage, stage + 1))
         got = hop(out, pairs)
         if got is not None:
-            for i, k in pairs:
-                arrived[(k, tick - begins(kind, i))] = got
-            if tick < half:
+            received[(stage + 1, group)] = got
+        if stage < last:
+            got = hop(out, [(stage, last - 1 - stage)])
+            arrived[(last - 1 - stage, group)] = got
+            if stage < half:
                 late.append(got)
-        if saved[1] is None and tick + 1 >= groups:
-            run_forward(1, [mirrored[0, 0]])
+        if saved[1] is None and group == groups - 1:
+            run_forward(1, order + [mirrored[0, 0]])
 
     came = []
-    for g in range(groups):
-        options = []
-        for k in range(last):
-            value = arrived[(k, g)]
-            if not any(value is x for x, _ in options):
-                options.append((value, []))
-            next(places for x, places in options if x is value).append(k)
-        value = options[0][0]
-        for other, places in options[1:]:
-            here = either([position == k for k in places])
-            value = jnp.where(here, other, value)
+    for group in range(groups):
+        value = arrived[(0, group)]
+        for k in range(1, last):
+            value = jnp.where(position == k, arrived[(k, group)], value)
         came.append(value)
     home_pre, home_sum = home_step(
         (position == last).astype(jnp.int32)[None], came, top_grad, saved_home, down_weight, order
@@ -548,13 +500,6 @@
     new_up_weight, new_up_moment = finish(up_weight, up_moment, up_sum)
     new_down_weight, new_down_moment = finish(down_weight, down_moment, down_sum)
     return (new_up_weight, new_down_weight, new_up_moment, new_down_moment)
-
-
-def either(conditions):
-    result = conditions[0]
-    for condition in conditions[1:]:
-        result = jnp.logical_or(result, condition)
-    return result
 
 
 def solution(mesh):

time: 291 us -> 280 us (0.962)
  local copies, waits for them, and re-layouts: 9.67 us -> 22.3 us
  waiting for transfers between devices: 120 us -> 108 us
  starting transfers between devices: 41 us -> 29.9 us
    ppermute x11 -> x12, waiting for transfers between devices: 26.5 us -> 14.1 us  [hop(): return lax.ppermute(value, 'section', pairs) if pairs else None]
    unnamed x24 -> x50, local copies, waits for them, and re-layouts: 8.12 us -> 19.9 us
    ppermute x11 -> x12, starting transfers between devices: 32.3 us -> 21.2 us  [hop(): return lax.ppermute(value, 'section', pairs) if pairs else None]
    pallas_call x6 -> x8, Pallas kernels: 33.7 us -> 34.7 us  [chain_step(): pl.pallas_call(body, grid_spec=pltpu.PrefetchScalarGridSpec(num_scalar_pr...]
  transfers between devices with their start and end apart: 16 -> 17, of which waited for: 7 -> 6; matrix products, arithmetic and copies ran while one was open for 1% -> 1% of each run, Pallas kernels for 28% -> 29%
where the time goes in v4:
time: 280 us; the launch traced here: 279 us
  waiting for transfers between devices  108 us (39%)
  Pallas kernels  101 us (36%)
  starting transfers between devices  29.9 us (11%)
  local copies, waits for them, and re-layouts  22.3 us (8%)
  between operations  14.4 us (5%)
  other arithmetic  3.66 us (1%)
    reduce_scatter x1, waiting for transfers between devices, on_device(): up_sum = lax.psum_scatter(up_part, 'dp', scatter_dimension=0, tiled=True)  43.5 us
    reduce_scatter x1, waiting for transfers between devices, on_device(): lax.psum_scatter(down_part, 'dp', scatter_dimension=0, tiled=True)  40.9 us
    pallas_call x3, Pallas kernels, forward(): pl.pallas_call(body, grid_spec=pltpu.PrefetchScalarGridSpec(num_scalar_pr...  36.6 us
    pallas_call x8, Pallas kernels, chain_step(): pl.pallas_call(body, grid_spec=pltpu.PrefetchScalarGridSpec(num_scalar_pr...  34.7 us
    ppermute x12, starting transfers between devices, hop(): return lax.ppermute(value, 'section', pairs) if pairs else None  21.2 us
    unnamed x50, local copies, waits for them, and re-layouts  19.9 us
    pallas_call x2, Pallas kernels, weight_gradient(): pl.pallas_call(body, grid=((rows if split_left else columns) // tile,), i...  17 us
    ppermute x12, waiting for transfers between devices, hop(): return lax.ppermute(value, 'section', pairs) if pairs else None  14.1 us
  transfers between devices with their start and end apart: 17, of which 6 were waited for; matrix products, arithmetic and copies ran while one was open for 1% of the time, Pallas kernels for 29%

profile of v4, /device:TPU:0, one launch (start us, length us, event | category | flops | bytes accessed | tf_op | source)
XLA Modules:
  0.0 279.0 jit_solution(14919440991782152760)
XLA Ops:
  7.2 2.3 slice_bitcast_fusion
  9.5 3.9 %collective-permute-start = (bf16[4,128,1024]{2,1,0:T(8,128)(2,1)}, bf16[4,128,1024]{2,1,0:T(8,128)(2,1)}, u32[]{:S(2)}, u32[]{:S(2)}) collective-permute-start(bf16[4,128,1024]{2,1,0:T(8,128)(2,1)} %slice_bitcast_fusion), channel_id=1, source_target_pairs={{0,24},{8,16},{16,8},{24,0},{1,25},{9,17},{17,9},{25,1},{2,26},{10... | collective-permute-start | bytes 3145736 | tf_op jit(solution)/shard_map/ppermute | solution.py:411
  15.4 12.2 %forward.3 = (bf16[2,2,256,1024]{3,2,1,0:T(8,128)(2,1)}, bf16[2,2,256,2048]{3,2,1,0:T(8,128)(2,1)}, bf16[2,256,2048]{2,1,0:T(8,128)(2,1)S(1)}, bf16[2,256,1024]{...) custom-call(s32[4]{0:T(128)S(1)} %stack.54.info_ref, ...), custom_call_target="tpu_custom_call" | custom-call | flops 8589934592 | bytes 8388608 | tf_op jit(solution)/shard_map/forward/pallas_call | solution.py:126
  27.6 2.1 copy-done.6
  29.7 1.9 copy-done.9
  31.8 3.1 %copy-done.7 = bf16[1024,2048]{1,0:T(8,128)(2,1)S(1)} copy-done((bf16[1024,2048]{1,0:T(8,128)(2,1)S(1)}, bf16[1024,2048]{1,0:T(8,128)(2,1)}, u32[]{:S(2)}) %copy-start.7) | copy-done | bytes 4194328
  35.0 2.2 copy-done.10
  37.2 7.9 %chain.8 = (bf16[256,1024]{1,0:T(8,128)(2,1)}, bf16[3,256,2048]{2,1,0:T(8,128)(2,1)}, bf16[3,256,1024]{2,1,0:T(8,128)(2,1)}) custom-call(s32[32]{0:T(128)S(1)} %reshape.15.info, bf16[2,4,128,1024]{3,2,1,0:T(8,128)(2,1)} %refs_2_.5, bf16[2,256,1024]{2,1,0:T(8,128)(2,1)S(1)} %get-tuple-element.53.y_ref, f32[2,256,1]{2,1,0:T(8,128)S(1)} %get-tuple-element.54.r_ref, ...), custom_call_target="tpu_custom_call" | custom-call | flops 4294967296 | bytes 8388608 | tf_op jit(solution)/shard_map/chain/pallas_call | solution.py:223
  45.0 1.3 collective-permute-start.2
  46.4 7.9 %chain.9 = (bf16[256,1024]{1,0:T(8,128)(2,1)}, bf16[3,256,2048]{2,1,0:T(8,128)(2,1)}, bf16[3,256,1024]{2,1,0:T(8,128)(2,1)}) custom-call(s32[32]{0:T(128)S(1)} %reshape.15.info, bf16[2,4,128,1024]{3,2,1,0:T(8,128)(2,1)} %refs_2_.5, bf16[2,256,1024]{2,1,0:T(8,128)(2,1)S(1)} %get-tuple-element.53.y_ref, ...), custom_call_target="tpu_custom_call", output_to_operand_aliasing={{1}: (7, {}), {2}: (8, {})} | custom-call | flops 4294967296 | bytes 8388608 | tf_op jit(solution)/shard_map/chain/pallas_call | solution.py:223
  54.3 1.3 collective-permute-start.1
  55.7 12.6 %forward.4 = (bf16[2,2,256,1024]{3,2,1,0:T(8,128)(2,1)}, bf16[2,2,256,2048]{3,2,1,0:T(8,128)(2,1)}, bf16[2,256,2048]{2,1,0:T(8,128)(2,1)S(1)}, bf16[2,256,1024]{...) custom-call(s32[4]{0:T(128)S(1)} %stack.53.info_ref, ...), custom_call_target="tpu_custom_call", output_to_operand_aliasing={{0}: (8, {}), {1}: (9, {})} | custom-call | flops 8589934592 | bytes 8388608 | tf_op jit(solution)/shard_map/forward/pallas_call | solution.py:126
  69.0 2.4 chain.10
  71.4 1.2 copy-done.3
  72.6 1.5 collective-permute-start.4
  74.1 1.9 chain.11
  76.0 1.5 collective-permute-start.3
  77.5 7.1 %collective-permute-start.8 = (bf16[256,1024]{1,0:T(8,128)(2,1)}, bf16[256,1024]{1,0:T(8,128)(2,1)}, u32[]{:S(2)}, u32[]{:S(2)}) collective-permute-start(bf16[256,1024]{1,0:T(8,128)(2,1)} %get-tuple-element.62), channel_id=1, source_target_pairs={{0,16},{1,17},{2,18},{3,19},{4,20},{5,21},{6,22},{7,23}} | collective-permute-start | bytes 1572872 | tf_op jit(solution)/shard_map/ppermute | solution.py:409
  84.5 2.1 collective-permute-start.7
  88.0 2.2 copy-done.1
  90.2 2.2 copy-done.4
  92.4 0.9 copy-done.17
  93.4 2.7 chain.12
  96.0 1.3 collective-permute-start.11
  97.3 2.7 chain.13
  100.0 2.8 %collective-permute-done.8.refs_8_ = bf16[256,1024]{1,0:T(8,128)(2,1)} collective-permute-done((bf16[256,1024]{1,0:T(8,128)(2,1)}, bf16[256,1024]{1,0:T(8,128)(2,1)}, u32[]{:S(2)}, u32[]{:S(2)}) %collective-permute-start.8) | collective-permute-done | bytes 524320 | tf_op jit(solution)/shard_map/ppermute | solution.py:409
  102.8 1.3 collective-permute-start.6
  104.1 9.9 %collective-permute-done.7.refs_7_ = bf16[256,1024]{1,0:T(8,128)(2,1)} collective-permute-done((bf16[256,1024]{1,0:T(8,128)(2,1)}, bf16[256,1024]{1,0:T(8,128)(2,1)}, u32[]{:S(2)}, u32[]{:S(2)}) %collective-permute-start.7) | collective-permute-done | bytes 524320 | tf_op jit(solution)/shard_map/ppermute | solution.py:409
  114.0 1.3 collective-permute-start.12
  115.3 1.3 collective-permute-start.5
  116.6 11.8 %forward.5 = (bf16[1,2,256,1024]{3,2,1,0:T(8,128)(2,1)}, bf16[1,2,256,2048]{3,2,1,0:T(8,128)(2,1)}, bf16[2,256,2048]{2,1,0:T(8,128)(2,1)S(1)}, bf16[2,256,1024]{2,1,0:T(8,128)(2,1)S(1)}, f32[2,256,1]{2,1,0:T(8,128)S(1)}) custom-call(s32[4]{0:T(128)S(1)} %copy-done.23, s32[2,4]{1,0:T(2,128)S(1)} %copy-done.22, ...), custom_call_target="tpu_custom_call" | custom-call | flops 8589934592 | bytes 8388608 | tf_op jit(solution)/shard_map/forward/pallas_call | solution.py:126
  128.4 1.4 collective-permute-done.12
  130.6 4.6 %chain.14 = (bf16[256,1024]{1,0:T(8,128)(2,1)}, bf16[3,256,2048]{2,1,0:T(8,128)(2,1)}, bf16[3,256,1024]{2,1,0:T(8,128)(2,1)}) custom-call(s32[32]{0:T(128)S(1)} %reshape.15.info, bf16[256,1024]{1,0:T(8,128)(2,1)S(1)} %collective-permute-done.6.e_ref, ...), custom_call_target="tpu_custom_call", output_to_operand_aliasing={{1}: (7, {}), {2}: (8, {})} | custom-call | flops 4294967296 | bytes 8388608 | tf_op jit(solution)/shard_map/chain/pallas_call | solution.py:223
  135.2 4.6 %chain.15 = (bf16[256,1024]{1,0:T(8,128)(2,1)}, bf16[3,256,2048]{2,1,0:T(8,128)(2,1)}, bf16[3,256,1024]{2,1,0:T(8,128)(2,1)}) custom-call(s32[32]{0:T(128)S(1)} %reshape.15.info, bf16[256,1024]{1,0:T(8,128)(2,1)S(1)} %collective-permute-done.5.e_ref, ...), custom_call_target="tpu_custom_call", output_to_operand_aliasing={{1}: (7, {}), {2}: (8, {})} | custom-call | flops 4294967296 | bytes 8388608 | tf_op jit(solution)/shard_map/chain/pallas_call | solution.py:223
  139.8 7.2 %home.1 = (bf16[2,256,2048]{2,1,0:T(8,128)(2,1)}, bf16[2,256,1024]{2,1,0:T(8,128)(2,1)}) custom-call(s32[1]{0:T(128)} %bitcast.7.info, bf16[256,1024]{1,0:T(8,128)(2,1)S(1)} %select_select_fusion.1.refs_0_, bf16[256,1024]{1,0:T(8,128)(2,1)S(1)} %select_select_fusion.refs_1_, bf16[2,4,128,1024]{3,2,1,0:T(8,128)(2,1)} %refs_2_.5, ...), custom_call_target="tpu_custom_call" | custom-call | flops 4294967296 | bytes 4194304 | tf_op jit(solution)/shard_map/home/pallas_call | solution.py:279
  147.0 8.4 %weights.3 = bf16[2048,1024]{1,0:T(8,128)(2,1)} custom-call(bf16[2,2,256,2048]{3,2,1,0:T(8,128)(2,1)} %get-tuple-element.91.la_ref, bf16[3,256,1024]{2,1,0:T(8,128)(2,1)} %get-tuple-element.92.ra_ref, bf16[1,2,256,2048]{3,2,1,0:T(8,128)(2,1)} %get-tuple-element.93.lb_ref, bf16[2,256,1024]{2,1,0:T(8,128)(2,1)} %get-tuple-element.94.rb_ref), custom_call_target="tpu_custom_call" | custom-call | flops 4294967296 | bytes 4194304 | tf_op jit(solution)/shard_map/weights/pallas_call | solution.py:340
  155.5 8.6 %weights.2 = bf16[1024,2048]{1,0:T(8,128)(2,1)} custom-call(bf16[2,2,256,1024]{3,2,1,0:T(8,128)(2,1)} %get-tuple-element.61.rest_2_.la_ref, bf16[3,256,2048]{2,1,0:T(8,128)(2,1)} %get-tuple-element.85.refs_7_.ra_ref, bf16[1,2,256,1024]{3,2,1,0:T(8,128)(2,1)} %get-tuple-element.82.rest_2_.lb_ref, bf16[2,256,2048]{2,1,0:T(8,128)(2,1)} %get-tuple-element.89.rb_ref), custom_call_target="tpu_custom_call" | custom-call | flops 4294967296 | bytes 4194304 | tf_op jit(solution)/shard_map/weights/pallas_call | solution.py:340
  164.1 40.9 %reduce-scatter.5.cloned.1.call-done.total_ref = bf16[256,1024]{1,0:T(8,128)(2,1)} async-done(((bf16[2048,1024]{1,0:T(8,128)(2,1)}), bf16[256,1024]{1,0:T(8,128)(2,1)}) %reduce-scatter.5.cloned.1.call-update) | async-done | bytes 524304 | tf_op jit(solution)/shard_map/reduce_scatter | solution.py:492
  205.0 1.0 copy-done.19
  206.0 3.5 %update.3 = (bf16[256,1024]{1,0:T(8,128)(2,1)S(1)}, f32[1,256,1024]{2,1,0:T(8,128)}) custom-call(s32[1]{0:T(128)} %bitcast.info, bf16[2,1,2048,1024]{3,2,1,0:T(8,128)(2,1)} %weight_ref.3, f32[1,256,1024]{2,1,0:T(8,128)} %moment_ref.3, bf16[256,1024]{1,0:T(8,128)(2,1)S(1)} %copy-done.19), custom_call_target="tpu_custom_call" | custom-call | flops 1048576 | bytes 3145728 | tf_op jit(solution)/shard_map/update/pallas_call | solution.py:372
  209.6 2.4 collective-permute-start.14
  211.9 43.5 %reduce-scatter.3.cloned.1.call-done.total_ref = bf16[128,2048]{1,0:T(8,128)(2,1)} async-done(((bf16[1024,2048]{1,0:T(8,128)(2,1)}), bf16[128,2048]{1,0:T(8,128)(2,1)}) %reduce-scatter.3.cloned.1.call-update) | async-done | bytes 524304 | tf_op jit(solution)/shard_map/reduce_scatter | solution.py:490
  255.4 1.0 copy-done.20
  256.5 2.2 update.2
  258.7 2.4 collective-permute-start.13
  261.1 1.1 maximum_bitcast_fusion.1
  262.1 9.0 %collective-permute-done.13 = bf16[128,2048]{1,0:T(8,128)(2,1)S(1)} collective-permute-done((bf16[128,2048]{1,0:T(8,128)(2,1)S(1)}, bf16[128,2048]{1,0:T(8,128)(2,1)S(1)}, u32[]{:S(2)}, u32[]{:S(2)}) %collective-permute-start.13) | collective-permute-done | bytes 524320 | tf_op jit(solution)/shard_map/ppermute | solution.py:497
  271.1 1.1 maximum_bitcast_fusion
  (67 shorter events, 5.2 us)
Async XLA Ops:
  7.2 197.8 %reduce-scatter.5.cloned.1.call-start = ((), (), s32[]{:S(2)}) async-start(), calls=%async_computation.3 | async-start | bytes 4718592 | tf_op jit(solution)/shard_map/reduce_scatter | solution.py:492
  9.5 46.1 %collective-permute-start = (bf16[4,128,1024]{2,1,0:T(8,128)(2,1)}, bf16[4,128,1024]{2,1,0:T(8,128)(2,1)}, u32[]{:S(2)}, u32[]{:S(2)}) collective-permute-start(bf16[4,128,1024]{2,1,0:T(8,128)(2,1)} %slice_bitcast_fusion), channel_id=1, source_target_pairs={{0,24},{8,16},{16,8},{24,0},{1,25},{9,17},{17,9},{25,1},{2,26},{10... | collective-permute-start | bytes 3145736 | tf_op jit(solution)/shard_map/ppermute | solution.py:411
  14.7 0.7 copy-start.21
  15.4 16.2 %copy-start.24 = (pred[8]{0:T(512)(128)(4,1)S(1)}, pred[8]{0:T(512)(128)(4,1)}, u32[]{:S(2)}) copy-start(pred[8]{0:T(512)(128)(4,1)} %constant.30.clone) | copy-start | bytes 28
  27.6 2.1 copy-start.6
  29.7 1.9 copy-start.9
  31.7 14.7 %copy-start.12 = (bf16[2,256,2048]{2,1,0:T(8,128)(2,1)}, bf16[2,256,2048]{2,1,0:T(8,128)(2,1)S(1)}, u32[]{:S(2)}) copy-start(bf16[2,256,2048]{2,1,0:T(8,128)(2,1)S(1)} %get-tuple-element.55.slope_ref) | copy-start | bytes 6291460
  31.7 14.7 %copy-start.14 = (bf16[2,256,1024]{2,1,0:T(8,128)(2,1)}, bf16[2,256,1024]{2,1,0:T(8,128)(2,1)S(1)}, u32[]{:S(2)}) copy-start(bf16[2,256,1024]{2,1,0:T(8,128)(2,1)S(1)} %get-tuple-element.53.y_ref) | copy-start | bytes 3145732
  31.8 3.1 %copy-start.7 = (bf16[1024,2048]{1,0:T(8,128)(2,1)S(1)}, bf16[1024,2048]{1,0:T(8,128)(2,1)}, u32[]{:S(2)}) copy-start(bf16[1024,2048]{1,0:T(8,128)(2,1)} %copy-done.6) | copy-start | bytes 12582916
  35.0 2.2 copy-start.10
  45.0 23.9 %collective-permute-start.2 = (bf16[256,1024]{1,0:T(8,128)(2,1)}, bf16[256,1024]{1,0:T(8,128)(2,1)S(1)}, u32[]{:S(2)}, u32[]{:S(2)}) collective-permute-start(bf16[256,1024]{1,0:T(8,128)(2,1)} %get-tuple-element.63), channel_id=1, source_target_pairs={{24,16},{0,8},{25,17},{1,9},{26,18},{2,10},{27,19},{3,11},{28,20},... | collective-permute-start | bytes 1572872 | tf_op jit(solution)/shard_map/ppermute | solution.py:409
  46.4 9.2 %copy-start.22 = (s32[2,4]{1,0:T(2,128)S(1)}, s32[2,4]{1,0:T(2,128)}, u32[]{:S(2)}) copy-start(s32[2,4]{1,0:T(2,128)} %plan_ref.5) | copy-start | bytes 100
  54.3 19.8 %collective-permute-start.1 = (bf16[256,1024]{1,0:T(8,128)(2,1)}, bf16[256,1024]{1,0:T(8,128)(2,1)S(1)}, u32[]{:S(2)}, u32[]{:S(2)}) collective-permute-start(bf16[256,1024]{1,0:T(8,128)(2,1)} %get-tuple-element.62), channel_id=1, source_target_pairs={{24,16},{0,8},{25,17},{1,9},{26,18},{2,10},{27,19},{3,11},{28,20},... | collective-permute-start | bytes 1572872 | tf_op jit(solution)/shard_map/ppermute | solution.py:409
  55.6 13.4 %copy-start.8 = (bf16[1024,2048]{1,0:T(8,128)(2,1)S(1)}, bf16[1024,2048]{1,0:T(8,128)(2,1)}, u32[]{:S(2)}) copy-start(bf16[1024,2048]{1,0:T(8,128)(2,1)} %copy-done.6) | copy-start | bytes 12582916
  55.6 13.4 %copy-start.11 = (bf16[2048,1024]{1,0:T(8,128)(2,1)S(1)}, bf16[2048,1024]{1,0:T(8,128)(2,1)}, u32[]{:S(2)}) copy-start(bf16[2048,1024]{1,0:T(8,128)(2,1)} %copy-done.9) | copy-start | bytes 12582916
  55.6 13.4 %copy-start.13 = (bf16[2,256,2048]{2,1,0:T(8,128)(2,1)S(1)}, bf16[2,256,2048]{2,1,0:T(8,128)(2,1)}, u32[]{:S(2)}) copy-start(bf16[2,256,2048]{2,1,0:T(8,128)(2,1)} %copy-done.12) | copy-start | bytes 6291460
  55.6 13.4 %copy-start.15 = (bf16[2,256,1024]{2,1,0:T(8,128)(2,1)S(1)}, bf16[2,256,1024]{2,1,0:T(8,128)(2,1)}, u32[]{:S(2)}) copy-start(bf16[2,256,1024]{2,1,0:T(8,128)(2,1)} %copy-done.14) | copy-start | bytes 3145732
  68.3 0.7 copy-start.16
  69.0 2.5 copy-start
  69.0 3.6 %copy-start.3 = (bf16[2048,1024]{1,0:T(8,128)(2,1)}, bf16[2048,1024]{1,0:T(8,128)(2,1)S(1)}, u32[]{:S(2)}) copy-start(bf16[2048,1024]{1,0:T(8,128)(2,1)S(1)} %get-tuple-element.72.q_ref) | copy-start | bytes 12582916
  72.6 14.7 %collective-permute-start.4 = (bf16[256,1024]{1,0:T(8,128)(2,1)}, bf16[256,1024]{1,0:T(8,128)(2,1)}, u32[]{:S(2)}, u32[]{:S(2)}) collective-permute-start(bf16[256,1024]{1,0:T(8,128)(2,1)} %get-tuple-element.73), channel_id=1, source_target_pairs={{16,8},{8,16},{17,9},{9,17},{18,10},{10,18},{19,11},{11,19},{20,12... | collective-permute-start | bytes 1572872 | tf_op jit(solution)/shard_map/ppermute | solution.py:409
  76.0 20.0 %collective-permute-start.3 = (bf16[256,1024]{1,0:T(8,128)(2,1)}, bf16[256,1024]{1,0:T(8,128)(2,1)}, u32[]{:S(2)}, u32[]{:S(2)}) collective-permute-start(bf16[256,1024]{1,0:T(8,128)(2,1)} %get-tuple-element.67), channel_id=1, source_target_pairs={{16,8},{8,16},{17,9},{9,17},{18,10},{10,18},{19,11},{11,19},{20,12... | collective-permute-start | bytes 1572872 | tf_op jit(solution)/shard_map/ppermute | solution.py:409
  77.5 25.4 %collective-permute-start.8 = (bf16[256,1024]{1,0:T(8,128)(2,1)}, bf16[256,1024]{1,0:T(8,128)(2,1)}, u32[]{:S(2)}, u32[]{:S(2)}) collective-permute-start(bf16[256,1024]{1,0:T(8,128)(2,1)} %get-tuple-element.62), channel_id=1, source_target_pairs={{0,16},{1,17},{2,18},{3,19},{4,20},{5,21},{6,22},{7,23}} | collective-permute-start | bytes 1572872 | tf_op jit(solution)/shard_map/ppermute | solution.py:409
  84.5 29.4 %collective-permute-start.7 = (bf16[256,1024]{1,0:T(8,128)(2,1)}, bf16[256,1024]{1,0:T(8,128)(2,1)}, u32[]{:S(2)}, u32[]{:S(2)}) collective-permute-start(bf16[256,1024]{1,0:T(8,128)(2,1)} %get-tuple-element.63), channel_id=1, source_target_pairs={{0,16},{1,17},{2,18},{3,19},{4,20},{5,21},{6,22},{7,23}} | collective-permute-start | bytes 1572872 | tf_op jit(solution)/shard_map/ppermute | solution.py:409
  86.6 28.6 %collective-permute-start.10 = (bf16[256,1024]{1,0:T(8,128)(2,1)}, bf16[256,1024]{1,0:T(8,128)(2,1)S(1)}, u32[]{:S(2)}, u32[]{:S(2)}) collective-permute-start(bf16[256,1024]{1,0:T(8,128)(2,1)} %get-tuple-element.67), channel_id=1, source_target_pairs={{8,8},{9,9},{10,10},{11,11},{12,12},{13,13},{14,14},{15,15}} | collective-permute-start | bytes 1572872 | tf_op jit(solution)/shard_map/ppermute | solution.py:409
  87.3 29.2 %collective-permute-start.9 = (bf16[256,1024]{1,0:T(8,128)(2,1)}, bf16[256,1024]{1,0:T(8,128)(2,1)S(1)}, u32[]{:S(2)}, u32[]{:S(2)}) collective-permute-start(bf16[256,1024]{1,0:T(8,128)(2,1)} %get-tuple-element.73), channel_id=1, source_target_pairs={{8,8},{9,9},{10,10},{11,11},{12,12},{13,13},{14,14},{15,15}} | collective-permute-start | bytes 1572872 | tf_op jit(solution)/shard_map/ppermute | solution.py:409
  88.0 2.2 copy-start.1
  90.2 2.2 copy-start.4
  92.4 0.9 copy-start.17
  96.0 33.9 %collective-permute-start.11 = (bf16[256,1024]{1,0:T(8,128)(2,1)S(1)}, bf16[256,1024]{1,0:T(8,128)(2,1)S(1)}, u32[]{:S(2)}, u32[]{:S(2)}) collective-permute-start(bf16[256,1024]{1,0:T(8,128)(2,1)S(1)} %get-tuple-element.79), channel_id=1, source_target_pairs={{16,0},{17,1},{18,2},{19,3},{20,4},{21,5},{22,6},{23,7}} | collective-permute-start | bytes 1572872 | tf_op jit(solution)/shard_map/ppermute | solution.py:409
  97.3 19.2 %copy-start.23 = (s32[4]{0:T(128)S(1)}, s32[4]{0:T(128)}, u32[]{:S(2)}) copy-start(s32[4]{0:T(128)} %constant.31.clone.info_ref) | copy-start | bytes 52
  102.8 27.2 %collective-permute-start.6 = (bf16[256,1024]{1,0:T(8,128)(2,1)S(1)}, bf16[256,1024]{1,0:T(8,128)(2,1)S(1)}, u32[]{:S(2)}, u32[]{:S(2)}) collective-permute-start(bf16[256,1024]{1,0:T(8,128)(2,1)S(1)} %get-tuple-element.79), channel_id=1, source_target_pairs={{8,0},{9,1},{10,2},{11,3},{12,4},{13,5},{14,6},{15,7}} | collective-permute-start | bytes 1572872 | tf_op jit(solution)/shard_map/ppermute | solution.py:409
  114.0 15.8 %collective-permute-start.12 = (bf16[256,1024]{1,0:T(8,128)(2,1)S(1)}, bf16[256,1024]{1,0:T(8,128)(2,1)S(1)}, u32[]{:S(2)}, u32[]{:S(2)}) collective-permute-start(bf16[256,1024]{1,0:T(8,128)(2,1)S(1)} %get-tuple-element.78), channel_id=1, source_target_pairs={{16,0},{17,1},{18,2},{19,3},{20,4},{21,5},{22,6},{23,7}} | collective-permute-start | bytes 1572872 | tf_op jit(solution)/shard_map/ppermute | solution.py:409
  115.3 19.9 %collective-permute-start.5 = (bf16[256,1024]{1,0:T(8,128)(2,1)S(1)}, bf16[256,1024]{1,0:T(8,128)(2,1)S(1)}, u32[]{:S(2)}, u32[]{:S(2)}) collective-permute-start(bf16[256,1024]{1,0:T(8,128)(2,1)S(1)} %get-tuple-element.78), channel_id=1, source_target_pairs={{8,0},{9,1},{10,2},{11,3},{12,4},{13,5},{14,6},{15,7}} | collective-permute-start | bytes 1572872 | tf_op jit(solution)/shard_map/ppermute | solution.py:409
  116.6 13.4 %copy-start.5 = (bf16[2048,1024]{1,0:T(8,128)(2,1)S(1)}, bf16[2048,1024]{1,0:T(8,128)(2,1)}, u32[]{:S(2)}) copy-start(bf16[2048,1024]{1,0:T(8,128)(2,1)} %copy-done.3) | copy-start | bytes 12582916
  116.6 13.4 %copy-start.18 = (f32[2,256,1]{2,1,0:T(8,128)S(1)}, f32[2,256,1]{2,1,0:T(8,128)}, u32[]{:S(2)}) copy-start(f32[2,256,1]{2,1,0:T(8,128)} %copy-done.16) | copy-start | bytes 6148
  128.4 2.2 copy-start.2
  155.4 100.0 %reduce-scatter.3.cloned.1.call-start = ((), (), s32[]{:S(2)}) async-start(), calls=%async_computation.2 | async-start | bytes 4718592 | tf_op jit(solution)/shard_map/reduce_scatter | solution.py:490
  205.0 1.0 copy-start.19
  209.6 51.5 %collective-permute-start.14 = (bf16[256,1024]{1,0:T(8,128)(2,1)S(1)}, bf16[256,1024]{1,0:T(8,128)(2,1)S(1)}, u32[]{:S(2)}, u32[]{:S(2)}) collective-permute-start(bf16[256,1024]{1,0:T(8,128)(2,1)S(1)} %get-tuple-element.95), channel_id=1, source_target_pairs={{0,24},{8,16},{16,8},{24,0},{1,25},{9,17},{17,9},{25,1},{2,26},{10... | collective-permute-start | bytes 1572872 | tf_op jit(solution)/shard_map/ppermute | solution.py:497
  255.4 1.0 copy-start.20
  258.7 12.4 %collective-permute-start.13 = (bf16[128,2048]{1,0:T(8,128)(2,1)S(1)}, bf16[128,2048]{1,0:T(8,128)(2,1)S(1)}, u32[]{:S(2)}, u32[]{:S(2)}) collective-permute-start(bf16[128,2048]{1,0:T(8,128)(2,1)S(1)} %get-tuple-element.90), channel_id=1, source_target_pairs={{0,24},{8,16},{16,8},{24,0},{1,25},{9,17},{17,9},{25,1},{2,26},{10... | collective-permute-start | bytes 1572872 | tf_op jit(solution)/shard_map/ppermute | solution.py:497
Sparse Core Ops, SparseCore 0:
  155.5 49.3 reduce-scatter.4
  207.3 48.1 reduce-scatter.2

commit v5 on v4

--- a/solution.py
+++ b/solution.py
@@ -35,14 +35,14 @@
     return lax.dot_general(left, right, (over, ((), ())), preferred_element_type=f32)
 
 
-def tile_of(width):
-    return min(512, width)
+def tile_of(width, most=512):
+    return min(most, width)
 
 
 def forward(per, inputs, w_up, w_down, info, plan, previous, after, places, resident):
     _, _, micro, tokens, model = inputs.shape
     width = w_up.shape[3]
-    tile = tile_of(width)
+    tile = tile_of(width, 256)
     groups, rows, every = micro // per, per * tokens, micro * tokens
 
     def body(info_ref, plan_ref, *refs):
@@ -134,7 +134,7 @@
         ),
         out_shape=out_shape,
         input_output_aliases=aliases,
-        compiler_params=params(30),
+        compiler_params=params(20),
         cost_estimate=pl.CostEstimate(
             flops=8 * every * model * width, bytes_accessed=4 * model * width, transcendentals=0
         ),
@@ -243,7 +243,7 @@
             pltpu.HBM((groups + 1, rows, model), bf16),
         ],
         input_output_aliases=aliases,
-        compiler_params=params(20),
+        compiler_params=params(16),
         cost_estimate=pl.CostEstimate(
             flops=8 * rows * model * width, bytes_accessed=4 * model * width, transcendentals=0
         ),
@@ -299,7 +299,7 @@
             pltpu.HBM((groups, rows, width), bf16),
             pltpu.HBM((groups, rows, model), bf16),
         ],
-        compiler_params=params(28),
+        compiler_params=params(20),
         cost_estimate=pl.CostEstimate(
             flops=4 * groups * rows * model * width,
             bytes_accessed=2 * model * width,
@@ -316,47 +316,79 @@
     )
 
 
-def weight_gradient(left_a, right_a, left_b, right_b, groups, split_left, after):
+def weight_gradient(core, left_a, right_a, left_b, right_b, groups, replicas, split_left, came):
     tokens = right_a.shape[-2]
-    rows, columns = left_a.shape[-1], right_a.shape[-1]
-    tile = tile_of(rows if split_left else columns)
-
-    def body(la_ref, ra_ref, lb_ref, rb_ref, *rest):
+    rows, columns = left_a.shape[-1] // replicas, right_a.shape[-1]
+    lines = replicas // 2
+    tile = columns if split_left else tile_of(columns)
+    steps = lines if split_left else columns // tile
+    lefts = 1 if split_left else lines
+    pair = rows % 128 != 0
+    wide = 2 * rows if pair else rows
+
+    def place(z, i):
+        return z if pair else 2 * z + i[0]
+
+    def body(info, *refs):
         def flat(ref):
             return ref[...].reshape(-1, ref.shape[-1])
 
-        total = dot(flat(la_ref), flat(ra_ref), ((0,), (0,)))
-        total += dot(flat(lb_ref), flat(rb_ref), ((0,), (0,)))
-        rest[-1][...] = total.astype(bf16)
-
-    def spec(array, split):
+        def product(left_refs, right_ref):
+            left = [flat(ref) for ref in left_refs]
+            if pair:
+                left = [jnp.where(info[0] == 0, x[:, :rows], x[:, rows:]) for x in left]
+            left = left[0] if len(left) == 1 else jnp.concatenate(left, axis=1)
+            return dot(left, flat(right_ref), ((0,), (0,)))
+
+        total = product(refs[:lefts], refs[lefts])
+        total += product(refs[lefts + 1 : 2 * lefts + 1], refs[2 * lefts + 1])
+        total = total.reshape(lefts, rows, tile)
+        if came is not None:
+            total += refs[2 * lefts + 2][...].astype(f32)
+        refs[-1][...] = total.astype(bf16)
+
+    def left_specs(array):
         lead = array.ndim - 3
-        block = (1,) * lead + (groups, tokens, tile if split else array.shape[-1])
-        if split:
-            return pl.BlockSpec(block, lambda j: (0,) * (lead + 2) + (j,))
-        return pl.BlockSpec(block, lambda j: (0,) * (lead + 3))
-
-    out_block = (tile, columns) if split_left else (rows, tile)
+        block = (1,) * lead + (groups, tokens, wide)
+        if split_left:
+            return [pl.BlockSpec(block, lambda j, i: (0,) * (lead + 2) + (place(j, i),))]
+        return [
+            pl.BlockSpec(block, lambda j, i, z=z: (0,) * (lead + 2) + (place(z, i),))
+            for z in range(lines)
+        ]
+
+    def right_spec(array):
+        lead = array.ndim - 3
+        block = (1,) * lead + (groups, tokens, tile)
+        if split_left:
+            return pl.BlockSpec(block, lambda j, i: (0,) * (lead + 3))
+        return pl.BlockSpec(block, lambda j, i: (0,) * (lead + 2) + (j,))
+
+    if split_left:
+        out_spec = pl.BlockSpec((1, rows, tile), lambda j, i: (j, 0, 0))
+    else:
+        out_spec = pl.BlockSpec((lines, rows, tile), lambda j, i: (0, 0, j))
+    operands = [in_hbm(left_a)] * lefts + [in_hbm(right_a)]
+    operands += [in_hbm(left_b)] * lefts + [in_hbm(right_b)]
+    in_specs = left_specs(left_a) + [right_spec(right_a)]
+    in_specs += left_specs(left_b) + [right_spec(right_b)]
+    if came is not None:
+        operands.append(came)
+        in_specs.append(out_spec)
     return pl.pallas_call(
         body,
-        grid=((rows if split_left else columns) // tile,),
-        in_specs=[
-            spec(left_a, split_left),
-            spec(right_a, not split_left),
-            spec(left_b, split_left),
-            spec(right_b, not split_left),
-        ]
-        + [any_space] * len(after),
-        out_specs=pl.BlockSpec(out_block, (lambda j: (j, 0)) if split_left else (lambda j: (0, j))),
-        out_shape=pltpu.HBM((rows, columns), bf16),
-        compiler_params=params(32),
+        grid_spec=pltpu.PrefetchScalarGridSpec(
+            num_scalar_prefetch=1, grid=(steps,), in_specs=in_specs, out_specs=out_spec
+        ),
+        out_shape=jax.ShapeDtypeStruct((lines, rows, columns), bf16),
+        compiler_params=params(28),
         cost_estimate=pl.CostEstimate(
-            flops=4 * groups * tokens * rows * columns,
-            bytes_accessed=2 * rows * columns,
+            flops=4 * groups * tokens * rows * lines * columns,
+            bytes_accessed=2 * rows * lines * columns,
             transcendentals=0,
         ),
         name="weights",
-    )(*[in_hbm(x) for x in (left_a, right_a, left_b, right_b)], *[in_hbm(x) for x in after])
+    )(core, *operands)
 
 
 def update(replica, weight, moment, total):
@@ -446,20 +478,20 @@
         order = [blocks[0]]
 
     run_forward(0, [])
-    late = []
     received = {}
     arrived = {}
     kept = None
     for call, (stage, group) in enumerate(calls):
         if stage == last and group == 0:
             *home_blocks, slopes, ys, rs = forward(
-                per, mirrored, up_weight, down_weight, home_kind, plan, None, order + late, 1, False
+                per, mirrored, up_weight, down_weight, home_kind, plan, None, order, 1, False
             )
             saved_home = (slopes, ys, rs)
             order = [home_blocks[0]]
         recv = received.pop((stage, group), None)
+        asked = [arrived[(last - 1, 1)]] if (stage, group) == (half, 0) and groups > 1 else []
         out, *kept = chain_step(
-            call, group, table, recv, top_grad, saved[int(stage >= half)], kept, order
+            call, group, table, recv, top_grad, saved[int(stage >= half)], kept, order + asked
         )
         order = [kept[0]]
         pairs = [(last - stage, last - stage - 1)] if stage < last else []
@@ -469,12 +501,10 @@
         if got is not None:
             received[(stage + 1, group)] = got
         if stage < last:
-            got = hop(out, [(stage, last - 1 - stage)])
-            arrived[(last - 1 - stage, group)] = got
-            if stage < half:
-                late.append(got)
+            to = last - 1 - stage
+            arrived[(to, group)] = out if to == stage else hop(out, [(stage, to)])
         if saved[1] is None and group == groups - 1:
-            run_forward(1, order + [mirrored[0, 0]])
+            run_forward(1, order + [mirrored[0, 0], arrived[(last - 1, 0)]])
 
     came = []
     for group in range(groups):
@@ -486,10 +516,27 @@
         (position == last).astype(jnp.int32)[None], came, top_grad, saved_home, down_weight, order
     )
 
-    up_part = weight_gradient(blocks[0], kept[0], home_blocks[0], home_pre, groups, False, [])
-    up_sum = lax.psum_scatter(up_part, "dp", scatter_dimension=0, tiled=True)
-    down_part = weight_gradient(blocks[1], kept[1], home_blocks[1], home_sum, groups, True, [])
-    down_sum = lax.psum_scatter(down_part, "dp", scatter_dimension=0, tiled=True)
+    replicas = lax.axis_size("dp")
+    core = (lax.axis_index("dp") % 2).astype(jnp.int32)[None]
+    swap = [(i, i ^ 1) for i in range(replicas)]
+    along = [list(range(c, replicas, 2)) for c in range(2)]
+    sources = (
+        (blocks[1], kept[1], home_blocks[1], home_sum, groups, replicas, True),
+        (blocks[0], kept[0], home_blocks[0], home_pre, groups, replicas, False),
+    )
+    came = [lax.ppermute(weight_gradient(1 - core, *x, None), "dp", swap) for x in sources]
+
+    def summed(x, other):
+        part = weight_gradient(core, *x, other)
+        return lax.psum_scatter(
+            part.reshape(-1, part.shape[-1]),
+            "dp",
+            scatter_dimension=0,
+            axis_index_groups=along,
+            tiled=True,
+        )
+
+    down_sum, up_sum = [summed(x, other) for x, other in zip(sources, came)]
     replica = lax.axis_index("dp").astype(jnp.int32)[None]
 
     def finish(weight, moment, total):

time: 280 us -> 289 us (1.032)
  Pallas kernels: 101 us -> 115 us
  starting transfers between devices: 29.9 us -> 23.2 us
    reduce_scatter x2, waiting for transfers between devices: 84.4 us -> 68 us  [summed(): lax.psum_scatter(part.reshape(-1, part.shape[-1]), 'dp', scatter_dimensio...]
    pallas_call x3, Pallas kernels: 36.6 us -> 45.1 us  [forward(): pl.pallas_call(body, grid_spec=pltpu.PrefetchScalarGridSpec(num_scalar_pr...]
    ppermute x12 -> x10, waiting for transfers between devices: 14.1 us -> 22.3 us  [hop(): return lax.ppermute(value, 'section', pairs) if pairs else None]
    ppermute x0 -> x2, waiting for transfers between devices: none -> 8.16 us  [on_device(): lax.ppermute(weight_gradient(1 - core, *x, None), 'dp', swap)]
    ppermute x12 -> x10, starting transfers between devices: 21.2 us -> 14.2 us  [hop(): return lax.ppermute(value, 'section', pairs) if pairs else None]
    pallas_call x2 -> x4, Pallas kernels: 17 us -> 22.6 us  [weight_gradient(): pl.pallas_call(body, grid_spec=pltpu.PrefetchScalarGridSpec(num_scalar_pr...]
    unnamed x50 -> x58, local copies, waits for them, and re-layouts: 19.9 us -> 20.8 us
  transfers between devices with their start and end apart: 17 -> 17, of which waited for: 6 -> 6; matrix products, arithmetic and copies ran while one was open for 1% -> 1% of each run, Pallas kernels for 29% -> 32%
where the time goes in v5:
time: 289 us; the launch traced here: 288 us
  Pallas kernels  115 us (40%)
  waiting for transfers between devices  109 us (38%)
  local copies, waits for them, and re-layouts  23.2 us (8%)
  starting transfers between devices  23.2 us (8%)
  between operations  14.4 us (5%)
    reduce_scatter x2, waiting for transfers between devices, summed(): lax.psum_scatter(part.reshape(-1, part.shape[-1]), 'dp', scatter_dimensio...  68 us
    pallas_call x3, Pallas kernels, forward(): pl.pallas_call(body, grid_spec=pltpu.PrefetchScalarGridSpec(num_scalar_pr...  45.1 us
    pallas_call x8, Pallas kernels, chain_step(): pl.pallas_call(body, grid_spec=pltpu.PrefetchScalarGridSpec(num_scalar_pr...  34.1 us
    pallas_call x4, Pallas kernels, weight_gradient(): pl.pallas_call(body, grid_spec=pltpu.PrefetchScalarGridSpec(num_scalar_pr...  22.6 us
    ppermute x10, waiting for transfers between devices, hop(): return lax.ppermute(value, 'section', pairs) if pairs else None  22.3 us
    unnamed x58, local copies, waits for them, and re-layouts  20.8 us
    ppermute x10, starting transfers between devices, hop(): return lax.ppermute(value, 'section', pairs) if pairs else None  14.2 us
    ppermute x2, waiting for transfers between devices, finish(): lax.ppermute(fresh, 'section', [(i, last - i) for i in range(sections)])  11 us
  transfers between devices with their start and end apart: 17, of which 6 were waited for; matrix products, arithmetic and copies ran while one was open for 1% of the time, Pallas kernels for 32%

profile of v5, /device:TPU:0, one launch (start us, length us, event | category | flops | bytes accessed | tf_op | source)
XLA Modules:
  0.0 287.6 jit_solution(13551550976166752705)
XLA Ops:
  7.3 2.3 slice_bitcast_fusion
  9.5 3.9 %collective-permute-start = (bf16[4,128,1024]{2,1,0:T(8,128)(2,1)}, bf16[4,128,1024]{2,1,0:T(8,128)(2,1)}, u32[]{:S(2)}, u32[]{:S(2)}) collective-permute-start(bf16[4,128,1024]{2,1,0:T(8,128)(2,1)} %slice_bitcast_fusion), channel_id=1, source_target_pairs={{0,24},{8,16},{16,8},{24,0},{1,25},{9,17},{17,9},{25,1},{2,26},{10... | collective-permute-start | bytes 3145736 | tf_op jit(solution)/shard_map/ppermute | solution.py:443
  13.5 15.1 %forward.3 = (bf16[2,2,256,1024]{3,2,1,0:T(8,128)(2,1)}, bf16[2,2,256,2048]{3,2,1,0:T(8,128)(2,1)}, bf16[2,256,2048]{2,1,0:T(8,128)(2,1)S(1)}, bf16[2,256,1024]{...) custom-call(s32[4]{0:T(128)S(1)} %stack.54.info_ref, ...), custom_call_target="tpu_custom_call" | custom-call | flops 8589934592 | bytes 8388608 | tf_op jit(solution)/shard_map/forward/pallas_call | solution.py:126
  28.6 2.1 copy-done.6
  30.6 1.9 copy-done.9
  32.8 3.1 %copy-done.7 = bf16[1024,2048]{1,0:T(8,128)(2,1)S(1)} copy-done((bf16[1024,2048]{1,0:T(8,128)(2,1)S(1)}, bf16[1024,2048]{1,0:T(8,128)(2,1)}, u32[]{:S(2)}) %copy-start.7) | copy-done | bytes 4194328
  35.9 2.2 copy-done.10
  38.1 7.7 %chain.8 = (bf16[256,1024]{1,0:T(8,128)(2,1)S(1)}, bf16[3,256,2048]{2,1,0:T(8,128)(2,1)}, bf16[3,256,1024]{2,1,0:T(8,128)(2,1)}) custom-call(s32[32]{0:T(128)S(1)} %reshape.21.info, bf16[2,4,128,1024]{3,2,1,0:T(8,128)(2,1)} %refs_2_.5, bf16[2,256,1024]{2,1,0:T(8,128)(2,1)S(1)} %get-tuple-element.53.y_ref, f32[2,256,1]{2,1,0:T(8,128)S(1)} %get-tuple-element.54.r_ref, ...), custom_call_target="tpu_custom_call" | custom-call | flops 4294967296 | bytes 8388608 | tf_op jit(solution)/shard_map/chain/pallas_call | solution.py:223
  45.8 1.3 collective-permute-start.1
  47.1 1.3 collective-permute-start.3
  48.5 7.9 %chain.9 = (bf16[256,1024]{1,0:T(8,128)(2,1)}, bf16[3,256,2048]{2,1,0:T(8,128)(2,1)}, bf16[3,256,1024]{2,1,0:T(8,128)(2,1)}) custom-call(s32[32]{0:T(128)S(1)} %reshape.21.info, bf16[2,4,128,1024]{3,2,1,0:T(8,128)(2,1)} %refs_2_.5, bf16[2,256,1024]{2,1,0:T(8,128)(2,1)S(1)} %get-tuple-element.53.y_ref, ...), custom_call_target="tpu_custom_call", output_to_operand_aliasing={{1}: (7, {}), {2}: (8, {})} | custom-call | flops 4294967296 | bytes 8388608 | tf_op jit(solution)/shard_map/chain/pallas_call | solution.py:223
  56.4 1.3 collective-permute-start.2
  57.7 2.1 collective-permute-start.6
  59.9 15.7 %forward.4 = (bf16[2,2,256,1024]{3,2,1,0:T(8,128)(2,1)}, bf16[2,2,256,2048]{3,2,1,0:T(8,128)(2,1)}, bf16[2,256,2048]{2,1,0:T(8,128)(2,1)S(1)}, bf16[2,256,1024]{...) custom-call(s32[4]{0:T(128)S(1)} %stack.53.info_ref, ...), custom_call_target="tpu_custom_call", output_to_operand_aliasing={{0}: (8, {}), {1}: (9, {})} | custom-call | flops 8589934592 | bytes 8388608 | tf_op jit(solution)/shard_map/forward/pallas_call | solution.py:126
  75.6 2.0 copy-done
  77.6 2.0 copy-done.3
  79.6 2.0 chain.10
  81.6 1.5 collective-permute-start.5
  83.1 2.0 chain.11
  85.0 1.5 collective-permute-start.4
  86.6 2.2 copy-done.1
  88.8 2.2 copy-done.4
  91.9 2.6 chain.12
  94.5 1.3 collective-permute-start.9
  95.8 1.3 collective-permute-start.8
  97.2 2.6 chain.13
  99.8 1.3 collective-permute-start.10
  101.1 1.3 collective-permute-start.7
  102.4 14.4 %forward.5 = (bf16[1,2,256,1024]{3,2,1,0:T(8,128)(2,1)}, bf16[1,2,256,2048]{3,2,1,0:T(8,128)(2,1)}, bf16[2,256,2048]{2,1,0:T(8,128)(2,1)S(1)}, bf16[2,256,1024]{2,1,0:T(8,128)(2,1)S(1)}, f32[2,256,1]{2,1,0:T(8,128)S(1)}) custom-call(s32[4]{0:T(128)S(1)} %copy-done.24, s32[2,4]{1,0:T(2,128)S(1)} %copy-done.23, ...), custom_call_target="tpu_custom_call" | custom-call | flops 8589934592 | bytes 8388608 | tf_op jit(solution)/shard_map/forward/pallas_call | solution.py:126
  116.8 22.3 %collective-permute-done.10 = bf16[256,1024]{1,0:T(8,128)(2,1)S(1)} collective-permute-done((bf16[256,1024]{1,0:T(8,128)(2,1)S(1)}, bf16[256,1024]{1,0:T(8,128)(2,1)S(1)}, u32[]{:S(2)}, u32[]{:S(2)}) %collective-permute-start.10) | collective-permute-done | bytes 524320 | tf_op jit(solution)/shard_map/ppermute | solution.py:441
  139.5 4.6 %chain.14 = (bf16[256,1024]{1,0:T(8,128)(2,1)}, bf16[3,256,2048]{2,1,0:T(8,128)(2,1)}, bf16[3,256,1024]{2,1,0:T(8,128)(2,1)}) custom-call(s32[32]{0:T(128)S(1)} %reshape.21.info, bf16[256,1024]{1,0:T(8,128)(2,1)S(1)} %collective-permute-done.8.e_ref, ...), custom_call_target="tpu_custom_call", output_to_operand_aliasing={{1}: (7, {}), {2}: (8, {})} | custom-call | flops 4294967296 | bytes 8388608 | tf_op jit(solution)/shard_map/chain/pallas_call | solution.py:223
  144.1 4.6 %chain.15 = (bf16[256,1024]{1,0:T(8,128)(2,1)}, bf16[3,256,2048]{2,1,0:T(8,128)(2,1)}, bf16[3,256,1024]{2,1,0:T(8,128)(2,1)}) custom-call(s32[32]{0:T(128)S(1)} %reshape.21.info, bf16[256,1024]{1,0:T(8,128)(2,1)S(1)} %collective-permute-done.7.e_ref, ...), custom_call_target="tpu_custom_call", output_to_operand_aliasing={{1}: (7, {}), {2}: (8, {})} | custom-call | flops 4294967296 | bytes 8388608 | tf_op jit(solution)/shard_map/chain/pallas_call | solution.py:223
  148.7 7.2 %home.1 = (bf16[2,256,2048]{2,1,0:T(8,128)(2,1)}, bf16[2,256,1024]{2,1,0:T(8,128)(2,1)}) custom-call(s32[1]{0:T(128)} %bitcast.8.info, bf16[256,1024]{1,0:T(8,128)(2,1)S(1)} %select_select_fusion.1.refs_0_, bf16[256,1024]{1,0:T(8,128)(2,1)S(1)} %select_select_fusion.refs_1_, bf16[2,4,128,1024]{3,2,1,0:T(8,128)(2,1)} %refs_2_.5, ...), custom_call_target="tpu_custom_call" | custom-call | flops 4294967296 | bytes 4194304 | tf_op jit(solution)/shard_map/home/pallas_call | solution.py:279
  155.9 5.0 %weights.6 = bf16[4,256,1024]{2,1,0:T(8,128)(2,1)S(1)} custom-call(s32[1]{0:T(128)S(6)} %sub.12.info, bf16[2,2,256,2048]{3,2,1,0:T(8,128)(2,1)} %get-tuple-element.91.refs_0_, bf16[3,256,1024]{2,1,0:T(8,128)(2,1)} %get-tuple-element.92.refs_1_, bf16[1,2,256,2048]{3,2,1,0:T(8,128)(2,1)} %get-tuple-element.93.refs_2_, ...), custom_call_target="tpu_custom_call" | custom-call | flops 2147483648 | bytes 2097152 | tf_op jit(solution)/shard_map/weights/pallas_call | solution.py:378
  161.1 4.1 %collective-permute-done.13.refs_4_ = bf16[4,256,1024]{2,1,0:T(8,128)(2,1)S(1)} collective-permute-done((bf16[4,256,1024]{2,1,0:T(8,128)(2,1)S(1)}, bf16[4,256,1024]{2,1,0:T(8,128)(2,1)S(1)}, u32[]{:S(2)}, u32[]{:S(2)}) %collective-permute-start.13) | collective-permute-done | bytes 2097184 | tf_op jit(solution)/shard_map/ppermute | solution.py:527
  165.2 6.1 %weights.7 = bf16[4,256,1024]{2,1,0:T(8,128)(2,1)} custom-call(s32[1]{0:T(128)} %bitcast.1.info, bf16[2,2,256,2048]{3,2,1,0:T(8,128)(2,1)} %get-tuple-element.91.refs_0_, bf16[3,256,1024]{2,1,0:T(8,128)(2,1)} %get-tuple-element.92.refs_1_, bf16[1,2,256,2048]{3,2,1,0:T(8,128)(2,1)} %get-tuple-element.93.refs_2_, ...), custom_call_target="tpu_custom_call" | custom-call | flops 2147483648 | bytes 2097152 | tf_op jit(solution)/shard_map/weights/pallas_call | solution.py:378
  171.4 5.3 %weights.4 = bf16[4,128,2048]{2,1,0:T(8,128)(2,1)S(1)} custom-call(s32[1]{0:T(128)S(6)} %sub.12.info, bf16[2,2,256,1024]{3,2,1,0:T(8,128)(2,1)} %get-tuple-element.62.rest_2_.refs_0_.refs_1_.refs_2_.refs_3_, bf16[2,2,256,1024]{3,2,1,0:T(8,128)(2,1)} %get-tuple-element.62.rest_2_.refs_0_.refs_1_.refs_2_.refs_3_, ...), custom_call_target="tpu_custom_call" | custom-call | flops 2147483648 | bytes 2097152 | tf_op jit(solution)/shard_map/weights/pallas_call | solution.py:378
  176.9 4.0 %collective-permute-done.11.refs_10_ = bf16[4,128,2048]{2,1,0:T(8,128)(2,1)S(1)} collective-permute-done((bf16[4,128,2048]{2,1,0:T(8,128)(2,1)S(1)}, bf16[4,128,2048]{2,1,0:T(8,128)(2,1)S(1)}, u32[]{:S(2)}, u32[]{:S(2)}) %collective-permute-start.11) | collective-permute-done | bytes 2097184 | tf_op jit(solution)/shard_map/ppermute | solution.py:527
  180.9 6.2 %weights.5 = bf16[4,128,2048]{2,1,0:T(8,128)(2,1)} custom-call(s32[1]{0:T(128)} %bitcast.1.info, bf16[2,2,256,1024]{3,2,1,0:T(8,128)(2,1)} %get-tuple-element.62.rest_2_.refs_0_.refs_1_.refs_2_.refs_3_, bf16[2,2,256,1024]{3,2,1,0:T(8,128)(2,1)} %get-tuple-element.62.rest_2_.refs_0_.refs_1_.refs_2_.refs_3_, ...), custom_call_target="tpu_custom_call" | custom-call | flops 2147483648 | bytes 2097152 | tf_op jit(solution)/shard_map/weights/pallas_call | solution.py:378
  187.1 29.3 %reduce-scatter.5.cloned.1.call-done.total_ref = bf16[256,1024]{1,0:T(8,128)(2,1)} async-done(((bf16[1024,1024]{1,0:T(8,128)(2,1)}), bf16[256,1024]{1,0:T(8,128)(2,1)}) %reduce-scatter.5.cloned.1.call-update) | async-done | bytes 524304 | tf_op jit(solution)/shard_map/reduce_scatter | solution.py:531
  217.5 3.5 %update.3 = (bf16[256,1024]{1,0:T(8,128)(2,1)S(1)}, f32[1,256,1024]{2,1,0:T(8,128)}) custom-call(s32[1]{0:T(128)} %bitcast.info, bf16[2,1,2048,1024]{3,2,1,0:T(8,128)(2,1)} %weight_ref.3, f32[1,256,1024]{2,1,0:T(8,128)} %moment_ref.3, bf16[256,1024]{1,0:T(8,128)(2,1)S(1)} %copy-done.21), custom_call_target="tpu_custom_call" | custom-call | flops 1048576 | bytes 3145728 | tf_op jit(solution)/shard_map/update/pallas_call | solution.py:404
  221.0 2.4 collective-permute-start.14
  223.4 38.7 %reduce-scatter.3.cloned.1.call-done.total_ref = bf16[128,2048]{1,0:T(8,128)(2,1)} async-done(((bf16[512,2048]{1,0:T(8,128)(2,1)}), bf16[128,2048]{1,0:T(8,128)(2,1)}) %reduce-scatter.3.cloned.1.call-update) | async-done | bytes 524304 | tf_op jit(solution)/shard_map/reduce_scatter | solution.py:531
  263.1 2.2 update.2
  265.3 2.4 collective-permute-start.12
  267.7 1.1 maximum_bitcast_fusion.1
  268.8 11.0 %collective-permute-done.12 = bf16[128,2048]{1,0:T(8,128)(2,1)S(1)} collective-permute-done((bf16[128,2048]{1,0:T(8,128)(2,1)S(1)}, bf16[128,2048]{1,0:T(8,128)(2,1)S(1)}, u32[]{:S(2)}, u32[]{:S(2)}) %collective-permute-start.12) | collective-permute-done | bytes 524320 | tf_op jit(solution)/shard_map/ppermute | solution.py:544
  279.7 1.1 maximum_bitcast_fusion
  (77 shorter events, 4.1 us)
Async XLA Ops:
  7.2 6.3 %copy-start.25 = (pred[8]{0:T(512)(128)(4,1)S(1)}, pred[8]{0:T(512)(128)(4,1)}, u32[]{:S(2)}) copy-start(pred[8]{0:T(512)(128)(4,1)} %constant.38.clone) | copy-start | bytes 28
  7.2 6.2 %copy-start.27 = (s32[8]{0:T(128)S(1)}, s32[8]{0:T(128)}, u32[]{:S(2)}) copy-start(s32[8]{0:T(128)} %constant.39.clone) | copy-start | bytes 100
  7.2 6.2 %copy-start.26 = (s32[8]{0:T(128)S(1)}, s32[8]{0:T(128)}, u32[]{:S(2)}) copy-start(s32[8]{0:T(128)} %constant.40.clone) | copy-start | bytes 100
  7.2 6.3 %copy-start.23 = (s32[2,4]{1,0:T(2,128)S(1)}, s32[2,4]{1,0:T(2,128)}, u32[]{:S(2)}) copy-start(s32[2,4]{1,0:T(2,128)} %plan_ref.5) | copy-start | bytes 100
  7.2 209.2 %reduce-scatter.5.cloned.1.call-start = ((), (), s32[]{:S(2)}) async-start(), calls=%async_computation.3 | async-start | bytes 2621440 | tf_op jit(solution)/shard_map/reduce_scatter | solution.py:531
  9.5 50.3 %collective-permute-start = (bf16[4,128,1024]{2,1,0:T(8,128)(2,1)}, bf16[4,128,1024]{2,1,0:T(8,128)(2,1)}, u32[]{:S(2)}, u32[]{:S(2)}) collective-permute-start(bf16[4,128,1024]{2,1,0:T(8,128)(2,1)} %slice_bitcast_fusion), channel_id=1, source_target_pairs={{0,24},{8,16},{16,8},{24,0},{1,25},{9,17},{17,9},{25,1},{2,26},{10... | collective-permute-start | bytes 3145736 | tf_op jit(solution)/shard_map/ppermute | solution.py:443
  13.5 19.1 %copy-start.28 = (pred[8]{0:T(512)(128)(4,1)S(1)}, pred[8]{0:T(512)(128)(4,1)}, u32[]{:S(2)}) copy-start(pred[8]{0:T(512)(128)(4,1)} %constant.41.clone) | copy-start | bytes 28
  28.6 2.1 copy-start.6
  30.6 1.9 copy-start.9
  32.6 15.9 %copy-start.12 = (bf16[2,256,2048]{2,1,0:T(8,128)(2,1)}, bf16[2,256,2048]{2,1,0:T(8,128)(2,1)S(1)}, u32[]{:S(2)}) copy-start(bf16[2,256,2048]{2,1,0:T(8,128)(2,1)S(1)} %get-tuple-element.55.slope_ref) | copy-start | bytes 6291460
  32.6 15.9 %copy-start.14 = (bf16[2,256,1024]{2,1,0:T(8,128)(2,1)}, bf16[2,256,1024]{2,1,0:T(8,128)(2,1)S(1)}, u32[]{:S(2)}) copy-start(bf16[2,256,1024]{2,1,0:T(8,128)(2,1)S(1)} %get-tuple-element.53.y_ref) | copy-start | bytes 3145732
  32.8 3.1 %copy-start.7 = (bf16[1024,2048]{1,0:T(8,128)(2,1)S(1)}, bf16[1024,2048]{1,0:T(8,128)(2,1)}, u32[]{:S(2)}) copy-start(bf16[1024,2048]{1,0:T(8,128)(2,1)} %copy-done.6) | copy-start | bytes 12582916
  35.9 2.2 copy-start.10
  45.8 14.0 %collective-permute-start.1 = (bf16[256,1024]{1,0:T(8,128)(2,1)S(1)}, bf16[256,1024]{1,0:T(8,128)(2,1)S(1)}, u32[]{:S(2)}, u32[]{:S(2)}) collective-permute-start(bf16[256,1024]{1,0:T(8,128)(2,1)S(1)} %get-tuple-element.61), channel_id=1, source_target_pairs={{0,16},{1,17},{2,18},{3,19},{4,20},{5,21},{6,22},{7,23}} | collective-permute-start | bytes 1572872 | tf_op jit(solution)/shard_map/ppermute | solution.py:441
  47.1 32.4 %collective-permute-start.3 = (bf16[256,1024]{1,0:T(8,128)(2,1)S(1)}, bf16[256,1024]{1,0:T(8,128)(2,1)S(1)}, u32[]{:S(2)}, u32[]{:S(2)}) collective-permute-start(bf16[256,1024]{1,0:T(8,128)(2,1)S(1)} %get-tuple-element.61), channel_id=1, source_target_pairs={{24,16},{0,8},{25,17},{1,9},{26,18},{2,10},{27,19},{3,11},{28,20},... | collective-permute-start | bytes 1572872 | tf_op jit(solution)/shard_map/ppermute | solution.py:441
  56.4 26.7 %collective-permute-start.2 = (bf16[256,1024]{1,0:T(8,128)(2,1)}, bf16[256,1024]{1,0:T(8,128)(2,1)S(1)}, u32[]{:S(2)}, u32[]{:S(2)}) collective-permute-start(bf16[256,1024]{1,0:T(8,128)(2,1)} %get-tuple-element.63), channel_id=1, source_target_pairs={{24,16},{0,8},{25,17},{1,9},{26,18},{2,10},{27,19},{3,11},{28,20},... | collective-permute-start | bytes 1572872 | tf_op jit(solution)/shard_map/ppermute | solution.py:441
  57.7 28.9 %collective-permute-start.6 = (bf16[256,1024]{1,0:T(8,128)(2,1)}, bf16[256,1024]{1,0:T(8,128)(2,1)}, u32[]{:S(2)}, u32[]{:S(2)}) collective-permute-start(bf16[256,1024]{1,0:T(8,128)(2,1)} %get-tuple-element.63), channel_id=1, source_target_pairs={{0,16},{1,17},{2,18},{3,19},{4,20},{5,21},{6,22},{7,23}} | collective-permute-start | bytes 1572872 | tf_op jit(solution)/shard_map/ppermute | solution.py:441
  59.8 15.8 %copy-start.19 = (bf16[256,1024]{1,0:T(8,128)(2,1)}, bf16[256,1024]{1,0:T(8,128)(2,1)S(1)}, u32[]{:S(2)}) copy-start(bf16[256,1024]{1,0:T(8,128)(2,1)S(1)} %collective-permute-done.1.refs_10_) | copy-start | bytes 1572868
  59.8 19.8 %copy-start.8 = (bf16[1024,2048]{1,0:T(8,128)(2,1)S(1)}, bf16[1024,2048]{1,0:T(8,128)(2,1)}, u32[]{:S(2)}) copy-start(bf16[1024,2048]{1,0:T(8,128)(2,1)} %copy-done.6) | copy-start | bytes 12582916
  59.8 19.8 %copy-start.11 = (bf16[2048,1024]{1,0:T(8,128)(2,1)S(1)}, bf16[2048,1024]{1,0:T(8,128)(2,1)}, u32[]{:S(2)}) copy-start(bf16[2048,1024]{1,0:T(8,128)(2,1)} %copy-done.9) | copy-start | bytes 12582916
  59.8 19.8 %copy-start.13 = (bf16[2,256,2048]{2,1,0:T(8,128)(2,1)S(1)}, bf16[2,256,2048]{2,1,0:T(8,128)(2,1)}, u32[]{:S(2)}) copy-start(bf16[2,256,2048]{2,1,0:T(8,128)(2,1)} %copy-done.12) | copy-start | bytes 6291460
  59.8 19.8 %copy-start.15 = (bf16[2,256,1024]{2,1,0:T(8,128)(2,1)S(1)}, bf16[2,256,1024]{2,1,0:T(8,128)(2,1)}, u32[]{:S(2)}) copy-start(bf16[2,256,1024]{2,1,0:T(8,128)(2,1)} %copy-done.14) | copy-start | bytes 3145732
  75.6 2.0 copy-start
  77.6 2.0 copy-start.3
  79.6 2.0 copy-start.16
  81.6 5.0 %collective-permute-start.5 = (bf16[256,1024]{1,0:T(8,128)(2,1)}, bf16[256,1024]{1,0:T(8,128)(2,1)}, u32[]{:S(2)}, u32[]{:S(2)}) collective-permute-start(bf16[256,1024]{1,0:T(8,128)(2,1)} %get-tuple-element.73), channel_id=1, source_target_pairs={{16,8},{8,16},{17,9},{9,17},{18,10},{10,18},{19,11},{11,19},{20,12... | collective-permute-start | bytes 1572872 | tf_op jit(solution)/shard_map/ppermute | solution.py:441
  85.0 12.1 %collective-permute-start.4 = (bf16[256,1024]{1,0:T(8,128)(2,1)}, bf16[256,1024]{1,0:T(8,128)(2,1)}, u32[]{:S(2)}, u32[]{:S(2)}) collective-permute-start(bf16[256,1024]{1,0:T(8,128)(2,1)} %get-tuple-element.67), channel_id=1, source_target_pairs={{16,8},{8,16},{17,9},{9,17},{18,10},{10,18},{19,11},{11,19},{20,12... | collective-permute-start | bytes 1572872 | tf_op jit(solution)/shard_map/ppermute | solution.py:441
  86.6 2.2 copy-start.1
  88.8 2.2 copy-start.4
  91.0 0.9 copy-start.17
  94.5 44.7 %collective-permute-start.9 = (bf16[256,1024]{1,0:T(8,128)(2,1)S(1)}, bf16[256,1024]{1,0:T(8,128)(2,1)S(1)}, u32[]{:S(2)}, u32[]{:S(2)}) collective-permute-start(bf16[256,1024]{1,0:T(8,128)(2,1)S(1)} %get-tuple-element.79), channel_id=1, source_target_pairs={{16,0},{17,1},{18,2},{19,3},{20,4},{21,5},{22,6},{23,7}} | collective-permute-start | bytes 1572872 | tf_op jit(solution)/shard_map/ppermute | solution.py:441
  95.8 43.6 %collective-permute-start.8 = (bf16[256,1024]{1,0:T(8,128)(2,1)S(1)}, bf16[256,1024]{1,0:T(8,128)(2,1)S(1)}, u32[]{:S(2)}, u32[]{:S(2)}) collective-permute-start(bf16[256,1024]{1,0:T(8,128)(2,1)S(1)} %get-tuple-element.79), channel_id=1, source_target_pairs={{8,0},{9,1},{10,2},{11,3},{12,4},{13,5},{14,6},{15,7}} | collective-permute-start | bytes 1572872 | tf_op jit(solution)/shard_map/ppermute | solution.py:441
  97.1 5.3 %copy-start.24 = (s32[4]{0:T(128)S(1)}, s32[4]{0:T(128)}, u32[]{:S(2)}) copy-start(s32[4]{0:T(128)} %constant.42.clone.info_ref) | copy-start | bytes 52
  99.8 39.3 %collective-permute-start.10 = (bf16[256,1024]{1,0:T(8,128)(2,1)S(1)}, bf16[256,1024]{1,0:T(8,128)(2,1)S(1)}, u32[]{:S(2)}, u32[]{:S(2)}) collective-permute-start(bf16[256,1024]{1,0:T(8,128)(2,1)S(1)} %get-tuple-element.78), channel_id=1, source_target_pairs={{16,0},{17,1},{18,2},{19,3},{20,4},{21,5},{22,6},{23,7}} | collective-permute-start | bytes 1572872 | tf_op jit(solution)/shard_map/ppermute | solution.py:441
  101.1 43.0 %collective-permute-start.7 = (bf16[256,1024]{1,0:T(8,128)(2,1)S(1)}, bf16[256,1024]{1,0:T(8,128)(2,1)S(1)}, u32[]{:S(2)}, u32[]{:S(2)}) collective-permute-start(bf16[256,1024]{1,0:T(8,128)(2,1)S(1)} %get-tuple-element.78), channel_id=1, source_target_pairs={{8,0},{9,1},{10,2},{11,3},{12,4},{13,5},{14,6},{15,7}} | collective-permute-start | bytes 1572872 | tf_op jit(solution)/shard_map/ppermute | solution.py:441
  102.4 36.8 %copy-start.20 = (bf16[256,1024]{1,0:T(8,128)(2,1)S(1)}, bf16[256,1024]{1,0:T(8,128)(2,1)}, u32[]{:S(2)}) copy-start(bf16[256,1024]{1,0:T(8,128)(2,1)} %copy-done.19) | copy-start | bytes 1572868
  102.4 37.0 %copy-start.5 = (bf16[2048,1024]{1,0:T(8,128)(2,1)S(1)}, bf16[2048,1024]{1,0:T(8,128)(2,1)}, u32[]{:S(2)}) copy-start(bf16[2048,1024]{1,0:T(8,128)(2,1)} %copy-done.3) | copy-start | bytes 12582916
  102.4 37.0 %copy-start.18 = (f32[2,256,1]{2,1,0:T(8,128)S(1)}, f32[2,256,1]{2,1,0:T(8,128)}, u32[]{:S(2)}) copy-start(f32[2,256,1]{2,1,0:T(8,128)} %copy-done.16) | copy-start | bytes 6148
  116.8 22.7 %copy-start.2 = (bf16[1024,2048]{1,0:T(8,128)(2,1)S(1)}, bf16[1024,2048]{1,0:T(8,128)(2,1)}, u32[]{:S(2)}) copy-start(bf16[1024,2048]{1,0:T(8,128)(2,1)} %copy-done) | copy-start | bytes 12582916
  161.0 4.2 %collective-permute-start.13 = (bf16[4,256,1024]{2,1,0:T(8,128)(2,1)S(1)}, bf16[4,256,1024]{2,1,0:T(8,128)(2,1)S(1)}, u32[]{:S(2)}, u32[]{:S(2)}) collective-permute-start(bf16[4,256,1024]{2,1,0:T(8,128)(2,1)S(1)} %weights.6), channel_id=1, source_target_pairs={{0,1},{1,0},{2,3},{3,2},{4,5},{5,4},{6,7},{7,6},{8,9},{9,8},{10,11... | collective-permute-start | bytes 6291464 | tf_op jit(solution)/shard_map/ppermute | solution.py:527
  171.3 90.8 %reduce-scatter.3.cloned.1.call-start = ((), (), s32[]{:S(2)}) async-start(), calls=%async_computation.2 | async-start | bytes 2621440 | tf_op jit(solution)/shard_map/reduce_scatter | solution.py:531
  176.7 4.2 %collective-permute-start.11 = (bf16[4,128,2048]{2,1,0:T(8,128)(2,1)S(1)}, bf16[4,128,2048]{2,1,0:T(8,128)(2,1)S(1)}, u32[]{:S(2)}, u32[]{:S(2)}) collective-permute-start(bf16[4,128,2048]{2,1,0:T(8,128)(2,1)S(1)} %weights.4), channel_id=1, source_target_pairs={{0,1},{1,0},{2,3},{3,2},{4,5},{5,4},{6,7},{7,6},{8,9},{9,8},{10,11... | collective-permute-start | bytes 6291464 | tf_op jit(solution)/shard_map/ppermute | solution.py:527
  216.4 1.0 copy-start.21
  221.0 46.7 %collective-permute-start.14 = (bf16[256,1024]{1,0:T(8,128)(2,1)S(1)}, bf16[256,1024]{1,0:T(8,128)(2,1)S(1)}, u32[]{:S(2)}, u32[]{:S(2)}) collective-permute-start(bf16[256,1024]{1,0:T(8,128)(2,1)S(1)} %get-tuple-element.95), channel_id=1, source_target_pairs={{0,24},{8,16},{16,8},{24,0},{1,25},{9,17},{17,9},{25,1},{2,26},{10... | collective-permute-start | bytes 1572872 | tf_op jit(solution)/shard_map/ppermute | solution.py:544
  262.1 1.0 copy-start.22
  265.3 14.4 %collective-permute-start.12 = (bf16[128,2048]{1,0:T(8,128)(2,1)S(1)}, bf16[128,2048]{1,0:T(8,128)(2,1)S(1)}, u32[]{:S(2)}, u32[]{:S(2)}) collective-permute-start(bf16[128,2048]{1,0:T(8,128)(2,1)S(1)} %get-tuple-element.90), channel_id=1, source_target_pairs={{0,24},{8,16},{16,8},{24,0},{1,25},{9,17},{17,9},{25,1},{2,26},{10... | collective-permute-start | bytes 1572872 | tf_op jit(solution)/shard_map/ppermute | solution.py:544
Sparse Core Ops, SparseCore 0:
  171.4 44.9 reduce-scatter.4
  218.8 43.1 reduce-scatter.2

commit v6 on v4

--- a/solution.py
+++ b/solution.py
@@ -15,6 +15,7 @@
 f32 = jnp.float32
 bf16 = jnp.bfloat16
 any_space = pl.BlockSpec(memory_space=pl.ANY)
+light = pl.CostEstimate(flops=1000, bytes_accessed=1000, transcendentals=0)
 
 
 def params(mib):
@@ -39,7 +40,7 @@
     return min(512, width)
 
 
-def forward(per, inputs, w_up, w_down, info, plan, previous, after, places, resident):
+def forward(per, inputs, w_up, w_down, info, plan, previous, after, places):
     _, _, micro, tokens, model = inputs.shape
     width = w_up.shape[3]
     tile = tile_of(width)
@@ -60,9 +61,6 @@
                 rows_ref[k * tokens : (k + 1) * tokens] = u
                 us_ref[0, k // per, k % per * tokens : (k % per + 1) * tokens] = u
 
-        if resident:
-            outs[5][...] = p_ref[0, 0]
-            outs[6][...] = q_ref[0, 0]
         for g in range(groups):
             here = slice(g * rows, (g + 1) * rows)
             u = rows_ref[here]
@@ -117,12 +115,6 @@
         pl.BlockSpec((groups, rows, model), lambda j, i, p: (0, 0, 0)),
         pl.BlockSpec((groups, rows, 1), lambda j, i, p: (0, 0, 0)),
     ]
-    if resident:
-        out_shape += [pltpu.VMEM((model, width), bf16), pltpu.VMEM((width, model), bf16)]
-        out_specs += [
-            pl.BlockSpec((model, tile), lambda j, i, p: (0, j)),
-            pl.BlockSpec((tile, model), lambda j, i, p: (j, 0)),
-        ]
     return pl.pallas_call(
         body,
         grid_spec=pltpu.PrefetchScalarGridSpec(
@@ -135,9 +127,7 @@
         out_shape=out_shape,
         input_output_aliases=aliases,
         compiler_params=params(30),
-        cost_estimate=pl.CostEstimate(
-            flops=8 * every * model * width, bytes_accessed=4 * model * width, transcendentals=0
-        ),
+        cost_estimate=light,
         name="forward",
     )(info, plan, *operands)
 
@@ -151,11 +141,11 @@
 columns_of_table = 4
 
 
-def chain_step(call, group, table, recv, top_grad, saved, previous, after):
+def chain_step(call, group, table, recv, top_grad, saved, w_up, w_down, previous, after):
     base = call * columns_of_table
-    slopes, ys, rs, w_up, w_down = saved
+    slopes, ys, rs = saved
     groups, rows, model = ys.shape
-    width = w_up.shape[1]
+    width = w_up.shape[3]
     tile = tile_of(width)
     tokens = top_grad.shape[2]
     per = rows // tokens
@@ -176,13 +166,13 @@
         @pl.when(active)
         def _():
             grad_pre = (
-                dot(low[...], q_ref[...], ((1,), (1,))) * slope_ref[0].astype(f32)
+                dot(low[...], q_ref[0, 0], ((1,), (1,))) * slope_ref[0].astype(f32)
             ).astype(bf16)
             pre_ref[0] = grad_pre
 
             @pl.when(info[base + 3] > 0)
             def _():
-                part = dot(grad_pre, p_ref[...], ((1,), (1,)))
+                part = dot(grad_pre, p_ref[0, 0], ((1,), (1,)))
 
                 @pl.when(j == 0)
                 def _():
@@ -207,10 +197,10 @@
         pl.BlockSpec((1, rows, model), lambda j, i: (group, 0, 0)),
         pl.BlockSpec((1, rows, 1), lambda j, i: (group, 0, 0)),
         pl.BlockSpec((1, rows, tile), lambda j, i: (group, 0, j * i[base])),
-        pl.BlockSpec((model, tile), lambda j, i: (0, j * i[base + 3])),
-        pl.BlockSpec((tile, model), lambda j, i: (j * i[base], 0)),
+        pl.BlockSpec((1, 1, model, tile), lambda j, i: (i[base + 1], 0, 0, j * i[base + 3])),
+        pl.BlockSpec((1, 1, tile, model), lambda j, i: (i[base + 1], 0, j * i[base], 0)),
     ]
-    operands += [in_vmem(x) for x in (ys, rs, slopes, w_up, w_down)]
+    operands += [in_vmem(x) for x in (ys, rs, slopes)] + [in_hbm(w_up), in_hbm(w_down)]
     aliases = {}
     if previous is not None:
         aliases = {1 + len(operands): 1, 2 + len(operands): 2}
@@ -244,9 +234,7 @@
         ],
         input_output_aliases=aliases,
         compiler_params=params(20),
-        cost_estimate=pl.CostEstimate(
-            flops=8 * rows * model * width, bytes_accessed=4 * model * width, transcendentals=0
-        ),
+        cost_estimate=light,
         name="chain",
     )(table, *operands)
 
@@ -300,11 +288,7 @@
             pltpu.HBM((groups, rows, model), bf16),
         ],
         compiler_params=params(28),
-        cost_estimate=pl.CostEstimate(
-            flops=4 * groups * rows * model * width,
-            bytes_accessed=2 * model * width,
-            transcendentals=0,
-        ),
+        cost_estimate=light,
         name="home",
     )(
         info,
@@ -350,11 +334,7 @@
         out_specs=pl.BlockSpec(out_block, (lambda j: (j, 0)) if split_left else (lambda j: (0, j))),
         out_shape=pltpu.HBM((rows, columns), bf16),
         compiler_params=params(32),
-        cost_estimate=pl.CostEstimate(
-            flops=4 * groups * tokens * rows * columns,
-            bytes_accessed=2 * rows * columns,
-            transcendentals=0,
-        ),
+        cost_estimate=light,
         name="weights",
     )(*[in_hbm(x) for x in (left_a, right_a, left_b, right_b)], *[in_hbm(x) for x in after])
 
@@ -389,9 +369,7 @@
             pltpu.HBM((1, rows, columns), f32),
         ],
         compiler_params=params(24),
-        cost_estimate=pl.CostEstimate(
-            flops=4 * rows * columns, bytes_accessed=12 * rows * columns, transcendentals=0
-        ),
+        cost_estimate=light,
         name="update",
     )(replica, in_hbm(weight), in_hbm(moment), total)
 
@@ -439,27 +417,36 @@
 
     def run_forward(kind, after):
         nonlocal blocks, order
-        *blocks, slopes, ys, rs, w_up, w_down = forward(
-            per, section_inputs, up_weight, down_weight, kinds[kind], plan, blocks, after, 2, True
+        *blocks, slopes, ys, rs = forward(
+            per, section_inputs, up_weight, down_weight, kinds[kind], plan, blocks, after, 2
         )
-        saved[kind] = (slopes, ys, rs, w_up, w_down)
+        saved[kind] = (slopes, ys, rs)
         order = [blocks[0]]
 
     run_forward(0, [])
-    late = []
     received = {}
     arrived = {}
+    asked = {(1, 0): [(last - 1, 0)], (half, 0): [(last - 1, g) for g in range(1, groups)]}
     kept = None
     for call, (stage, group) in enumerate(calls):
         if stage == last and group == 0:
             *home_blocks, slopes, ys, rs = forward(
-                per, mirrored, up_weight, down_weight, home_kind, plan, None, order + late, 1, False
+                per, mirrored, up_weight, down_weight, home_kind, plan, None, order, 1
             )
             saved_home = (slopes, ys, rs)
             order = [home_blocks[0]]
         recv = received.pop((stage, group), None)
         out, *kept = chain_step(
-            call, group, table, recv, top_grad, saved[int(stage >= half)], kept, order
+            call,
+            group,
+            table,
+            recv,
+            top_grad,
+            saved[int(stage >= half)],
+            up_weight,
+            down_weight,
+            kept,
+            order + [arrived[x] for x in asked.get((stage, group), [])],
         )
         order = [kept[0]]
         pairs = [(last - stage, last - stage - 1)] if stage < last else []
@@ -469,10 +456,8 @@
         if got is not None:
             received[(stage + 1, group)] = got
         if stage < last:
-            got = hop(out, [(stage, last - 1 - stage)])
-            arrived[(last - 1 - stage, group)] = got
-            if stage < half:
-                late.append(got)
+            to = last - 1 - stage
+            arrived[(to, group)] = out if to == stage else hop(out, [(stage, to)])
         if saved[1] is None and group == groups - 1:
             run_forward(1, order + [mirrored[0, 0]])
 

time: 280 us -> 265 us (0.946)
  local copies, waits for them, and re-layouts: 22.3 us -> 4.62 us
  starting transfers between devices: 29.9 us -> 20.7 us
  Pallas kernels: 101 us -> 108 us
  waiting for transfers between devices: 108 us -> 112 us
    unnamed x50 -> x44, local copies, waits for them, and re-layouts: 19.9 us -> 2.18 us
    ppermute x12 -> x10, starting transfers between devices: 21.2 us -> 12 us  [hop(): return lax.ppermute(value, 'section', pairs) if pairs else None]
    pallas_call x8, Pallas kernels: 34.7 us -> 43.6 us  [chain_step(): pl.pallas_call(body, grid_spec=pltpu.PrefetchScalarGridSpec(num_scalar_pr...]
    ppermute x12 -> x10, waiting for transfers between devices: 14.1 us -> 18.3 us  [hop(): return lax.ppermute(value, 'section', pairs) if pairs else None]
  transfers between devices with their start and end apart: 17 -> 15, of which waited for: 6 -> 6; matrix products, arithmetic and copies ran while one was open for 1% -> 1% of each run, Pallas kernels for 29% -> 32%
where the time goes in v6:
time: 265 us; the launch traced here: 264 us
  waiting for transfers between devices  112 us (42%)
  Pallas kernels  108 us (41%)
  starting transfers between devices  20.7 us (8%)
  between operations  14.4 us (5%)
  local copies, waits for them, and re-layouts  4.62 us (2%)
  other arithmetic  4.45 us (2%)
    pallas_call x8, Pallas kernels, chain_step(): pl.pallas_call(body, grid_spec=pltpu.PrefetchScalarGridSpec(num_scalar_pr...  43.6 us
    reduce_scatter x1, waiting for transfers between devices, on_device(): up_sum = lax.psum_scatter(up_part, 'dp', scatter_dimension=0, tiled=True)  43.5 us
    reduce_scatter x1, waiting for transfers between devices, on_device(): lax.psum_scatter(down_part, 'dp', scatter_dimension=0, tiled=True)  40.9 us
    pallas_call x3, Pallas kernels, forward(): pl.pallas_call(body, grid_spec=pltpu.PrefetchScalarGridSpec(num_scalar_pr...  34.4 us
    ppermute x10, waiting for transfers between devices, hop(): return lax.ppermute(value, 'section', pairs) if pairs else None  18.3 us
    pallas_call x2, Pallas kernels, weight_gradient(): pl.pallas_call(body, grid=((rows if split_left else columns) // tile,), i...  17 us
    ppermute x10, starting transfers between devices, hop(): return lax.ppermute(value, 'section', pairs) if pairs else None  12 us
    ppermute x2, waiting for transfers between devices, finish(): lax.ppermute(fresh, 'section', [(i, last - i) for i in range(sections)])  8.99 us
  transfers between devices with their start and end apart: 15, of which 6 were waited for; matrix products, arithmetic and copies ran while one was open for 1% of the time, Pallas kernels for 32%

profile of v6, /device:TPU:0, one launch (start us, length us, event | category | flops | bytes accessed | tf_op | source)
XLA Modules:
  0.0 264.0 jit_solution(13956812210226401175)
XLA Ops:
  7.2 0.0 reduce-scatter.5.cloned.1.call-start
  7.2 2.3 slice_bitcast_fusion
  9.5 3.9 %collective-permute-start = (bf16[4,128,1024]{2,1,0:T(8,128)(2,1)}, bf16[4,128,1024]{2,1,0:T(8,128)(2,1)}, u32[]{:S(2)}, u32[]{:S(2)}) collective-permute-start(bf16[4,128,1024]{2,1,0:T(8,128)(2,1)} %slice_bitcast_fusion), channel_id=1, source_target_pairs={{0,24},{8,16},{16,8},{24,0},{1,25},{9,17},{17,9},{25,1},{2,26},{10... | collective-permute-start | bytes 3145736 | tf_op jit(solution)/shard_map/ppermute | solution.py:389
  13.5 11.5 %forward.3 = (bf16[2,2,256,1024]{3,2,1,0:T(8,128)(2,1)}, bf16[2,2,256,2048]{3,2,1,0:T(8,128)(2,1)}, bf16[2,256,2048]{2,1,0:T(8,128)(2,1)S(1)}, bf16[2,256,1024]{2,1,0:T(8,128)(2,1)S(1)}, f32[2,256,1]{2,1,0:T(8,128)S(1)}) custom-call(s32[4]{0:T(128)S(1)} %stack.54.info_ref, s32[2,4]{1,0:T(2,128)S(1)} %copy-done.16, bf16[2,1,4,128,1024]{4,3,2,1,0:T(8,128)(2,1)} %refs_3_.3, ...), custom_call_target="tpu_custom_call" | custom-call | flops 1000 | bytes 1000 | tf_op jit(solution)/shard_map/forward/pallas_call | solution.py:118
  25.0 0.1 copy.35
  25.1 0.1 reshape.15.info
  25.2 8.8 %chain.8 = (bf16[256,1024]{1,0:T(8,128)(2,1)S(1)}, bf16[3,256,2048]{2,1,0:T(8,128)(2,1)}, bf16[3,256,1024]{2,1,0:T(8,128)(2,1)}) custom-call(s32[32]{0:T(128)S(1)} %reshape.15.info, bf16[2,4,128,1024]{3,2,1,0:T(8,128)(2,1)} %refs_2_.5, bf16[2,256,1024]{2,1,0:T(8,128)(2,1)S(1)} %get-tuple-element.49.y_ref, f32[2,256,1]{2,1,0:T(8,128)S(1)} %get-tuple-element.50.r_ref, ...), custom_call_target="tpu_custom_call" | custom-call | flops 1000 | bytes 1000 | tf_op jit(solution)/shard_map/chain/pallas_call | solution.py:213
  33.9 1.3 collective-permute-start.3
  35.3 1.3 collective-permute-start.2
  36.6 8.8 %chain.9 = (bf16[256,1024]{1,0:T(8,128)(2,1)S(1)}, bf16[3,256,2048]{2,1,0:T(8,128)(2,1)}, bf16[3,256,1024]{2,1,0:T(8,128)(2,1)}) custom-call(s32[32]{0:T(128)S(1)} %reshape.15.info, bf16[2,4,128,1024]{3,2,1,0:T(8,128)(2,1)} %refs_2_.5, bf16[2,256,1024]{2,1,0:T(8,128)(2,1)S(1)} %get-tuple-element.49.y_ref, ...), custom_call_target="tpu_custom_call", output_to_operand_aliasing={{1}: (7, {}), {2}: (8, {})} | custom-call | flops 1000 | bytes 1000 | tf_op jit(solution)/shard_map/chain/pallas_call | solution.py:213
  45.4 1.3 collective-permute-start.1
  46.7 1.3 collective-permute-start.6
  48.1 11.5 %forward.4 = (bf16[2,2,256,1024]{3,2,1,0:T(8,128)(2,1)}, bf16[2,2,256,2048]{3,2,1,0:T(8,128)(2,1)}, bf16[2,256,2048]{2,1,0:T(8,128)(2,1)S(1)}, bf16[2,256,1024]{2,1,0:T(8,128)(2,1)S(1)}, f32[2,256,1]{2,1,0:T(8,128)S(1)}) custom-call(s32[4]{0:T(128)S(1)} %stack.53.info_ref, s32[2,4]{1,0:T(2,128)S(1)} %copy-done.16, ...), custom_call_target="tpu_custom_call", output_to_operand_aliasing={{0}: (8, {}), {1}: (9, {})} | custom-call | flops 1000 | bytes 1000 | tf_op jit(solution)/shard_map/forward/pallas_call | solution.py:118
  59.6 3.3 %chain.10 = (bf16[256,1024]{1,0:T(8,128)(2,1)S(1)}, bf16[3,256,2048]{2,1,0:T(8,128)(2,1)}, bf16[3,256,1024]{2,1,0:T(8,128)(2,1)}) custom-call(s32[32]{0:T(128)S(1)} %reshape.15.info, bf16[256,1024]{1,0:T(8,128)(2,1)S(1)} %collective-permute-done.2.e_ref, bf16[2,256,1024]{2,1,0:T(8,128)(2,1)S(1)} %copy-done.3, ...), custom_call_target="tpu_custom_call", output_to_operand_aliasing={{1}: (7, {}), {2}: (8, {})} | custom-call | flops 1000 | bytes 1000 | tf_op jit(solution)/shard_map/chain/pallas_call | solution.py:213
  62.9 0.7 collective-permute-start.5
  63.6 3.0 %chain.11 = (bf16[256,1024]{1,0:T(8,128)(2,1)S(1)}, bf16[3,256,2048]{2,1,0:T(8,128)(2,1)}, bf16[3,256,1024]{2,1,0:T(8,128)(2,1)}) custom-call(s32[32]{0:T(128)S(1)} %reshape.15.info, bf16[256,1024]{1,0:T(8,128)(2,1)S(1)} %collective-permute-done.1.e_ref, bf16[2,256,1024]{2,1,0:T(8,128)(2,1)S(1)} %copy-done.3, ...), custom_call_target="tpu_custom_call", output_to_operand_aliasing={{1}: (7, {}), {2}: (8, {})} | custom-call | flops 1000 | bytes 1000 | tf_op jit(solution)/shard_map/chain/pallas_call | solution.py:213
  66.7 0.9 collective-permute-start.4
  67.6 3.0 %chain.12 = (bf16[256,1024]{1,0:T(8,128)(2,1)S(1)}, bf16[3,256,2048]{2,1,0:T(8,128)(2,1)}, bf16[3,256,1024]{2,1,0:T(8,128)(2,1)}) custom-call(s32[32]{0:T(128)S(1)} %reshape.15.info, bf16[256,1024]{1,0:T(8,128)(2,1)S(1)} %collective-permute-done.5.e_ref, ...), custom_call_target="tpu_custom_call", output_to_operand_aliasing={{1}: (7, {}), {2}: (8, {})} | custom-call | flops 1000 | bytes 1000 | tf_op jit(solution)/shard_map/chain/pallas_call | solution.py:213
  70.7 1.3 collective-permute-start.8
  72.0 3.2 %chain.13 = (bf16[256,1024]{1,0:T(8,128)(2,1)}, bf16[3,256,2048]{2,1,0:T(8,128)(2,1)}, bf16[3,256,1024]{2,1,0:T(8,128)(2,1)}) custom-call(s32[32]{0:T(128)S(1)} %reshape.15.info, bf16[256,1024]{1,0:T(8,128)(2,1)S(1)} %collective-permute-done.4.e_ref, ...), custom_call_target="tpu_custom_call", output_to_operand_aliasing={{1}: (7, {}), {2}: (8, {})} | custom-call | flops 1000 | bytes 1000 | tf_op jit(solution)/shard_map/chain/pallas_call | solution.py:213
  75.2 1.3 collective-permute-start.10
  76.5 1.3 collective-permute-start.9
  77.8 1.3 collective-permute-start.7
  79.1 11.5 %forward.5 = (bf16[1,2,256,1024]{3,2,1,0:T(8,128)(2,1)}, bf16[1,2,256,2048]{3,2,1,0:T(8,128)(2,1)}, bf16[2,256,2048]{2,1,0:T(8,128)(2,1)S(1)}, bf16[2,256,1024]{2,1,0:T(8,128)(2,1)S(1)}, f32[2,256,1]{2,1,0:T(8,128)S(1)}) custom-call(s32[4]{0:T(128)S(1)} %copy-done.17, s32[2,4]{1,0:T(2,128)S(1)} %copy-done.16, ...), custom_call_target="tpu_custom_call" | custom-call | flops 1000 | bytes 1000 | tf_op jit(solution)/shard_map/forward/pallas_call | solution.py:118
  90.6 5.5 %collective-permute-done.8.e_ref = bf16[256,1024]{1,0:T(8,128)(2,1)S(1)} collective-permute-done((bf16[256,1024]{1,0:T(8,128)(2,1)S(1)}, bf16[256,1024]{1,0:T(8,128)(2,1)S(1)}, u32[]{:S(2)}, u32[]{:S(2)}) %collective-permute-start.8) | collective-permute-done | bytes 524320 | tf_op jit(solution)/shard_map/ppermute | solution.py:387
  96.1 6.8 %chain.14 = (bf16[256,1024]{1,0:T(8,128)(2,1)}, bf16[3,256,2048]{2,1,0:T(8,128)(2,1)}, bf16[3,256,1024]{2,1,0:T(8,128)(2,1)}) custom-call(s32[32]{0:T(128)S(1)} %reshape.15.info, bf16[256,1024]{1,0:T(8,128)(2,1)S(1)} %collective-permute-done.8.e_ref, ...), custom_call_target="tpu_custom_call", output_to_operand_aliasing={{1}: (7, {}), {2}: (8, {})} | custom-call | flops 1000 | bytes 1000 | tf_op jit(solution)/shard_map/chain/pallas_call | solution.py:213
  102.9 7.7 %collective-permute-done.10 = bf16[256,1024]{1,0:T(8,128)(2,1)} collective-permute-done((bf16[256,1024]{1,0:T(8,128)(2,1)}, bf16[256,1024]{1,0:T(8,128)(2,1)}, u32[]{:S(2)}, u32[]{:S(2)}) %collective-permute-start.10) | collective-permute-done | bytes 524320 | tf_op jit(solution)/shard_map/ppermute | solution.py:387
  110.6 1.2 select_select_fusion.refs_1_
  111.7 5.1 %collective-permute-done.9 = bf16[256,1024]{1,0:T(8,128)(2,1)} collective-permute-done((bf16[256,1024]{1,0:T(8,128)(2,1)S(1)}, bf16[256,1024]{1,0:T(8,128)(2,1)}, u32[]{:S(2)}, u32[]{:S(2)}) %collective-permute-start.9) | collective-permute-done | bytes 524320 | tf_op jit(solution)/shard_map/ppermute | solution.py:387
  116.8 1.1 select_select_fusion.1.refs_0_
  118.0 6.7 %chain.15 = (bf16[256,1024]{1,0:T(8,128)(2,1)}, bf16[3,256,2048]{2,1,0:T(8,128)(2,1)}, bf16[3,256,1024]{2,1,0:T(8,128)(2,1)}) custom-call(s32[32]{0:T(128)S(1)} %reshape.15.info, bf16[256,1024]{1,0:T(8,128)(2,1)S(1)} %collective-permute-done.7.e_ref, ...), custom_call_target="tpu_custom_call", output_to_operand_aliasing={{1}: (7, {}), {2}: (8, {})} | custom-call | flops 1000 | bytes 1000 | tf_op jit(solution)/shard_map/chain/pallas_call | solution.py:213
  124.7 7.3 %home.1 = (bf16[2,256,2048]{2,1,0:T(8,128)(2,1)}, bf16[2,256,1024]{2,1,0:T(8,128)(2,1)}) custom-call(s32[1]{0:T(128)} %bitcast.7.info, bf16[256,1024]{1,0:T(8,128)(2,1)S(1)} %select_select_fusion.1.refs_0_, bf16[256,1024]{1,0:T(8,128)(2,1)S(1)} %select_select_fusion.refs_1_, bf16[2,4,128,1024]{3,2,1,0:T(8,128)(2,1)} %refs_2_.5, ...), custom_call_target="tpu_custom_call" | custom-call | flops 1000 | bytes 1000 | tf_op jit(solution)/shard_map/home/pallas_call | solution.py:267
  132.0 8.4 %weights.3 = bf16[2048,1024]{1,0:T(8,128)(2,1)} custom-call(bf16[2,2,256,2048]{3,2,1,0:T(8,128)(2,1)} %get-tuple-element.83.la_ref, bf16[3,256,1024]{2,1,0:T(8,128)(2,1)} %get-tuple-element.84.ra_ref, bf16[1,2,256,2048]{3,2,1,0:T(8,128)(2,1)} %get-tuple-element.85.lb_ref, bf16[2,256,1024]{2,1,0:T(8,128)(2,1)} %get-tuple-element.86.rb_ref), custom_call_target="tpu_custom_call" | custom-call | flops 1000 | bytes 1000 | tf_op jit(solution)/shard_map/weights/pallas_call | solution.py:324
  140.4 0.0 reduce-scatter.5.cloned.1.call-update
  140.4 0.0 reduce-scatter.3.cloned.1.call-start
  140.5 8.5 %weights.2 = bf16[1024,2048]{1,0:T(8,128)(2,1)} custom-call(bf16[2,2,256,1024]{3,2,1,0:T(8,128)(2,1)} %get-tuple-element.55.rest_2_.la_ref, bf16[3,256,2048]{2,1,0:T(8,128)(2,1)} %get-tuple-element.77.refs_7_.ra_ref, bf16[1,2,256,1024]{3,2,1,0:T(8,128)(2,1)} %get-tuple-element.74.rest_2_.lb_ref, bf16[2,256,2048]{2,1,0:T(8,128)(2,1)} %get-tuple-element.81.rb_ref), custom_call_target="tpu_custom_call" | custom-call | flops 1000 | bytes 1000 | tf_op jit(solution)/shard_map/weights/pallas_call | solution.py:324
  149.0 0.0 reduce-scatter.3.cloned.1.call-update
  149.0 40.9 %reduce-scatter.5.cloned.1.call-done.total_ref = bf16[256,1024]{1,0:T(8,128)(2,1)} async-done(((bf16[2048,1024]{1,0:T(8,128)(2,1)}), bf16[256,1024]{1,0:T(8,128)(2,1)}) %reduce-scatter.5.cloned.1.call-update) | async-done | bytes 524304 | tf_op jit(solution)/shard_map/reduce_scatter | solution.py:477
  190.0 1.0 copy-done.10
  191.0 3.5 %update.3 = (bf16[256,1024]{1,0:T(8,128)(2,1)S(1)}, f32[1,256,1024]{2,1,0:T(8,128)}) custom-call(s32[1]{0:T(128)} %bitcast.info, bf16[2,1,2048,1024]{3,2,1,0:T(8,128)(2,1)} %weight_ref.3, f32[1,256,1024]{2,1,0:T(8,128)} %moment_ref.3, bf16[256,1024]{1,0:T(8,128)(2,1)S(1)} %copy-done.10), custom_call_target="tpu_custom_call" | custom-call | flops 1000 | bytes 1000 | tf_op jit(solution)/shard_map/update/pallas_call | solution.py:352
  194.6 2.4 collective-permute-start.12
  196.9 43.5 %reduce-scatter.3.cloned.1.call-done.total_ref = bf16[128,2048]{1,0:T(8,128)(2,1)} async-done(((bf16[1024,2048]{1,0:T(8,128)(2,1)}), bf16[128,2048]{1,0:T(8,128)(2,1)}) %reduce-scatter.3.cloned.1.call-update) | async-done | bytes 524304 | tf_op jit(solution)/shard_map/reduce_scatter | solution.py:475
  240.4 1.0 copy-done.11
  241.5 2.2 update.2
  243.7 2.4 collective-permute-start.11
  246.1 1.1 maximum_bitcast_fusion.1
  247.2 9.0 %collective-permute-done.11 = bf16[128,2048]{1,0:T(8,128)(2,1)S(1)} collective-permute-done((bf16[128,2048]{1,0:T(8,128)(2,1)S(1)}, bf16[128,2048]{1,0:T(8,128)(2,1)S(1)}, u32[]{:S(2)}, u32[]{:S(2)}) %collective-permute-start.11) | collective-permute-done | bytes 524320 | tf_op jit(solution)/shard_map/ppermute | solution.py:482
  256.1 1.1 maximum_bitcast_fusion
  (57 shorter events, 0.2 us)
Async XLA Ops:
  7.2 6.2 %copy-start.18 = (pred[8]{0:T(512)(128)(4,1)S(1)}, pred[8]{0:T(512)(128)(4,1)}, u32[]{:S(2)}) copy-start(pred[8]{0:T(512)(128)(4,1)} %constant.27.clone) | copy-start | bytes 28
  7.2 6.2 %copy-start.20 = (s32[8]{0:T(128)S(1)}, s32[8]{0:T(128)}, u32[]{:S(2)}) copy-start(s32[8]{0:T(128)} %constant.28.clone) | copy-start | bytes 100
  7.2 6.2 %copy-start.16 = (s32[2,4]{1,0:T(2,128)S(1)}, s32[2,4]{1,0:T(2,128)}, u32[]{:S(2)}) copy-start(s32[2,4]{1,0:T(2,128)} %plan_ref.5) | copy-start | bytes 100
  7.2 182.8 %reduce-scatter.5.cloned.1.call-start = ((), (), s32[]{:S(2)}) async-start(), calls=%async_computation.3 | async-start | bytes 4718592 | tf_op jit(solution)/shard_map/reduce_scatter | solution.py:477
  9.5 38.5 %collective-permute-start = (bf16[4,128,1024]{2,1,0:T(8,128)(2,1)}, bf16[4,128,1024]{2,1,0:T(8,128)(2,1)}, u32[]{:S(2)}, u32[]{:S(2)}) collective-permute-start(bf16[4,128,1024]{2,1,0:T(8,128)(2,1)} %slice_bitcast_fusion), channel_id=1, source_target_pairs={{0,24},{8,16},{16,8},{24,0},{1,25},{9,17},{17,9},{25,1},{2,26},{10... | collective-permute-start | bytes 3145736 | tf_op jit(solution)/shard_map/ppermute | solution.py:389
  13.4 11.5 %copy-start.21 = (pred[8]{0:T(512)(128)(4,1)S(1)}, pred[8]{0:T(512)(128)(4,1)}, u32[]{:S(2)}) copy-start(pred[8]{0:T(512)(128)(4,1)} %constant.30.clone) | copy-start | bytes 28
  13.5 11.5 %copy-start.19 = (s32[8]{0:T(128)S(1)}, s32[8]{0:T(128)}, u32[]{:S(2)}) copy-start(s32[8]{0:T(128)} %constant.29.clone) | copy-start | bytes 100
  24.9 11.7 %copy-start.2 = (bf16[2,256,1024]{2,1,0:T(8,128)(2,1)}, bf16[2,256,1024]{2,1,0:T(8,128)(2,1)S(1)}, u32[]{:S(2)}) copy-start(bf16[2,256,1024]{2,1,0:T(8,128)(2,1)S(1)} %get-tuple-element.49.y_ref) | copy-start | bytes 3145732
  24.9 11.7 %copy-start.4 = (f32[2,256,1]{2,1,0:T(8,128)}, f32[2,256,1]{2,1,0:T(8,128)S(1)}, u32[]{:S(2)}) copy-start(f32[2,256,1]{2,1,0:T(8,128)S(1)} %get-tuple-element.50.r_ref) | copy-start | bytes 6148
  33.9 25.6 %collective-permute-start.3 = (bf16[256,1024]{1,0:T(8,128)(2,1)S(1)}, bf16[256,1024]{1,0:T(8,128)(2,1)S(1)}, u32[]{:S(2)}, u32[]{:S(2)}) collective-permute-start(bf16[256,1024]{1,0:T(8,128)(2,1)S(1)} %get-tuple-element.57), channel_id=1, source_target_pairs={{0,16},{1,17},{2,18},{3,19},{4,20},{5,21},{6,22},{7,23}} | collective-permute-start | bytes 1572872 | tf_op jit(solution)/shard_map/ppermute | solution.py:387
  35.3 24.3 %collective-permute-start.2 = (bf16[256,1024]{1,0:T(8,128)(2,1)S(1)}, bf16[256,1024]{1,0:T(8,128)(2,1)S(1)}, u32[]{:S(2)}, u32[]{:S(2)}) collective-permute-start(bf16[256,1024]{1,0:T(8,128)(2,1)S(1)} %get-tuple-element.57), channel_id=1, source_target_pairs={{24,16},{0,8},{25,17},{1,9},{26,18},{2,10},{27,19},{3,11},{28,20},... | collective-permute-start | bytes 1572872 | tf_op jit(solution)/shard_map/ppermute | solution.py:387
  45.4 18.2 %collective-permute-start.1 = (bf16[256,1024]{1,0:T(8,128)(2,1)S(1)}, bf16[256,1024]{1,0:T(8,128)(2,1)S(1)}, u32[]{:S(2)}, u32[]{:S(2)}) collective-permute-start(bf16[256,1024]{1,0:T(8,128)(2,1)S(1)} %get-tuple-element.56), channel_id=1, source_target_pairs={{24,16},{0,8},{25,17},{1,9},{26,18},{2,10},{27,19},{3,11},{28,20},... | collective-permute-start | bytes 1572872 | tf_op jit(solution)/shard_map/ppermute | solution.py:387
  46.7 20.9 %collective-permute-start.6 = (bf16[256,1024]{1,0:T(8,128)(2,1)S(1)}, bf16[256,1024]{1,0:T(8,128)(2,1)S(1)}, u32[]{:S(2)}, u32[]{:S(2)}) collective-permute-start(bf16[256,1024]{1,0:T(8,128)(2,1)S(1)} %get-tuple-element.56), channel_id=1, source_target_pairs={{0,16},{1,17},{2,18},{3,19},{4,20},{5,21},{6,22},{7,23}} | collective-permute-start | bytes 1572872 | tf_op jit(solution)/shard_map/ppermute | solution.py:387
  48.1 11.5 %copy-start.3 = (bf16[2,256,1024]{2,1,0:T(8,128)(2,1)S(1)}, bf16[2,256,1024]{2,1,0:T(8,128)(2,1)}, u32[]{:S(2)}) copy-start(bf16[2,256,1024]{2,1,0:T(8,128)(2,1)} %copy-done.2) | copy-start | bytes 3145732
  48.1 11.5 %copy-start.5 = (f32[2,256,1]{2,1,0:T(8,128)S(1)}, f32[2,256,1]{2,1,0:T(8,128)}, u32[]{:S(2)}) copy-start(f32[2,256,1]{2,1,0:T(8,128)} %copy-done.4) | copy-start | bytes 6148
  59.6 12.4 %copy-start = (bf16[2,256,2048]{2,1,0:T(8,128)(2,1)}, bf16[2,256,2048]{2,1,0:T(8,128)(2,1)S(1)}, u32[]{:S(2)}) copy-start(bf16[2,256,2048]{2,1,0:T(8,128)(2,1)S(1)} %get-tuple-element.64.slope_ref) | copy-start | bytes 6291460
  59.6 3.3 %copy-start.6 = (bf16[256,1024]{1,0:T(8,128)(2,1)}, bf16[256,1024]{1,0:T(8,128)(2,1)S(1)}, u32[]{:S(2)}) copy-start(bf16[256,1024]{1,0:T(8,128)(2,1)S(1)} %collective-permute-done.3.rest_3_) | copy-start | bytes 1572868
  62.9 3.8 %copy-start.12 = (bf16[256,1024]{1,0:T(8,128)(2,1)}, bf16[256,1024]{1,0:T(8,128)(2,1)S(1)}, u32[]{:S(2)}) copy-start(bf16[256,1024]{1,0:T(8,128)(2,1)S(1)} %get-tuple-element.65) | copy-start | bytes 1572868
  62.9 4.7 %collective-permute-start.5 = (bf16[256,1024]{1,0:T(8,128)(2,1)S(1)}, bf16[256,1024]{1,0:T(8,128)(2,1)S(1)}, u32[]{:S(2)}, u32[]{:S(2)}) collective-permute-start(bf16[256,1024]{1,0:T(8,128)(2,1)S(1)} %get-tuple-element.65), channel_id=1, source_target_pairs={{16,8},{8,16},{17,9},{9,17},{18,10},{10,18},{19,11},{11,19},{20,12... | collective-permute-start | bytes 1572872 | tf_op jit(solution)/shard_map/ppermute | solution.py:387
  66.7 4.0 %copy-start.14 = (bf16[256,1024]{1,0:T(8,128)(2,1)}, bf16[256,1024]{1,0:T(8,128)(2,1)S(1)}, u32[]{:S(2)}) copy-start(bf16[256,1024]{1,0:T(8,128)(2,1)S(1)} %get-tuple-element.61) | copy-start | bytes 1572868
  66.7 5.3 %collective-permute-start.4 = (bf16[256,1024]{1,0:T(8,128)(2,1)S(1)}, bf16[256,1024]{1,0:T(8,128)(2,1)S(1)}, u32[]{:S(2)}, u32[]{:S(2)}) collective-permute-start(bf16[256,1024]{1,0:T(8,128)(2,1)S(1)} %get-tuple-element.61), channel_id=1, source_target_pairs={{16,8},{8,16},{17,9},{9,17},{18,10},{10,18},{19,11},{11,19},{20,12... | collective-permute-start | bytes 1572872 | tf_op jit(solution)/shard_map/ppermute | solution.py:387
  67.6 3.1 %copy-start.8 = (bf16[256,1024]{1,0:T(8,128)(2,1)}, bf16[256,1024]{1,0:T(8,128)(2,1)S(1)}, u32[]{:S(2)}) copy-start(bf16[256,1024]{1,0:T(8,128)(2,1)S(1)} %collective-permute-done.6.rest_2_) | copy-start | bytes 1572868
  70.7 25.4 %collective-permute-start.8 = (bf16[256,1024]{1,0:T(8,128)(2,1)S(1)}, bf16[256,1024]{1,0:T(8,128)(2,1)S(1)}, u32[]{:S(2)}, u32[]{:S(2)}) collective-permute-start(bf16[256,1024]{1,0:T(8,128)(2,1)S(1)} %get-tuple-element.71), channel_id=1, source_target_pairs={{8,0},{9,1},{10,2},{11,3},{12,4},{13,5},{14,6},{15,7}} | collective-permute-start | bytes 1572872 | tf_op jit(solution)/shard_map/ppermute | solution.py:387
  72.0 7.1 %copy-start.17 = (s32[4]{0:T(128)S(1)}, s32[4]{0:T(128)}, u32[]{:S(2)}) copy-start(s32[4]{0:T(128)} %constant.31.clone.info_ref) | copy-start | bytes 52
  75.2 35.3 %collective-permute-start.10 = (bf16[256,1024]{1,0:T(8,128)(2,1)}, bf16[256,1024]{1,0:T(8,128)(2,1)}, u32[]{:S(2)}, u32[]{:S(2)}) collective-permute-start(bf16[256,1024]{1,0:T(8,128)(2,1)} %get-tuple-element.70), channel_id=1, source_target_pairs={{16,0},{17,1},{18,2},{19,3},{20,4},{21,5},{22,6},{23,7}} | collective-permute-start | bytes 1572872 | tf_op jit(solution)/shard_map/ppermute | solution.py:387
  76.5 40.3 %collective-permute-start.9 = (bf16[256,1024]{1,0:T(8,128)(2,1)S(1)}, bf16[256,1024]{1,0:T(8,128)(2,1)}, u32[]{:S(2)}, u32[]{:S(2)}) collective-permute-start(bf16[256,1024]{1,0:T(8,128)(2,1)S(1)} %get-tuple-element.71), channel_id=1, source_target_pairs={{16,0},{17,1},{18,2},{19,3},{20,4},{21,5},{22,6},{23,7}} | collective-permute-start | bytes 1572872 | tf_op jit(solution)/shard_map/ppermute | solution.py:387
  77.8 40.2 %collective-permute-start.7 = (bf16[256,1024]{1,0:T(8,128)(2,1)}, bf16[256,1024]{1,0:T(8,128)(2,1)S(1)}, u32[]{:S(2)}, u32[]{:S(2)}) collective-permute-start(bf16[256,1024]{1,0:T(8,128)(2,1)} %get-tuple-element.70), channel_id=1, source_target_pairs={{8,0},{9,1},{10,2},{11,3},{12,4},{13,5},{14,6},{15,7}} | collective-permute-start | bytes 1572872 | tf_op jit(solution)/shard_map/ppermute | solution.py:387
  79.1 17.0 %copy-start.1 = (bf16[2,256,2048]{2,1,0:T(8,128)(2,1)S(1)}, bf16[2,256,2048]{2,1,0:T(8,128)(2,1)}, u32[]{:S(2)}) copy-start(bf16[2,256,2048]{2,1,0:T(8,128)(2,1)} %copy-done) | copy-start | bytes 6291460
  96.1 14.4 %copy-start.9 = (bf16[256,1024]{1,0:T(8,128)(2,1)S(1)}, bf16[256,1024]{1,0:T(8,128)(2,1)}, u32[]{:S(2)}) copy-start(bf16[256,1024]{1,0:T(8,128)(2,1)} %copy-done.8) | copy-start | bytes 1572868
  96.1 14.4 %copy-start.15 = (bf16[256,1024]{1,0:T(8,128)(2,1)S(1)}, bf16[256,1024]{1,0:T(8,128)(2,1)}, u32[]{:S(2)}) copy-start(bf16[256,1024]{1,0:T(8,128)(2,1)} %copy-done.14) | copy-start | bytes 1572868
  102.9 14.0 %copy-start.7 = (bf16[256,1024]{1,0:T(8,128)(2,1)S(1)}, bf16[256,1024]{1,0:T(8,128)(2,1)}, u32[]{:S(2)}) copy-start(bf16[256,1024]{1,0:T(8,128)(2,1)} %copy-done.6) | copy-start | bytes 1572868
  102.9 14.0 %copy-start.13 = (bf16[256,1024]{1,0:T(8,128)(2,1)S(1)}, bf16[256,1024]{1,0:T(8,128)(2,1)}, u32[]{:S(2)}) copy-start(bf16[256,1024]{1,0:T(8,128)(2,1)} %copy-done.12) | copy-start | bytes 1572868
  140.4 100.0 %reduce-scatter.3.cloned.1.call-start = ((), (), s32[]{:S(2)}) async-start(), calls=%async_computation.2 | async-start | bytes 4718592 | tf_op jit(solution)/shard_map/reduce_scatter | solution.py:475
  190.0 1.0 copy-start.10
  194.6 51.5 %collective-permute-start.12 = (bf16[256,1024]{1,0:T(8,128)(2,1)S(1)}, bf16[256,1024]{1,0:T(8,128)(2,1)S(1)}, u32[]{:S(2)}, u32[]{:S(2)}) collective-permute-start(bf16[256,1024]{1,0:T(8,128)(2,1)S(1)} %get-tuple-element.87), channel_id=1, source_target_pairs={{0,24},{8,16},{16,8},{24,0},{1,25},{9,17},{17,9},{25,1},{2,26},{10... | collective-permute-start | bytes 1572872 | tf_op jit(solution)/shard_map/ppermute | solution.py:482
  240.4 1.0 copy-start.11
  243.7 12.4 %collective-permute-start.11 = (bf16[128,2048]{1,0:T(8,128)(2,1)S(1)}, bf16[128,2048]{1,0:T(8,128)(2,1)S(1)}, u32[]{:S(2)}, u32[]{:S(2)}) collective-permute-start(bf16[128,2048]{1,0:T(8,128)(2,1)S(1)} %get-tuple-element.82), channel_id=1, source_target_pairs={{0,24},{8,16},{16,8},{24,0},{1,25},{9,17},{17,9},{25,1},{2,26},{10... | collective-permute-start | bytes 1572872 | tf_op jit(solution)/shard_map/ppermute | solution.py:482
Sparse Core Ops, SparseCore 0:
  140.5 49.3 reduce-scatter.4
  192.3 48.1 reduce-scatter.2

commit v7 on v6

--- a/solution.py
+++ b/solution.py
@@ -300,52 +300,118 @@
     )
 
 
-def weight_gradient(left_a, right_a, left_b, right_b, groups, split_left, after):
+def weight_gradient(core, left_a, right_a, left_b, right_b, groups, replicas, split_left, came, after):
     tokens = right_a.shape[-2]
-    rows, columns = left_a.shape[-1], right_a.shape[-1]
-    tile = tile_of(rows if split_left else columns)
-
-    def body(la_ref, ra_ref, lb_ref, rb_ref, *rest):
+    rows, columns = left_a.shape[-1] // replicas, right_a.shape[-1]
+    lines = replicas // 2
+    tile = columns if split_left else tile_of(columns)
+    steps = lines if split_left else columns // tile
+    lefts = 1 if split_left else lines
+    pair = rows % 128 != 0
+    wide = 2 * rows if pair else rows
+
+    def place(z, i):
+        return z if pair else 2 * z + i[0]
+
+    def body(info, *refs):
         def flat(ref):
             return ref[...].reshape(-1, ref.shape[-1])
 
-        total = dot(flat(la_ref), flat(ra_ref), ((0,), (0,)))
-        total += dot(flat(lb_ref), flat(rb_ref), ((0,), (0,)))
-        rest[-1][...] = total.astype(bf16)
-
-    def spec(array, split):
+        def product(left_refs, right_ref):
+            left = [flat(ref) for ref in left_refs]
+            if pair:
+                left = [jnp.where(info[0] == 0, x[:, :rows], x[:, rows:]) for x in left]
+            left = left[0] if len(left) == 1 else jnp.concatenate(left, axis=1)
+            return dot(left, flat(right_ref), ((0,), (0,)))
+
+        total = product(refs[:lefts], refs[lefts])
+        total += product(refs[lefts + 1 : 2 * lefts + 1], refs[2 * lefts + 1])
+        total = total.reshape(lefts, rows, tile)
+        if came is not None:
+            total += refs[2 * lefts + 2][...].astype(f32)
+        refs[-1][...] = total.astype(bf16)
+
+    def left_specs(array):
         lead = array.ndim - 3
-        block = (1,) * lead + (groups, tokens, tile if split else array.shape[-1])
-        if split:
-            return pl.BlockSpec(block, lambda j: (0,) * (lead + 2) + (j,))
-        return pl.BlockSpec(block, lambda j: (0,) * (lead + 3))
-
-    out_block = (tile, columns) if split_left else (rows, tile)
+        block = (1,) * lead + (groups, tokens, wide)
+        if split_left:
+            return [pl.BlockSpec(block, lambda j, i: (0,) * (lead + 2) + (place(j, i),))]
+        return [
+            pl.BlockSpec(block, lambda j, i, z=z: (0,) * (lead + 2) + (place(z, i),))
+            for z in range(lines)
+        ]
+
+    def right_spec(array):
+        lead = array.ndim - 3
+        block = (1,) * lead + (groups, tokens, tile)
+        if split_left:
+            return pl.BlockSpec(block, lambda j, i: (0,) * (lead + 3))
+        return pl.BlockSpec(block, lambda j, i: (0,) * (lead + 2) + (j,))
+
+    if split_left:
+        out_spec = pl.BlockSpec((1, rows, tile), lambda j, i: (j, 0, 0))
+    else:
+        out_spec = pl.BlockSpec((lines, rows, tile), lambda j, i: (0, 0, j))
+    operands = [in_hbm(left_a)] * lefts + [in_hbm(right_a)]
+    operands += [in_hbm(left_b)] * lefts + [in_hbm(right_b)]
+    in_specs = left_specs(left_a) + [right_spec(right_a)]
+    in_specs += left_specs(left_b) + [right_spec(right_b)]
+    if came is not None:
+        operands.append(came)
+        in_specs.append(out_spec)
+    in_specs += [any_space] * len(after)
+    operands += [in_hbm(x) for x in after]
     return pl.pallas_call(
         body,
-        grid=((rows if split_left else columns) // tile,),
-        in_specs=[
-            spec(left_a, split_left),
-            spec(right_a, not split_left),
-            spec(left_b, split_left),
-            spec(right_b, not split_left),
-        ]
-        + [any_space] * len(after),
-        out_specs=pl.BlockSpec(out_block, (lambda j: (j, 0)) if split_left else (lambda j: (0, j))),
-        out_shape=pltpu.HBM((rows, columns), bf16),
-        compiler_params=params(32),
+        grid_spec=pltpu.PrefetchScalarGridSpec(
+            num_scalar_prefetch=1, grid=(steps,), in_specs=in_specs, out_specs=out_spec
+        ),
+        out_shape=pltpu.HBM((lines, rows, columns), bf16),
+        compiler_params=params(28),
         cost_estimate=light,
         name="weights",
-    )(*[in_hbm(x) for x in (left_a, right_a, left_b, right_b)], *[in_hbm(x) for x in after])
-
-
-def update(replica, weight, moment, total):
+    )(core, *operands)
+
+
+def fold(places, part, came):
+    _, rows, columns = part.shape
+    tile = min(64, rows)
+
+    def body(info, *refs):
+        for k in range(2):
+            value = refs[k][0].astype(f32)
+            if came:
+                value += refs[2 + k][...].astype(f32)
+            refs[k - 2][...] = value.astype(bf16)
+
+    plain = pl.BlockSpec((tile, columns), lambda j, i: (j, 0))
+    return pl.pallas_call(
+        body,
+        grid_spec=pltpu.PrefetchScalarGridSpec(
+            num_scalar_prefetch=1,
+            grid=(rows // tile,),
+            in_specs=[
+                pl.BlockSpec((1, tile, columns), lambda j, i: (i[0], j, 0)),
+                pl.BlockSpec((1, tile, columns), lambda j, i: (i[1], j, 0)),
+            ]
+            + [plain] * len(came),
+            out_specs=[plain] * 2,
+        ),
+        out_shape=[jax.ShapeDtypeStruct((rows, columns), bf16)] * 2,
+        compiler_params=params(16),
+        cost_estimate=light,
+        name="fold",
+    )(places, in_hbm(part), in_hbm(part), *came)
+
+
+def update(replica, weight, moment, part, came):
     _, rows, columns = moment.shape
     tile = min(64, rows)
     steps = rows // tile
 
-    def body(info, weight_ref, moment_ref, total_ref, fresh_ref, out_ref):
-        fresh_moment = momentum_decay * moment_ref[0] + total_ref[...].astype(f32)
+    def body(info, weight_ref, moment_ref, part_ref, right_ref, left_ref, fresh_ref, out_ref):
+        total = part_ref[0].astype(f32) + right_ref[...].astype(f32) + left_ref[...].astype(f32)
+        fresh_moment = momentum_decay * moment_ref[0] + total
         out_ref[0] = fresh_moment
         fresh_ref[...] = (weight_ref[0, 0].astype(f32) - step_size * fresh_moment).astype(bf16)
 
@@ -357,6 +423,8 @@
             in_specs=[
                 pl.BlockSpec((1, 1, tile, columns), lambda j, i: (0, 0, i[0] * steps + j, 0)),
                 pl.BlockSpec((1, tile, columns), lambda j, i: (0, j, 0)),
+                pl.BlockSpec((1, tile, columns), lambda j, i: (i[1], j, 0)),
+                pl.BlockSpec((tile, columns), lambda j, i: (j, 0)),
                 pl.BlockSpec((tile, columns), lambda j, i: (j, 0)),
             ],
             out_specs=[
@@ -371,7 +439,7 @@
         compiler_params=params(24),
         cost_estimate=light,
         name="update",
-    )(replica, in_hbm(weight), in_hbm(moment), total)
+    )(replica, in_hbm(weight), in_hbm(moment), in_hbm(part), *came)
 
 
 def on_device(section_inputs, top_grad, plan, up_weight, down_weight, up_moment, down_moment):
@@ -461,6 +529,9 @@
         if saved[1] is None and group == groups - 1:
             run_forward(1, order + [mirrored[0, 0]])
 
+    side = sorted(arrived)
+    *values, kept[1] = lax.optimization_barrier([arrived[x] for x in side] + [kept[1]])
+    arrived = dict(zip(side, values))
     came = []
     for group in range(groups):
         value = arrived[(0, group)]
@@ -471,19 +542,43 @@
         (position == last).astype(jnp.int32)[None], came, top_grad, saved_home, down_weight, order
     )
 
-    up_part = weight_gradient(blocks[0], kept[0], home_blocks[0], home_pre, groups, False, [])
-    up_sum = lax.psum_scatter(up_part, "dp", scatter_dimension=0, tiled=True)
-    down_part = weight_gradient(blocks[1], kept[1], home_blocks[1], home_sum, groups, True, [])
-    down_sum = lax.psum_scatter(down_part, "dp", scatter_dimension=0, tiled=True)
-    replica = lax.axis_index("dp").astype(jnp.int32)[None]
-
-    def finish(weight, moment, total):
-        fresh, fresh_moment = update(replica, weight, moment, total)
+    replicas = lax.axis_size("dp")
+    replica = lax.axis_index("dp").astype(jnp.int32)
+    lines, place, core = replicas // 2, replica // 2, replica % 2
+    swap = [(i, i ^ 1) for i in range(replicas)]
+    sources = (
+        (blocks[1], kept[1], home_blocks[1], home_sum, groups, replicas, True),
+        (blocks[0], kept[0], home_blocks[0], home_pre, groups, replicas, False),
+    )
+    other = (1 - core)[None]
+    sent_down = weight_gradient(other, *sources[0], None, [])
+    came_down = lax.ppermute(sent_down, "dp", swap)
+    sent_up = weight_gradient(other, *sources[1], None, [sent_down])
+    came_up = lax.ppermute(sent_up, "dp", swap)
+    parts = [weight_gradient(core[None], *sources[0], came_down, [sent_up])]
+    parts.append(weight_gradient(core[None], *sources[1], came_up, [parts[0]]))
+
+    came = [[], []]
+    for step in range(1, lines):
+        places = jnp.stack(
+            [jnp.minimum(place + lines - step, lines - 1), jnp.maximum(place - lines + step, 0)]
+        )
+        starts = [z for z in range(step) if z + 1 < lines]
+        right = [(2 * z + c, 2 * z + 2 + c) for z in starts for c in range(2)]
+        left = [(replicas - 1 - i, replicas - 1 - k) for i, k in right]
+        for k in range(2):
+            to_right, to_left = fold(places, parts[k], came[k])
+            came[k] = [lax.ppermute(to_right, "dp", right), lax.ppermute(to_left, "dp", left)]
+
+    where = jnp.stack([replica, place])
+
+    def finish(weight, moment, part, arrivals):
+        fresh, fresh_moment = update(where, weight, moment, part, arrivals)
         far = lax.ppermute(fresh, "section", [(i, last - i) for i in range(sections)])
         return jnp.stack([fresh, far])[:, None], fresh_moment
 
-    new_up_weight, new_up_moment = finish(up_weight, up_moment, up_sum)
-    new_down_weight, new_down_moment = finish(down_weight, down_moment, down_sum)
+    new_down_weight, new_down_moment = finish(down_weight, down_moment, parts[0], came[0])
+    new_up_weight, new_up_moment = finish(up_weight, up_moment, parts[1], came[1])
     return (new_up_weight, new_down_weight, new_up_moment, new_down_moment)
 
 

time: 265 us -> 234 us (0.88)
  waiting for transfers between devices: 112 us -> 46.4 us
  Pallas kernels: 108 us -> 136 us
  starting transfers between devices: 20.7 us -> 44.2 us
  between operations: 14.4 us -> 1.18 us
    reduce_scatter x2 -> x0, waiting for transfers between devices: 84.4 us -> none  [the longest x1 43.5 us: on_device(): up_sum = lax.psum_scatter(up_part, 'dp', scatter_dimension=0, tiled=True)]
    ppermute x0 -> x14, starting transfers between devices: none -> 28.3 us  [the longest x6 22.5 us: on_device(): lax.ppermute(to_right, 'dp', right)]
    pallas_call x2 -> x10, Pallas kernels: 17 us -> 42.7 us  [the longest x4 25 us: weight_gradient(): pl.pallas_call(body, grid_spec=pltpu.PrefetchScalarGridSpec(num_scalar_pr...]
    ppermute x0 -> x14, waiting for transfers between devices: none -> 18.3 us  [the longest x6 18.3 us: on_device(): lax.ppermute(to_right, 'dp', right)]
    ppermute x2, waiting for transfers between devices: 8.99 us -> 14.1 us  [finish(): lax.ppermute(fresh, 'section', [(i, last - i) for i in range(sections)])]
    ppermute x2, starting transfers between devices: 4.75 us -> 0.01 us  [finish(): lax.ppermute(fresh, 'section', [(i, last - i) for i in range(sections)])]
    ppermute x10, waiting for transfers between devices: 18.3 us -> 14 us  [hop(): return lax.ppermute(value, 'section', pairs) if pairs else None]
  transfers between devices with their start and end apart: 15 -> 27, of which waited for: 6 -> 10; matrix products, arithmetic and copies ran while one was open for 1% -> 1% of each run, Pallas kernels for 32% -> 53%
where the time goes in v7:
time: 234 us; the launch traced here: 233 us
  Pallas kernels  136 us (58%)
  waiting for transfers between devices  46.4 us (20%)
  starting transfers between devices  44.2 us (19%)
  other arithmetic  2.67 us (1%)
  local copies, waits for them, and re-layouts  2.54 us (1%)
    pallas_call x8, Pallas kernels, chain_step(): pl.pallas_call(body, grid_spec=pltpu.PrefetchScalarGridSpec(num_scalar_pr...  44 us
    pallas_call x3, Pallas kernels, forward(): pl.pallas_call(body, grid_spec=pltpu.PrefetchScalarGridSpec(num_scalar_pr...  34.4 us
    pallas_call x4, Pallas kernels, weight_gradient(): pl.pallas_call(body, grid_spec=pltpu.PrefetchScalarGridSpec(num_scalar_pr...  25 us
    ppermute x6, starting transfers between devices, on_device(): lax.ppermute(to_right, 'dp', right)  22.5 us
    ppermute x6, waiting for transfers between devices, on_device(): lax.ppermute(to_right, 'dp', right)  18.3 us
    pallas_call x6, Pallas kernels, fold(): pl.pallas_call(body, grid_spec=pltpu.PrefetchScalarGridSpec(num_scalar_pr...  17.7 us
    ppermute x2, waiting for transfers between devices, finish(): lax.ppermute(fresh, 'section', [(i, last - i) for i in range(sections)])  14.1 us
    ppermute x10, waiting for transfers between devices, hop(): return lax.ppermute(value, 'section', pairs) if pairs else None  14 us
  transfers between devices with their start and end apart: 27, of which 10 were waited for; matrix products, arithmetic and copies ran while one was open for 1% of the time, Pallas kernels for 53%

profile of v7, /device:TPU:0, one launch (start us, length us, event | category | flops | bytes accessed | tf_op | source)
XLA Modules:
  0.0 232.6 jit_solution(11339985087823886039)
XLA Ops:
  0.7 2.3 slice_bitcast_fusion
  2.9 3.9 %collective-permute-start = (bf16[4,128,1024]{2,1,0:T(8,128)(2,1)}, bf16[4,128,1024]{2,1,0:T(8,128)(2,1)}, u32[]{:S(2)}, u32[]{:S(2)}) collective-permute-start(bf16[4,128,1024]{2,1,0:T(8,128)(2,1)} %slice_bitcast_fusion), channel_id=1, source_target_pairs={{0,24},{8,16},{16,8},{24,0},{1,25},{9,17},{17,9},{25,1},{2,26},{10... | collective-permute-start | bytes 3145736 | tf_op jit(solution)/shard_map/ppermute | solution.py:457
  6.9 11.5 %forward.3 = (bf16[2,2,256,1024]{3,2,1,0:T(8,128)(2,1)}, bf16[2,2,256,2048]{3,2,1,0:T(8,128)(2,1)}, bf16[2,256,2048]{2,1,0:T(8,128)(2,1)S(1)}, bf16[2,256,1024]{2,1,0:T(8,128)(2,1)S(1)}, f32[2,256,1]{2,1,0:T(8,128)S(1)}) custom-call(s32[4]{0:T(128)S(1)} %stack.93.info_ref, s32[2,4]{1,0:T(2,128)S(1)} %copy-done.14, bf16[2,1,4,128,1024]{4,3,2,1,0:T(8,128)(2,1)} %refs_3_.3, ...), custom_call_target="tpu_custom_call" | custom-call | flops 1000 | bytes 1000 | tf_op jit(solution)/shard_map/forward/pallas_call | solution.py:118
  18.6 8.8 %chain.8 = (bf16[256,1024]{1,0:T(8,128)(2,1)S(1)}, bf16[3,256,2048]{2,1,0:T(8,128)(2,1)}, bf16[3,256,1024]{2,1,0:T(8,128)(2,1)}) custom-call(s32[32]{0:T(128)S(1)} %reshape.15.info, bf16[2,4,128,1024]{3,2,1,0:T(8,128)(2,1)} %refs_2_.5, bf16[2,256,1024]{2,1,0:T(8,128)(2,1)S(1)} %get-tuple-element.68.y_ref, f32[2,256,1]{2,1,0:T(8,128)S(1)} %get-tuple-element.69.r_ref, ...), custom_call_target="tpu_custom_call" | custom-call | flops 1000 | bytes 1000 | tf_op jit(solution)/shard_map/chain/pallas_call | solution.py:213
  27.4 1.3 collective-permute-start.2
  28.8 1.3 collective-permute-start.3
  30.1 8.8 %chain.9 = (bf16[256,1024]{1,0:T(8,128)(2,1)S(1)}, bf16[3,256,2048]{2,1,0:T(8,128)(2,1)}, bf16[3,256,1024]{2,1,0:T(8,128)(2,1)}) custom-call(s32[32]{0:T(128)S(1)} %reshape.15.info, bf16[2,4,128,1024]{3,2,1,0:T(8,128)(2,1)} %refs_2_.5, bf16[2,256,1024]{2,1,0:T(8,128)(2,1)S(1)} %get-tuple-element.68.y_ref, ...), custom_call_target="tpu_custom_call", output_to_operand_aliasing={{1}: (7, {}), {2}: (8, {})} | custom-call | flops 1000 | bytes 1000 | tf_op jit(solution)/shard_map/chain/pallas_call | solution.py:213
  38.9 1.3 collective-permute-start.1
  40.2 1.3 collective-permute-start.6
  41.6 11.5 %forward.4 = (bf16[2,2,256,1024]{3,2,1,0:T(8,128)(2,1)}, bf16[2,2,256,2048]{3,2,1,0:T(8,128)(2,1)}, bf16[2,256,2048]{2,1,0:T(8,128)(2,1)S(1)}, bf16[2,256,1024]{2,1,0:T(8,128)(2,1)S(1)}, f32[2,256,1]{2,1,0:T(8,128)S(1)}) custom-call(s32[4]{0:T(128)S(1)} %stack.92.info_ref, s32[2,4]{1,0:T(2,128)S(1)} %copy-done.14, ...), custom_call_target="tpu_custom_call", output_to_operand_aliasing={{0}: (8, {}), {1}: (9, {})} | custom-call | flops 1000 | bytes 1000 | tf_op jit(solution)/shard_map/forward/pallas_call | solution.py:118
  53.1 3.3 %chain.10 = (bf16[256,1024]{1,0:T(8,128)(2,1)S(1)}, bf16[3,256,2048]{2,1,0:T(8,128)(2,1)}, bf16[3,256,1024]{2,1,0:T(8,128)(2,1)}) custom-call(s32[32]{0:T(128)S(1)} %reshape.15.info, bf16[256,1024]{1,0:T(8,128)(2,1)S(1)} %collective-permute-done.2.e_ref, bf16[2,256,1024]{2,1,0:T(8,128)(2,1)S(1)} %copy-done.3, ...), custom_call_target="tpu_custom_call", output_to_operand_aliasing={{1}: (7, {}), {2}: (8, {})} | custom-call | flops 1000 | bytes 1000 | tf_op jit(solution)/shard_map/chain/pallas_call | solution.py:213
  57.2 3.1 %chain.11 = (bf16[256,1024]{1,0:T(8,128)(2,1)S(1)}, bf16[3,256,2048]{2,1,0:T(8,128)(2,1)}, bf16[3,256,1024]{2,1,0:T(8,128)(2,1)}) custom-call(s32[32]{0:T(128)S(1)} %reshape.15.info, bf16[256,1024]{1,0:T(8,128)(2,1)S(1)} %collective-permute-done.1.e_ref, bf16[2,256,1024]{2,1,0:T(8,128)(2,1)S(1)} %copy-done.3, ...), custom_call_target="tpu_custom_call", output_to_operand_aliasing={{1}: (7, {}), {2}: (8, {})} | custom-call | flops 1000 | bytes 1000 | tf_op jit(solution)/shard_map/chain/pallas_call | solution.py:213
  61.2 3.2 %chain.12 = (bf16[256,1024]{1,0:T(8,128)(2,1)}, bf16[3,256,2048]{2,1,0:T(8,128)(2,1)}, bf16[3,256,1024]{2,1,0:T(8,128)(2,1)}) custom-call(s32[32]{0:T(128)S(1)} %reshape.15.info, bf16[256,1024]{1,0:T(8,128)(2,1)S(1)} %collective-permute-done.5.e_ref, ...), custom_call_target="tpu_custom_call", output_to_operand_aliasing={{1}: (7, {}), {2}: (8, {})} | custom-call | flops 1000 | bytes 1000 | tf_op jit(solution)/shard_map/chain/pallas_call | solution.py:213
  64.4 1.3 collective-permute-start.8
  65.7 3.2 %chain.13 = (bf16[256,1024]{1,0:T(8,128)(2,1)}, bf16[3,256,2048]{2,1,0:T(8,128)(2,1)}, bf16[3,256,1024]{2,1,0:T(8,128)(2,1)}) custom-call(s32[32]{0:T(128)S(1)} %reshape.15.info, bf16[256,1024]{1,0:T(8,128)(2,1)S(1)} %collective-permute-done.4.e_ref, ...), custom_call_target="tpu_custom_call", output_to_operand_aliasing={{1}: (7, {}), {2}: (8, {})} | custom-call | flops 1000 | bytes 1000 | tf_op jit(solution)/shard_map/chain/pallas_call | solution.py:213
  70.2 1.3 collective-permute-start.10
  72.9 11.5 %forward.5 = (bf16[1,2,256,1024]{3,2,1,0:T(8,128)(2,1)}, bf16[1,2,256,2048]{3,2,1,0:T(8,128)(2,1)}, bf16[2,256,2048]{2,1,0:T(8,128)(2,1)S(1)}, bf16[2,256,1024]{2,1,0:T(8,128)(2,1)S(1)}, f32[2,256,1]{2,1,0:T(8,128)S(1)}) custom-call(s32[4]{0:T(128)S(1)} %copy-done.15, s32[2,4]{1,0:T(2,128)S(1)} %copy-done.14, ...), custom_call_target="tpu_custom_call" | custom-call | flops 1000 | bytes 1000 | tf_op jit(solution)/shard_map/forward/pallas_call | solution.py:118
  84.4 6.0 %collective-permute-done.8.e_ref = bf16[256,1024]{1,0:T(8,128)(2,1)S(1)} collective-permute-done((bf16[256,1024]{1,0:T(8,128)(2,1)}, bf16[256,1024]{1,0:T(8,128)(2,1)S(1)}, u32[]{:S(2)}, u32[]{:S(2)}) %collective-permute-start.8) | collective-permute-done | bytes 524320 | tf_op jit(solution)/shard_map/ppermute | solution.py:455
  90.4 6.8 %chain.14 = (bf16[256,1024]{1,0:T(8,128)(2,1)}, bf16[3,256,2048]{2,1,0:T(8,128)(2,1)}, bf16[3,256,1024]{2,1,0:T(8,128)(2,1)}) custom-call(s32[32]{0:T(128)S(1)} %reshape.15.info, bf16[256,1024]{1,0:T(8,128)(2,1)S(1)} %collective-permute-done.8.e_ref, ...), custom_call_target="tpu_custom_call", output_to_operand_aliasing={{1}: (7, {}), {2}: (8, {})} | custom-call | flops 1000 | bytes 1000 | tf_op jit(solution)/shard_map/chain/pallas_call | solution.py:213
  97.1 3.7 %collective-permute-done.7.e_ref = bf16[256,1024]{1,0:T(8,128)(2,1)S(1)} collective-permute-done((bf16[256,1024]{1,0:T(8,128)(2,1)}, bf16[256,1024]{1,0:T(8,128)(2,1)S(1)}, u32[]{:S(2)}, u32[]{:S(2)}) %collective-permute-start.7) | collective-permute-done | bytes 524320 | tf_op jit(solution)/shard_map/ppermute | solution.py:455
  100.8 6.8 %chain.15 = (bf16[256,1024]{1,0:T(8,128)(2,1)}, bf16[3,256,2048]{2,1,0:T(8,128)(2,1)}, bf16[3,256,1024]{2,1,0:T(8,128)(2,1)}) custom-call(s32[32]{0:T(128)S(1)} %reshape.15.info, bf16[256,1024]{1,0:T(8,128)(2,1)S(1)} %collective-permute-done.7.e_ref, ...), custom_call_target="tpu_custom_call", output_to_operand_aliasing={{1}: (7, {}), {2}: (8, {})} | custom-call | flops 1000 | bytes 1000 | tf_op jit(solution)/shard_map/chain/pallas_call | solution.py:213
  107.7 4.2 %collective-permute-done.9 = bf16[256,1024]{1,0:T(8,128)(2,1)S(1)} collective-permute-done((bf16[256,1024]{1,0:T(8,128)(2,1)}, bf16[256,1024]{1,0:T(8,128)(2,1)S(1)}, u32[]{:S(2)}, u32[]{:S(2)}) %collective-permute-start.9) | collective-permute-done | bytes 524320 | tf_op jit(solution)/shard_map/ppermute | solution.py:455
  112.1 7.3 %home.1 = (bf16[2,256,2048]{2,1,0:T(8,128)(2,1)}, bf16[2,256,1024]{2,1,0:T(8,128)(2,1)}) custom-call(s32[1]{0:T(128)} %bitcast.9.info, bf16[256,1024]{1,0:T(8,128)(2,1)S(1)} %get-tuple-element.141.refs_0_, bf16[256,1024]{1,0:T(8,128)(2,1)S(1)} %get-tuple-element.140.refs_1_, bf16[2,4,128,1024]{3,2,1,0:T(8,128)(2,1)} %refs_2_.5, ...), custom_call_target="tpu_custom_call" | custom-call | flops 1000 | bytes 1000 | tf_op jit(solution)/shard_map/home/pallas_call | solution.py:267
  119.4 6.0 %weights.4.refs_10_ = bf16[4,256,1024]{2,1,0:T(8,128)(2,1)} custom-call(s32[1]{0:T(128)} %bitcast.10.info, bf16[2,2,256,2048]{3,2,1,0:T(8,128)(2,1)} %get-tuple-element.108.refs_0_, bf16[3,256,1024]{2,1,0:T(8,128)(2,1)} %get-tuple-element.109.refs_1_, bf16[1,2,256,2048]{3,2,1,0:T(8,128)(2,1)} %get-tuple-element.110.refs_2_, ...), custom_call_target="tpu_custom_call" | custom-call | flops 1000 | bytes 1000 | tf_op jit(solution)/shard_map/weights/pallas_call | solution.py:364
  125.4 6.2 %weights.5.refs_5_ = bf16[4,128,2048]{2,1,0:T(8,128)(2,1)} custom-call(s32[1]{0:T(128)} %bitcast.10.info, bf16[2,2,256,1024]{3,2,1,0:T(8,128)(2,1)} %get-tuple-element.74.rest_2_.refs_0_.refs_1_.refs_2_.refs_3_, bf16[2,2,256,1024]{3,2,1,0:T(8,128)(2,1)} %get-tuple-element.74.rest_2_.refs_0_.refs_1_.refs_2_.refs_3_, ...), custom_call_target="tpu_custom_call" | custom-call | flops 1000 | bytes 1000 | tf_op jit(solution)/shard_map/weights/pallas_call | solution.py:364
  132.1 6.0 %weights.6.refs_11_.refs_0_.refs_1_.part_ref = bf16[4,256,1024]{2,1,0:T(8,128)(2,1)} custom-call(s32[1]{0:T(128)} %bitcast.2.info, bf16[2,2,256,2048]{3,2,1,0:T(8,128)(2,1)} %get-tuple-element.108.refs_0_, bf16[3,256,1024]{2,1,0:T(8,128)(2,1)} %get-tuple-element.109.refs_1_, bf16[1,2,256,2048]{3,2,1,0:T(8,128)(2,1)} %get-tuple-element.110.refs_2_, ...), custom_call_target="tpu_custom_call" | custom-call | flops 1000 | bytes 1000 | tf_op jit(solution)/shard_map/weights/pallas_call | solution.py:364
  138.1 3.9 %fold.9 = (bf16[256,1024]{1,0:T(8,128)(2,1)}, bf16[256,1024]{1,0:T(8,128)(2,1)S(1)}) custom-call(s32[2]{0:T(128)S(1)} %pad_add_fusion.4.info, bf16[4,256,1024]{2,1,0:T(8,128)(2,1)} %weights.6.refs_11_.refs_0_.refs_1_.part_ref, bf16[4,256,1024]{2,1,0:T(8,128)(2,1)} %weights.6.refs_11_.refs_0_.refs_1_.part_ref), custom_call_target="tpu_custom_call" | custom-call | flops 1000 | bytes 1000 | tf_op jit(solution)/shard_map/fold/pallas_call | solution.py:388
  142.0 3.5 %collective-permute-start.20 = (bf16[256,1024]{1,0:T(8,128)(2,1)}, bf16[256,1024]{1,0:T(8,128)(2,1)S(1)}, u32[]{:S(2)}, u32[]{:S(2)}) collective-permute-start(bf16[256,1024]{1,0:T(8,128)(2,1)} %get-tuple-element.119), channel_id=1, source_target_pairs={{0,2},{1,3},{8,10},{9,11},{16,18},{17,19},{24,26},{25,27}} | collective-permute-start | bytes 1572872 | tf_op jit(solution)/shard_map/ppermute | solution.py:571
  146.2 6.7 %weights.7.refs_0_.refs_1_.part_ref = bf16[4,128,2048]{2,1,0:T(8,128)(2,1)} custom-call(s32[1]{0:T(128)} %bitcast.2.info, bf16[2,2,256,1024]{3,2,1,0:T(8,128)(2,1)} %get-tuple-element.74.rest_2_.refs_0_.refs_1_.refs_2_.refs_3_, bf16[2,2,256,1024]{3,2,1,0:T(8,128)(2,1)} %get-tuple-element.74.rest_2_.refs_0_.refs_1_.refs_2_.refs_3_, ...), custom_call_target="tpu_custom_call" | custom-call | flops 1000 | bytes 1000 | tf_op jit(solution)/shard_map/weights/pallas_call | solution.py:364
  153.0 2.5 %fold.6 = (bf16[128,2048]{1,0:T(8,128)(2,1)}, bf16[128,2048]{1,0:T(8,128)(2,1)S(1)}) custom-call(s32[2]{0:T(128)S(1)} %pad_add_fusion.4.info, bf16[4,128,2048]{2,1,0:T(8,128)(2,1)} %weights.7.refs_0_.refs_1_.part_ref, bf16[4,128,2048]{2,1,0:T(8,128)(2,1)} %weights.7.refs_0_.refs_1_.part_ref), custom_call_target="tpu_custom_call" | custom-call | flops 1000 | bytes 1000 | tf_op jit(solution)/shard_map/fold/pallas_call | solution.py:388
  155.4 1.3 collective-permute-start.13
  157.6 3.9 %fold.10 = (bf16[256,1024]{1,0:T(8,128)(2,1)}, bf16[256,1024]{1,0:T(8,128)(2,1)S(1)}) custom-call(s32[2]{0:T(128)S(1)} %pad_add_fusion.3.info, bf16[4,256,1024]{2,1,0:T(8,128)(2,1)} %weights.6.refs_11_.refs_0_.refs_1_.part_ref, bf16[4,256,1024]{2,1,0:T(8,128)(2,1)} %weights.6.refs_11_.refs_0_.refs_1_.part_ref, ...), custom_call_target="tpu_custom_call" | custom-call | flops 1000 | bytes 1000 | tf_op jit(solution)/shard_map/fold/pallas_call | solution.py:388
  161.5 4.0 %collective-permute-start.22 = (bf16[256,1024]{1,0:T(8,128)(2,1)}, bf16[256,1024]{1,0:T(8,128)(2,1)S(1)}, u32[]{:S(2)}, u32[]{:S(2)}) collective-permute-start(bf16[256,1024]{1,0:T(8,128)(2,1)} %get-tuple-element.121), channel_id=1, source_target_pairs={{0,2},{1,3},{2,4},{3,5},{8,10},{9,11},{10,12},{11,13},{16,18},{17,... | collective-permute-start | bytes 1572872 | tf_op jit(solution)/shard_map/ppermute | solution.py:571
  166.2 3.1 %collective-permute-done.13.refs_2_ = bf16[128,2048]{1,0:T(8,128)(2,1)S(1)} collective-permute-done((bf16[128,2048]{1,0:T(8,128)(2,1)}, bf16[128,2048]{1,0:T(8,128)(2,1)S(1)}, u32[]{:S(2)}, u32[]{:S(2)}) %collective-permute-start.13) | collective-permute-done | bytes 524320 | tf_op jit(solution)/shard_map/ppermute | solution.py:571
  169.3 2.6 %fold.7 = (bf16[128,2048]{1,0:T(8,128)(2,1)}, bf16[128,2048]{1,0:T(8,128)(2,1)S(1)}) custom-call(s32[2]{0:T(128)S(1)} %pad_add_fusion.3.info, bf16[4,128,2048]{2,1,0:T(8,128)(2,1)} %weights.7.refs_0_.refs_1_.part_ref, bf16[4,128,2048]{2,1,0:T(8,128)(2,1)} %weights.7.refs_0_.refs_1_.part_ref, bf16[128,2048]{1,0:T(8,128)(2,1)S(1)} %collective-permute-done.13.refs_2_, ...), custom_call_target="tpu_custom_call" | custom-call | flops 1000 | bytes 1000 | tf_op jit(solution)/shard_map/fold/pallas_call | solution.py:388
  171.9 4.3 %collective-permute-start.15 = (bf16[128,2048]{1,0:T(8,128)(2,1)}, bf16[128,2048]{1,0:T(8,128)(2,1)S(1)}, u32[]{:S(2)}, u32[]{:S(2)}) collective-permute-start(bf16[128,2048]{1,0:T(8,128)(2,1)} %get-tuple-element.114), channel_id=1, source_target_pairs={{0,2},{1,3},{2,4},{3,5},{8,10},{9,11},{10,12},{11,13},{16,18},{17,... | collective-permute-start | bytes 1572872 | tf_op jit(solution)/shard_map/ppermute | solution.py:571
  177.0 3.6 %collective-permute-done.22.refs_2_ = bf16[256,1024]{1,0:T(8,128)(2,1)S(1)} collective-permute-done((bf16[256,1024]{1,0:T(8,128)(2,1)}, bf16[256,1024]{1,0:T(8,128)(2,1)S(1)}, u32[]{:S(2)}, u32[]{:S(2)}) %collective-permute-start.22) | collective-permute-done | bytes 524320 | tf_op jit(solution)/shard_map/ppermute | solution.py:571
  180.6 2.9 %fold.11 = (bf16[256,1024]{1,0:T(8,128)(2,1)S(1)}, bf16[256,1024]{1,0:T(8,128)(2,1)S(1)}) custom-call(s32[2]{0:T(128)S(1)} %pad_add_fusion.2.info, bf16[4,256,1024]{2,1,0:T(8,128)(2,1)} %weights.6.refs_11_.refs_0_.refs_1_.part_ref, bf16[4,256,1024]{2,1,0:T(8,128)(2,1)} %weights.6.refs_11_.refs_0_.refs_1_.part_ref, ...), custom_call_target="tpu_custom_call" | custom-call | flops 1000 | bytes 1000 | tf_op jit(solution)/shard_map/fold/pallas_call | solution.py:388
  183.4 4.9 %collective-permute-start.24 = (bf16[256,1024]{1,0:T(8,128)(2,1)S(1)}, bf16[256,1024]{1,0:T(8,128)(2,1)S(1)}, u32[]{:S(2)}, u32[]{:S(2)}) collective-permute-start(bf16[256,1024]{1,0:T(8,128)(2,1)S(1)} %get-tuple-element.123), channel_id=1, source_target_pairs={{0,2},{1,3},{2,4},{3,5},{4,6},{5,7},{8,10},{9,11},{10,12},{11,13},... | collective-permute-start | bytes 1572872 | tf_op jit(solution)/shard_map/ppermute | solution.py:571
  189.6 2.2 collective-permute-done.15.refs_2_
  191.8 2.0 fold.8
  193.8 4.6 %collective-permute-start.17 = (bf16[128,2048]{1,0:T(8,128)(2,1)S(1)}, bf16[128,2048]{1,0:T(8,128)(2,1)S(1)}, u32[]{:S(2)}, u32[]{:S(2)}) collective-permute-start(bf16[128,2048]{1,0:T(8,128)(2,1)S(1)} %get-tuple-element.116), channel_id=1, source_target_pairs={{0,2},{1,3},{2,4},{3,5},{4,6},{5,7},{8,10},{9,11},{10,12},{11,13},... | collective-permute-start | bytes 1572872 | tf_op jit(solution)/shard_map/ppermute | solution.py:571
  199.7 3.2 %collective-permute-done.24.right_ref = bf16[256,1024]{1,0:T(8,128)(2,1)S(1)} collective-permute-done((bf16[256,1024]{1,0:T(8,128)(2,1)S(1)}, bf16[256,1024]{1,0:T(8,128)(2,1)S(1)}, u32[]{:S(2)}, u32[]{:S(2)}) %collective-permute-start.24) | collective-permute-done | bytes 524320 | tf_op jit(solution)/shard_map/ppermute | solution.py:571
  202.9 4.2 %update.3 = (bf16[256,1024]{1,0:T(8,128)(2,1)S(1)}, f32[1,256,1024]{2,1,0:T(8,128)}) custom-call(s32[2]{0:T(128)S(1)} %pad_add_fusion.1.info, bf16[2,1,2048,1024]{3,2,1,0:T(8,128)(2,1)} %weight_ref.3, f32[1,256,1024]{2,1,0:T(8,128)} %moment_ref.3, bf16[4,256,1024]{2,1,0:T(8,128)(2,1)} %weights.6.refs_11_.refs_0_.refs_1_.part_ref, ...), custom_call_target="tpu_custom_call" | custom-call | flops 1000 | bytes 1000 | tf_op jit(solution)/shard_map/update/pallas_call | solution.py:418
  207.1 6.2 %collective-permute-done.17.right_ref = bf16[128,2048]{1,0:T(8,128)(2,1)S(1)} collective-permute-done((bf16[128,2048]{1,0:T(8,128)(2,1)S(1)}, bf16[128,2048]{1,0:T(8,128)(2,1)S(1)}, u32[]{:S(2)}, u32[]{:S(2)}) %collective-permute-start.17) | collective-permute-done | bytes 524320 | tf_op jit(solution)/shard_map/ppermute | solution.py:571
  213.3 3.0 %update.2 = (bf16[128,2048]{1,0:T(8,128)(2,1)S(1)}, f32[1,128,2048]{2,1,0:T(8,128)}) custom-call(s32[2]{0:T(128)S(1)} %pad_add_fusion.1.info, bf16[2,1,1024,2048]{3,2,1,0:T(8,128)(2,1)} %weight_ref.2, f32[1,128,2048]{2,1,0:T(8,128)} %moment_ref.2, bf16[4,128,2048]{2,1,0:T(8,128)(2,1)} %weights.7.refs_0_.refs_1_.part_ref, ...), custom_call_target="tpu_custom_call" | custom-call | flops 1000 | bytes 1000 | tf_op jit(solution)/shard_map/update/pallas_call | solution.py:418
  216.3 5.1 %collective-permute-done.26 = bf16[256,1024]{1,0:T(8,128)(2,1)S(1)} collective-permute-done((bf16[256,1024]{1,0:T(8,128)(2,1)S(1)}, bf16[256,1024]{1,0:T(8,128)(2,1)S(1)}, u32[]{:S(2)}, u32[]{:S(2)}) %collective-permute-start.26) | collective-permute-done | bytes 524320 | tf_op jit(solution)/shard_map/ppermute | solution.py:577
  222.5 9.0 %collective-permute-done.19 = bf16[128,2048]{1,0:T(8,128)(2,1)S(1)} collective-permute-done((bf16[128,2048]{1,0:T(8,128)(2,1)S(1)}, bf16[128,2048]{1,0:T(8,128)(2,1)S(1)}, u32[]{:S(2)}, u32[]{:S(2)}) %collective-permute-start.19) | collective-permute-done | bytes 524320 | tf_op jit(solution)/shard_map/ppermute | solution.py:577
  (86 shorter events, 12.9 us)
Async XLA Ops:
  0.6 6.2 %copy-start.16 = (pred[8]{0:T(512)(128)(4,1)S(1)}, pred[8]{0:T(512)(128)(4,1)}, u32[]{:S(2)}) copy-start(pred[8]{0:T(512)(128)(4,1)} %constant.61.clone) | copy-start | bytes 28
  0.6 6.2 %copy-start.18 = (s32[8]{0:T(128)S(1)}, s32[8]{0:T(128)}, u32[]{:S(2)}) copy-start(s32[8]{0:T(128)} %constant.62.clone) | copy-start | bytes 100
  0.7 6.2 %copy-start.14 = (s32[2,4]{1,0:T(2,128)S(1)}, s32[2,4]{1,0:T(2,128)}, u32[]{:S(2)}) copy-start(s32[2,4]{1,0:T(2,128)} %plan_ref.5) | copy-start | bytes 100
  2.9 38.6 %collective-permute-start = (bf16[4,128,1024]{2,1,0:T(8,128)(2,1)}, bf16[4,128,1024]{2,1,0:T(8,128)(2,1)}, u32[]{:S(2)}, u32[]{:S(2)}) collective-permute-start(bf16[4,128,1024]{2,1,0:T(8,128)(2,1)} %slice_bitcast_fusion), channel_id=1, source_target_pairs={{0,24},{8,16},{16,8},{24,0},{1,25},{9,17},{17,9},{25,1},{2,26},{10... | collective-permute-start | bytes 3145736 | tf_op jit(solution)/shard_map/ppermute | solution.py:457
  6.9 11.5 %copy-start.19 = (pred[8]{0:T(512)(128)(4,1)S(1)}, pred[8]{0:T(512)(128)(4,1)}, u32[]{:S(2)}) copy-start(pred[8]{0:T(512)(128)(4,1)} %constant.64.clone) | copy-start | bytes 28
  6.9 11.5 %copy-start.17 = (s32[8]{0:T(128)S(1)}, s32[8]{0:T(128)}, u32[]{:S(2)}) copy-start(s32[8]{0:T(128)} %constant.63.clone) | copy-start | bytes 100
  18.4 11.7 %copy-start.2 = (bf16[2,256,1024]{2,1,0:T(8,128)(2,1)}, bf16[2,256,1024]{2,1,0:T(8,128)(2,1)S(1)}, u32[]{:S(2)}) copy-start(bf16[2,256,1024]{2,1,0:T(8,128)(2,1)S(1)} %get-tuple-element.68.y_ref) | copy-start | bytes 3145732
  18.4 11.7 %copy-start.4 = (f32[2,256,1]{2,1,0:T(8,128)}, f32[2,256,1]{2,1,0:T(8,128)S(1)}, u32[]{:S(2)}) copy-start(f32[2,256,1]{2,1,0:T(8,128)S(1)} %get-tuple-element.69.r_ref) | copy-start | bytes 6148
  27.4 25.7 %collective-permute-start.2 = (bf16[256,1024]{1,0:T(8,128)(2,1)S(1)}, bf16[256,1024]{1,0:T(8,128)(2,1)S(1)}, u32[]{:S(2)}, u32[]{:S(2)}) collective-permute-start(bf16[256,1024]{1,0:T(8,128)(2,1)S(1)} %get-tuple-element.76), channel_id=1, source_target_pairs={{24,16},{0,8},{25,17},{1,9},{26,18},{2,10},{27,19},{3,11},{28,20},... | collective-permute-start | bytes 1572872 | tf_op jit(solution)/shard_map/ppermute | solution.py:455
  28.8 24.3 %collective-permute-start.3 = (bf16[256,1024]{1,0:T(8,128)(2,1)S(1)}, bf16[256,1024]{1,0:T(8,128)(2,1)S(1)}, u32[]{:S(2)}, u32[]{:S(2)}) collective-permute-start(bf16[256,1024]{1,0:T(8,128)(2,1)S(1)} %get-tuple-element.76), channel_id=1, source_target_pairs={{0,16},{1,17},{2,18},{3,19},{4,20},{5,21},{6,22},{7,23}} | collective-permute-start | bytes 1572872 | tf_op jit(solution)/shard_map/ppermute | solution.py:455
  38.9 18.3 %collective-permute-start.1 = (bf16[256,1024]{1,0:T(8,128)(2,1)S(1)}, bf16[256,1024]{1,0:T(8,128)(2,1)S(1)}, u32[]{:S(2)}, u32[]{:S(2)}) collective-permute-start(bf16[256,1024]{1,0:T(8,128)(2,1)S(1)} %get-tuple-element.75), channel_id=1, source_target_pairs={{24,16},{0,8},{25,17},{1,9},{26,18},{2,10},{27,19},{3,11},{28,20},... | collective-permute-start | bytes 1572872 | tf_op jit(solution)/shard_map/ppermute | solution.py:455
  40.2 20.9 %collective-permute-start.6 = (bf16[256,1024]{1,0:T(8,128)(2,1)S(1)}, bf16[256,1024]{1,0:T(8,128)(2,1)S(1)}, u32[]{:S(2)}, u32[]{:S(2)}) collective-permute-start(bf16[256,1024]{1,0:T(8,128)(2,1)S(1)} %get-tuple-element.75), channel_id=1, source_target_pairs={{0,16},{1,17},{2,18},{3,19},{4,20},{5,21},{6,22},{7,23}} | collective-permute-start | bytes 1572872 | tf_op jit(solution)/shard_map/ppermute | solution.py:455
  41.6 11.5 %copy-start.3 = (bf16[2,256,1024]{2,1,0:T(8,128)(2,1)S(1)}, bf16[2,256,1024]{2,1,0:T(8,128)(2,1)}, u32[]{:S(2)}) copy-start(bf16[2,256,1024]{2,1,0:T(8,128)(2,1)} %copy-done.2) | copy-start | bytes 3145732
  41.6 11.5 %copy-start.5 = (f32[2,256,1]{2,1,0:T(8,128)S(1)}, f32[2,256,1]{2,1,0:T(8,128)}, u32[]{:S(2)}) copy-start(f32[2,256,1]{2,1,0:T(8,128)} %copy-done.4) | copy-start | bytes 6148
  53.1 12.6 %copy-start = (bf16[2,256,2048]{2,1,0:T(8,128)(2,1)}, bf16[2,256,2048]{2,1,0:T(8,128)(2,1)S(1)}, u32[]{:S(2)}) copy-start(bf16[2,256,2048]{2,1,0:T(8,128)(2,1)S(1)} %get-tuple-element.83.slope_ref) | copy-start | bytes 6291460
  53.1 3.4 %copy-start.6 = (bf16[256,1024]{1,0:T(8,128)(2,1)}, bf16[256,1024]{1,0:T(8,128)(2,1)S(1)}, u32[]{:S(2)}) copy-start(bf16[256,1024]{1,0:T(8,128)(2,1)S(1)} %collective-permute-done.3.rest_3_) | copy-start | bytes 1572868
  56.5 3.8 %copy-start.10 = (bf16[256,1024]{1,0:T(8,128)(2,1)}, bf16[256,1024]{1,0:T(8,128)(2,1)S(1)}, u32[]{:S(2)}) copy-start(bf16[256,1024]{1,0:T(8,128)(2,1)S(1)} %get-tuple-element.99) | copy-start | bytes 1572868
  56.5 4.7 %collective-permute-start.5 = (bf16[256,1024]{1,0:T(8,128)(2,1)S(1)}, bf16[256,1024]{1,0:T(8,128)(2,1)S(1)}, u32[]{:S(2)}, u32[]{:S(2)}) collective-permute-start(bf16[256,1024]{1,0:T(8,128)(2,1)S(1)} %get-tuple-element.99), channel_id=1, source_target_pairs={{16,8},{8,16},{17,9},{9,17},{18,10},{10,18},{19,11},{11,19},{20,12... | collective-permute-start | bytes 1572872 | tf_op jit(solution)/shard_map/ppermute | solution.py:455
  60.3 4.1 %copy-start.12 = (bf16[256,1024]{1,0:T(8,128)(2,1)}, bf16[256,1024]{1,0:T(8,128)(2,1)S(1)}, u32[]{:S(2)}) copy-start(bf16[256,1024]{1,0:T(8,128)(2,1)S(1)} %get-tuple-element.102) | copy-start | bytes 1572868
  60.3 5.4 %collective-permute-start.4 = (bf16[256,1024]{1,0:T(8,128)(2,1)S(1)}, bf16[256,1024]{1,0:T(8,128)(2,1)S(1)}, u32[]{:S(2)}, u32[]{:S(2)}) collective-permute-start(bf16[256,1024]{1,0:T(8,128)(2,1)S(1)} %get-tuple-element.102), channel_id=1, source_target_pairs={{16,8},{8,16},{17,9},{9,17},{18,10},{10,18},{19,11},{11,19},{20,12... | collective-permute-start | bytes 1572872 | tf_op jit(solution)/shard_map/ppermute | solution.py:455
  61.2 3.2 %copy-start.8 = (bf16[256,1024]{1,0:T(8,128)(2,1)}, bf16[256,1024]{1,0:T(8,128)(2,1)S(1)}, u32[]{:S(2)}) copy-start(bf16[256,1024]{1,0:T(8,128)(2,1)S(1)} %collective-permute-done.6.rest_2_) | copy-start | bytes 1572868
  64.4 26.0 %collective-permute-start.8 = (bf16[256,1024]{1,0:T(8,128)(2,1)}, bf16[256,1024]{1,0:T(8,128)(2,1)S(1)}, u32[]{:S(2)}, u32[]{:S(2)}) collective-permute-start(bf16[256,1024]{1,0:T(8,128)(2,1)} %get-tuple-element.90), channel_id=1, source_target_pairs={{8,0},{9,1},{10,2},{11,3},{12,4},{13,5},{14,6},{15,7}} | collective-permute-start | bytes 1572872 | tf_op jit(solution)/shard_map/ppermute | solution.py:455
  65.7 7.1 %copy-start.15 = (s32[4]{0:T(128)S(1)}, s32[4]{0:T(128)}, u32[]{:S(2)}) copy-start(s32[4]{0:T(128)} %constant.65.clone.info_ref) | copy-start | bytes 52
  69.0 31.9 %collective-permute-start.7 = (bf16[256,1024]{1,0:T(8,128)(2,1)}, bf16[256,1024]{1,0:T(8,128)(2,1)S(1)}, u32[]{:S(2)}, u32[]{:S(2)}) collective-permute-start(bf16[256,1024]{1,0:T(8,128)(2,1)} %get-tuple-element.89), channel_id=1, source_target_pairs={{8,0},{9,1},{10,2},{11,3},{12,4},{13,5},{14,6},{15,7}} | collective-permute-start | bytes 1572872 | tf_op jit(solution)/shard_map/ppermute | solution.py:455
  70.2 37.4 %collective-permute-start.10 = (bf16[256,1024]{1,0:T(8,128)(2,1)}, bf16[256,1024]{1,0:T(8,128)(2,1)S(1)}, u32[]{:S(2)}, u32[]{:S(2)}) collective-permute-start(bf16[256,1024]{1,0:T(8,128)(2,1)} %get-tuple-element.89), channel_id=1, source_target_pairs={{16,0},{17,1},{18,2},{19,3},{20,4},{21,5},{22,6},{23,7}} | collective-permute-start | bytes 1572872 | tf_op jit(solution)/shard_map/ppermute | solution.py:455
  71.5 40.3 %collective-permute-start.9 = (bf16[256,1024]{1,0:T(8,128)(2,1)}, bf16[256,1024]{1,0:T(8,128)(2,1)S(1)}, u32[]{:S(2)}, u32[]{:S(2)}) collective-permute-start(bf16[256,1024]{1,0:T(8,128)(2,1)} %get-tuple-element.90), channel_id=1, source_target_pairs={{16,0},{17,1},{18,2},{19,3},{20,4},{21,5},{22,6},{23,7}} | collective-permute-start | bytes 1572872 | tf_op jit(solution)/shard_map/ppermute | solution.py:455
  72.9 17.5 %copy-start.1 = (bf16[2,256,2048]{2,1,0:T(8,128)(2,1)S(1)}, bf16[2,256,2048]{2,1,0:T(8,128)(2,1)}, u32[]{:S(2)}) copy-start(bf16[2,256,2048]{2,1,0:T(8,128)(2,1)} %copy-done) | copy-start | bytes 6291460
  100.8 11.1 %copy-start.7 = (bf16[256,1024]{1,0:T(8,128)(2,1)S(1)}, bf16[256,1024]{1,0:T(8,128)(2,1)}, u32[]{:S(2)}) copy-start(bf16[256,1024]{1,0:T(8,128)(2,1)} %copy-done.6) | copy-start | bytes 1572868
  100.8 11.1 %copy-start.9 = (bf16[256,1024]{1,0:T(8,128)(2,1)S(1)}, bf16[256,1024]{1,0:T(8,128)(2,1)}, u32[]{:S(2)}) copy-start(bf16[256,1024]{1,0:T(8,128)(2,1)} %copy-done.8) | copy-start | bytes 1572868
  100.8 11.1 %copy-start.11 = (bf16[256,1024]{1,0:T(8,128)(2,1)S(1)}, bf16[256,1024]{1,0:T(8,128)(2,1)}, u32[]{:S(2)}) copy-start(bf16[256,1024]{1,0:T(8,128)(2,1)} %copy-done.10) | copy-start | bytes 1572868
  100.8 11.1 %copy-start.13 = (bf16[256,1024]{1,0:T(8,128)(2,1)S(1)}, bf16[256,1024]{1,0:T(8,128)(2,1)}, u32[]{:S(2)}) copy-start(bf16[256,1024]{1,0:T(8,128)(2,1)} %copy-done.12) | copy-start | bytes 1572868
  125.4 6.7 %collective-permute-start.12 = (bf16[4,256,1024]{2,1,0:T(8,128)(2,1)}, bf16[4,256,1024]{2,1,0:T(8,128)(2,1)S(1)}, u32[]{:S(2)}, u32[]{:S(2)}) collective-permute-start(bf16[4,256,1024]{2,1,0:T(8,128)(2,1)} %weights.4.refs_10_), channel_id=1, source_target_pairs={{0,1},{1,0},{2,3},{3,2},{4,5},{5,4},{6,7},{7,6},{8,9},{9,8},{10,11... | collective-permute-start | bytes 6291464 | tf_op jit(solution)/shard_map/ppermute | solution.py:555
  131.6 14.6 %collective-permute-start.11 = (bf16[4,128,2048]{2,1,0:T(8,128)(2,1)}, bf16[4,128,2048]{2,1,0:T(8,128)(2,1)}, u32[]{:S(2)}, u32[]{:S(2)}) collective-permute-start(bf16[4,128,2048]{2,1,0:T(8,128)(2,1)} %weights.5.refs_5_), channel_id=1, source_target_pairs={{0,1},{1,0},{2,3},{3,2},{4,5},{5,4},{6,7},{7,6},{8,9},{9,8},{10,11... | collective-permute-start | bytes 6291464 | tf_op jit(solution)/shard_map/ppermute | solution.py:557
  142.0 15.5 %collective-permute-start.20 = (bf16[256,1024]{1,0:T(8,128)(2,1)}, bf16[256,1024]{1,0:T(8,128)(2,1)S(1)}, u32[]{:S(2)}, u32[]{:S(2)}) collective-permute-start(bf16[256,1024]{1,0:T(8,128)(2,1)} %get-tuple-element.119), channel_id=1, source_target_pairs={{0,2},{1,3},{8,10},{9,11},{16,18},{17,19},{24,26},{25,27}} | collective-permute-start | bytes 1572872 | tf_op jit(solution)/shard_map/ppermute | solution.py:571
  145.5 12.0 %collective-permute-start.21 = (bf16[256,1024]{1,0:T(8,128)(2,1)S(1)}, bf16[256,1024]{1,0:T(8,128)(2,1)S(1)}, u32[]{:S(2)}, u32[]{:S(2)}) collective-permute-start(bf16[256,1024]{1,0:T(8,128)(2,1)S(1)} %get-tuple-element.120), channel_id=1, source_target_pairs={{7,5},{6,4},{15,13},{14,12},{23,21},{22,20},{31,29},{30,28}} | collective-permute-start | bytes 1572872 | tf_op jit(solution)/shard_map/ppermute | solution.py:571
  155.4 13.9 %collective-permute-start.13 = (bf16[128,2048]{1,0:T(8,128)(2,1)}, bf16[128,2048]{1,0:T(8,128)(2,1)S(1)}, u32[]{:S(2)}, u32[]{:S(2)}) collective-permute-start(bf16[128,2048]{1,0:T(8,128)(2,1)} %get-tuple-element.112), channel_id=1, source_target_pairs={{0,2},{1,3},{8,10},{9,11},{16,18},{17,19},{24,26},{25,27}} | collective-permute-start | bytes 1572872 | tf_op jit(solution)/shard_map/ppermute | solution.py:571
  156.8 12.6 %collective-permute-start.14 = (bf16[128,2048]{1,0:T(8,128)(2,1)S(1)}, bf16[128,2048]{1,0:T(8,128)(2,1)S(1)}, u32[]{:S(2)}, u32[]{:S(2)}) collective-permute-start(bf16[128,2048]{1,0:T(8,128)(2,1)S(1)} %get-tuple-element.113), channel_id=1, source_target_pairs={{7,5},{6,4},{15,13},{14,12},{23,21},{22,20},{31,29},{30,28}} | collective-permute-start | bytes 1572872 | tf_op jit(solution)/shard_map/ppermute | solution.py:571
  161.5 19.1 %collective-permute-start.22 = (bf16[256,1024]{1,0:T(8,128)(2,1)}, bf16[256,1024]{1,0:T(8,128)(2,1)S(1)}, u32[]{:S(2)}, u32[]{:S(2)}) collective-permute-start(bf16[256,1024]{1,0:T(8,128)(2,1)} %get-tuple-element.121), channel_id=1, source_target_pairs={{0,2},{1,3},{2,4},{3,5},{8,10},{9,11},{10,12},{11,13},{16,18},{17,... | collective-permute-start | bytes 1572872 | tf_op jit(solution)/shard_map/ppermute | solution.py:571
  165.5 15.1 %collective-permute-start.23 = (bf16[256,1024]{1,0:T(8,128)(2,1)S(1)}, bf16[256,1024]{1,0:T(8,128)(2,1)S(1)}, u32[]{:S(2)}, u32[]{:S(2)}) collective-permute-start(bf16[256,1024]{1,0:T(8,128)(2,1)S(1)} %get-tuple-element.122), channel_id=1, source_target_pairs={{7,5},{6,4},{5,3},{4,2},{15,13},{14,12},{13,11},{12,10},{23,21},{2... | collective-permute-start | bytes 1572872 | tf_op jit(solution)/shard_map/ppermute | solution.py:571
  171.9 19.9 %collective-permute-start.15 = (bf16[128,2048]{1,0:T(8,128)(2,1)}, bf16[128,2048]{1,0:T(8,128)(2,1)S(1)}, u32[]{:S(2)}, u32[]{:S(2)}) collective-permute-start(bf16[128,2048]{1,0:T(8,128)(2,1)} %get-tuple-element.114), channel_id=1, source_target_pairs={{0,2},{1,3},{2,4},{3,5},{8,10},{9,11},{10,12},{11,13},{16,18},{17,... | collective-permute-start | bytes 1572872 | tf_op jit(solution)/shard_map/ppermute | solution.py:571
  176.2 15.6 %collective-permute-start.16 = (bf16[128,2048]{1,0:T(8,128)(2,1)S(1)}, bf16[128,2048]{1,0:T(8,128)(2,1)S(1)}, u32[]{:S(2)}, u32[]{:S(2)}) collective-permute-start(bf16[128,2048]{1,0:T(8,128)(2,1)S(1)} %get-tuple-element.115), channel_id=1, source_target_pairs={{7,5},{6,4},{5,3},{4,2},{15,13},{14,12},{13,11},{12,10},{23,21},{2... | collective-permute-start | bytes 1572872 | tf_op jit(solution)/shard_map/ppermute | solution.py:571
  183.4 19.5 %collective-permute-start.24 = (bf16[256,1024]{1,0:T(8,128)(2,1)S(1)}, bf16[256,1024]{1,0:T(8,128)(2,1)S(1)}, u32[]{:S(2)}, u32[]{:S(2)}) collective-permute-start(bf16[256,1024]{1,0:T(8,128)(2,1)S(1)} %get-tuple-element.123), channel_id=1, source_target_pairs={{0,2},{1,3},{2,4},{3,5},{4,6},{5,7},{8,10},{9,11},{10,12},{11,13},... | collective-permute-start | bytes 1572872 | tf_op jit(solution)/shard_map/ppermute | solution.py:571
  188.3 14.6 %collective-permute-start.25 = (bf16[256,1024]{1,0:T(8,128)(2,1)S(1)}, bf16[256,1024]{1,0:T(8,128)(2,1)S(1)}, u32[]{:S(2)}, u32[]{:S(2)}) collective-permute-start(bf16[256,1024]{1,0:T(8,128)(2,1)S(1)} %get-tuple-element.124), channel_id=1, source_target_pairs={{7,5},{6,4},{5,3},{4,2},{3,1},{2,0},{15,13},{14,12},{13,11},{12,10... | collective-permute-start | bytes 1572872 | tf_op jit(solution)/shard_map/ppermute | solution.py:571
  193.8 19.6 %collective-permute-start.17 = (bf16[128,2048]{1,0:T(8,128)(2,1)S(1)}, bf16[128,2048]{1,0:T(8,128)(2,1)S(1)}, u32[]{:S(2)}, u32[]{:S(2)}) collective-permute-start(bf16[128,2048]{1,0:T(8,128)(2,1)S(1)} %get-tuple-element.116), channel_id=1, source_target_pairs={{0,2},{1,3},{2,4},{3,5},{4,6},{5,7},{8,10},{9,11},{10,12},{11,13},... | collective-permute-start | bytes 1572872 | tf_op jit(solution)/shard_map/ppermute | solution.py:571
  198.3 15.0 %collective-permute-start.18 = (bf16[128,2048]{1,0:T(8,128)(2,1)S(1)}, bf16[128,2048]{1,0:T(8,128)(2,1)S(1)}, u32[]{:S(2)}, u32[]{:S(2)}) collective-permute-start(bf16[128,2048]{1,0:T(8,128)(2,1)S(1)} %get-tuple-element.117), channel_id=1, source_target_pairs={{7,5},{6,4},{5,3},{4,2},{3,1},{2,0},{15,13},{14,12},{13,11},{12,10... | collective-permute-start | bytes 1572872 | tf_op jit(solution)/shard_map/ppermute | solution.py:571
  207.1 14.3 %collective-permute-start.26 = (bf16[256,1024]{1,0:T(8,128)(2,1)S(1)}, bf16[256,1024]{1,0:T(8,128)(2,1)S(1)}, u32[]{:S(2)}, u32[]{:S(2)}) collective-permute-start(bf16[256,1024]{1,0:T(8,128)(2,1)S(1)} %get-tuple-element.125), channel_id=1, source_target_pairs={{0,24},{8,16},{16,8},{24,0},{1,25},{9,17},{17,9},{25,1},{2,26},{10... | collective-permute-start | bytes 1572872 | tf_op jit(solution)/shard_map/ppermute | solution.py:577
  216.3 15.2 %collective-permute-start.19 = (bf16[128,2048]{1,0:T(8,128)(2,1)S(1)}, bf16[128,2048]{1,0:T(8,128)(2,1)S(1)}, u32[]{:S(2)}, u32[]{:S(2)}) collective-permute-start(bf16[128,2048]{1,0:T(8,128)(2,1)S(1)} %get-tuple-element.118), channel_id=1, source_target_pairs={{0,24},{8,16},{16,8},{24,0},{1,25},{9,17},{17,9},{25,1},{2,26},{10... | collective-permute-start | bytes 1572872 | tf_op jit(solution)/shard_map/ppermute | solution.py:577

commit v8 on v7

--- a/solution.py
+++ b/solution.py
@@ -160,23 +160,21 @@
             e = e_ref[...].reshape(rows, model).astype(f32)
             grad = sum_gradient(e, y_ref[0].astype(f32), r_ref[0])
             whole[...] = grad
-            low[...] = grad.astype(bf16)
+            low[...] = grad.T.astype(bf16)
             sum_ref[0] = grad.astype(bf16)
 
         @pl.when(active)
         def _():
-            grad_pre = (
-                dot(low[...], q_ref[0, 0], ((1,), (1,))) * slope_ref[0].astype(f32)
-            ).astype(bf16)
-            pre_ref[0] = grad_pre
+            grad_pre = dot(q_ref[0, 0], low[...], ((1,), (0,))) * slope_ref[0].astype(f32).T
+            pre_ref[0] = grad_pre.T.astype(bf16)
 
             @pl.when(info[base + 3] > 0)
             def _():
-                part = dot(grad_pre, p_ref[0, 0], ((1,), (1,)))
+                part = dot(p_ref[0, 0], grad_pre.astype(bf16), ((1,), (0,)))
 
                 @pl.when(j == 0)
                 def _():
-                    total[...] = whole[...] + part
+                    total[...] = part
 
                 @pl.when(j > 0)
                 def _():
@@ -184,7 +182,7 @@
 
                 @pl.when(j == pl.num_programs(0) - 1)
                 def _():
-                    out_ref[...] = total[...].astype(bf16)
+                    out_ref[...] = (whole[...] + total[...].T).astype(bf16)
 
     if recv is None:
         e_spec = pl.BlockSpec((1, per, tokens, model), lambda j, i: (i[base + 1], group, 0, 0))
@@ -223,8 +221,8 @@
             ],
             scratch_shapes=[
                 pltpu.VMEM((rows, model), f32),
-                pltpu.VMEM((rows, model), bf16),
-                pltpu.VMEM((rows, model), f32),
+                pltpu.VMEM((model, rows), bf16),
+                pltpu.VMEM((model, rows), f32),
             ],
         ),
         out_shape=[

time: 234 us -> 235 us (level)
  no operation moved by 1% of the time
where the time goes in v8:
time: 235 us; the launch traced here: 234 us
  Pallas kernels  137 us (58%)
  waiting for transfers between devices  46.6 us (20%)
  starting transfers between devices  44.2 us (19%)
  other arithmetic  2.67 us (1%)
  local copies, waits for them, and re-layouts  2.54 us (1%)
    pallas_call x8, Pallas kernels, chain_step(): pl.pallas_call(body, grid_spec=pltpu.PrefetchScalarGridSpec(num_scalar_pr...  45.1 us
    pallas_call x3, Pallas kernels, forward(): pl.pallas_call(body, grid_spec=pltpu.PrefetchScalarGridSpec(num_scalar_pr...  34.4 us
    pallas_call x4, Pallas kernels, weight_gradient(): pl.pallas_call(body, grid_spec=pltpu.PrefetchScalarGridSpec(num_scalar_pr...  25 us
    ppermute x6, starting transfers between devices, on_device(): lax.ppermute(to_right, 'dp', right)  22.5 us
    ppermute x6, waiting for transfers between devices, on_device(): lax.ppermute(to_right, 'dp', right)  18.3 us
    pallas_call x6, Pallas kernels, fold(): pl.pallas_call(body, grid_spec=pltpu.PrefetchScalarGridSpec(num_scalar_pr...  17.7 us
    ppermute x2, waiting for transfers between devices, finish(): lax.ppermute(fresh, 'section', [(i, last - i) for i in range(sections)])  14.1 us
    ppermute x10, waiting for transfers between devices, hop(): return lax.ppermute(value, 'section', pairs) if pairs else None  14.1 us
  transfers between devices with their start and end apart: 27, of which 10 were waited for; matrix products, arithmetic and copies ran while one was open for 1% of the time, Pallas kernels for 53%

profile of v8, /device:TPU:0, one launch (start us, length us, event | category | flops | bytes accessed | tf_op | source)
XLA Modules:
  0.0 233.8 jit_solution(18419777699998442728)
XLA Ops:
  0.7 2.3 slice_bitcast_fusion
  2.9 3.9 %collective-permute-start = (bf16[4,128,1024]{2,1,0:T(8,128)(2,1)}, bf16[4,128,1024]{2,1,0:T(8,128)(2,1)}, u32[]{:S(2)}, u32[]{:S(2)}) collective-permute-start(bf16[4,128,1024]{2,1,0:T(8,128)(2,1)} %slice_bitcast_fusion), channel_id=1, source_target_pairs={{0,24},{8,16},{16,8},{24,0},{1,25},{9,17},{17,9},{25,1},{2,26},{10... | collective-permute-start | bytes 3145736 | tf_op jit(solution)/shard_map/ppermute | solution.py:455
  6.9 11.5 %forward.3 = (bf16[2,2,256,1024]{3,2,1,0:T(8,128)(2,1)}, bf16[2,2,256,2048]{3,2,1,0:T(8,128)(2,1)}, bf16[2,256,2048]{2,1,0:T(8,128)(2,1)S(1)}, bf16[2,256,1024]{2,1,0:T(8,128)(2,1)S(1)}, f32[2,256,1]{2,1,0:T(8,128)S(1)}) custom-call(s32[4]{0:T(128)S(1)} %stack.93.info_ref, s32[2,4]{1,0:T(2,128)S(1)} %copy-done.14, bf16[2,1,4,128,1024]{4,3,2,1,0:T(8,128)(2,1)} %refs_3_.3, ...), custom_call_target="tpu_custom_call" | custom-call | flops 1000 | bytes 1000 | tf_op jit(solution)/shard_map/forward/pallas_call | solution.py:118
  18.6 9.2 %chain.8 = (bf16[256,1024]{1,0:T(8,128)(2,1)S(1)}, bf16[3,256,2048]{2,1,0:T(8,128)(2,1)}, bf16[3,256,1024]{2,1,0:T(8,128)(2,1)}) custom-call(s32[32]{0:T(128)S(1)} %reshape.15.info, bf16[2,4,128,1024]{3,2,1,0:T(8,128)(2,1)} %refs_2_.5, bf16[2,256,1024]{2,1,0:T(8,128)(2,1)S(1)} %get-tuple-element.68.y_ref, f32[2,256,1]{2,1,0:T(8,128)S(1)} %get-tuple-element.69.r_ref, ...), custom_call_target="tpu_custom_call" | custom-call | flops 1000 | bytes 1000 | tf_op jit(solution)/shard_map/chain/pallas_call | solution.py:211
  27.8 1.3 collective-permute-start.2
  29.1 1.3 collective-permute-start.3
  30.5 9.2 %chain.9 = (bf16[256,1024]{1,0:T(8,128)(2,1)S(1)}, bf16[3,256,2048]{2,1,0:T(8,128)(2,1)}, bf16[3,256,1024]{2,1,0:T(8,128)(2,1)}) custom-call(s32[32]{0:T(128)S(1)} %reshape.15.info, bf16[2,4,128,1024]{3,2,1,0:T(8,128)(2,1)} %refs_2_.5, bf16[2,256,1024]{2,1,0:T(8,128)(2,1)S(1)} %get-tuple-element.68.y_ref, ...), custom_call_target="tpu_custom_call", output_to_operand_aliasing={{1}: (7, {}), {2}: (8, {})} | custom-call | flops 1000 | bytes 1000 | tf_op jit(solution)/shard_map/chain/pallas_call | solution.py:211
  39.6 1.3 collective-permute-start.1
  40.9 1.3 collective-permute-start.6
  42.3 11.5 %forward.4 = (bf16[2,2,256,1024]{3,2,1,0:T(8,128)(2,1)}, bf16[2,2,256,2048]{3,2,1,0:T(8,128)(2,1)}, bf16[2,256,2048]{2,1,0:T(8,128)(2,1)S(1)}, bf16[2,256,1024]{2,1,0:T(8,128)(2,1)S(1)}, f32[2,256,1]{2,1,0:T(8,128)S(1)}) custom-call(s32[4]{0:T(128)S(1)} %stack.92.info_ref, s32[2,4]{1,0:T(2,128)S(1)} %copy-done.14, ...), custom_call_target="tpu_custom_call", output_to_operand_aliasing={{0}: (8, {}), {1}: (9, {})} | custom-call | flops 1000 | bytes 1000 | tf_op jit(solution)/shard_map/forward/pallas_call | solution.py:118
  53.8 3.3 %chain.10 = (bf16[256,1024]{1,0:T(8,128)(2,1)S(1)}, bf16[3,256,2048]{2,1,0:T(8,128)(2,1)}, bf16[3,256,1024]{2,1,0:T(8,128)(2,1)}) custom-call(s32[32]{0:T(128)S(1)} %reshape.15.info, bf16[256,1024]{1,0:T(8,128)(2,1)S(1)} %collective-permute-done.2.e_ref, bf16[2,256,1024]{2,1,0:T(8,128)(2,1)S(1)} %copy-done.3, ...), custom_call_target="tpu_custom_call", output_to_operand_aliasing={{1}: (7, {}), {2}: (8, {})} | custom-call | flops 1000 | bytes 1000 | tf_op jit(solution)/shard_map/chain/pallas_call | solution.py:211
  58.1 3.1 %chain.11 = (bf16[256,1024]{1,0:T(8,128)(2,1)S(1)}, bf16[3,256,2048]{2,1,0:T(8,128)(2,1)}, bf16[3,256,1024]{2,1,0:T(8,128)(2,1)}) custom-call(s32[32]{0:T(128)S(1)} %reshape.15.info, bf16[256,1024]{1,0:T(8,128)(2,1)S(1)} %collective-permute-done.1.e_ref, bf16[2,256,1024]{2,1,0:T(8,128)(2,1)S(1)} %copy-done.3, ...), custom_call_target="tpu_custom_call", output_to_operand_aliasing={{1}: (7, {}), {2}: (8, {})} | custom-call | flops 1000 | bytes 1000 | tf_op jit(solution)/shard_map/chain/pallas_call | solution.py:211
  61.9 3.2 %chain.12 = (bf16[256,1024]{1,0:T(8,128)(2,1)}, bf16[3,256,2048]{2,1,0:T(8,128)(2,1)}, bf16[3,256,1024]{2,1,0:T(8,128)(2,1)}) custom-call(s32[32]{0:T(128)S(1)} %reshape.15.info, bf16[256,1024]{1,0:T(8,128)(2,1)S(1)} %collective-permute-done.5.e_ref, ...), custom_call_target="tpu_custom_call", output_to_operand_aliasing={{1}: (7, {}), {2}: (8, {})} | custom-call | flops 1000 | bytes 1000 | tf_op jit(solution)/shard_map/chain/pallas_call | solution.py:211
  66.4 3.2 %chain.13 = (bf16[256,1024]{1,0:T(8,128)(2,1)}, bf16[3,256,2048]{2,1,0:T(8,128)(2,1)}, bf16[3,256,1024]{2,1,0:T(8,128)(2,1)}) custom-call(s32[32]{0:T(128)S(1)} %reshape.15.info, bf16[256,1024]{1,0:T(8,128)(2,1)S(1)} %collective-permute-done.4.e_ref, ...), custom_call_target="tpu_custom_call", output_to_operand_aliasing={{1}: (7, {}), {2}: (8, {})} | custom-call | flops 1000 | bytes 1000 | tf_op jit(solution)/shard_map/chain/pallas_call | solution.py:211
  71.0 1.3 collective-permute-start.10
  72.3 1.3 collective-permute-start.9
  73.6 11.5 %forward.5 = (bf16[1,2,256,1024]{3,2,1,0:T(8,128)(2,1)}, bf16[1,2,256,2048]{3,2,1,0:T(8,128)(2,1)}, bf16[2,256,2048]{2,1,0:T(8,128)(2,1)S(1)}, bf16[2,256,1024]{2,1,0:T(8,128)(2,1)S(1)}, f32[2,256,1]{2,1,0:T(8,128)S(1)}) custom-call(s32[4]{0:T(128)S(1)} %copy-done.15, s32[2,4]{1,0:T(2,128)S(1)} %copy-done.14, ...), custom_call_target="tpu_custom_call" | custom-call | flops 1000 | bytes 1000 | tf_op jit(solution)/shard_map/forward/pallas_call | solution.py:118
  85.1 5.6 %collective-permute-done.8.e_ref = bf16[256,1024]{1,0:T(8,128)(2,1)S(1)} collective-permute-done((bf16[256,1024]{1,0:T(8,128)(2,1)}, bf16[256,1024]{1,0:T(8,128)(2,1)S(1)}, u32[]{:S(2)}, u32[]{:S(2)}) %collective-permute-start.8) | collective-permute-done | bytes 524320 | tf_op jit(solution)/shard_map/ppermute | solution.py:453
  90.7 6.9 %chain.14 = (bf16[256,1024]{1,0:T(8,128)(2,1)}, bf16[3,256,2048]{2,1,0:T(8,128)(2,1)}, bf16[3,256,1024]{2,1,0:T(8,128)(2,1)}) custom-call(s32[32]{0:T(128)S(1)} %reshape.15.info, bf16[256,1024]{1,0:T(8,128)(2,1)S(1)} %collective-permute-done.8.e_ref, ...), custom_call_target="tpu_custom_call", output_to_operand_aliasing={{1}: (7, {}), {2}: (8, {})} | custom-call | flops 1000 | bytes 1000 | tf_op jit(solution)/shard_map/chain/pallas_call | solution.py:211
  97.6 4.1 %collective-permute-done.7.e_ref = bf16[256,1024]{1,0:T(8,128)(2,1)S(1)} collective-permute-done((bf16[256,1024]{1,0:T(8,128)(2,1)}, bf16[256,1024]{1,0:T(8,128)(2,1)S(1)}, u32[]{:S(2)}, u32[]{:S(2)}) %collective-permute-start.7) | collective-permute-done | bytes 524320 | tf_op jit(solution)/shard_map/ppermute | solution.py:453
  101.7 7.0 %chain.15 = (bf16[256,1024]{1,0:T(8,128)(2,1)}, bf16[3,256,2048]{2,1,0:T(8,128)(2,1)}, bf16[3,256,1024]{2,1,0:T(8,128)(2,1)}) custom-call(s32[32]{0:T(128)S(1)} %reshape.15.info, bf16[256,1024]{1,0:T(8,128)(2,1)S(1)} %collective-permute-done.7.e_ref, ...), custom_call_target="tpu_custom_call", output_to_operand_aliasing={{1}: (7, {}), {2}: (8, {})} | custom-call | flops 1000 | bytes 1000 | tf_op jit(solution)/shard_map/chain/pallas_call | solution.py:211
  108.7 4.4 %collective-permute-done.9 = bf16[256,1024]{1,0:T(8,128)(2,1)S(1)} collective-permute-done((bf16[256,1024]{1,0:T(8,128)(2,1)}, bf16[256,1024]{1,0:T(8,128)(2,1)S(1)}, u32[]{:S(2)}, u32[]{:S(2)}) %collective-permute-start.9) | collective-permute-done | bytes 524320 | tf_op jit(solution)/shard_map/ppermute | solution.py:453
  113.3 7.3 %home.1 = (bf16[2,256,2048]{2,1,0:T(8,128)(2,1)}, bf16[2,256,1024]{2,1,0:T(8,128)(2,1)}) custom-call(s32[1]{0:T(128)} %bitcast.9.info, bf16[256,1024]{1,0:T(8,128)(2,1)S(1)} %get-tuple-element.141.refs_0_, bf16[256,1024]{1,0:T(8,128)(2,1)S(1)} %get-tuple-element.140.refs_1_, bf16[2,4,128,1024]{3,2,1,0:T(8,128)(2,1)} %refs_2_.5, ...), custom_call_target="tpu_custom_call" | custom-call | flops 1000 | bytes 1000 | tf_op jit(solution)/shard_map/home/pallas_call | solution.py:265
  120.6 6.0 %weights.4.refs_10_ = bf16[4,256,1024]{2,1,0:T(8,128)(2,1)} custom-call(s32[1]{0:T(128)} %bitcast.10.info, bf16[2,2,256,2048]{3,2,1,0:T(8,128)(2,1)} %get-tuple-element.108.refs_0_, bf16[3,256,1024]{2,1,0:T(8,128)(2,1)} %get-tuple-element.109.refs_1_, bf16[1,2,256,2048]{3,2,1,0:T(8,128)(2,1)} %get-tuple-element.110.refs_2_, ...), custom_call_target="tpu_custom_call" | custom-call | flops 1000 | bytes 1000 | tf_op jit(solution)/shard_map/weights/pallas_call | solution.py:362
  126.6 6.2 %weights.5.refs_5_ = bf16[4,128,2048]{2,1,0:T(8,128)(2,1)} custom-call(s32[1]{0:T(128)} %bitcast.10.info, bf16[2,2,256,1024]{3,2,1,0:T(8,128)(2,1)} %get-tuple-element.74.rest_2_.refs_0_.refs_1_.refs_2_.refs_3_, bf16[2,2,256,1024]{3,2,1,0:T(8,128)(2,1)} %get-tuple-element.74.rest_2_.refs_0_.refs_1_.refs_2_.refs_3_, ...), custom_call_target="tpu_custom_call" | custom-call | flops 1000 | bytes 1000 | tf_op jit(solution)/shard_map/weights/pallas_call | solution.py:362
  133.3 6.0 %weights.6.refs_11_.refs_0_.refs_1_.part_ref = bf16[4,256,1024]{2,1,0:T(8,128)(2,1)} custom-call(s32[1]{0:T(128)} %bitcast.2.info, bf16[2,2,256,2048]{3,2,1,0:T(8,128)(2,1)} %get-tuple-element.108.refs_0_, bf16[3,256,1024]{2,1,0:T(8,128)(2,1)} %get-tuple-element.109.refs_1_, bf16[1,2,256,2048]{3,2,1,0:T(8,128)(2,1)} %get-tuple-element.110.refs_2_, ...), custom_call_target="tpu_custom_call" | custom-call | flops 1000 | bytes 1000 | tf_op jit(solution)/shard_map/weights/pallas_call | solution.py:362
  139.3 3.9 %fold.9 = (bf16[256,1024]{1,0:T(8,128)(2,1)}, bf16[256,1024]{1,0:T(8,128)(2,1)S(1)}) custom-call(s32[2]{0:T(128)S(1)} %pad_add_fusion.4.info, bf16[4,256,1024]{2,1,0:T(8,128)(2,1)} %weights.6.refs_11_.refs_0_.refs_1_.part_ref, bf16[4,256,1024]{2,1,0:T(8,128)(2,1)} %weights.6.refs_11_.refs_0_.refs_1_.part_ref), custom_call_target="tpu_custom_call" | custom-call | flops 1000 | bytes 1000 | tf_op jit(solution)/shard_map/fold/pallas_call | solution.py:386
  143.2 3.5 %collective-permute-start.20 = (bf16[256,1024]{1,0:T(8,128)(2,1)}, bf16[256,1024]{1,0:T(8,128)(2,1)S(1)}, u32[]{:S(2)}, u32[]{:S(2)}) collective-permute-start(bf16[256,1024]{1,0:T(8,128)(2,1)} %get-tuple-element.119), channel_id=1, source_target_pairs={{0,2},{1,3},{8,10},{9,11},{16,18},{17,19},{24,26},{25,27}} | collective-permute-start | bytes 1572872 | tf_op jit(solution)/shard_map/ppermute | solution.py:569
  147.4 6.7 %weights.7.refs_0_.refs_1_.part_ref = bf16[4,128,2048]{2,1,0:T(8,128)(2,1)} custom-call(s32[1]{0:T(128)} %bitcast.2.info, bf16[2,2,256,1024]{3,2,1,0:T(8,128)(2,1)} %get-tuple-element.74.rest_2_.refs_0_.refs_1_.refs_2_.refs_3_, bf16[2,2,256,1024]{3,2,1,0:T(8,128)(2,1)} %get-tuple-element.74.rest_2_.refs_0_.refs_1_.refs_2_.refs_3_, ...), custom_call_target="tpu_custom_call" | custom-call | flops 1000 | bytes 1000 | tf_op jit(solution)/shard_map/weights/pallas_call | solution.py:362
  154.2 2.5 %fold.6 = (bf16[128,2048]{1,0:T(8,128)(2,1)}, bf16[128,2048]{1,0:T(8,128)(2,1)S(1)}) custom-call(s32[2]{0:T(128)S(1)} %pad_add_fusion.4.info, bf16[4,128,2048]{2,1,0:T(8,128)(2,1)} %weights.7.refs_0_.refs_1_.part_ref, bf16[4,128,2048]{2,1,0:T(8,128)(2,1)} %weights.7.refs_0_.refs_1_.part_ref), custom_call_target="tpu_custom_call" | custom-call | flops 1000 | bytes 1000 | tf_op jit(solution)/shard_map/fold/pallas_call | solution.py:386
  156.6 1.3 collective-permute-start.13
  158.8 3.9 %fold.10 = (bf16[256,1024]{1,0:T(8,128)(2,1)}, bf16[256,1024]{1,0:T(8,128)(2,1)S(1)}) custom-call(s32[2]{0:T(128)S(1)} %pad_add_fusion.3.info, bf16[4,256,1024]{2,1,0:T(8,128)(2,1)} %weights.6.refs_11_.refs_0_.refs_1_.part_ref, bf16[4,256,1024]{2,1,0:T(8,128)(2,1)} %weights.6.refs_11_.refs_0_.refs_1_.part_ref, ...), custom_call_target="tpu_custom_call" | custom-call | flops 1000 | bytes 1000 | tf_op jit(solution)/shard_map/fold/pallas_call | solution.py:386
  162.7 4.0 %collective-permute-start.22 = (bf16[256,1024]{1,0:T(8,128)(2,1)}, bf16[256,1024]{1,0:T(8,128)(2,1)S(1)}, u32[]{:S(2)}, u32[]{:S(2)}) collective-permute-start(bf16[256,1024]{1,0:T(8,128)(2,1)} %get-tuple-element.121), channel_id=1, source_target_pairs={{0,2},{1,3},{2,4},{3,5},{8,10},{9,11},{10,12},{11,13},{16,18},{17,... | collective-permute-start | bytes 1572872 | tf_op jit(solution)/shard_map/ppermute | solution.py:569
  167.4 3.1 %collective-permute-done.13.refs_2_ = bf16[128,2048]{1,0:T(8,128)(2,1)S(1)} collective-permute-done((bf16[128,2048]{1,0:T(8,128)(2,1)}, bf16[128,2048]{1,0:T(8,128)(2,1)S(1)}, u32[]{:S(2)}, u32[]{:S(2)}) %collective-permute-start.13) | collective-permute-done | bytes 524320 | tf_op jit(solution)/shard_map/ppermute | solution.py:569
  170.5 2.6 %fold.7 = (bf16[128,2048]{1,0:T(8,128)(2,1)}, bf16[128,2048]{1,0:T(8,128)(2,1)S(1)}) custom-call(s32[2]{0:T(128)S(1)} %pad_add_fusion.3.info, bf16[4,128,2048]{2,1,0:T(8,128)(2,1)} %weights.7.refs_0_.refs_1_.part_ref, bf16[4,128,2048]{2,1,0:T(8,128)(2,1)} %weights.7.refs_0_.refs_1_.part_ref, bf16[128,2048]{1,0:T(8,128)(2,1)S(1)} %collective-permute-done.13.refs_2_, ...), custom_call_target="tpu_custom_call" | custom-call | flops 1000 | bytes 1000 | tf_op jit(solution)/shard_map/fold/pallas_call | solution.py:386
  173.1 4.3 %collective-permute-start.15 = (bf16[128,2048]{1,0:T(8,128)(2,1)}, bf16[128,2048]{1,0:T(8,128)(2,1)S(1)}, u32[]{:S(2)}, u32[]{:S(2)}) collective-permute-start(bf16[128,2048]{1,0:T(8,128)(2,1)} %get-tuple-element.114), channel_id=1, source_target_pairs={{0,2},{1,3},{2,4},{3,5},{8,10},{9,11},{10,12},{11,13},{16,18},{17,... | collective-permute-start | bytes 1572872 | tf_op jit(solution)/shard_map/ppermute | solution.py:569
  178.2 3.6 %collective-permute-done.22.refs_2_ = bf16[256,1024]{1,0:T(8,128)(2,1)S(1)} collective-permute-done((bf16[256,1024]{1,0:T(8,128)(2,1)}, bf16[256,1024]{1,0:T(8,128)(2,1)S(1)}, u32[]{:S(2)}, u32[]{:S(2)}) %collective-permute-start.22) | collective-permute-done | bytes 524320 | tf_op jit(solution)/shard_map/ppermute | solution.py:569
  181.8 2.9 %fold.11 = (bf16[256,1024]{1,0:T(8,128)(2,1)S(1)}, bf16[256,1024]{1,0:T(8,128)(2,1)S(1)}) custom-call(s32[2]{0:T(128)S(1)} %pad_add_fusion.2.info, bf16[4,256,1024]{2,1,0:T(8,128)(2,1)} %weights.6.refs_11_.refs_0_.refs_1_.part_ref, bf16[4,256,1024]{2,1,0:T(8,128)(2,1)} %weights.6.refs_11_.refs_0_.refs_1_.part_ref, ...), custom_call_target="tpu_custom_call" | custom-call | flops 1000 | bytes 1000 | tf_op jit(solution)/shard_map/fold/pallas_call | solution.py:386
  184.6 4.9 %collective-permute-start.24 = (bf16[256,1024]{1,0:T(8,128)(2,1)S(1)}, bf16[256,1024]{1,0:T(8,128)(2,1)S(1)}, u32[]{:S(2)}, u32[]{:S(2)}) collective-permute-start(bf16[256,1024]{1,0:T(8,128)(2,1)S(1)} %get-tuple-element.123), channel_id=1, source_target_pairs={{0,2},{1,3},{2,4},{3,5},{4,6},{5,7},{8,10},{9,11},{10,12},{11,13},... | collective-permute-start | bytes 1572872 | tf_op jit(solution)/shard_map/ppermute | solution.py:569
  190.8 2.2 collective-permute-done.15.refs_2_
  193.0 2.0 fold.8
  195.0 4.6 %collective-permute-start.17 = (bf16[128,2048]{1,0:T(8,128)(2,1)S(1)}, bf16[128,2048]{1,0:T(8,128)(2,1)S(1)}, u32[]{:S(2)}, u32[]{:S(2)}) collective-permute-start(bf16[128,2048]{1,0:T(8,128)(2,1)S(1)} %get-tuple-element.116), channel_id=1, source_target_pairs={{0,2},{1,3},{2,4},{3,5},{4,6},{5,7},{8,10},{9,11},{10,12},{11,13},... | collective-permute-start | bytes 1572872 | tf_op jit(solution)/shard_map/ppermute | solution.py:569
  200.9 3.2 %collective-permute-done.24.right_ref = bf16[256,1024]{1,0:T(8,128)(2,1)S(1)} collective-permute-done((bf16[256,1024]{1,0:T(8,128)(2,1)S(1)}, bf16[256,1024]{1,0:T(8,128)(2,1)S(1)}, u32[]{:S(2)}, u32[]{:S(2)}) %collective-permute-start.24) | collective-permute-done | bytes 524320 | tf_op jit(solution)/shard_map/ppermute | solution.py:569
  204.1 4.2 %update.3 = (bf16[256,1024]{1,0:T(8,128)(2,1)S(1)}, f32[1,256,1024]{2,1,0:T(8,128)}) custom-call(s32[2]{0:T(128)S(1)} %pad_add_fusion.1.info, bf16[2,1,2048,1024]{3,2,1,0:T(8,128)(2,1)} %weight_ref.3, f32[1,256,1024]{2,1,0:T(8,128)} %moment_ref.3, bf16[4,256,1024]{2,1,0:T(8,128)(2,1)} %weights.6.refs_11_.refs_0_.refs_1_.part_ref, ...), custom_call_target="tpu_custom_call" | custom-call | flops 1000 | bytes 1000 | tf_op jit(solution)/shard_map/update/pallas_call | solution.py:416
  208.3 6.2 %collective-permute-done.17.right_ref = bf16[128,2048]{1,0:T(8,128)(2,1)S(1)} collective-permute-done((bf16[128,2048]{1,0:T(8,128)(2,1)S(1)}, bf16[128,2048]{1,0:T(8,128)(2,1)S(1)}, u32[]{:S(2)}, u32[]{:S(2)}) %collective-permute-start.17) | collective-permute-done | bytes 524320 | tf_op jit(solution)/shard_map/ppermute | solution.py:569
  214.5 3.0 %update.2 = (bf16[128,2048]{1,0:T(8,128)(2,1)S(1)}, f32[1,128,2048]{2,1,0:T(8,128)}) custom-call(s32[2]{0:T(128)S(1)} %pad_add_fusion.1.info, bf16[2,1,1024,2048]{3,2,1,0:T(8,128)(2,1)} %weight_ref.2, f32[1,128,2048]{2,1,0:T(8,128)} %moment_ref.2, bf16[4,128,2048]{2,1,0:T(8,128)(2,1)} %weights.7.refs_0_.refs_1_.part_ref, ...), custom_call_target="tpu_custom_call" | custom-call | flops 1000 | bytes 1000 | tf_op jit(solution)/shard_map/update/pallas_call | solution.py:416
  217.5 5.1 %collective-permute-done.26 = bf16[256,1024]{1,0:T(8,128)(2,1)S(1)} collective-permute-done((bf16[256,1024]{1,0:T(8,128)(2,1)S(1)}, bf16[256,1024]{1,0:T(8,128)(2,1)S(1)}, u32[]{:S(2)}, u32[]{:S(2)}) %collective-permute-start.26) | collective-permute-done | bytes 524320 | tf_op jit(solution)/shard_map/ppermute | solution.py:575
  223.7 9.0 %collective-permute-done.19 = bf16[128,2048]{1,0:T(8,128)(2,1)S(1)} collective-permute-done((bf16[128,2048]{1,0:T(8,128)(2,1)S(1)}, bf16[128,2048]{1,0:T(8,128)(2,1)S(1)}, u32[]{:S(2)}, u32[]{:S(2)}) %collective-permute-start.19) | collective-permute-done | bytes 524320 | tf_op jit(solution)/shard_map/ppermute | solution.py:575
  (86 shorter events, 12.9 us)
Async XLA Ops:
  0.6 6.2 %copy-start.16 = (pred[8]{0:T(512)(128)(4,1)S(1)}, pred[8]{0:T(512)(128)(4,1)}, u32[]{:S(2)}) copy-start(pred[8]{0:T(512)(128)(4,1)} %constant.61.clone) | copy-start | bytes 28
  0.6 6.2 %copy-start.18 = (s32[8]{0:T(128)S(1)}, s32[8]{0:T(128)}, u32[]{:S(2)}) copy-start(s32[8]{0:T(128)} %constant.62.clone) | copy-start | bytes 100
  0.7 6.2 %copy-start.14 = (s32[2,4]{1,0:T(2,128)S(1)}, s32[2,4]{1,0:T(2,128)}, u32[]{:S(2)}) copy-start(s32[2,4]{1,0:T(2,128)} %plan_ref.5) | copy-start | bytes 100
  2.9 39.3 %collective-permute-start = (bf16[4,128,1024]{2,1,0:T(8,128)(2,1)}, bf16[4,128,1024]{2,1,0:T(8,128)(2,1)}, u32[]{:S(2)}, u32[]{:S(2)}) collective-permute-start(bf16[4,128,1024]{2,1,0:T(8,128)(2,1)} %slice_bitcast_fusion), channel_id=1, source_target_pairs={{0,24},{8,16},{16,8},{24,0},{1,25},{9,17},{17,9},{25,1},{2,26},{10... | collective-permute-start | bytes 3145736 | tf_op jit(solution)/shard_map/ppermute | solution.py:455
  6.9 11.5 %copy-start.19 = (pred[8]{0:T(512)(128)(4,1)S(1)}, pred[8]{0:T(512)(128)(4,1)}, u32[]{:S(2)}) copy-start(pred[8]{0:T(512)(128)(4,1)} %constant.64.clone) | copy-start | bytes 28
  6.9 11.5 %copy-start.17 = (s32[8]{0:T(128)S(1)}, s32[8]{0:T(128)}, u32[]{:S(2)}) copy-start(s32[8]{0:T(128)} %constant.63.clone) | copy-start | bytes 100
  18.4 12.1 %copy-start.2 = (bf16[2,256,1024]{2,1,0:T(8,128)(2,1)}, bf16[2,256,1024]{2,1,0:T(8,128)(2,1)S(1)}, u32[]{:S(2)}) copy-start(bf16[2,256,1024]{2,1,0:T(8,128)(2,1)S(1)} %get-tuple-element.68.y_ref) | copy-start | bytes 3145732
  18.4 12.1 %copy-start.4 = (f32[2,256,1]{2,1,0:T(8,128)}, f32[2,256,1]{2,1,0:T(8,128)S(1)}, u32[]{:S(2)}) copy-start(f32[2,256,1]{2,1,0:T(8,128)S(1)} %get-tuple-element.69.r_ref) | copy-start | bytes 6148
  27.8 26.0 %collective-permute-start.2 = (bf16[256,1024]{1,0:T(8,128)(2,1)S(1)}, bf16[256,1024]{1,0:T(8,128)(2,1)S(1)}, u32[]{:S(2)}, u32[]{:S(2)}) collective-permute-start(bf16[256,1024]{1,0:T(8,128)(2,1)S(1)} %get-tuple-element.76), channel_id=1, source_target_pairs={{24,16},{0,8},{25,17},{1,9},{26,18},{2,10},{27,19},{3,11},{28,20},... | collective-permute-start | bytes 1572872 | tf_op jit(solution)/shard_map/ppermute | solution.py:453
  29.1 24.7 %collective-permute-start.3 = (bf16[256,1024]{1,0:T(8,128)(2,1)S(1)}, bf16[256,1024]{1,0:T(8,128)(2,1)S(1)}, u32[]{:S(2)}, u32[]{:S(2)}) collective-permute-start(bf16[256,1024]{1,0:T(8,128)(2,1)S(1)} %get-tuple-element.76), channel_id=1, source_target_pairs={{0,16},{1,17},{2,18},{3,19},{4,20},{5,21},{6,22},{7,23}} | collective-permute-start | bytes 1572872 | tf_op jit(solution)/shard_map/ppermute | solution.py:453
  39.6 18.4 %collective-permute-start.1 = (bf16[256,1024]{1,0:T(8,128)(2,1)S(1)}, bf16[256,1024]{1,0:T(8,128)(2,1)S(1)}, u32[]{:S(2)}, u32[]{:S(2)}) collective-permute-start(bf16[256,1024]{1,0:T(8,128)(2,1)S(1)} %get-tuple-element.75), channel_id=1, source_target_pairs={{24,16},{0,8},{25,17},{1,9},{26,18},{2,10},{27,19},{3,11},{28,20},... | collective-permute-start | bytes 1572872 | tf_op jit(solution)/shard_map/ppermute | solution.py:453
  40.9 20.9 %collective-permute-start.6 = (bf16[256,1024]{1,0:T(8,128)(2,1)S(1)}, bf16[256,1024]{1,0:T(8,128)(2,1)S(1)}, u32[]{:S(2)}, u32[]{:S(2)}) collective-permute-start(bf16[256,1024]{1,0:T(8,128)(2,1)S(1)} %get-tuple-element.75), channel_id=1, source_target_pairs={{0,16},{1,17},{2,18},{3,19},{4,20},{5,21},{6,22},{7,23}} | collective-permute-start | bytes 1572872 | tf_op jit(solution)/shard_map/ppermute | solution.py:453
  42.3 11.5 %copy-start.3 = (bf16[2,256,1024]{2,1,0:T(8,128)(2,1)S(1)}, bf16[2,256,1024]{2,1,0:T(8,128)(2,1)}, u32[]{:S(2)}) copy-start(bf16[2,256,1024]{2,1,0:T(8,128)(2,1)} %copy-done.2) | copy-start | bytes 3145732
  42.3 11.5 %copy-start.5 = (f32[2,256,1]{2,1,0:T(8,128)S(1)}, f32[2,256,1]{2,1,0:T(8,128)}, u32[]{:S(2)}) copy-start(f32[2,256,1]{2,1,0:T(8,128)} %copy-done.4) | copy-start | bytes 6148
  53.8 12.6 %copy-start = (bf16[2,256,2048]{2,1,0:T(8,128)(2,1)}, bf16[2,256,2048]{2,1,0:T(8,128)(2,1)S(1)}, u32[]{:S(2)}) copy-start(bf16[2,256,2048]{2,1,0:T(8,128)(2,1)S(1)} %get-tuple-element.83.slope_ref) | copy-start | bytes 6291460
  53.8 3.4 %copy-start.6 = (bf16[256,1024]{1,0:T(8,128)(2,1)}, bf16[256,1024]{1,0:T(8,128)(2,1)S(1)}, u32[]{:S(2)}) copy-start(bf16[256,1024]{1,0:T(8,128)(2,1)S(1)} %collective-permute-done.3.rest_3_) | copy-start | bytes 1572868
  57.2 4.0 %copy-start.10 = (bf16[256,1024]{1,0:T(8,128)(2,1)}, bf16[256,1024]{1,0:T(8,128)(2,1)S(1)}, u32[]{:S(2)}) copy-start(bf16[256,1024]{1,0:T(8,128)(2,1)S(1)} %get-tuple-element.99) | copy-start | bytes 1572868
  57.2 4.7 %collective-permute-start.5 = (bf16[256,1024]{1,0:T(8,128)(2,1)S(1)}, bf16[256,1024]{1,0:T(8,128)(2,1)S(1)}, u32[]{:S(2)}, u32[]{:S(2)}) collective-permute-start(bf16[256,1024]{1,0:T(8,128)(2,1)S(1)} %get-tuple-element.99), channel_id=1, source_target_pairs={{16,8},{8,16},{17,9},{9,17},{18,10},{10,18},{19,11},{11,19},{20,12... | collective-permute-start | bytes 1572872 | tf_op jit(solution)/shard_map/ppermute | solution.py:453
  61.1 4.0 %copy-start.12 = (bf16[256,1024]{1,0:T(8,128)(2,1)}, bf16[256,1024]{1,0:T(8,128)(2,1)S(1)}, u32[]{:S(2)}) copy-start(bf16[256,1024]{1,0:T(8,128)(2,1)S(1)} %get-tuple-element.102) | copy-start | bytes 1572868
  61.1 5.3 %collective-permute-start.4 = (bf16[256,1024]{1,0:T(8,128)(2,1)S(1)}, bf16[256,1024]{1,0:T(8,128)(2,1)S(1)}, u32[]{:S(2)}, u32[]{:S(2)}) collective-permute-start(bf16[256,1024]{1,0:T(8,128)(2,1)S(1)} %get-tuple-element.102), channel_id=1, source_target_pairs={{16,8},{8,16},{17,9},{9,17},{18,10},{10,18},{19,11},{11,19},{20,12... | collective-permute-start | bytes 1572872 | tf_op jit(solution)/shard_map/ppermute | solution.py:453
  61.9 3.2 %copy-start.8 = (bf16[256,1024]{1,0:T(8,128)(2,1)}, bf16[256,1024]{1,0:T(8,128)(2,1)S(1)}, u32[]{:S(2)}) copy-start(bf16[256,1024]{1,0:T(8,128)(2,1)S(1)} %collective-permute-done.6.rest_2_) | copy-start | bytes 1572868
  65.1 25.5 %collective-permute-start.8 = (bf16[256,1024]{1,0:T(8,128)(2,1)}, bf16[256,1024]{1,0:T(8,128)(2,1)S(1)}, u32[]{:S(2)}, u32[]{:S(2)}) collective-permute-start(bf16[256,1024]{1,0:T(8,128)(2,1)} %get-tuple-element.90), channel_id=1, source_target_pairs={{8,0},{9,1},{10,2},{11,3},{12,4},{13,5},{14,6},{15,7}} | collective-permute-start | bytes 1572872 | tf_op jit(solution)/shard_map/ppermute | solution.py:453
  66.4 7.1 %copy-start.15 = (s32[4]{0:T(128)S(1)}, s32[4]{0:T(128)}, u32[]{:S(2)}) copy-start(s32[4]{0:T(128)} %constant.65.clone.info_ref) | copy-start | bytes 52
  69.7 32.0 %collective-permute-start.7 = (bf16[256,1024]{1,0:T(8,128)(2,1)}, bf16[256,1024]{1,0:T(8,128)(2,1)S(1)}, u32[]{:S(2)}, u32[]{:S(2)}) collective-permute-start(bf16[256,1024]{1,0:T(8,128)(2,1)} %get-tuple-element.89), channel_id=1, source_target_pairs={{8,0},{9,1},{10,2},{11,3},{12,4},{13,5},{14,6},{15,7}} | collective-permute-start | bytes 1572872 | tf_op jit(solution)/shard_map/ppermute | solution.py:453
  71.0 37.7 %collective-permute-start.10 = (bf16[256,1024]{1,0:T(8,128)(2,1)}, bf16[256,1024]{1,0:T(8,128)(2,1)S(1)}, u32[]{:S(2)}, u32[]{:S(2)}) collective-permute-start(bf16[256,1024]{1,0:T(8,128)(2,1)} %get-tuple-element.89), channel_id=1, source_target_pairs={{16,0},{17,1},{18,2},{19,3},{20,4},{21,5},{22,6},{23,7}} | collective-permute-start | bytes 1572872 | tf_op jit(solution)/shard_map/ppermute | solution.py:453
  72.3 40.8 %collective-permute-start.9 = (bf16[256,1024]{1,0:T(8,128)(2,1)}, bf16[256,1024]{1,0:T(8,128)(2,1)S(1)}, u32[]{:S(2)}, u32[]{:S(2)}) collective-permute-start(bf16[256,1024]{1,0:T(8,128)(2,1)} %get-tuple-element.90), channel_id=1, source_target_pairs={{16,0},{17,1},{18,2},{19,3},{20,4},{21,5},{22,6},{23,7}} | collective-permute-start | bytes 1572872 | tf_op jit(solution)/shard_map/ppermute | solution.py:453
  73.6 17.1 %copy-start.1 = (bf16[2,256,2048]{2,1,0:T(8,128)(2,1)S(1)}, bf16[2,256,2048]{2,1,0:T(8,128)(2,1)}, u32[]{:S(2)}) copy-start(bf16[2,256,2048]{2,1,0:T(8,128)(2,1)} %copy-done) | copy-start | bytes 6291460
  101.7 11.4 %copy-start.7 = (bf16[256,1024]{1,0:T(8,128)(2,1)S(1)}, bf16[256,1024]{1,0:T(8,128)(2,1)}, u32[]{:S(2)}) copy-start(bf16[256,1024]{1,0:T(8,128)(2,1)} %copy-done.6) | copy-start | bytes 1572868
  101.7 11.4 %copy-start.9 = (bf16[256,1024]{1,0:T(8,128)(2,1)S(1)}, bf16[256,1024]{1,0:T(8,128)(2,1)}, u32[]{:S(2)}) copy-start(bf16[256,1024]{1,0:T(8,128)(2,1)} %copy-done.8) | copy-start | bytes 1572868
  101.7 11.4 %copy-start.11 = (bf16[256,1024]{1,0:T(8,128)(2,1)S(1)}, bf16[256,1024]{1,0:T(8,128)(2,1)}, u32[]{:S(2)}) copy-start(bf16[256,1024]{1,0:T(8,128)(2,1)} %copy-done.10) | copy-start | bytes 1572868
  101.7 11.4 %copy-start.13 = (bf16[256,1024]{1,0:T(8,128)(2,1)S(1)}, bf16[256,1024]{1,0:T(8,128)(2,1)}, u32[]{:S(2)}) copy-start(bf16[256,1024]{1,0:T(8,128)(2,1)} %copy-done.12) | copy-start | bytes 1572868
  126.6 6.7 %collective-permute-start.12 = (bf16[4,256,1024]{2,1,0:T(8,128)(2,1)}, bf16[4,256,1024]{2,1,0:T(8,128)(2,1)S(1)}, u32[]{:S(2)}, u32[]{:S(2)}) collective-permute-start(bf16[4,256,1024]{2,1,0:T(8,128)(2,1)} %weights.4.refs_10_), channel_id=1, source_target_pairs={{0,1},{1,0},{2,3},{3,2},{4,5},{5,4},{6,7},{7,6},{8,9},{9,8},{10,11... | collective-permute-start | bytes 6291464 | tf_op jit(solution)/shard_map/ppermute | solution.py:553
  132.8 14.6 %collective-permute-start.11 = (bf16[4,128,2048]{2,1,0:T(8,128)(2,1)}, bf16[4,128,2048]{2,1,0:T(8,128)(2,1)}, u32[]{:S(2)}, u32[]{:S(2)}) collective-permute-start(bf16[4,128,2048]{2,1,0:T(8,128)(2,1)} %weights.5.refs_5_), channel_id=1, source_target_pairs={{0,1},{1,0},{2,3},{3,2},{4,5},{5,4},{6,7},{7,6},{8,9},{9,8},{10,11... | collective-permute-start | bytes 6291464 | tf_op jit(solution)/shard_map/ppermute | solution.py:555
  143.2 15.5 %collective-permute-start.20 = (bf16[256,1024]{1,0:T(8,128)(2,1)}, bf16[256,1024]{1,0:T(8,128)(2,1)S(1)}, u32[]{:S(2)}, u32[]{:S(2)}) collective-permute-start(bf16[256,1024]{1,0:T(8,128)(2,1)} %get-tuple-element.119), channel_id=1, source_target_pairs={{0,2},{1,3},{8,10},{9,11},{16,18},{17,19},{24,26},{25,27}} | collective-permute-start | bytes 1572872 | tf_op jit(solution)/shard_map/ppermute | solution.py:569
  146.7 12.0 %collective-permute-start.21 = (bf16[256,1024]{1,0:T(8,128)(2,1)S(1)}, bf16[256,1024]{1,0:T(8,128)(2,1)S(1)}, u32[]{:S(2)}, u32[]{:S(2)}) collective-permute-start(bf16[256,1024]{1,0:T(8,128)(2,1)S(1)} %get-tuple-element.120), channel_id=1, source_target_pairs={{7,5},{6,4},{15,13},{14,12},{23,21},{22,20},{31,29},{30,28}} | collective-permute-start | bytes 1572872 | tf_op jit(solution)/shard_map/ppermute | solution.py:569
  156.6 13.9 %collective-permute-start.13 = (bf16[128,2048]{1,0:T(8,128)(2,1)}, bf16[128,2048]{1,0:T(8,128)(2,1)S(1)}, u32[]{:S(2)}, u32[]{:S(2)}) collective-permute-start(bf16[128,2048]{1,0:T(8,128)(2,1)} %get-tuple-element.112), channel_id=1, source_target_pairs={{0,2},{1,3},{8,10},{9,11},{16,18},{17,19},{24,26},{25,27}} | collective-permute-start | bytes 1572872 | tf_op jit(solution)/shard_map/ppermute | solution.py:569
  158.0 12.6 %collective-permute-start.14 = (bf16[128,2048]{1,0:T(8,128)(2,1)S(1)}, bf16[128,2048]{1,0:T(8,128)(2,1)S(1)}, u32[]{:S(2)}, u32[]{:S(2)}) collective-permute-start(bf16[128,2048]{1,0:T(8,128)(2,1)S(1)} %get-tuple-element.113), channel_id=1, source_target_pairs={{7,5},{6,4},{15,13},{14,12},{23,21},{22,20},{31,29},{30,28}} | collective-permute-start | bytes 1572872 | tf_op jit(solution)/shard_map/ppermute | solution.py:569
  162.7 19.1 %collective-permute-start.22 = (bf16[256,1024]{1,0:T(8,128)(2,1)}, bf16[256,1024]{1,0:T(8,128)(2,1)S(1)}, u32[]{:S(2)}, u32[]{:S(2)}) collective-permute-start(bf16[256,1024]{1,0:T(8,128)(2,1)} %get-tuple-element.121), channel_id=1, source_target_pairs={{0,2},{1,3},{2,4},{3,5},{8,10},{9,11},{10,12},{11,13},{16,18},{17,... | collective-permute-start | bytes 1572872 | tf_op jit(solution)/shard_map/ppermute | solution.py:569
  166.7 15.1 %collective-permute-start.23 = (bf16[256,1024]{1,0:T(8,128)(2,1)S(1)}, bf16[256,1024]{1,0:T(8,128)(2,1)S(1)}, u32[]{:S(2)}, u32[]{:S(2)}) collective-permute-start(bf16[256,1024]{1,0:T(8,128)(2,1)S(1)} %get-tuple-element.122), channel_id=1, source_target_pairs={{7,5},{6,4},{5,3},{4,2},{15,13},{14,12},{13,11},{12,10},{23,21},{2... | collective-permute-start | bytes 1572872 | tf_op jit(solution)/shard_map/ppermute | solution.py:569
  173.1 19.9 %collective-permute-start.15 = (bf16[128,2048]{1,0:T(8,128)(2,1)}, bf16[128,2048]{1,0:T(8,128)(2,1)S(1)}, u32[]{:S(2)}, u32[]{:S(2)}) collective-permute-start(bf16[128,2048]{1,0:T(8,128)(2,1)} %get-tuple-element.114), channel_id=1, source_target_pairs={{0,2},{1,3},{2,4},{3,5},{8,10},{9,11},{10,12},{11,13},{16,18},{17,... | collective-permute-start | bytes 1572872 | tf_op jit(solution)/shard_map/ppermute | solution.py:569
  177.4 15.6 %collective-permute-start.16 = (bf16[128,2048]{1,0:T(8,128)(2,1)S(1)}, bf16[128,2048]{1,0:T(8,128)(2,1)S(1)}, u32[]{:S(2)}, u32[]{:S(2)}) collective-permute-start(bf16[128,2048]{1,0:T(8,128)(2,1)S(1)} %get-tuple-element.115), channel_id=1, source_target_pairs={{7,5},{6,4},{5,3},{4,2},{15,13},{14,12},{13,11},{12,10},{23,21},{2... | collective-permute-start | bytes 1572872 | tf_op jit(solution)/shard_map/ppermute | solution.py:569
  184.6 19.5 %collective-permute-start.24 = (bf16[256,1024]{1,0:T(8,128)(2,1)S(1)}, bf16[256,1024]{1,0:T(8,128)(2,1)S(1)}, u32[]{:S(2)}, u32[]{:S(2)}) collective-permute-start(bf16[256,1024]{1,0:T(8,128)(2,1)S(1)} %get-tuple-element.123), channel_id=1, source_target_pairs={{0,2},{1,3},{2,4},{3,5},{4,6},{5,7},{8,10},{9,11},{10,12},{11,13},... | collective-permute-start | bytes 1572872 | tf_op jit(solution)/shard_map/ppermute | solution.py:569
  189.5 14.6 %collective-permute-start.25 = (bf16[256,1024]{1,0:T(8,128)(2,1)S(1)}, bf16[256,1024]{1,0:T(8,128)(2,1)S(1)}, u32[]{:S(2)}, u32[]{:S(2)}) collective-permute-start(bf16[256,1024]{1,0:T(8,128)(2,1)S(1)} %get-tuple-element.124), channel_id=1, source_target_pairs={{7,5},{6,4},{5,3},{4,2},{3,1},{2,0},{15,13},{14,12},{13,11},{12,10... | collective-permute-start | bytes 1572872 | tf_op jit(solution)/shard_map/ppermute | solution.py:569
  195.0 19.6 %collective-permute-start.17 = (bf16[128,2048]{1,0:T(8,128)(2,1)S(1)}, bf16[128,2048]{1,0:T(8,128)(2,1)S(1)}, u32[]{:S(2)}, u32[]{:S(2)}) collective-permute-start(bf16[128,2048]{1,0:T(8,128)(2,1)S(1)} %get-tuple-element.116), channel_id=1, source_target_pairs={{0,2},{1,3},{2,4},{3,5},{4,6},{5,7},{8,10},{9,11},{10,12},{11,13},... | collective-permute-start | bytes 1572872 | tf_op jit(solution)/shard_map/ppermute | solution.py:569
  199.5 15.0 %collective-permute-start.18 = (bf16[128,2048]{1,0:T(8,128)(2,1)S(1)}, bf16[128,2048]{1,0:T(8,128)(2,1)S(1)}, u32[]{:S(2)}, u32[]{:S(2)}) collective-permute-start(bf16[128,2048]{1,0:T(8,128)(2,1)S(1)} %get-tuple-element.117), channel_id=1, source_target_pairs={{7,5},{6,4},{5,3},{4,2},{3,1},{2,0},{15,13},{14,12},{13,11},{12,10... | collective-permute-start | bytes 1572872 | tf_op jit(solution)/shard_map/ppermute | solution.py:569
  208.3 14.3 %collective-permute-start.26 = (bf16[256,1024]{1,0:T(8,128)(2,1)S(1)}, bf16[256,1024]{1,0:T(8,128)(2,1)S(1)}, u32[]{:S(2)}, u32[]{:S(2)}) collective-permute-start(bf16[256,1024]{1,0:T(8,128)(2,1)S(1)} %get-tuple-element.125), channel_id=1, source_target_pairs={{0,24},{8,16},{16,8},{24,0},{1,25},{9,17},{17,9},{25,1},{2,26},{10... | collective-permute-start | bytes 1572872 | tf_op jit(solution)/shard_map/ppermute | solution.py:575
  217.5 15.2 %collective-permute-start.19 = (bf16[128,2048]{1,0:T(8,128)(2,1)S(1)}, bf16[128,2048]{1,0:T(8,128)(2,1)S(1)}, u32[]{:S(2)}, u32[]{:S(2)}) collective-permute-start(bf16[128,2048]{1,0:T(8,128)(2,1)S(1)} %get-tuple-element.118), channel_id=1, source_target_pairs={{0,24},{8,16},{16,8},{24,0},{1,25},{9,17},{17,9},{25,1},{2,26},{10... | collective-permute-start | bytes 1572872 | tf_op jit(solution)/shard_map/ppermute | solution.py:575

commit v9 on v7

--- a/solution.py
+++ b/solution.py
@@ -141,6 +141,10 @@
 columns_of_table = 4
 
 
+def by_halves(left, refs):
+    return jnp.concatenate([dot(left, ref[0, 0], ((1,), (1,))) for ref in refs], axis=1)
+
+
 def chain_step(call, group, table, recv, top_grad, saved, w_up, w_down, previous, after):
     base = call * columns_of_table
     slopes, ys, rs = saved
@@ -150,7 +154,8 @@
     tokens = top_grad.shape[2]
     per = rows // tokens
 
-    def body(info, e_ref, y_ref, r_ref, slope_ref, p_ref, q_ref, *rest):
+    def body(info, e_ref, y_ref, r_ref, slope_ref, *rest):
+        p_refs, q_refs = rest[:2], rest[2:4]
         out_ref, pre_ref, sum_ref, whole, low, total = rest[-6:]
         j = pl.program_id(0)
         active = info[base] > 0
@@ -166,13 +171,13 @@
         @pl.when(active)
         def _():
             grad_pre = (
-                dot(low[...], q_ref[0, 0], ((1,), (1,))) * slope_ref[0].astype(f32)
+                by_halves(low[...], q_refs) * slope_ref[0].astype(f32)
             ).astype(bf16)
             pre_ref[0] = grad_pre
 
             @pl.when(info[base + 3] > 0)
             def _():
-                part = dot(grad_pre, p_ref[0, 0], ((1,), (1,)))
+                part = by_halves(grad_pre, p_refs)
 
                 @pl.when(j == 0)
                 def _():
@@ -197,10 +202,20 @@
         pl.BlockSpec((1, rows, model), lambda j, i: (group, 0, 0)),
         pl.BlockSpec((1, rows, 1), lambda j, i: (group, 0, 0)),
         pl.BlockSpec((1, rows, tile), lambda j, i: (group, 0, j * i[base])),
-        pl.BlockSpec((1, 1, model, tile), lambda j, i: (i[base + 1], 0, 0, j * i[base + 3])),
-        pl.BlockSpec((1, 1, tile, model), lambda j, i: (i[base + 1], 0, j * i[base], 0)),
+        *[
+            pl.BlockSpec(
+                (1, 1, model // 2, tile), lambda j, i, k=k: (i[base + 1], 0, k, j * i[base + 3])
+            )
+            for k in range(2)
+        ],
+        *[
+            pl.BlockSpec(
+                (1, 1, tile // 2, model), lambda j, i, k=k: (i[base + 1], 0, 2 * j * i[base] + k, 0)
+            )
+            for k in range(2)
+        ],
     ]
-    operands += [in_vmem(x) for x in (ys, rs, slopes)] + [in_hbm(w_up), in_hbm(w_down)]
+    operands += [in_vmem(x) for x in (ys, rs, slopes)] + [in_hbm(w_up)] * 2 + [in_hbm(w_down)] * 2
     aliases = {}
     if previous is not None:
         aliases = {1 + len(operands): 1, 2 + len(operands): 2}

time: 234 us -> 236 us (level)
  transfers between devices with their start and end apart: 27 -> 27, of which waited for: 10 -> 10; matrix products, arithmetic and copies ran while one was open for 1% -> 1% of each run, Pallas kernels for 53% -> 52%
where the time goes in v9:
time: 236 us; the launch traced here: 235 us
  Pallas kernels  136 us (58%)
  waiting for transfers between devices  47.2 us (20%)
  starting transfers between devices  43.8 us (19%)
  other arithmetic  3.95 us (2%)
  local copies, waits for them, and re-layouts  2.54 us (1%)
    pallas_call x8, Pallas kernels, chain_step(): pl.pallas_call(body, grid_spec=pltpu.PrefetchScalarGridSpec(num_scalar_pr...  44.4 us
    pallas_call x3, Pallas kernels, forward(): pl.pallas_call(body, grid_spec=pltpu.PrefetchScalarGridSpec(num_scalar_pr...  34.8 us
    pallas_call x4, Pallas kernels, weight_gradient(): pl.pallas_call(body, grid_spec=pltpu.PrefetchScalarGridSpec(num_scalar_pr...  25 us
    ppermute x6, starting transfers between devices, on_device(): lax.ppermute(to_right, 'dp', right)  22 us
    ppermute x6, waiting for transfers between devices, on_device(): lax.ppermute(to_right, 'dp', right)  18.9 us
    pallas_call x6, Pallas kernels, fold(): pl.pallas_call(body, grid_spec=pltpu.PrefetchScalarGridSpec(num_scalar_pr...  17.5 us
    ppermute x10, waiting for transfers between devices, hop(): return lax.ppermute(value, 'section', pairs) if pairs else None  14.2 us
    ppermute x2, waiting for transfers between devices, finish(): lax.ppermute(fresh, 'section', [(i, last - i) for i in range(sections)])  14.1 us
  transfers between devices with their start and end apart: 27, of which 10 were waited for; matrix products, arithmetic and copies ran while one was open for 1% of the time, Pallas kernels for 52%

profile of v9, /device:TPU:0, one launch (start us, length us, event | category | flops | bytes accessed | tf_op | source)
XLA Modules:
  0.0 234.6 jit_solution(14527701213858223787)
XLA Ops:
  0.7 2.3 slice_bitcast_fusion
  2.9 3.9 %collective-permute-start = (bf16[4,128,1024]{2,1,0:T(8,128)(2,1)}, bf16[4,128,1024]{2,1,0:T(8,128)(2,1)}, u32[]{:S(2)}, u32[]{:S(2)}) collective-permute-start(bf16[4,128,1024]{2,1,0:T(8,128)(2,1)} %slice_bitcast_fusion), channel_id=1, source_target_pairs={{0,24},{8,16},{16,8},{24,0},{1,25},{9,17},{17,9},{25,1},{2,26},{10... | collective-permute-start | bytes 3145736 | tf_op jit(solution)/shard_map/ppermute | solution.py:472
  6.9 11.5 %forward.3 = (bf16[2,2,256,1024]{3,2,1,0:T(8,128)(2,1)}, bf16[2,2,256,2048]{3,2,1,0:T(8,128)(2,1)}, bf16[2,256,2048]{2,1,0:T(8,128)(2,1)S(1)}, bf16[2,256,1024]{2,1,0:T(8,128)(2,1)S(1)}, f32[2,256,1]{2,1,0:T(8,128)S(1)}) custom-call(s32[4]{0:T(128)S(1)} %stack.93.info_ref, s32[2,4]{1,0:T(2,128)S(1)} %copy-done.14, bf16[2,1,4,128,1024]{4,3,2,1,0:T(8,128)(2,1)} %refs_3_.3, ...), custom_call_target="tpu_custom_call" | custom-call | flops 1000 | bytes 1000 | tf_op jit(solution)/shard_map/forward/pallas_call | solution.py:118
  18.6 9.1 %chain.8 = (bf16[256,1024]{1,0:T(8,128)(2,1)S(1)}, bf16[3,256,2048]{2,1,0:T(8,128)(2,1)}, bf16[3,256,1024]{2,1,0:T(8,128)(2,1)}) custom-call(s32[32]{0:T(128)S(1)} %reshape.15.info, bf16[2,4,128,1024]{3,2,1,0:T(8,128)(2,1)} %refs_2_.5, bf16[2,256,1024]{2,1,0:T(8,128)(2,1)S(1)} %get-tuple-element.68.y_ref, f32[2,256,1]{2,1,0:T(8,128)S(1)} %get-tuple-element.69.r_ref, ...), custom_call_target="tpu_custom_call" | custom-call | flops 1000 | bytes 1000 | tf_op jit(solution)/shard_map/chain/pallas_call | solution.py:228
  27.7 1.3 collective-permute-start.2
  29.1 1.3 collective-permute-start.3
  30.4 8.8 %chain.9 = (bf16[256,1024]{1,0:T(8,128)(2,1)S(1)}, bf16[3,256,2048]{2,1,0:T(8,128)(2,1)}, bf16[3,256,1024]{2,1,0:T(8,128)(2,1)}) custom-call(s32[32]{0:T(128)S(1)} %reshape.15.info, bf16[2,4,128,1024]{3,2,1,0:T(8,128)(2,1)} %refs_2_.5, bf16[2,256,1024]{2,1,0:T(8,128)(2,1)S(1)} %get-tuple-element.68.y_ref, ...), custom_call_target="tpu_custom_call", output_to_operand_aliasing={{1}: (9, {}), {2}: (10, {})} | custom-call | flops 1000 | bytes 1000 | tf_op jit(solution)/shard_map/chain/pallas_call | solution.py:228
  39.3 1.3 collective-permute-start.1
  40.6 1.3 collective-permute-start.6
  42.0 11.8 %forward.4 = (bf16[2,2,256,1024]{3,2,1,0:T(8,128)(2,1)}, bf16[2,2,256,2048]{3,2,1,0:T(8,128)(2,1)}, bf16[2,256,2048]{2,1,0:T(8,128)(2,1)S(1)}, bf16[2,256,1024]{2,1,0:T(8,128)(2,1)S(1)}, f32[2,256,1]{2,1,0:T(8,128)S(1)}) custom-call(s32[4]{0:T(128)S(1)} %stack.92.info_ref, s32[2,4]{1,0:T(2,128)S(1)} %copy-done.14, ...), custom_call_target="tpu_custom_call", output_to_operand_aliasing={{0}: (8, {}), {1}: (9, {})} | custom-call | flops 1000 | bytes 1000 | tf_op jit(solution)/shard_map/forward/pallas_call | solution.py:118
  53.8 3.1 %chain.10 = (bf16[256,1024]{1,0:T(8,128)(2,1)S(1)}, bf16[3,256,2048]{2,1,0:T(8,128)(2,1)}, bf16[3,256,1024]{2,1,0:T(8,128)(2,1)}) custom-call(s32[32]{0:T(128)S(1)} %reshape.15.info, bf16[256,1024]{1,0:T(8,128)(2,1)S(1)} %collective-permute-done.2.e_ref, bf16[2,256,1024]{2,1,0:T(8,128)(2,1)S(1)} %copy-done.3, ...), custom_call_target="tpu_custom_call", output_to_operand_aliasing={{1}: (9, {}), {2}: (10, {})} | custom-call | flops 1000 | bytes 1000 | tf_op jit(solution)/shard_map/chain/pallas_call | solution.py:228
  57.6 3.1 %chain.11 = (bf16[256,1024]{1,0:T(8,128)(2,1)S(1)}, bf16[3,256,2048]{2,1,0:T(8,128)(2,1)}, bf16[3,256,1024]{2,1,0:T(8,128)(2,1)}) custom-call(s32[32]{0:T(128)S(1)} %reshape.15.info, bf16[256,1024]{1,0:T(8,128)(2,1)S(1)} %collective-permute-done.1.e_ref, bf16[2,256,1024]{2,1,0:T(8,128)(2,1)S(1)} %copy-done.3, ...), custom_call_target="tpu_custom_call", output_to_operand_aliasing={{1}: (9, {}), {2}: (10, {})} | custom-call | flops 1000 | bytes 1000 | tf_op jit(solution)/shard_map/chain/pallas_call | solution.py:228
  61.6 3.2 %chain.12 = (bf16[256,1024]{1,0:T(8,128)(2,1)}, bf16[3,256,2048]{2,1,0:T(8,128)(2,1)}, bf16[3,256,1024]{2,1,0:T(8,128)(2,1)}) custom-call(s32[32]{0:T(128)S(1)} %reshape.15.info, bf16[256,1024]{1,0:T(8,128)(2,1)S(1)} %collective-permute-done.5.e_ref, ...), custom_call_target="tpu_custom_call", output_to_operand_aliasing={{1}: (9, {}), {2}: (10, {})} | custom-call | flops 1000 | bytes 1000 | tf_op jit(solution)/shard_map/chain/pallas_call | solution.py:228
  66.2 3.2 %chain.13 = (bf16[256,1024]{1,0:T(8,128)(2,1)}, bf16[3,256,2048]{2,1,0:T(8,128)(2,1)}, bf16[3,256,1024]{2,1,0:T(8,128)(2,1)}) custom-call(s32[32]{0:T(128)S(1)} %reshape.15.info, bf16[256,1024]{1,0:T(8,128)(2,1)S(1)} %collective-permute-done.4.e_ref, ...), custom_call_target="tpu_custom_call", output_to_operand_aliasing={{1}: (9, {}), {2}: (10, {})} | custom-call | flops 1000 | bytes 1000 | tf_op jit(solution)/shard_map/chain/pallas_call | solution.py:228
  70.7 1.3 collective-permute-start.10
  73.3 11.5 %forward.5 = (bf16[1,2,256,1024]{3,2,1,0:T(8,128)(2,1)}, bf16[1,2,256,2048]{3,2,1,0:T(8,128)(2,1)}, bf16[2,256,2048]{2,1,0:T(8,128)(2,1)S(1)}, bf16[2,256,1024]{2,1,0:T(8,128)(2,1)S(1)}, f32[2,256,1]{2,1,0:T(8,128)S(1)}) custom-call(s32[4]{0:T(128)S(1)} %copy-done.15, s32[2,4]{1,0:T(2,128)S(1)} %copy-done.14, ...), custom_call_target="tpu_custom_call" | custom-call | flops 1000 | bytes 1000 | tf_op jit(solution)/shard_map/forward/pallas_call | solution.py:118
  84.8 5.6 %collective-permute-done.8.e_ref = bf16[256,1024]{1,0:T(8,128)(2,1)} collective-permute-done((bf16[256,1024]{1,0:T(8,128)(2,1)}, bf16[256,1024]{1,0:T(8,128)(2,1)}, u32[]{:S(2)}, u32[]{:S(2)}) %collective-permute-start.8) | collective-permute-done | bytes 524320 | tf_op jit(solution)/shard_map/ppermute | solution.py:470
  90.4 6.9 %chain.14 = (bf16[256,1024]{1,0:T(8,128)(2,1)}, bf16[3,256,2048]{2,1,0:T(8,128)(2,1)}, bf16[3,256,1024]{2,1,0:T(8,128)(2,1)}) custom-call(s32[32]{0:T(128)S(1)} %reshape.15.info, bf16[256,1024]{1,0:T(8,128)(2,1)} %collective-permute-done.8.e_ref, bf16[2,256,1024]{2,1,0:T(8,128)(2,1)S(1)} %get-tuple-element.81.y_ref, ...), custom_call_target="tpu_custom_call", output_to_operand_aliasing={{1}: (9, {}), {2}: (10, {})} | custom-call | flops 1000 | bytes 1000 | tf_op jit(solution)/shard_map/chain/pallas_call | solution.py:228
  97.3 3.7 %collective-permute-done.7.e_ref = bf16[256,1024]{1,0:T(8,128)(2,1)} collective-permute-done((bf16[256,1024]{1,0:T(8,128)(2,1)}, bf16[256,1024]{1,0:T(8,128)(2,1)}, u32[]{:S(2)}, u32[]{:S(2)}) %collective-permute-start.7) | collective-permute-done | bytes 524320 | tf_op jit(solution)/shard_map/ppermute | solution.py:470
  101.0 6.9 %chain.15 = (bf16[256,1024]{1,0:T(8,128)(2,1)}, bf16[3,256,2048]{2,1,0:T(8,128)(2,1)}, bf16[3,256,1024]{2,1,0:T(8,128)(2,1)}) custom-call(s32[32]{0:T(128)S(1)} %reshape.15.info, bf16[256,1024]{1,0:T(8,128)(2,1)} %collective-permute-done.7.e_ref, bf16[2,256,1024]{2,1,0:T(8,128)(2,1)S(1)} %get-tuple-element.81.y_ref, ...), custom_call_target="tpu_custom_call", output_to_operand_aliasing={{1}: (9, {}), {2}: (10, {})} | custom-call | flops 1000 | bytes 1000 | tf_op jit(solution)/shard_map/chain/pallas_call | solution.py:228
  108.0 4.9 %collective-permute-done.9 = bf16[256,1024]{1,0:T(8,128)(2,1)} collective-permute-done((bf16[256,1024]{1,0:T(8,128)(2,1)}, bf16[256,1024]{1,0:T(8,128)(2,1)}, u32[]{:S(2)}, u32[]{:S(2)}) %collective-permute-start.9) | collective-permute-done | bytes 524320 | tf_op jit(solution)/shard_map/ppermute | solution.py:470
  112.8 1.5 select_select_fusion
  114.3 7.2 %home.1 = (bf16[2,256,2048]{2,1,0:T(8,128)(2,1)}, bf16[2,256,1024]{2,1,0:T(8,128)(2,1)}) custom-call(s32[1]{0:T(128)} %bitcast.9.info, bf16[256,1024]{1,0:T(8,128)(2,1)S(1)} %get-tuple-element.141.refs_0_, bf16[256,1024]{1,0:T(8,128)(2,1)S(1)} %get-tuple-element.140.refs_1_, bf16[2,4,128,1024]{3,2,1,0:T(8,128)(2,1)} %refs_2_.5, ...), custom_call_target="tpu_custom_call" | custom-call | flops 1000 | bytes 1000 | tf_op jit(solution)/shard_map/home/pallas_call | solution.py:282
  121.6 6.0 %weights.4.refs_10_ = bf16[4,256,1024]{2,1,0:T(8,128)(2,1)} custom-call(s32[1]{0:T(128)} %bitcast.10.info, bf16[2,2,256,2048]{3,2,1,0:T(8,128)(2,1)} %get-tuple-element.108.refs_0_, bf16[3,256,1024]{2,1,0:T(8,128)(2,1)} %get-tuple-element.109.refs_1_, bf16[1,2,256,2048]{3,2,1,0:T(8,128)(2,1)} %get-tuple-element.110.refs_2_, ...), custom_call_target="tpu_custom_call" | custom-call | flops 1000 | bytes 1000 | tf_op jit(solution)/shard_map/weights/pallas_call | solution.py:379
  127.6 6.2 %weights.5.refs_5_ = bf16[4,128,2048]{2,1,0:T(8,128)(2,1)} custom-call(s32[1]{0:T(128)} %bitcast.10.info, bf16[2,2,256,1024]{3,2,1,0:T(8,128)(2,1)} %get-tuple-element.74.rest_6_.refs_0_.refs_1_.refs_2_.refs_3_, bf16[2,2,256,1024]{3,2,1,0:T(8,128)(2,1)} %get-tuple-element.74.rest_6_.refs_0_.refs_1_.refs_2_.refs_3_, ...), custom_call_target="tpu_custom_call" | custom-call | flops 1000 | bytes 1000 | tf_op jit(solution)/shard_map/weights/pallas_call | solution.py:379
  134.3 6.0 %weights.6.refs_11_.refs_0_.refs_1_.part_ref = bf16[4,256,1024]{2,1,0:T(8,128)(2,1)} custom-call(s32[1]{0:T(128)} %bitcast.2.info, bf16[2,2,256,2048]{3,2,1,0:T(8,128)(2,1)} %get-tuple-element.108.refs_0_, bf16[3,256,1024]{2,1,0:T(8,128)(2,1)} %get-tuple-element.109.refs_1_, bf16[1,2,256,2048]{3,2,1,0:T(8,128)(2,1)} %get-tuple-element.110.refs_2_, ...), custom_call_target="tpu_custom_call" | custom-call | flops 1000 | bytes 1000 | tf_op jit(solution)/shard_map/weights/pallas_call | solution.py:379
  140.3 3.9 %fold.9 = (bf16[256,1024]{1,0:T(8,128)(2,1)}, bf16[256,1024]{1,0:T(8,128)(2,1)S(1)}) custom-call(s32[2]{0:T(128)S(1)} %pad_add_fusion.4.info, bf16[4,256,1024]{2,1,0:T(8,128)(2,1)} %weights.6.refs_11_.refs_0_.refs_1_.part_ref, bf16[4,256,1024]{2,1,0:T(8,128)(2,1)} %weights.6.refs_11_.refs_0_.refs_1_.part_ref), custom_call_target="tpu_custom_call" | custom-call | flops 1000 | bytes 1000 | tf_op jit(solution)/shard_map/fold/pallas_call | solution.py:403
  144.2 3.5 %collective-permute-start.20 = (bf16[256,1024]{1,0:T(8,128)(2,1)}, bf16[256,1024]{1,0:T(8,128)(2,1)S(1)}, u32[]{:S(2)}, u32[]{:S(2)}) collective-permute-start(bf16[256,1024]{1,0:T(8,128)(2,1)} %get-tuple-element.119), channel_id=1, source_target_pairs={{0,2},{1,3},{8,10},{9,11},{16,18},{17,19},{24,26},{25,27}} | collective-permute-start | bytes 1572872 | tf_op jit(solution)/shard_map/ppermute | solution.py:586
  148.4 6.7 %weights.7.refs_0_.refs_1_.part_ref = bf16[4,128,2048]{2,1,0:T(8,128)(2,1)} custom-call(s32[1]{0:T(128)} %bitcast.2.info, bf16[2,2,256,1024]{3,2,1,0:T(8,128)(2,1)} %get-tuple-element.74.rest_6_.refs_0_.refs_1_.refs_2_.refs_3_, bf16[2,2,256,1024]{3,2,1,0:T(8,128)(2,1)} %get-tuple-element.74.rest_6_.refs_0_.refs_1_.refs_2_.refs_3_, ...), custom_call_target="tpu_custom_call" | custom-call | flops 1000 | bytes 1000 | tf_op jit(solution)/shard_map/weights/pallas_call | solution.py:379
  155.1 2.5 %fold.6 = (bf16[128,2048]{1,0:T(8,128)(2,1)}, bf16[128,2048]{1,0:T(8,128)(2,1)S(1)}) custom-call(s32[2]{0:T(128)S(1)} %pad_add_fusion.4.info, bf16[4,128,2048]{2,1,0:T(8,128)(2,1)} %weights.7.refs_0_.refs_1_.part_ref, bf16[4,128,2048]{2,1,0:T(8,128)(2,1)} %weights.7.refs_0_.refs_1_.part_ref), custom_call_target="tpu_custom_call" | custom-call | flops 1000 | bytes 1000 | tf_op jit(solution)/shard_map/fold/pallas_call | solution.py:403
  157.6 1.3 collective-permute-start.13
  159.7 3.9 %fold.10 = (bf16[256,1024]{1,0:T(8,128)(2,1)}, bf16[256,1024]{1,0:T(8,128)(2,1)S(1)}) custom-call(s32[2]{0:T(128)S(1)} %pad_add_fusion.3.info, bf16[4,256,1024]{2,1,0:T(8,128)(2,1)} %weights.6.refs_11_.refs_0_.refs_1_.part_ref, bf16[4,256,1024]{2,1,0:T(8,128)(2,1)} %weights.6.refs_11_.refs_0_.refs_1_.part_ref, ...), custom_call_target="tpu_custom_call" | custom-call | flops 1000 | bytes 1000 | tf_op jit(solution)/shard_map/fold/pallas_call | solution.py:403
  163.6 3.9 %collective-permute-start.22 = (bf16[256,1024]{1,0:T(8,128)(2,1)}, bf16[256,1024]{1,0:T(8,128)(2,1)S(1)}, u32[]{:S(2)}, u32[]{:S(2)}) collective-permute-start(bf16[256,1024]{1,0:T(8,128)(2,1)} %get-tuple-element.121), channel_id=1, source_target_pairs={{0,2},{1,3},{2,4},{3,5},{8,10},{9,11},{10,12},{11,13},{16,18},{17,... | collective-permute-start | bytes 1572872 | tf_op jit(solution)/shard_map/ppermute | solution.py:586
  168.3 3.3 %collective-permute-done.13.refs_2_ = bf16[128,2048]{1,0:T(8,128)(2,1)S(1)} collective-permute-done((bf16[128,2048]{1,0:T(8,128)(2,1)}, bf16[128,2048]{1,0:T(8,128)(2,1)S(1)}, u32[]{:S(2)}, u32[]{:S(2)}) %collective-permute-start.13) | collective-permute-done | bytes 524320 | tf_op jit(solution)/shard_map/ppermute | solution.py:586
  171.5 2.5 %fold.7 = (bf16[128,2048]{1,0:T(8,128)(2,1)}, bf16[128,2048]{1,0:T(8,128)(2,1)S(1)}) custom-call(s32[2]{0:T(128)S(1)} %pad_add_fusion.3.info, bf16[4,128,2048]{2,1,0:T(8,128)(2,1)} %weights.7.refs_0_.refs_1_.part_ref, bf16[4,128,2048]{2,1,0:T(8,128)(2,1)} %weights.7.refs_0_.refs_1_.part_ref, bf16[128,2048]{1,0:T(8,128)(2,1)S(1)} %collective-permute-done.13.refs_2_, ...), custom_call_target="tpu_custom_call" | custom-call | flops 1000 | bytes 1000 | tf_op jit(solution)/shard_map/fold/pallas_call | solution.py:403
  174.0 4.3 %collective-permute-start.15 = (bf16[128,2048]{1,0:T(8,128)(2,1)}, bf16[128,2048]{1,0:T(8,128)(2,1)S(1)}, u32[]{:S(2)}, u32[]{:S(2)}) collective-permute-start(bf16[128,2048]{1,0:T(8,128)(2,1)} %get-tuple-element.114), channel_id=1, source_target_pairs={{0,2},{1,3},{2,4},{3,5},{8,10},{9,11},{10,12},{11,13},{16,18},{17,... | collective-permute-start | bytes 1572872 | tf_op jit(solution)/shard_map/ppermute | solution.py:586
  179.1 3.6 %collective-permute-done.22.refs_2_ = bf16[256,1024]{1,0:T(8,128)(2,1)S(1)} collective-permute-done((bf16[256,1024]{1,0:T(8,128)(2,1)}, bf16[256,1024]{1,0:T(8,128)(2,1)S(1)}, u32[]{:S(2)}, u32[]{:S(2)}) %collective-permute-start.22) | collective-permute-done | bytes 524320 | tf_op jit(solution)/shard_map/ppermute | solution.py:586
  182.8 2.8 %fold.11 = (bf16[256,1024]{1,0:T(8,128)(2,1)S(1)}, bf16[256,1024]{1,0:T(8,128)(2,1)S(1)}) custom-call(s32[2]{0:T(128)S(1)} %pad_add_fusion.2.info, bf16[4,256,1024]{2,1,0:T(8,128)(2,1)} %weights.6.refs_11_.refs_0_.refs_1_.part_ref, bf16[4,256,1024]{2,1,0:T(8,128)(2,1)} %weights.6.refs_11_.refs_0_.refs_1_.part_ref, ...), custom_call_target="tpu_custom_call" | custom-call | flops 1000 | bytes 1000 | tf_op jit(solution)/shard_map/fold/pallas_call | solution.py:403
  185.6 4.7 %collective-permute-start.24 = (bf16[256,1024]{1,0:T(8,128)(2,1)S(1)}, bf16[256,1024]{1,0:T(8,128)(2,1)S(1)}, u32[]{:S(2)}, u32[]{:S(2)}) collective-permute-start(bf16[256,1024]{1,0:T(8,128)(2,1)S(1)} %get-tuple-element.123), channel_id=1, source_target_pairs={{0,2},{1,3},{2,4},{3,5},{4,6},{5,7},{8,10},{9,11},{10,12},{11,13},... | collective-permute-start | bytes 1572872 | tf_op jit(solution)/shard_map/ppermute | solution.py:586
  191.6 2.4 %collective-permute-done.15.refs_2_ = bf16[128,2048]{1,0:T(8,128)(2,1)S(1)} collective-permute-done((bf16[128,2048]{1,0:T(8,128)(2,1)}, bf16[128,2048]{1,0:T(8,128)(2,1)S(1)}, u32[]{:S(2)}, u32[]{:S(2)}) %collective-permute-start.15) | collective-permute-done | bytes 524320 | tf_op jit(solution)/shard_map/ppermute | solution.py:586
  194.0 1.9 fold.8
  195.9 4.4 %collective-permute-start.17 = (bf16[128,2048]{1,0:T(8,128)(2,1)S(1)}, bf16[128,2048]{1,0:T(8,128)(2,1)S(1)}, u32[]{:S(2)}, u32[]{:S(2)}) collective-permute-start(bf16[128,2048]{1,0:T(8,128)(2,1)S(1)} %get-tuple-element.116), channel_id=1, source_target_pairs={{0,2},{1,3},{2,4},{3,5},{4,6},{5,7},{8,10},{9,11},{10,12},{11,13},... | collective-permute-start | bytes 1572872 | tf_op jit(solution)/shard_map/ppermute | solution.py:586
  201.6 3.5 %collective-permute-done.24.right_ref = bf16[256,1024]{1,0:T(8,128)(2,1)S(1)} collective-permute-done((bf16[256,1024]{1,0:T(8,128)(2,1)S(1)}, bf16[256,1024]{1,0:T(8,128)(2,1)S(1)}, u32[]{:S(2)}, u32[]{:S(2)}) %collective-permute-start.24) | collective-permute-done | bytes 524320 | tf_op jit(solution)/shard_map/ppermute | solution.py:586
  205.1 4.2 %update.3 = (bf16[256,1024]{1,0:T(8,128)(2,1)S(1)}, f32[1,256,1024]{2,1,0:T(8,128)}) custom-call(s32[2]{0:T(128)S(1)} %pad_add_fusion.1.info, bf16[2,1,2048,1024]{3,2,1,0:T(8,128)(2,1)} %weight_ref.3, f32[1,256,1024]{2,1,0:T(8,128)} %moment_ref.3, bf16[4,256,1024]{2,1,0:T(8,128)(2,1)} %weights.6.refs_11_.refs_0_.refs_1_.part_ref, ...), custom_call_target="tpu_custom_call" | custom-call | flops 1000 | bytes 1000 | tf_op jit(solution)/shard_map/update/pallas_call | solution.py:433
  209.3 6.1 %collective-permute-done.17.right_ref = bf16[128,2048]{1,0:T(8,128)(2,1)S(1)} collective-permute-done((bf16[128,2048]{1,0:T(8,128)(2,1)S(1)}, bf16[128,2048]{1,0:T(8,128)(2,1)S(1)}, u32[]{:S(2)}, u32[]{:S(2)}) %collective-permute-start.17) | collective-permute-done | bytes 524320 | tf_op jit(solution)/shard_map/ppermute | solution.py:586
  215.5 3.0 %update.2 = (bf16[128,2048]{1,0:T(8,128)(2,1)S(1)}, f32[1,128,2048]{2,1,0:T(8,128)}) custom-call(s32[2]{0:T(128)S(1)} %pad_add_fusion.1.info, bf16[2,1,1024,2048]{3,2,1,0:T(8,128)(2,1)} %weight_ref.2, f32[1,128,2048]{2,1,0:T(8,128)} %moment_ref.2, bf16[4,128,2048]{2,1,0:T(8,128)(2,1)} %weights.7.refs_0_.refs_1_.part_ref, ...), custom_call_target="tpu_custom_call" | custom-call | flops 1000 | bytes 1000 | tf_op jit(solution)/shard_map/update/pallas_call | solution.py:433
  218.4 5.0 %collective-permute-done.26 = bf16[256,1024]{1,0:T(8,128)(2,1)S(1)} collective-permute-done((bf16[256,1024]{1,0:T(8,128)(2,1)S(1)}, bf16[256,1024]{1,0:T(8,128)(2,1)S(1)}, u32[]{:S(2)}, u32[]{:S(2)}) %collective-permute-start.26) | collective-permute-done | bytes 524320 | tf_op jit(solution)/shard_map/ppermute | solution.py:592
  224.6 9.0 %collective-permute-done.19 = bf16[128,2048]{1,0:T(8,128)(2,1)S(1)} collective-permute-done((bf16[128,2048]{1,0:T(8,128)(2,1)S(1)}, bf16[128,2048]{1,0:T(8,128)(2,1)S(1)}, u32[]{:S(2)}, u32[]{:S(2)}) %collective-permute-start.19) | collective-permute-done | bytes 524320 | tf_op jit(solution)/shard_map/ppermute | solution.py:592
  (86 shorter events, 14.0 us)
Async XLA Ops:
  0.6 6.2 %copy-start.16 = (pred[8]{0:T(512)(128)(4,1)S(1)}, pred[8]{0:T(512)(128)(4,1)}, u32[]{:S(2)}) copy-start(pred[8]{0:T(512)(128)(4,1)} %constant.61.clone) | copy-start | bytes 28
  0.6 6.2 %copy-start.18 = (s32[8]{0:T(128)S(1)}, s32[8]{0:T(128)}, u32[]{:S(2)}) copy-start(s32[8]{0:T(128)} %constant.62.clone) | copy-start | bytes 100
  0.7 6.2 %copy-start.14 = (s32[2,4]{1,0:T(2,128)S(1)}, s32[2,4]{1,0:T(2,128)}, u32[]{:S(2)}) copy-start(s32[2,4]{1,0:T(2,128)} %plan_ref.5) | copy-start | bytes 100
  2.9 39.0 %collective-permute-start = (bf16[4,128,1024]{2,1,0:T(8,128)(2,1)}, bf16[4,128,1024]{2,1,0:T(8,128)(2,1)}, u32[]{:S(2)}, u32[]{:S(2)}) collective-permute-start(bf16[4,128,1024]{2,1,0:T(8,128)(2,1)} %slice_bitcast_fusion), channel_id=1, source_target_pairs={{0,24},{8,16},{16,8},{24,0},{1,25},{9,17},{17,9},{25,1},{2,26},{10... | collective-permute-start | bytes 3145736 | tf_op jit(solution)/shard_map/ppermute | solution.py:472
  6.9 11.5 %copy-start.19 = (pred[8]{0:T(512)(128)(4,1)S(1)}, pred[8]{0:T(512)(128)(4,1)}, u32[]{:S(2)}) copy-start(pred[8]{0:T(512)(128)(4,1)} %constant.64.clone) | copy-start | bytes 28
  6.9 11.5 %copy-start.17 = (s32[8]{0:T(128)S(1)}, s32[8]{0:T(128)}, u32[]{:S(2)}) copy-start(s32[8]{0:T(128)} %constant.63.clone) | copy-start | bytes 100
  18.4 12.0 %copy-start = (bf16[2,256,2048]{2,1,0:T(8,128)(2,1)}, bf16[2,256,2048]{2,1,0:T(8,128)(2,1)S(1)}, u32[]{:S(2)}) copy-start(bf16[2,256,2048]{2,1,0:T(8,128)(2,1)S(1)} %get-tuple-element.70.slope_ref) | copy-start | bytes 6291460
  18.4 12.0 %copy-start.2 = (bf16[2,256,1024]{2,1,0:T(8,128)(2,1)}, bf16[2,256,1024]{2,1,0:T(8,128)(2,1)S(1)}, u32[]{:S(2)}) copy-start(bf16[2,256,1024]{2,1,0:T(8,128)(2,1)S(1)} %get-tuple-element.68.y_ref) | copy-start | bytes 3145732
  18.4 12.0 %copy-start.4 = (f32[2,256,1]{2,1,0:T(8,128)}, f32[2,256,1]{2,1,0:T(8,128)S(1)}, u32[]{:S(2)}) copy-start(f32[2,256,1]{2,1,0:T(8,128)S(1)} %get-tuple-element.69.r_ref) | copy-start | bytes 6148
  27.7 26.0 %collective-permute-start.2 = (bf16[256,1024]{1,0:T(8,128)(2,1)S(1)}, bf16[256,1024]{1,0:T(8,128)(2,1)S(1)}, u32[]{:S(2)}, u32[]{:S(2)}) collective-permute-start(bf16[256,1024]{1,0:T(8,128)(2,1)S(1)} %get-tuple-element.76), channel_id=1, source_target_pairs={{24,16},{0,8},{25,17},{1,9},{26,18},{2,10},{27,19},{3,11},{28,20},... | collective-permute-start | bytes 1572872 | tf_op jit(solution)/shard_map/ppermute | solution.py:470
  29.1 24.7 %collective-permute-start.3 = (bf16[256,1024]{1,0:T(8,128)(2,1)S(1)}, bf16[256,1024]{1,0:T(8,128)(2,1)S(1)}, u32[]{:S(2)}, u32[]{:S(2)}) collective-permute-start(bf16[256,1024]{1,0:T(8,128)(2,1)S(1)} %get-tuple-element.76), channel_id=1, source_target_pairs={{0,16},{1,17},{2,18},{3,19},{4,20},{5,21},{6,22},{7,23}} | collective-permute-start | bytes 1572872 | tf_op jit(solution)/shard_map/ppermute | solution.py:470
  39.3 18.3 %collective-permute-start.1 = (bf16[256,1024]{1,0:T(8,128)(2,1)S(1)}, bf16[256,1024]{1,0:T(8,128)(2,1)S(1)}, u32[]{:S(2)}, u32[]{:S(2)}) collective-permute-start(bf16[256,1024]{1,0:T(8,128)(2,1)S(1)} %get-tuple-element.75), channel_id=1, source_target_pairs={{24,16},{0,8},{25,17},{1,9},{26,18},{2,10},{27,19},{3,11},{28,20},... | collective-permute-start | bytes 1572872 | tf_op jit(solution)/shard_map/ppermute | solution.py:470
  40.6 21.0 %collective-permute-start.6 = (bf16[256,1024]{1,0:T(8,128)(2,1)S(1)}, bf16[256,1024]{1,0:T(8,128)(2,1)S(1)}, u32[]{:S(2)}, u32[]{:S(2)}) collective-permute-start(bf16[256,1024]{1,0:T(8,128)(2,1)S(1)} %get-tuple-element.75), channel_id=1, source_target_pairs={{0,16},{1,17},{2,18},{3,19},{4,20},{5,21},{6,22},{7,23}} | collective-permute-start | bytes 1572872 | tf_op jit(solution)/shard_map/ppermute | solution.py:470
  41.9 11.8 %copy-start.1 = (bf16[2,256,2048]{2,1,0:T(8,128)(2,1)S(1)}, bf16[2,256,2048]{2,1,0:T(8,128)(2,1)}, u32[]{:S(2)}) copy-start(bf16[2,256,2048]{2,1,0:T(8,128)(2,1)} %copy-done) | copy-start | bytes 6291460
  41.9 11.8 %copy-start.3 = (bf16[2,256,1024]{2,1,0:T(8,128)(2,1)S(1)}, bf16[2,256,1024]{2,1,0:T(8,128)(2,1)}, u32[]{:S(2)}) copy-start(bf16[2,256,1024]{2,1,0:T(8,128)(2,1)} %copy-done.2) | copy-start | bytes 3145732
  42.0 11.8 %copy-start.5 = (f32[2,256,1]{2,1,0:T(8,128)S(1)}, f32[2,256,1]{2,1,0:T(8,128)}, u32[]{:S(2)}) copy-start(f32[2,256,1]{2,1,0:T(8,128)} %copy-done.4) | copy-start | bytes 6148
  53.8 3.1 %copy-start.6 = (bf16[256,1024]{1,0:T(8,128)(2,1)}, bf16[256,1024]{1,0:T(8,128)(2,1)S(1)}, u32[]{:S(2)}) copy-start(bf16[256,1024]{1,0:T(8,128)(2,1)S(1)} %collective-permute-done.3.rest_7_) | copy-start | bytes 1572868
  56.9 3.8 %copy-start.10 = (bf16[256,1024]{1,0:T(8,128)(2,1)}, bf16[256,1024]{1,0:T(8,128)(2,1)S(1)}, u32[]{:S(2)}) copy-start(bf16[256,1024]{1,0:T(8,128)(2,1)S(1)} %get-tuple-element.99) | copy-start | bytes 1572868
  56.9 4.7 %collective-permute-start.5 = (bf16[256,1024]{1,0:T(8,128)(2,1)S(1)}, bf16[256,1024]{1,0:T(8,128)(2,1)S(1)}, u32[]{:S(2)}, u32[]{:S(2)}) collective-permute-start(bf16[256,1024]{1,0:T(8,128)(2,1)S(1)} %get-tuple-element.99), channel_id=1, source_target_pairs={{16,8},{8,16},{17,9},{9,17},{18,10},{10,18},{19,11},{11,19},{20,12... | collective-permute-start | bytes 1572872 | tf_op jit(solution)/shard_map/ppermute | solution.py:470
  60.7 4.1 %copy-start.12 = (bf16[256,1024]{1,0:T(8,128)(2,1)}, bf16[256,1024]{1,0:T(8,128)(2,1)S(1)}, u32[]{:S(2)}) copy-start(bf16[256,1024]{1,0:T(8,128)(2,1)S(1)} %get-tuple-element.102) | copy-start | bytes 1572868
  60.7 5.5 %collective-permute-start.4 = (bf16[256,1024]{1,0:T(8,128)(2,1)S(1)}, bf16[256,1024]{1,0:T(8,128)(2,1)S(1)}, u32[]{:S(2)}, u32[]{:S(2)}) collective-permute-start(bf16[256,1024]{1,0:T(8,128)(2,1)S(1)} %get-tuple-element.102), channel_id=1, source_target_pairs={{16,8},{8,16},{17,9},{9,17},{18,10},{10,18},{19,11},{11,19},{20,12... | collective-permute-start | bytes 1572872 | tf_op jit(solution)/shard_map/ppermute | solution.py:470
  61.6 3.2 %copy-start.8 = (bf16[256,1024]{1,0:T(8,128)(2,1)}, bf16[256,1024]{1,0:T(8,128)(2,1)S(1)}, u32[]{:S(2)}) copy-start(bf16[256,1024]{1,0:T(8,128)(2,1)S(1)} %collective-permute-done.6.rest_6_) | copy-start | bytes 1572868
  64.8 25.6 %collective-permute-start.8 = (bf16[256,1024]{1,0:T(8,128)(2,1)}, bf16[256,1024]{1,0:T(8,128)(2,1)}, u32[]{:S(2)}, u32[]{:S(2)}) collective-permute-start(bf16[256,1024]{1,0:T(8,128)(2,1)} %get-tuple-element.90), channel_id=1, source_target_pairs={{8,0},{9,1},{10,2},{11,3},{12,4},{13,5},{14,6},{15,7}} | collective-permute-start | bytes 1572872 | tf_op jit(solution)/shard_map/ppermute | solution.py:470
  66.1 7.1 %copy-start.15 = (s32[4]{0:T(128)S(1)}, s32[4]{0:T(128)}, u32[]{:S(2)}) copy-start(s32[4]{0:T(128)} %constant.65.clone.info_ref) | copy-start | bytes 52
  69.4 31.6 %collective-permute-start.7 = (bf16[256,1024]{1,0:T(8,128)(2,1)}, bf16[256,1024]{1,0:T(8,128)(2,1)}, u32[]{:S(2)}, u32[]{:S(2)}) collective-permute-start(bf16[256,1024]{1,0:T(8,128)(2,1)} %get-tuple-element.89), channel_id=1, source_target_pairs={{8,0},{9,1},{10,2},{11,3},{12,4},{13,5},{14,6},{15,7}} | collective-permute-start | bytes 1572872 | tf_op jit(solution)/shard_map/ppermute | solution.py:470
  70.7 37.3 %collective-permute-start.10 = (bf16[256,1024]{1,0:T(8,128)(2,1)}, bf16[256,1024]{1,0:T(8,128)(2,1)}, u32[]{:S(2)}, u32[]{:S(2)}) collective-permute-start(bf16[256,1024]{1,0:T(8,128)(2,1)} %get-tuple-element.89), channel_id=1, source_target_pairs={{16,0},{17,1},{18,2},{19,3},{20,4},{21,5},{22,6},{23,7}} | collective-permute-start | bytes 1572872 | tf_op jit(solution)/shard_map/ppermute | solution.py:470
  72.0 40.8 %collective-permute-start.9 = (bf16[256,1024]{1,0:T(8,128)(2,1)}, bf16[256,1024]{1,0:T(8,128)(2,1)}, u32[]{:S(2)}, u32[]{:S(2)}) collective-permute-start(bf16[256,1024]{1,0:T(8,128)(2,1)} %get-tuple-element.90), channel_id=1, source_target_pairs={{16,0},{17,1},{18,2},{19,3},{20,4},{21,5},{22,6},{23,7}} | collective-permute-start | bytes 1572872 | tf_op jit(solution)/shard_map/ppermute | solution.py:470
  101.0 11.8 %copy-start.7 = (bf16[256,1024]{1,0:T(8,128)(2,1)S(1)}, bf16[256,1024]{1,0:T(8,128)(2,1)}, u32[]{:S(2)}) copy-start(bf16[256,1024]{1,0:T(8,128)(2,1)} %copy-done.6) | copy-start | bytes 1572868
  101.0 11.8 %copy-start.9 = (bf16[256,1024]{1,0:T(8,128)(2,1)S(1)}, bf16[256,1024]{1,0:T(8,128)(2,1)}, u32[]{:S(2)}) copy-start(bf16[256,1024]{1,0:T(8,128)(2,1)} %copy-done.8) | copy-start | bytes 1572868
  101.0 11.8 %copy-start.11 = (bf16[256,1024]{1,0:T(8,128)(2,1)S(1)}, bf16[256,1024]{1,0:T(8,128)(2,1)}, u32[]{:S(2)}) copy-start(bf16[256,1024]{1,0:T(8,128)(2,1)} %copy-done.10) | copy-start | bytes 1572868
  101.0 11.8 %copy-start.13 = (bf16[256,1024]{1,0:T(8,128)(2,1)S(1)}, bf16[256,1024]{1,0:T(8,128)(2,1)}, u32[]{:S(2)}) copy-start(bf16[256,1024]{1,0:T(8,128)(2,1)} %copy-done.12) | copy-start | bytes 1572868
  127.6 6.7 %collective-permute-start.12 = (bf16[4,256,1024]{2,1,0:T(8,128)(2,1)}, bf16[4,256,1024]{2,1,0:T(8,128)(2,1)S(1)}, u32[]{:S(2)}, u32[]{:S(2)}) collective-permute-start(bf16[4,256,1024]{2,1,0:T(8,128)(2,1)} %weights.4.refs_10_), channel_id=1, source_target_pairs={{0,1},{1,0},{2,3},{3,2},{4,5},{5,4},{6,7},{7,6},{8,9},{9,8},{10,11... | collective-permute-start | bytes 6291464 | tf_op jit(solution)/shard_map/ppermute | solution.py:570
  133.8 14.6 %collective-permute-start.11 = (bf16[4,128,2048]{2,1,0:T(8,128)(2,1)}, bf16[4,128,2048]{2,1,0:T(8,128)(2,1)}, u32[]{:S(2)}, u32[]{:S(2)}) collective-permute-start(bf16[4,128,2048]{2,1,0:T(8,128)(2,1)} %weights.5.refs_5_), channel_id=1, source_target_pairs={{0,1},{1,0},{2,3},{3,2},{4,5},{5,4},{6,7},{7,6},{8,9},{9,8},{10,11... | collective-permute-start | bytes 6291464 | tf_op jit(solution)/shard_map/ppermute | solution.py:572
  144.2 15.6 %collective-permute-start.20 = (bf16[256,1024]{1,0:T(8,128)(2,1)}, bf16[256,1024]{1,0:T(8,128)(2,1)S(1)}, u32[]{:S(2)}, u32[]{:S(2)}) collective-permute-start(bf16[256,1024]{1,0:T(8,128)(2,1)} %get-tuple-element.119), channel_id=1, source_target_pairs={{0,2},{1,3},{8,10},{9,11},{16,18},{17,19},{24,26},{25,27}} | collective-permute-start | bytes 1572872 | tf_op jit(solution)/shard_map/ppermute | solution.py:586
  147.7 12.1 %collective-permute-start.21 = (bf16[256,1024]{1,0:T(8,128)(2,1)S(1)}, bf16[256,1024]{1,0:T(8,128)(2,1)S(1)}, u32[]{:S(2)}, u32[]{:S(2)}) collective-permute-start(bf16[256,1024]{1,0:T(8,128)(2,1)S(1)} %get-tuple-element.120), channel_id=1, source_target_pairs={{7,5},{6,4},{15,13},{14,12},{23,21},{22,20},{31,29},{30,28}} | collective-permute-start | bytes 1572872 | tf_op jit(solution)/shard_map/ppermute | solution.py:586
  157.6 13.9 %collective-permute-start.13 = (bf16[128,2048]{1,0:T(8,128)(2,1)}, bf16[128,2048]{1,0:T(8,128)(2,1)S(1)}, u32[]{:S(2)}, u32[]{:S(2)}) collective-permute-start(bf16[128,2048]{1,0:T(8,128)(2,1)} %get-tuple-element.112), channel_id=1, source_target_pairs={{0,2},{1,3},{8,10},{9,11},{16,18},{17,19},{24,26},{25,27}} | collective-permute-start | bytes 1572872 | tf_op jit(solution)/shard_map/ppermute | solution.py:586
  159.0 12.6 %collective-permute-start.14 = (bf16[128,2048]{1,0:T(8,128)(2,1)S(1)}, bf16[128,2048]{1,0:T(8,128)(2,1)S(1)}, u32[]{:S(2)}, u32[]{:S(2)}) collective-permute-start(bf16[128,2048]{1,0:T(8,128)(2,1)S(1)} %get-tuple-element.113), channel_id=1, source_target_pairs={{7,5},{6,4},{15,13},{14,12},{23,21},{22,20},{31,29},{30,28}} | collective-permute-start | bytes 1572872 | tf_op jit(solution)/shard_map/ppermute | solution.py:586
  163.6 19.1 %collective-permute-start.22 = (bf16[256,1024]{1,0:T(8,128)(2,1)}, bf16[256,1024]{1,0:T(8,128)(2,1)S(1)}, u32[]{:S(2)}, u32[]{:S(2)}) collective-permute-start(bf16[256,1024]{1,0:T(8,128)(2,1)} %get-tuple-element.121), channel_id=1, source_target_pairs={{0,2},{1,3},{2,4},{3,5},{8,10},{9,11},{10,12},{11,13},{16,18},{17,... | collective-permute-start | bytes 1572872 | tf_op jit(solution)/shard_map/ppermute | solution.py:586
  167.6 15.2 %collective-permute-start.23 = (bf16[256,1024]{1,0:T(8,128)(2,1)S(1)}, bf16[256,1024]{1,0:T(8,128)(2,1)S(1)}, u32[]{:S(2)}, u32[]{:S(2)}) collective-permute-start(bf16[256,1024]{1,0:T(8,128)(2,1)S(1)} %get-tuple-element.122), channel_id=1, source_target_pairs={{7,5},{6,4},{5,3},{4,2},{15,13},{14,12},{13,11},{12,10},{23,21},{2... | collective-permute-start | bytes 1572872 | tf_op jit(solution)/shard_map/ppermute | solution.py:586
  174.0 19.9 %collective-permute-start.15 = (bf16[128,2048]{1,0:T(8,128)(2,1)}, bf16[128,2048]{1,0:T(8,128)(2,1)S(1)}, u32[]{:S(2)}, u32[]{:S(2)}) collective-permute-start(bf16[128,2048]{1,0:T(8,128)(2,1)} %get-tuple-element.114), channel_id=1, source_target_pairs={{0,2},{1,3},{2,4},{3,5},{8,10},{9,11},{10,12},{11,13},{16,18},{17,... | collective-permute-start | bytes 1572872 | tf_op jit(solution)/shard_map/ppermute | solution.py:586
  178.4 15.6 %collective-permute-start.16 = (bf16[128,2048]{1,0:T(8,128)(2,1)S(1)}, bf16[128,2048]{1,0:T(8,128)(2,1)S(1)}, u32[]{:S(2)}, u32[]{:S(2)}) collective-permute-start(bf16[128,2048]{1,0:T(8,128)(2,1)S(1)} %get-tuple-element.115), channel_id=1, source_target_pairs={{7,5},{6,4},{5,3},{4,2},{15,13},{14,12},{13,11},{12,10},{23,21},{2... | collective-permute-start | bytes 1572872 | tf_op jit(solution)/shard_map/ppermute | solution.py:586
  185.6 19.5 %collective-permute-start.24 = (bf16[256,1024]{1,0:T(8,128)(2,1)S(1)}, bf16[256,1024]{1,0:T(8,128)(2,1)S(1)}, u32[]{:S(2)}, u32[]{:S(2)}) collective-permute-start(bf16[256,1024]{1,0:T(8,128)(2,1)S(1)} %get-tuple-element.123), channel_id=1, source_target_pairs={{0,2},{1,3},{2,4},{3,5},{4,6},{5,7},{8,10},{9,11},{10,12},{11,13},... | collective-permute-start | bytes 1572872 | tf_op jit(solution)/shard_map/ppermute | solution.py:586
  190.3 14.9 %collective-permute-start.25 = (bf16[256,1024]{1,0:T(8,128)(2,1)S(1)}, bf16[256,1024]{1,0:T(8,128)(2,1)S(1)}, u32[]{:S(2)}, u32[]{:S(2)}) collective-permute-start(bf16[256,1024]{1,0:T(8,128)(2,1)S(1)} %get-tuple-element.124), channel_id=1, source_target_pairs={{7,5},{6,4},{5,3},{4,2},{3,1},{2,0},{15,13},{14,12},{13,11},{12,10... | collective-permute-start | bytes 1572872 | tf_op jit(solution)/shard_map/ppermute | solution.py:586
  195.9 19.6 %collective-permute-start.17 = (bf16[128,2048]{1,0:T(8,128)(2,1)S(1)}, bf16[128,2048]{1,0:T(8,128)(2,1)S(1)}, u32[]{:S(2)}, u32[]{:S(2)}) collective-permute-start(bf16[128,2048]{1,0:T(8,128)(2,1)S(1)} %get-tuple-element.116), channel_id=1, source_target_pairs={{0,2},{1,3},{2,4},{3,5},{4,6},{5,7},{8,10},{9,11},{10,12},{11,13},... | collective-permute-start | bytes 1572872 | tf_op jit(solution)/shard_map/ppermute | solution.py:586
  200.3 15.2 %collective-permute-start.18 = (bf16[128,2048]{1,0:T(8,128)(2,1)S(1)}, bf16[128,2048]{1,0:T(8,128)(2,1)S(1)}, u32[]{:S(2)}, u32[]{:S(2)}) collective-permute-start(bf16[128,2048]{1,0:T(8,128)(2,1)S(1)} %get-tuple-element.117), channel_id=1, source_target_pairs={{7,5},{6,4},{5,3},{4,2},{3,1},{2,0},{15,13},{14,12},{13,11},{12,10... | collective-permute-start | bytes 1572872 | tf_op jit(solution)/shard_map/ppermute | solution.py:586
  209.3 14.2 %collective-permute-start.26 = (bf16[256,1024]{1,0:T(8,128)(2,1)S(1)}, bf16[256,1024]{1,0:T(8,128)(2,1)S(1)}, u32[]{:S(2)}, u32[]{:S(2)}) collective-permute-start(bf16[256,1024]{1,0:T(8,128)(2,1)S(1)} %get-tuple-element.125), channel_id=1, source_target_pairs={{0,24},{8,16},{16,8},{24,0},{1,25},{9,17},{17,9},{25,1},{2,26},{10... | collective-permute-start | bytes 1572872 | tf_op jit(solution)/shard_map/ppermute | solution.py:592
  218.4 15.1 %collective-permute-start.19 = (bf16[128,2048]{1,0:T(8,128)(2,1)S(1)}, bf16[128,2048]{1,0:T(8,128)(2,1)S(1)}, u32[]{:S(2)}, u32[]{:S(2)}) collective-permute-start(bf16[128,2048]{1,0:T(8,128)(2,1)S(1)} %get-tuple-element.118), channel_id=1, source_target_pairs={{0,24},{8,16},{16,8},{24,0},{1,25},{9,17},{17,9},{25,1},{2,26},{10... | collective-permute-start | bytes 1572872 | tf_op jit(solution)/shard_map/ppermute | solution.py:592

commit v10 on v7

--- a/solution.py
+++ b/solution.py
@@ -375,7 +375,7 @@
 
 def fold(places, part, came):
     _, rows, columns = part.shape
-    tile = min(64, rows)
+    tile = min(rows, max(8, 131072 // columns))
 
     def body(info, *refs):
         for k in range(2):
@@ -406,7 +406,7 @@
 
 def update(replica, weight, moment, part, came):
     _, rows, columns = moment.shape
-    tile = min(64, rows)
+    tile = min(rows, max(8, 131072 // columns))
     steps = rows // tile
 
     def body(info, weight_ref, moment_ref, part_ref, right_ref, left_ref, fresh_ref, out_ref):

time: 234 us -> 231 us (0.987)
  Pallas kernels: 136 us -> 131 us
  waiting for transfers between devices: 46.4 us -> 49.5 us
    ppermute x6, waiting for transfers between devices: 18.3 us -> 22.5 us  [on_device(): lax.ppermute(to_right, 'dp', right)]
    pallas_call x6, Pallas kernels: 17.7 us -> 14.1 us  [fold(): pl.pallas_call(body, grid_spec=pltpu.PrefetchScalarGridSpec(num_scalar_pr...]
  transfers between devices with their start and end apart: 27 -> 27, of which waited for: 10 -> 10; matrix products, arithmetic and copies ran while one was open for 1% -> 1% of each run, Pallas kernels for 53% -> 51%
where the time goes in v10:
time: 231 us; the launch traced here: 230 us
  Pallas kernels  131 us (57%)
  waiting for transfers between devices  49.5 us (21%)
  starting transfers between devices  43.4 us (19%)
  other arithmetic  2.67 us (1%)
  local copies, waits for them, and re-layouts  2.54 us (1%)
    pallas_call x8, Pallas kernels, chain_step(): pl.pallas_call(body, grid_spec=pltpu.PrefetchScalarGridSpec(num_scalar_pr...  44 us
    pallas_call x3, Pallas kernels, forward(): pl.pallas_call(body, grid_spec=pltpu.PrefetchScalarGridSpec(num_scalar_pr...  34.4 us
    pallas_call x4, Pallas kernels, weight_gradient(): pl.pallas_call(body, grid_spec=pltpu.PrefetchScalarGridSpec(num_scalar_pr...  25 us
    ppermute x6, waiting for transfers between devices, on_device(): lax.ppermute(to_right, 'dp', right)  22.5 us
    ppermute x6, starting transfers between devices, on_device(): lax.ppermute(to_right, 'dp', right)  21.7 us
    pallas_call x6, Pallas kernels, fold(): pl.pallas_call(body, grid_spec=pltpu.PrefetchScalarGridSpec(num_scalar_pr...  14.1 us
    ppermute x10, waiting for transfers between devices, hop(): return lax.ppermute(value, 'section', pairs) if pairs else None  14 us
    ppermute x2, waiting for transfers between devices, finish(): lax.ppermute(fresh, 'section', [(i, last - i) for i in range(sections)])  12.9 us
  transfers between devices with their start and end apart: 27, of which 10 were waited for; matrix products, arithmetic and copies ran while one was open for 1% of the time, Pallas kernels for 51%

profile of v10, /device:TPU:0, one launch (start us, length us, event | category | flops | bytes accessed | tf_op | source)
XLA Modules:
  0.0 230.0 jit_solution(18325467438107373097)
XLA Ops:
  0.7 2.3 slice_bitcast_fusion
  2.9 3.9 %collective-permute-start = (bf16[4,128,1024]{2,1,0:T(8,128)(2,1)}, bf16[4,128,1024]{2,1,0:T(8,128)(2,1)}, u32[]{:S(2)}, u32[]{:S(2)}) collective-permute-start(bf16[4,128,1024]{2,1,0:T(8,128)(2,1)} %slice_bitcast_fusion), channel_id=1, source_target_pairs={{0,24},{8,16},{16,8},{24,0},{1,25},{9,17},{17,9},{25,1},{2,26},{10... | collective-permute-start | bytes 3145736 | tf_op jit(solution)/shard_map/ppermute | solution.py:457
  6.9 11.5 %forward.3 = (bf16[2,2,256,1024]{3,2,1,0:T(8,128)(2,1)}, bf16[2,2,256,2048]{3,2,1,0:T(8,128)(2,1)}, bf16[2,256,2048]{2,1,0:T(8,128)(2,1)S(1)}, bf16[2,256,1024]{2,1,0:T(8,128)(2,1)S(1)}, f32[2,256,1]{2,1,0:T(8,128)S(1)}) custom-call(s32[4]{0:T(128)S(1)} %stack.93.info_ref, s32[2,4]{1,0:T(2,128)S(1)} %copy-done.14, bf16[2,1,4,128,1024]{4,3,2,1,0:T(8,128)(2,1)} %refs_3_.3, ...), custom_call_target="tpu_custom_call" | custom-call | flops 1000 | bytes 1000 | tf_op jit(solution)/shard_map/forward/pallas_call | solution.py:118
  18.6 8.8 %chain.8 = (bf16[256,1024]{1,0:T(8,128)(2,1)S(1)}, bf16[3,256,2048]{2,1,0:T(8,128)(2,1)}, bf16[3,256,1024]{2,1,0:T(8,128)(2,1)}) custom-call(s32[32]{0:T(128)S(1)} %reshape.15.info, bf16[2,4,128,1024]{3,2,1,0:T(8,128)(2,1)} %refs_2_.5, bf16[2,256,1024]{2,1,0:T(8,128)(2,1)S(1)} %get-tuple-element.68.y_ref, f32[2,256,1]{2,1,0:T(8,128)S(1)} %get-tuple-element.69.r_ref, ...), custom_call_target="tpu_custom_call" | custom-call | flops 1000 | bytes 1000 | tf_op jit(solution)/shard_map/chain/pallas_call | solution.py:213
  27.4 1.3 collective-permute-start.2
  28.8 1.3 collective-permute-start.3
  30.1 8.8 %chain.9 = (bf16[256,1024]{1,0:T(8,128)(2,1)S(1)}, bf16[3,256,2048]{2,1,0:T(8,128)(2,1)}, bf16[3,256,1024]{2,1,0:T(8,128)(2,1)}) custom-call(s32[32]{0:T(128)S(1)} %reshape.15.info, bf16[2,4,128,1024]{3,2,1,0:T(8,128)(2,1)} %refs_2_.5, bf16[2,256,1024]{2,1,0:T(8,128)(2,1)S(1)} %get-tuple-element.68.y_ref, ...), custom_call_target="tpu_custom_call", output_to_operand_aliasing={{1}: (7, {}), {2}: (8, {})} | custom-call | flops 1000 | bytes 1000 | tf_op jit(solution)/shard_map/chain/pallas_call | solution.py:213
  38.9 1.3 collective-permute-start.1
  40.2 1.3 collective-permute-start.6
  41.6 11.5 %forward.4 = (bf16[2,2,256,1024]{3,2,1,0:T(8,128)(2,1)}, bf16[2,2,256,2048]{3,2,1,0:T(8,128)(2,1)}, bf16[2,256,2048]{2,1,0:T(8,128)(2,1)S(1)}, bf16[2,256,1024]{2,1,0:T(8,128)(2,1)S(1)}, f32[2,256,1]{2,1,0:T(8,128)S(1)}) custom-call(s32[4]{0:T(128)S(1)} %stack.92.info_ref, s32[2,4]{1,0:T(2,128)S(1)} %copy-done.14, ...), custom_call_target="tpu_custom_call", output_to_operand_aliasing={{0}: (8, {}), {1}: (9, {})} | custom-call | flops 1000 | bytes 1000 | tf_op jit(solution)/shard_map/forward/pallas_call | solution.py:118
  53.1 3.3 %chain.10 = (bf16[256,1024]{1,0:T(8,128)(2,1)S(1)}, bf16[3,256,2048]{2,1,0:T(8,128)(2,1)}, bf16[3,256,1024]{2,1,0:T(8,128)(2,1)}) custom-call(s32[32]{0:T(128)S(1)} %reshape.15.info, bf16[256,1024]{1,0:T(8,128)(2,1)S(1)} %collective-permute-done.2.e_ref, bf16[2,256,1024]{2,1,0:T(8,128)(2,1)S(1)} %copy-done.3, ...), custom_call_target="tpu_custom_call", output_to_operand_aliasing={{1}: (7, {}), {2}: (8, {})} | custom-call | flops 1000 | bytes 1000 | tf_op jit(solution)/shard_map/chain/pallas_call | solution.py:213
  57.2 3.1 %chain.11 = (bf16[256,1024]{1,0:T(8,128)(2,1)S(1)}, bf16[3,256,2048]{2,1,0:T(8,128)(2,1)}, bf16[3,256,1024]{2,1,0:T(8,128)(2,1)}) custom-call(s32[32]{0:T(128)S(1)} %reshape.15.info, bf16[256,1024]{1,0:T(8,128)(2,1)S(1)} %collective-permute-done.1.e_ref, bf16[2,256,1024]{2,1,0:T(8,128)(2,1)S(1)} %copy-done.3, ...), custom_call_target="tpu_custom_call", output_to_operand_aliasing={{1}: (7, {}), {2}: (8, {})} | custom-call | flops 1000 | bytes 1000 | tf_op jit(solution)/shard_map/chain/pallas_call | solution.py:213
  61.2 3.2 %chain.12 = (bf16[256,1024]{1,0:T(8,128)(2,1)}, bf16[3,256,2048]{2,1,0:T(8,128)(2,1)}, bf16[3,256,1024]{2,1,0:T(8,128)(2,1)}) custom-call(s32[32]{0:T(128)S(1)} %reshape.15.info, bf16[256,1024]{1,0:T(8,128)(2,1)S(1)} %collective-permute-done.5.e_ref, ...), custom_call_target="tpu_custom_call", output_to_operand_aliasing={{1}: (7, {}), {2}: (8, {})} | custom-call | flops 1000 | bytes 1000 | tf_op jit(solution)/shard_map/chain/pallas_call | solution.py:213
  64.4 1.3 collective-permute-start.8
  65.7 3.2 %chain.13 = (bf16[256,1024]{1,0:T(8,128)(2,1)}, bf16[3,256,2048]{2,1,0:T(8,128)(2,1)}, bf16[3,256,1024]{2,1,0:T(8,128)(2,1)}) custom-call(s32[32]{0:T(128)S(1)} %reshape.15.info, bf16[256,1024]{1,0:T(8,128)(2,1)S(1)} %collective-permute-done.4.e_ref, ...), custom_call_target="tpu_custom_call", output_to_operand_aliasing={{1}: (7, {}), {2}: (8, {})} | custom-call | flops 1000 | bytes 1000 | tf_op jit(solution)/shard_map/chain/pallas_call | solution.py:213
  72.9 11.5 %forward.5 = (bf16[1,2,256,1024]{3,2,1,0:T(8,128)(2,1)}, bf16[1,2,256,2048]{3,2,1,0:T(8,128)(2,1)}, bf16[2,256,2048]{2,1,0:T(8,128)(2,1)S(1)}, bf16[2,256,1024]{2,1,0:T(8,128)(2,1)S(1)}, f32[2,256,1]{2,1,0:T(8,128)S(1)}) custom-call(s32[4]{0:T(128)S(1)} %copy-done.15, s32[2,4]{1,0:T(2,128)S(1)} %copy-done.14, ...), custom_call_target="tpu_custom_call" | custom-call | flops 1000 | bytes 1000 | tf_op jit(solution)/shard_map/forward/pallas_call | solution.py:118
  84.4 6.0 %collective-permute-done.8.e_ref = bf16[256,1024]{1,0:T(8,128)(2,1)S(1)} collective-permute-done((bf16[256,1024]{1,0:T(8,128)(2,1)}, bf16[256,1024]{1,0:T(8,128)(2,1)S(1)}, u32[]{:S(2)}, u32[]{:S(2)}) %collective-permute-start.8) | collective-permute-done | bytes 524320 | tf_op jit(solution)/shard_map/ppermute | solution.py:455
  90.4 6.8 %chain.14 = (bf16[256,1024]{1,0:T(8,128)(2,1)}, bf16[3,256,2048]{2,1,0:T(8,128)(2,1)}, bf16[3,256,1024]{2,1,0:T(8,128)(2,1)}) custom-call(s32[32]{0:T(128)S(1)} %reshape.15.info, bf16[256,1024]{1,0:T(8,128)(2,1)S(1)} %collective-permute-done.8.e_ref, ...), custom_call_target="tpu_custom_call", output_to_operand_aliasing={{1}: (7, {}), {2}: (8, {})} | custom-call | flops 1000 | bytes 1000 | tf_op jit(solution)/shard_map/chain/pallas_call | solution.py:213
  97.1 3.7 %collective-permute-done.7.e_ref = bf16[256,1024]{1,0:T(8,128)(2,1)S(1)} collective-permute-done((bf16[256,1024]{1,0:T(8,128)(2,1)}, bf16[256,1024]{1,0:T(8,128)(2,1)S(1)}, u32[]{:S(2)}, u32[]{:S(2)}) %collective-permute-start.7) | collective-permute-done | bytes 524320 | tf_op jit(solution)/shard_map/ppermute | solution.py:455
  100.8 6.8 %chain.15 = (bf16[256,1024]{1,0:T(8,128)(2,1)}, bf16[3,256,2048]{2,1,0:T(8,128)(2,1)}, bf16[3,256,1024]{2,1,0:T(8,128)(2,1)}) custom-call(s32[32]{0:T(128)S(1)} %reshape.15.info, bf16[256,1024]{1,0:T(8,128)(2,1)S(1)} %collective-permute-done.7.e_ref, ...), custom_call_target="tpu_custom_call", output_to_operand_aliasing={{1}: (7, {}), {2}: (8, {})} | custom-call | flops 1000 | bytes 1000 | tf_op jit(solution)/shard_map/chain/pallas_call | solution.py:213
  107.7 4.2 %collective-permute-done.9 = bf16[256,1024]{1,0:T(8,128)(2,1)S(1)} collective-permute-done((bf16[256,1024]{1,0:T(8,128)(2,1)}, bf16[256,1024]{1,0:T(8,128)(2,1)S(1)}, u32[]{:S(2)}, u32[]{:S(2)}) %collective-permute-start.9) | collective-permute-done | bytes 524320 | tf_op jit(solution)/shard_map/ppermute | solution.py:455
  112.1 7.3 %home.1 = (bf16[2,256,2048]{2,1,0:T(8,128)(2,1)}, bf16[2,256,1024]{2,1,0:T(8,128)(2,1)}) custom-call(s32[1]{0:T(128)} %bitcast.9.info, bf16[256,1024]{1,0:T(8,128)(2,1)S(1)} %get-tuple-element.141.refs_0_, bf16[256,1024]{1,0:T(8,128)(2,1)S(1)} %get-tuple-element.140.refs_1_, bf16[2,4,128,1024]{3,2,1,0:T(8,128)(2,1)} %refs_2_.5, ...), custom_call_target="tpu_custom_call" | custom-call | flops 1000 | bytes 1000 | tf_op jit(solution)/shard_map/home/pallas_call | solution.py:267
  119.4 6.0 %weights.4.refs_10_ = bf16[4,256,1024]{2,1,0:T(8,128)(2,1)} custom-call(s32[1]{0:T(128)} %bitcast.10.info, bf16[2,2,256,2048]{3,2,1,0:T(8,128)(2,1)} %get-tuple-element.108.refs_0_, bf16[3,256,1024]{2,1,0:T(8,128)(2,1)} %get-tuple-element.109.refs_1_, bf16[1,2,256,2048]{3,2,1,0:T(8,128)(2,1)} %get-tuple-element.110.refs_2_, ...), custom_call_target="tpu_custom_call" | custom-call | flops 1000 | bytes 1000 | tf_op jit(solution)/shard_map/weights/pallas_call | solution.py:364
  125.4 6.2 %weights.5.refs_5_ = bf16[4,128,2048]{2,1,0:T(8,128)(2,1)} custom-call(s32[1]{0:T(128)} %bitcast.10.info, bf16[2,2,256,1024]{3,2,1,0:T(8,128)(2,1)} %get-tuple-element.74.rest_2_.refs_0_.refs_1_.refs_2_.refs_3_, bf16[2,2,256,1024]{3,2,1,0:T(8,128)(2,1)} %get-tuple-element.74.rest_2_.refs_0_.refs_1_.refs_2_.refs_3_, ...), custom_call_target="tpu_custom_call" | custom-call | flops 1000 | bytes 1000 | tf_op jit(solution)/shard_map/weights/pallas_call | solution.py:364
  132.1 6.0 %weights.6.refs_11_.refs_0_.refs_1_.part_ref = bf16[4,256,1024]{2,1,0:T(8,128)(2,1)} custom-call(s32[1]{0:T(128)} %bitcast.2.info, bf16[2,2,256,2048]{3,2,1,0:T(8,128)(2,1)} %get-tuple-element.108.refs_0_, bf16[3,256,1024]{2,1,0:T(8,128)(2,1)} %get-tuple-element.109.refs_1_, bf16[1,2,256,2048]{3,2,1,0:T(8,128)(2,1)} %get-tuple-element.110.refs_2_, ...), custom_call_target="tpu_custom_call" | custom-call | flops 1000 | bytes 1000 | tf_op jit(solution)/shard_map/weights/pallas_call | solution.py:364
  138.1 2.5 %fold.9 = (bf16[256,1024]{1,0:T(8,128)(2,1)}, bf16[256,1024]{1,0:T(8,128)(2,1)S(1)}) custom-call(s32[2]{0:T(128)S(1)} %pad_add_fusion.4.info, bf16[4,256,1024]{2,1,0:T(8,128)(2,1)} %weights.6.refs_11_.refs_0_.refs_1_.part_ref, bf16[4,256,1024]{2,1,0:T(8,128)(2,1)} %weights.6.refs_11_.refs_0_.refs_1_.part_ref), custom_call_target="tpu_custom_call" | custom-call | flops 1000 | bytes 1000 | tf_op jit(solution)/shard_map/fold/pallas_call | solution.py:388
  140.6 3.5 %collective-permute-start.20 = (bf16[256,1024]{1,0:T(8,128)(2,1)}, bf16[256,1024]{1,0:T(8,128)(2,1)S(1)}, u32[]{:S(2)}, u32[]{:S(2)}) collective-permute-start(bf16[256,1024]{1,0:T(8,128)(2,1)} %get-tuple-element.119), channel_id=1, source_target_pairs={{0,2},{1,3},{8,10},{9,11},{16,18},{17,19},{24,26},{25,27}} | collective-permute-start | bytes 1572872 | tf_op jit(solution)/shard_map/ppermute | solution.py:571
  144.9 6.7 %weights.7.refs_0_.refs_1_.part_ref = bf16[4,128,2048]{2,1,0:T(8,128)(2,1)} custom-call(s32[1]{0:T(128)} %bitcast.2.info, bf16[2,2,256,1024]{3,2,1,0:T(8,128)(2,1)} %get-tuple-element.74.rest_2_.refs_0_.refs_1_.refs_2_.refs_3_, bf16[2,2,256,1024]{3,2,1,0:T(8,128)(2,1)} %get-tuple-element.74.rest_2_.refs_0_.refs_1_.refs_2_.refs_3_, ...), custom_call_target="tpu_custom_call" | custom-call | flops 1000 | bytes 1000 | tf_op jit(solution)/shard_map/weights/pallas_call | solution.py:364
  151.6 2.5 %fold.6 = (bf16[128,2048]{1,0:T(8,128)(2,1)}, bf16[128,2048]{1,0:T(8,128)(2,1)S(1)}) custom-call(s32[2]{0:T(128)S(1)} %pad_add_fusion.4.info, bf16[4,128,2048]{2,1,0:T(8,128)(2,1)} %weights.7.refs_0_.refs_1_.part_ref, bf16[4,128,2048]{2,1,0:T(8,128)(2,1)} %weights.7.refs_0_.refs_1_.part_ref), custom_call_target="tpu_custom_call" | custom-call | flops 1000 | bytes 1000 | tf_op jit(solution)/shard_map/fold/pallas_call | solution.py:388
  154.1 1.3 collective-permute-start.13
  156.2 2.6 %fold.10 = (bf16[256,1024]{1,0:T(8,128)(2,1)}, bf16[256,1024]{1,0:T(8,128)(2,1)S(1)}) custom-call(s32[2]{0:T(128)S(1)} %pad_add_fusion.3.info, bf16[4,256,1024]{2,1,0:T(8,128)(2,1)} %weights.6.refs_11_.refs_0_.refs_1_.part_ref, bf16[4,256,1024]{2,1,0:T(8,128)(2,1)} %weights.6.refs_11_.refs_0_.refs_1_.part_ref, ...), custom_call_target="tpu_custom_call" | custom-call | flops 1000 | bytes 1000 | tf_op jit(solution)/shard_map/fold/pallas_call | solution.py:388
  158.8 4.0 %collective-permute-start.22 = (bf16[256,1024]{1,0:T(8,128)(2,1)}, bf16[256,1024]{1,0:T(8,128)(2,1)S(1)}, u32[]{:S(2)}, u32[]{:S(2)}) collective-permute-start(bf16[256,1024]{1,0:T(8,128)(2,1)} %get-tuple-element.121), channel_id=1, source_target_pairs={{0,2},{1,3},{2,4},{3,5},{8,10},{9,11},{10,12},{11,13},{16,18},{17,... | collective-permute-start | bytes 1572872 | tf_op jit(solution)/shard_map/ppermute | solution.py:571
  163.5 4.5 %collective-permute-done.13.refs_2_ = bf16[128,2048]{1,0:T(8,128)(2,1)S(1)} collective-permute-done((bf16[128,2048]{1,0:T(8,128)(2,1)}, bf16[128,2048]{1,0:T(8,128)(2,1)S(1)}, u32[]{:S(2)}, u32[]{:S(2)}) %collective-permute-start.13) | collective-permute-done | bytes 524320 | tf_op jit(solution)/shard_map/ppermute | solution.py:571
  167.9 2.6 %fold.7 = (bf16[128,2048]{1,0:T(8,128)(2,1)}, bf16[128,2048]{1,0:T(8,128)(2,1)S(1)}) custom-call(s32[2]{0:T(128)S(1)} %pad_add_fusion.3.info, bf16[4,128,2048]{2,1,0:T(8,128)(2,1)} %weights.7.refs_0_.refs_1_.part_ref, bf16[4,128,2048]{2,1,0:T(8,128)(2,1)} %weights.7.refs_0_.refs_1_.part_ref, bf16[128,2048]{1,0:T(8,128)(2,1)S(1)} %collective-permute-done.13.refs_2_, ...), custom_call_target="tpu_custom_call" | custom-call | flops 1000 | bytes 1000 | tf_op jit(solution)/shard_map/fold/pallas_call | solution.py:388
  170.5 4.3 %collective-permute-start.15 = (bf16[128,2048]{1,0:T(8,128)(2,1)}, bf16[128,2048]{1,0:T(8,128)(2,1)S(1)}, u32[]{:S(2)}, u32[]{:S(2)}) collective-permute-start(bf16[128,2048]{1,0:T(8,128)(2,1)} %get-tuple-element.114), channel_id=1, source_target_pairs={{0,2},{1,3},{2,4},{3,5},{8,10},{9,11},{10,12},{11,13},{16,18},{17,... | collective-permute-start | bytes 1572872 | tf_op jit(solution)/shard_map/ppermute | solution.py:571
  175.6 3.6 %collective-permute-done.22.refs_2_ = bf16[256,1024]{1,0:T(8,128)(2,1)S(1)} collective-permute-done((bf16[256,1024]{1,0:T(8,128)(2,1)}, bf16[256,1024]{1,0:T(8,128)(2,1)S(1)}, u32[]{:S(2)}, u32[]{:S(2)}) %collective-permute-start.22) | collective-permute-done | bytes 524320 | tf_op jit(solution)/shard_map/ppermute | solution.py:571
  179.2 2.0 fold.11
  181.1 4.3 %collective-permute-start.24 = (bf16[256,1024]{1,0:T(8,128)(2,1)S(1)}, bf16[256,1024]{1,0:T(8,128)(2,1)S(1)}, u32[]{:S(2)}, u32[]{:S(2)}) collective-permute-start(bf16[256,1024]{1,0:T(8,128)(2,1)S(1)} %get-tuple-element.123), channel_id=1, source_target_pairs={{0,2},{1,3},{2,4},{3,5},{4,6},{5,7},{8,10},{9,11},{10,12},{11,13},... | collective-permute-start | bytes 1572872 | tf_op jit(solution)/shard_map/ppermute | solution.py:571
  185.5 1.3 collective-permute-start.25
  186.8 3.6 %collective-permute-done.15.refs_2_ = bf16[128,2048]{1,0:T(8,128)(2,1)S(1)} collective-permute-done((bf16[128,2048]{1,0:T(8,128)(2,1)}, bf16[128,2048]{1,0:T(8,128)(2,1)S(1)}, u32[]{:S(2)}, u32[]{:S(2)}) %collective-permute-start.15) | collective-permute-done | bytes 524320 | tf_op jit(solution)/shard_map/ppermute | solution.py:571
  190.4 2.0 fold.8
  192.4 4.3 %collective-permute-start.17 = (bf16[128,2048]{1,0:T(8,128)(2,1)S(1)}, bf16[128,2048]{1,0:T(8,128)(2,1)S(1)}, u32[]{:S(2)}, u32[]{:S(2)}) collective-permute-start(bf16[128,2048]{1,0:T(8,128)(2,1)S(1)} %get-tuple-element.116), channel_id=1, source_target_pairs={{0,2},{1,3},{2,4},{3,5},{4,6},{5,7},{8,10},{9,11},{10,12},{11,13},... | collective-permute-start | bytes 1572872 | tf_op jit(solution)/shard_map/ppermute | solution.py:571
  198.1 3.5 %collective-permute-done.24.right_ref = bf16[256,1024]{1,0:T(8,128)(2,1)S(1)} collective-permute-done((bf16[256,1024]{1,0:T(8,128)(2,1)S(1)}, bf16[256,1024]{1,0:T(8,128)(2,1)S(1)}, u32[]{:S(2)}, u32[]{:S(2)}) %collective-permute-start.24) | collective-permute-done | bytes 524320 | tf_op jit(solution)/shard_map/ppermute | solution.py:571
  201.5 3.0 %update.3 = (bf16[256,1024]{1,0:T(8,128)(2,1)S(1)}, f32[1,256,1024]{2,1,0:T(8,128)}) custom-call(s32[2]{0:T(128)S(1)} %pad_add_fusion.1.info, bf16[2,1,2048,1024]{3,2,1,0:T(8,128)(2,1)} %weight_ref.3, f32[1,256,1024]{2,1,0:T(8,128)} %moment_ref.3, bf16[4,256,1024]{2,1,0:T(8,128)(2,1)} %weights.6.refs_11_.refs_0_.refs_1_.part_ref, ...), custom_call_target="tpu_custom_call" | custom-call | flops 1000 | bytes 1000 | tf_op jit(solution)/shard_map/update/pallas_call | solution.py:418
  204.6 7.4 %collective-permute-done.17.right_ref = bf16[128,2048]{1,0:T(8,128)(2,1)S(1)} collective-permute-done((bf16[128,2048]{1,0:T(8,128)(2,1)S(1)}, bf16[128,2048]{1,0:T(8,128)(2,1)S(1)}, u32[]{:S(2)}, u32[]{:S(2)}) %collective-permute-start.17) | collective-permute-done | bytes 524320 | tf_op jit(solution)/shard_map/ppermute | solution.py:571
  211.9 3.0 %update.2 = (bf16[128,2048]{1,0:T(8,128)(2,1)S(1)}, f32[1,128,2048]{2,1,0:T(8,128)}) custom-call(s32[2]{0:T(128)S(1)} %pad_add_fusion.1.info, bf16[2,1,1024,2048]{3,2,1,0:T(8,128)(2,1)} %weight_ref.2, f32[1,128,2048]{2,1,0:T(8,128)} %moment_ref.2, bf16[4,128,2048]{2,1,0:T(8,128)(2,1)} %weights.7.refs_0_.refs_1_.part_ref, ...), custom_call_target="tpu_custom_call" | custom-call | flops 1000 | bytes 1000 | tf_op jit(solution)/shard_map/update/pallas_call | solution.py:418
  215.0 2.8 %collective-permute-done.26 = bf16[256,1024]{1,0:T(8,128)(2,1)S(1)} collective-permute-done((bf16[256,1024]{1,0:T(8,128)(2,1)S(1)}, bf16[256,1024]{1,0:T(8,128)(2,1)S(1)}, u32[]{:S(2)}, u32[]{:S(2)}) %collective-permute-start.26) | collective-permute-done | bytes 524320 | tf_op jit(solution)/shard_map/ppermute | solution.py:577
  218.8 10.2 %collective-permute-done.19 = bf16[128,2048]{1,0:T(8,128)(2,1)S(1)} collective-permute-done((bf16[128,2048]{1,0:T(8,128)(2,1)S(1)}, bf16[128,2048]{1,0:T(8,128)(2,1)S(1)}, u32[]{:S(2)}, u32[]{:S(2)}) %collective-permute-start.19) | collective-permute-done | bytes 524320 | tf_op jit(solution)/shard_map/ppermute | solution.py:577
  (86 shorter events, 12.9 us)
Async XLA Ops:
  0.6 6.2 %copy-start.16 = (pred[8]{0:T(512)(128)(4,1)S(1)}, pred[8]{0:T(512)(128)(4,1)}, u32[]{:S(2)}) copy-start(pred[8]{0:T(512)(128)(4,1)} %constant.61.clone) | copy-start | bytes 28
  0.6 6.2 %copy-start.18 = (s32[8]{0:T(128)S(1)}, s32[8]{0:T(128)}, u32[]{:S(2)}) copy-start(s32[8]{0:T(128)} %constant.62.clone) | copy-start | bytes 100
  0.7 6.2 %copy-start.14 = (s32[2,4]{1,0:T(2,128)S(1)}, s32[2,4]{1,0:T(2,128)}, u32[]{:S(2)}) copy-start(s32[2,4]{1,0:T(2,128)} %plan_ref.5) | copy-start | bytes 100
  2.9 38.6 %collective-permute-start = (bf16[4,128,1024]{2,1,0:T(8,128)(2,1)}, bf16[4,128,1024]{2,1,0:T(8,128)(2,1)}, u32[]{:S(2)}, u32[]{:S(2)}) collective-permute-start(bf16[4,128,1024]{2,1,0:T(8,128)(2,1)} %slice_bitcast_fusion), channel_id=1, source_target_pairs={{0,24},{8,16},{16,8},{24,0},{1,25},{9,17},{17,9},{25,1},{2,26},{10... | collective-permute-start | bytes 3145736 | tf_op jit(solution)/shard_map/ppermute | solution.py:457
  6.9 11.5 %copy-start.19 = (pred[8]{0:T(512)(128)(4,1)S(1)}, pred[8]{0:T(512)(128)(4,1)}, u32[]{:S(2)}) copy-start(pred[8]{0:T(512)(128)(4,1)} %constant.64.clone) | copy-start | bytes 28
  6.9 11.5 %copy-start.17 = (s32[8]{0:T(128)S(1)}, s32[8]{0:T(128)}, u32[]{:S(2)}) copy-start(s32[8]{0:T(128)} %constant.63.clone) | copy-start | bytes 100
  18.4 11.7 %copy-start.2 = (bf16[2,256,1024]{2,1,0:T(8,128)(2,1)}, bf16[2,256,1024]{2,1,0:T(8,128)(2,1)S(1)}, u32[]{:S(2)}) copy-start(bf16[2,256,1024]{2,1,0:T(8,128)(2,1)S(1)} %get-tuple-element.68.y_ref) | copy-start | bytes 3145732
  18.4 11.7 %copy-start.4 = (f32[2,256,1]{2,1,0:T(8,128)}, f32[2,256,1]{2,1,0:T(8,128)S(1)}, u32[]{:S(2)}) copy-start(f32[2,256,1]{2,1,0:T(8,128)S(1)} %get-tuple-element.69.r_ref) | copy-start | bytes 6148
  27.4 25.7 %collective-permute-start.2 = (bf16[256,1024]{1,0:T(8,128)(2,1)S(1)}, bf16[256,1024]{1,0:T(8,128)(2,1)S(1)}, u32[]{:S(2)}, u32[]{:S(2)}) collective-permute-start(bf16[256,1024]{1,0:T(8,128)(2,1)S(1)} %get-tuple-element.76), channel_id=1, source_target_pairs={{24,16},{0,8},{25,17},{1,9},{26,18},{2,10},{27,19},{3,11},{28,20},... | collective-permute-start | bytes 1572872 | tf_op jit(solution)/shard_map/ppermute | solution.py:455
  28.8 24.3 %collective-permute-start.3 = (bf16[256,1024]{1,0:T(8,128)(2,1)S(1)}, bf16[256,1024]{1,0:T(8,128)(2,1)S(1)}, u32[]{:S(2)}, u32[]{:S(2)}) collective-permute-start(bf16[256,1024]{1,0:T(8,128)(2,1)S(1)} %get-tuple-element.76), channel_id=1, source_target_pairs={{0,16},{1,17},{2,18},{3,19},{4,20},{5,21},{6,22},{7,23}} | collective-permute-start | bytes 1572872 | tf_op jit(solution)/shard_map/ppermute | solution.py:455
  38.9 18.3 %collective-permute-start.1 = (bf16[256,1024]{1,0:T(8,128)(2,1)S(1)}, bf16[256,1024]{1,0:T(8,128)(2,1)S(1)}, u32[]{:S(2)}, u32[]{:S(2)}) collective-permute-start(bf16[256,1024]{1,0:T(8,128)(2,1)S(1)} %get-tuple-element.75), channel_id=1, source_target_pairs={{24,16},{0,8},{25,17},{1,9},{26,18},{2,10},{27,19},{3,11},{28,20},... | collective-permute-start | bytes 1572872 | tf_op jit(solution)/shard_map/ppermute | solution.py:455
  40.2 20.9 %collective-permute-start.6 = (bf16[256,1024]{1,0:T(8,128)(2,1)S(1)}, bf16[256,1024]{1,0:T(8,128)(2,1)S(1)}, u32[]{:S(2)}, u32[]{:S(2)}) collective-permute-start(bf16[256,1024]{1,0:T(8,128)(2,1)S(1)} %get-tuple-element.75), channel_id=1, source_target_pairs={{0,16},{1,17},{2,18},{3,19},{4,20},{5,21},{6,22},{7,23}} | collective-permute-start | bytes 1572872 | tf_op jit(solution)/shard_map/ppermute | solution.py:455
  41.6 11.5 %copy-start.3 = (bf16[2,256,1024]{2,1,0:T(8,128)(2,1)S(1)}, bf16[2,256,1024]{2,1,0:T(8,128)(2,1)}, u32[]{:S(2)}) copy-start(bf16[2,256,1024]{2,1,0:T(8,128)(2,1)} %copy-done.2) | copy-start | bytes 3145732
  41.6 11.5 %copy-start.5 = (f32[2,256,1]{2,1,0:T(8,128)S(1)}, f32[2,256,1]{2,1,0:T(8,128)}, u32[]{:S(2)}) copy-start(f32[2,256,1]{2,1,0:T(8,128)} %copy-done.4) | copy-start | bytes 6148
  53.1 12.6 %copy-start = (bf16[2,256,2048]{2,1,0:T(8,128)(2,1)}, bf16[2,256,2048]{2,1,0:T(8,128)(2,1)S(1)}, u32[]{:S(2)}) copy-start(bf16[2,256,2048]{2,1,0:T(8,128)(2,1)S(1)} %get-tuple-element.83.slope_ref) | copy-start | bytes 6291460
  53.1 3.4 %copy-start.6 = (bf16[256,1024]{1,0:T(8,128)(2,1)}, bf16[256,1024]{1,0:T(8,128)(2,1)S(1)}, u32[]{:S(2)}) copy-start(bf16[256,1024]{1,0:T(8,128)(2,1)S(1)} %collective-permute-done.3.rest_3_) | copy-start | bytes 1572868
  56.5 3.8 %copy-start.10 = (bf16[256,1024]{1,0:T(8,128)(2,1)}, bf16[256,1024]{1,0:T(8,128)(2,1)S(1)}, u32[]{:S(2)}) copy-start(bf16[256,1024]{1,0:T(8,128)(2,1)S(1)} %get-tuple-element.99) | copy-start | bytes 1572868
  56.5 4.7 %collective-permute-start.5 = (bf16[256,1024]{1,0:T(8,128)(2,1)S(1)}, bf16[256,1024]{1,0:T(8,128)(2,1)S(1)}, u32[]{:S(2)}, u32[]{:S(2)}) collective-permute-start(bf16[256,1024]{1,0:T(8,128)(2,1)S(1)} %get-tuple-element.99), channel_id=1, source_target_pairs={{16,8},{8,16},{17,9},{9,17},{18,10},{10,18},{19,11},{11,19},{20,12... | collective-permute-start | bytes 1572872 | tf_op jit(solution)/shard_map/ppermute | solution.py:455
  60.3 4.1 %copy-start.12 = (bf16[256,1024]{1,0:T(8,128)(2,1)}, bf16[256,1024]{1,0:T(8,128)(2,1)S(1)}, u32[]{:S(2)}) copy-start(bf16[256,1024]{1,0:T(8,128)(2,1)S(1)} %get-tuple-element.102) | copy-start | bytes 1572868
  60.3 5.4 %collective-permute-start.4 = (bf16[256,1024]{1,0:T(8,128)(2,1)S(1)}, bf16[256,1024]{1,0:T(8,128)(2,1)S(1)}, u32[]{:S(2)}, u32[]{:S(2)}) collective-permute-start(bf16[256,1024]{1,0:T(8,128)(2,1)S(1)} %get-tuple-element.102), channel_id=1, source_target_pairs={{16,8},{8,16},{17,9},{9,17},{18,10},{10,18},{19,11},{11,19},{20,12... | collective-permute-start | bytes 1572872 | tf_op jit(solution)/shard_map/ppermute | solution.py:455
  61.2 3.2 %copy-start.8 = (bf16[256,1024]{1,0:T(8,128)(2,1)}, bf16[256,1024]{1,0:T(8,128)(2,1)S(1)}, u32[]{:S(2)}) copy-start(bf16[256,1024]{1,0:T(8,128)(2,1)S(1)} %collective-permute-done.6.rest_2_) | copy-start | bytes 1572868
  64.4 26.0 %collective-permute-start.8 = (bf16[256,1024]{1,0:T(8,128)(2,1)}, bf16[256,1024]{1,0:T(8,128)(2,1)S(1)}, u32[]{:S(2)}, u32[]{:S(2)}) collective-permute-start(bf16[256,1024]{1,0:T(8,128)(2,1)} %get-tuple-element.90), channel_id=1, source_target_pairs={{8,0},{9,1},{10,2},{11,3},{12,4},{13,5},{14,6},{15,7}} | collective-permute-start | bytes 1572872 | tf_op jit(solution)/shard_map/ppermute | solution.py:455
  65.7 7.1 %copy-start.15 = (s32[4]{0:T(128)S(1)}, s32[4]{0:T(128)}, u32[]{:S(2)}) copy-start(s32[4]{0:T(128)} %constant.65.clone.info_ref) | copy-start | bytes 52
  69.0 31.9 %collective-permute-start.7 = (bf16[256,1024]{1,0:T(8,128)(2,1)}, bf16[256,1024]{1,0:T(8,128)(2,1)S(1)}, u32[]{:S(2)}, u32[]{:S(2)}) collective-permute-start(bf16[256,1024]{1,0:T(8,128)(2,1)} %get-tuple-element.89), channel_id=1, source_target_pairs={{8,0},{9,1},{10,2},{11,3},{12,4},{13,5},{14,6},{15,7}} | collective-permute-start | bytes 1572872 | tf_op jit(solution)/shard_map/ppermute | solution.py:455
  70.2 37.4 %collective-permute-start.10 = (bf16[256,1024]{1,0:T(8,128)(2,1)}, bf16[256,1024]{1,0:T(8,128)(2,1)S(1)}, u32[]{:S(2)}, u32[]{:S(2)}) collective-permute-start(bf16[256,1024]{1,0:T(8,128)(2,1)} %get-tuple-element.89), channel_id=1, source_target_pairs={{16,0},{17,1},{18,2},{19,3},{20,4},{21,5},{22,6},{23,7}} | collective-permute-start | bytes 1572872 | tf_op jit(solution)/shard_map/ppermute | solution.py:455
  71.5 40.3 %collective-permute-start.9 = (bf16[256,1024]{1,0:T(8,128)(2,1)}, bf16[256,1024]{1,0:T(8,128)(2,1)S(1)}, u32[]{:S(2)}, u32[]{:S(2)}) collective-permute-start(bf16[256,1024]{1,0:T(8,128)(2,1)} %get-tuple-element.90), channel_id=1, source_target_pairs={{16,0},{17,1},{18,2},{19,3},{20,4},{21,5},{22,6},{23,7}} | collective-permute-start | bytes 1572872 | tf_op jit(solution)/shard_map/ppermute | solution.py:455
  72.9 17.5 %copy-start.1 = (bf16[2,256,2048]{2,1,0:T(8,128)(2,1)S(1)}, bf16[2,256,2048]{2,1,0:T(8,128)(2,1)}, u32[]{:S(2)}) copy-start(bf16[2,256,2048]{2,1,0:T(8,128)(2,1)} %copy-done) | copy-start | bytes 6291460
  100.8 11.1 %copy-start.7 = (bf16[256,1024]{1,0:T(8,128)(2,1)S(1)}, bf16[256,1024]{1,0:T(8,128)(2,1)}, u32[]{:S(2)}) copy-start(bf16[256,1024]{1,0:T(8,128)(2,1)} %copy-done.6) | copy-start | bytes 1572868
  100.8 11.1 %copy-start.9 = (bf16[256,1024]{1,0:T(8,128)(2,1)S(1)}, bf16[256,1024]{1,0:T(8,128)(2,1)}, u32[]{:S(2)}) copy-start(bf16[256,1024]{1,0:T(8,128)(2,1)} %copy-done.8) | copy-start | bytes 1572868
  100.8 11.1 %copy-start.11 = (bf16[256,1024]{1,0:T(8,128)(2,1)S(1)}, bf16[256,1024]{1,0:T(8,128)(2,1)}, u32[]{:S(2)}) copy-start(bf16[256,1024]{1,0:T(8,128)(2,1)} %copy-done.10) | copy-start | bytes 1572868
  100.8 11.1 %copy-start.13 = (bf16[256,1024]{1,0:T(8,128)(2,1)S(1)}, bf16[256,1024]{1,0:T(8,128)(2,1)}, u32[]{:S(2)}) copy-start(bf16[256,1024]{1,0:T(8,128)(2,1)} %copy-done.12) | copy-start | bytes 1572868
  125.4 6.7 %collective-permute-start.12 = (bf16[4,256,1024]{2,1,0:T(8,128)(2,1)}, bf16[4,256,1024]{2,1,0:T(8,128)(2,1)S(1)}, u32[]{:S(2)}, u32[]{:S(2)}) collective-permute-start(bf16[4,256,1024]{2,1,0:T(8,128)(2,1)} %weights.4.refs_10_), channel_id=1, source_target_pairs={{0,1},{1,0},{2,3},{3,2},{4,5},{5,4},{6,7},{7,6},{8,9},{9,8},{10,11... | collective-permute-start | bytes 6291464 | tf_op jit(solution)/shard_map/ppermute | solution.py:555
  131.6 13.2 %collective-permute-start.11 = (bf16[4,128,2048]{2,1,0:T(8,128)(2,1)}, bf16[4,128,2048]{2,1,0:T(8,128)(2,1)}, u32[]{:S(2)}, u32[]{:S(2)}) collective-permute-start(bf16[4,128,2048]{2,1,0:T(8,128)(2,1)} %weights.5.refs_5_), channel_id=1, source_target_pairs={{0,1},{1,0},{2,3},{3,2},{4,5},{5,4},{6,7},{7,6},{8,9},{9,8},{10,11... | collective-permute-start | bytes 6291464 | tf_op jit(solution)/shard_map/ppermute | solution.py:557
  140.6 15.5 %collective-permute-start.20 = (bf16[256,1024]{1,0:T(8,128)(2,1)}, bf16[256,1024]{1,0:T(8,128)(2,1)S(1)}, u32[]{:S(2)}, u32[]{:S(2)}) collective-permute-start(bf16[256,1024]{1,0:T(8,128)(2,1)} %get-tuple-element.119), channel_id=1, source_target_pairs={{0,2},{1,3},{8,10},{9,11},{16,18},{17,19},{24,26},{25,27}} | collective-permute-start | bytes 1572872 | tf_op jit(solution)/shard_map/ppermute | solution.py:571
  144.1 12.0 %collective-permute-start.21 = (bf16[256,1024]{1,0:T(8,128)(2,1)S(1)}, bf16[256,1024]{1,0:T(8,128)(2,1)S(1)}, u32[]{:S(2)}, u32[]{:S(2)}) collective-permute-start(bf16[256,1024]{1,0:T(8,128)(2,1)S(1)} %get-tuple-element.120), channel_id=1, source_target_pairs={{7,5},{6,4},{15,13},{14,12},{23,21},{22,20},{31,29},{30,28}} | collective-permute-start | bytes 1572872 | tf_op jit(solution)/shard_map/ppermute | solution.py:571
  154.1 13.9 %collective-permute-start.13 = (bf16[128,2048]{1,0:T(8,128)(2,1)}, bf16[128,2048]{1,0:T(8,128)(2,1)S(1)}, u32[]{:S(2)}, u32[]{:S(2)}) collective-permute-start(bf16[128,2048]{1,0:T(8,128)(2,1)} %get-tuple-element.112), channel_id=1, source_target_pairs={{0,2},{1,3},{8,10},{9,11},{16,18},{17,19},{24,26},{25,27}} | collective-permute-start | bytes 1572872 | tf_op jit(solution)/shard_map/ppermute | solution.py:571
  155.4 12.6 %collective-permute-start.14 = (bf16[128,2048]{1,0:T(8,128)(2,1)S(1)}, bf16[128,2048]{1,0:T(8,128)(2,1)S(1)}, u32[]{:S(2)}, u32[]{:S(2)}) collective-permute-start(bf16[128,2048]{1,0:T(8,128)(2,1)S(1)} %get-tuple-element.113), channel_id=1, source_target_pairs={{7,5},{6,4},{15,13},{14,12},{23,21},{22,20},{31,29},{30,28}} | collective-permute-start | bytes 1572872 | tf_op jit(solution)/shard_map/ppermute | solution.py:571
  158.8 20.4 %collective-permute-start.22 = (bf16[256,1024]{1,0:T(8,128)(2,1)}, bf16[256,1024]{1,0:T(8,128)(2,1)S(1)}, u32[]{:S(2)}, u32[]{:S(2)}) collective-permute-start(bf16[256,1024]{1,0:T(8,128)(2,1)} %get-tuple-element.121), channel_id=1, source_target_pairs={{0,2},{1,3},{2,4},{3,5},{8,10},{9,11},{10,12},{11,13},{16,18},{17,... | collective-permute-start | bytes 1572872 | tf_op jit(solution)/shard_map/ppermute | solution.py:571
  162.8 16.4 %collective-permute-start.23 = (bf16[256,1024]{1,0:T(8,128)(2,1)S(1)}, bf16[256,1024]{1,0:T(8,128)(2,1)S(1)}, u32[]{:S(2)}, u32[]{:S(2)}) collective-permute-start(bf16[256,1024]{1,0:T(8,128)(2,1)S(1)} %get-tuple-element.122), channel_id=1, source_target_pairs={{7,5},{6,4},{5,3},{4,2},{15,13},{14,12},{13,11},{12,10},{23,21},{2... | collective-permute-start | bytes 1572872 | tf_op jit(solution)/shard_map/ppermute | solution.py:571
  170.5 19.9 %collective-permute-start.15 = (bf16[128,2048]{1,0:T(8,128)(2,1)}, bf16[128,2048]{1,0:T(8,128)(2,1)S(1)}, u32[]{:S(2)}, u32[]{:S(2)}) collective-permute-start(bf16[128,2048]{1,0:T(8,128)(2,1)} %get-tuple-element.114), channel_id=1, source_target_pairs={{0,2},{1,3},{2,4},{3,5},{8,10},{9,11},{10,12},{11,13},{16,18},{17,... | collective-permute-start | bytes 1572872 | tf_op jit(solution)/shard_map/ppermute | solution.py:571
  174.8 15.6 %collective-permute-start.16 = (bf16[128,2048]{1,0:T(8,128)(2,1)S(1)}, bf16[128,2048]{1,0:T(8,128)(2,1)S(1)}, u32[]{:S(2)}, u32[]{:S(2)}) collective-permute-start(bf16[128,2048]{1,0:T(8,128)(2,1)S(1)} %get-tuple-element.115), channel_id=1, source_target_pairs={{7,5},{6,4},{5,3},{4,2},{15,13},{14,12},{13,11},{12,10},{23,21},{2... | collective-permute-start | bytes 1572872 | tf_op jit(solution)/shard_map/ppermute | solution.py:571
  181.1 20.4 %collective-permute-start.24 = (bf16[256,1024]{1,0:T(8,128)(2,1)S(1)}, bf16[256,1024]{1,0:T(8,128)(2,1)S(1)}, u32[]{:S(2)}, u32[]{:S(2)}) collective-permute-start(bf16[256,1024]{1,0:T(8,128)(2,1)S(1)} %get-tuple-element.123), channel_id=1, source_target_pairs={{0,2},{1,3},{2,4},{3,5},{4,6},{5,7},{8,10},{9,11},{10,12},{11,13},... | collective-permute-start | bytes 1572872 | tf_op jit(solution)/shard_map/ppermute | solution.py:571
  185.5 16.1 %collective-permute-start.25 = (bf16[256,1024]{1,0:T(8,128)(2,1)S(1)}, bf16[256,1024]{1,0:T(8,128)(2,1)S(1)}, u32[]{:S(2)}, u32[]{:S(2)}) collective-permute-start(bf16[256,1024]{1,0:T(8,128)(2,1)S(1)} %get-tuple-element.124), channel_id=1, source_target_pairs={{7,5},{6,4},{5,3},{4,2},{3,1},{2,0},{15,13},{14,12},{13,11},{12,10... | collective-permute-start | bytes 1572872 | tf_op jit(solution)/shard_map/ppermute | solution.py:571
  192.4 19.6 %collective-permute-start.17 = (bf16[128,2048]{1,0:T(8,128)(2,1)S(1)}, bf16[128,2048]{1,0:T(8,128)(2,1)S(1)}, u32[]{:S(2)}, u32[]{:S(2)}) collective-permute-start(bf16[128,2048]{1,0:T(8,128)(2,1)S(1)} %get-tuple-element.116), channel_id=1, source_target_pairs={{0,2},{1,3},{2,4},{3,5},{4,6},{5,7},{8,10},{9,11},{10,12},{11,13},... | collective-permute-start | bytes 1572872 | tf_op jit(solution)/shard_map/ppermute | solution.py:571
  196.7 15.2 %collective-permute-start.18 = (bf16[128,2048]{1,0:T(8,128)(2,1)S(1)}, bf16[128,2048]{1,0:T(8,128)(2,1)S(1)}, u32[]{:S(2)}, u32[]{:S(2)}) collective-permute-start(bf16[128,2048]{1,0:T(8,128)(2,1)S(1)} %get-tuple-element.117), channel_id=1, source_target_pairs={{7,5},{6,4},{5,3},{4,2},{3,1},{2,0},{15,13},{14,12},{13,11},{12,10... | collective-permute-start | bytes 1572872 | tf_op jit(solution)/shard_map/ppermute | solution.py:571
  204.5 13.2 %collective-permute-start.26 = (bf16[256,1024]{1,0:T(8,128)(2,1)S(1)}, bf16[256,1024]{1,0:T(8,128)(2,1)S(1)}, u32[]{:S(2)}, u32[]{:S(2)}) collective-permute-start(bf16[256,1024]{1,0:T(8,128)(2,1)S(1)} %get-tuple-element.125), channel_id=1, source_target_pairs={{0,24},{8,16},{16,8},{24,0},{1,25},{9,17},{17,9},{25,1},{2,26},{10... | collective-permute-start | bytes 1572872 | tf_op jit(solution)/shard_map/ppermute | solution.py:577
  214.9 14.0 %collective-permute-start.19 = (bf16[128,2048]{1,0:T(8,128)(2,1)S(1)}, bf16[128,2048]{1,0:T(8,128)(2,1)S(1)}, u32[]{:S(2)}, u32[]{:S(2)}) collective-permute-start(bf16[128,2048]{1,0:T(8,128)(2,1)S(1)} %get-tuple-element.118), channel_id=1, source_target_pairs={{0,24},{8,16},{16,8},{24,0},{1,25},{9,17},{17,9},{25,1},{2,26},{10... | collective-permute-start | bytes 1572872 | tf_op jit(solution)/shard_map/ppermute | solution.py:577
